TPU v7x, 32 devices: a whole 2x2x4 slice. The times are simulated.
32 devices in a mesh: dp: 16 (over z, x, core), ctx: 2 (over y).
Axes of the slice: x: 2, y: 2, z: 4, core: 2. Of those that a mesh axis runs over, the one named last changes fastest.
Arguments:
- inputs: bfloat16 [18688, 1024], P(('dp', 'ctx')), may hold values from -6 to 6
- cotangent: bfloat16 [18688, 1024], P(('dp', 'ctx')), may hold values from -6 to 6
- segment: int32 [18688], P(('dp', 'ctx')), may hold values from -1 to 1, as said below
- w_qkv: bfloat16 [8192, 384], P(('dp', 'ctx')), may hold values from -0.1875 to 0.1875
- b_query: bfloat16 [1024], P(('dp', 'ctx')), may hold values from -4 to 4
- b_value: bfloat16 [1024], P(('dp', 'ctx')), may hold values from -0.4375 to 0.4375
- w_out: bfloat16 [8192, 128], P(('dp', 'ctx')), may hold values from -6 to 6
- b_out: bfloat16 [1024], P(('dp', 'ctx')), may hold values from -4 to 4
- norm1_gain: bfloat16 [1024], P(('dp', 'ctx')), may hold values from 0.5 to 1.5
- norm1_shift: bfloat16 [1024], P(('dp', 'ctx')), may hold values from -4 to 4
- norm2_gain: bfloat16 [1024], P(('dp', 'ctx')), may hold values from 0.5 to 1.5
- norm2_shift: bfloat16 [1024], P(('dp', 'ctx')), may hold values from -4 to 4
- w_up: bfloat16 [8192, 512], P(('dp', 'ctx')), may hold values from -0.1875 to 0.1875
- b_up: bfloat16 [4096], P(('dp', 'ctx')), may hold values from -4 to 4
- w_down: bfloat16 [32768, 128], P(('dp', 'ctx')), may hold values from -0.1875 to 0.1875
- b_down: bfloat16 [1024], P(('dp', 'ctx')), may hold values from -4 to 4
Outputs:
- outputs: bfloat16 [18688, 1024], P(('dp', 'ctx'))
- input_grad: float32 [18688, 1024], P(('dp', 'ctx'))
- grad_w_qkv: float32 [8192, 384], P(('dp', 'ctx'))
- grad_b_query: float32 [1024], P(('dp', 'ctx'))
- grad_b_value: float32 [1024], P(('dp', 'ctx'))
- grad_w_out: float32 [8192, 128], P(('dp', 'ctx'))
- grad_b_out: float32 [1024], P(('dp', 'ctx'))
- grad_norm1_gain: float32 [1024], P(('dp', 'ctx'))
- grad_norm1_shift: float32 [1024], P(('dp', 'ctx'))
- grad_norm2_gain: float32 [1024], P(('dp', 'ctx'))
- grad_norm2_shift: float32 [1024], P(('dp', 'ctx'))
- grad_w_up: float32 [8192, 512], P(('dp', 'ctx'))
- grad_b_up: float32 [4096], P(('dp', 'ctx'))
- grad_w_down: float32 [32768, 128], P(('dp', 'ctx'))
- grad_b_down: float32 [1024], P(('dp', 'ctx'))
Inputs may be any that keep to these rules, and one draw needn't show every extreme that they name: `segment`: each block of 1168 consecutive token slots holds 2 images of 577 tokens each, numbered 0 to 1, their slots in a drawn order over the whole block; the remaining slots are padding with id -1.
All inputs are finite; a program needn't handle non-finite values.
Results may differ from a plain program's by a relative error of at most 0.024.
Values may be sent and summed in bfloat16 or wider, within the bound.
No kernel may reach another device: no remote copies, remote signals or barrier semaphores. Data moves between devices by JAX's collectives and lax.ppermute only.
A program may use at most 384 MiB of HBM per device.

v0:
```python
import math

import jax
import jax.numpy as jnp
from jax import lax
from jax.sharding import PartitionSpec as P

HD = 64


EPSILON = 1e-06


def layer_norm(value, gain, shift):
    center = value - jnp.mean(value, axis=-1, keepdims=True)
    variance = jnp.mean(center * center, axis=-1, keepdims=True)
    return center * lax.rsqrt(variance + EPSILON) * gain + shift


def gelu_exact(value):
    return jax.nn.gelu(value, approximate=False)


def matmul(left, right):
    return jnp.dot(left, right, preferred_element_type=jnp.float32)


def unfold(stored):
    return stored.reshape(stored.shape[0] // 8, stored.shape[1] * 8)


def refold(matrix):
    return matrix.reshape(matrix.shape[0] * 8, matrix.shape[1] // 8)


def on_device(
    inputs,
    cotangent,
    segment,
    w_qkv,
    b_query,
    b_value,
    w_out,
    b_out,
    norm1_gain,
    norm1_shift,
    norm2_gain,
    norm2_shift,
    w_up,
    b_up,
    w_down,
    b_down,
):
    gathered = (
        lax.all_gather(w_qkv, ("dp", "ctx"), axis=0, tiled=True),
        lax.all_gather(b_query, ("dp", "ctx"), axis=0, tiled=True),
        lax.all_gather(b_value, ("dp", "ctx"), axis=0, tiled=True),
        lax.all_gather(w_out, ("dp", "ctx"), axis=0, tiled=True),
        lax.all_gather(b_out, ("dp", "ctx"), axis=0, tiled=True),
        lax.all_gather(norm1_gain, ("dp", "ctx"), axis=0, tiled=True),
        lax.all_gather(norm1_shift, ("dp", "ctx"), axis=0, tiled=True),
        lax.all_gather(norm2_gain, ("dp", "ctx"), axis=0, tiled=True),
        lax.all_gather(norm2_shift, ("dp", "ctx"), axis=0, tiled=True),
        lax.all_gather(w_up, ("dp", "ctx"), axis=0, tiled=True),
        lax.all_gather(b_up, ("dp", "ctx"), axis=0, tiled=True),
        lax.all_gather(w_down, ("dp", "ctx"), axis=0, tiled=True),
        lax.all_gather(b_down, ("dp", "ctx"), axis=0, tiled=True),
    )
    (
        qkv_stored,
        query_bias,
        value_bias,
        out_stored,
        out_bias,
        gain_one,
        shift_one,
        gain_two,
        shift_two,
        up_stored,
        up_bias,
        down_stored,
        down_bias,
    ) = gathered
    qkv_weight = unfold(qkv_stored)
    out_weight = unfold(out_stored)
    up_weight = unfold(up_stored)
    down_weight = unfold(down_stored)
    first_gain = gain_one.astype(jnp.float32)
    first_shift = shift_one.astype(jnp.float32)
    second_gain = gain_two.astype(jnp.float32)
    second_shift = shift_two.astype(jnp.float32)
    row_count = inputs.shape[0]
    model_width = out_weight.shape[0]
    head_count = model_width // HD
    score_scale = 1.0 / math.sqrt(HD)
    values_in = inputs.astype(jnp.float32)
    normed1 = layer_norm(values_in, first_gain, first_shift).astype(jnp.bfloat16)
    joined = matmul(normed1, qkv_weight)
    queries = (joined[:, :model_width] + query_bias.astype(jnp.float32)).astype(jnp.bfloat16)
    key_rows = joined[:, model_width : 2 * model_width].astype(jnp.bfloat16)
    value_rows = (joined[:, 2 * model_width :] + value_bias.astype(jnp.float32)).astype(
        jnp.bfloat16
    )
    key_all, value_all, seg_all = (
        lax.all_gather(key_rows, "ctx", axis=0, tiled=True),
        lax.all_gather(value_rows, "ctx", axis=0, tiled=True),
        lax.all_gather(segment.astype(jnp.bfloat16), "ctx", axis=0, tiled=True),
    )
    key_count = key_all.shape[0]
    query_heads = queries.reshape(row_count, head_count, HD)
    key_heads = key_all.reshape(key_count, head_count, HD)
    value_heads = value_all.reshape(key_count, head_count, HD)
    own_seg = segment.astype(jnp.float32)
    group_seg = seg_all.astype(jnp.float32)
    same_seg = own_seg[:, None] == group_seg[None, :]

    def make_scores():
        raw = (
            jnp.einsum("qhd,khd->hqk", query_heads, key_heads, preferred_element_type=jnp.float32)
            * score_scale
        )
        return jnp.where(same_seg[None], raw, -1e30)

    scores = make_scores()
    row_max = jnp.max(scores, axis=-1, keepdims=True)
    expo = jnp.exp(scores - row_max)
    row_total = jnp.sum(expo, axis=-1, keepdims=True)
    probs_low = (expo / row_total).astype(jnp.bfloat16)
    log_total = row_max + jnp.log(row_total)
    mixed = jnp.einsum("hqk,khd->qhd", probs_low, value_heads, preferred_element_type=jnp.float32)
    attended = mixed.reshape(row_count, model_width).astype(jnp.bfloat16)
    middle = values_in + matmul(attended, out_weight) + out_bias.astype(jnp.float32)
    normed2 = layer_norm(middle, second_gain, second_shift).astype(jnp.bfloat16)
    hidden = matmul(normed2, up_weight) + up_bias.astype(jnp.float32)
    active = gelu_exact(hidden).astype(jnp.bfloat16)
    outputs = (middle + matmul(active, down_weight) + down_bias.astype(jnp.float32)).astype(
        jnp.bfloat16
    )
    back_qkv, back_out, back_up, back_down = (qkv_weight, out_weight, up_weight, down_weight)
    valid = (segment >= 0).astype(jnp.float32)[:, None]
    d_out = cotangent.astype(jnp.float32) * valid
    d_out_low = d_out.astype(jnp.bfloat16)
    grad_down = refold(matmul(active.T, d_out_low))
    grad_down_bias = jnp.sum(d_out_low.astype(jnp.float32), axis=0)
    d_active = matmul(d_out_low, back_down.T)
    gelu_value, gelu_pull = jax.vjp(gelu_exact, hidden)
    d_hidden = gelu_pull(d_active)[0].astype(jnp.bfloat16)
    grad_up = refold(matmul(normed2.T, d_hidden))
    grad_up_bias = jnp.sum(d_hidden.astype(jnp.float32), axis=0)
    d_normed2 = matmul(d_hidden, back_up.T)
    norm_value, norm_pull = jax.vjp(layer_norm, middle, second_gain, second_shift)
    d_middle_norm, grad_gain_two, grad_shift_two = norm_pull(d_normed2)
    d_middle = d_out + d_middle_norm
    d_branch = d_middle.astype(jnp.bfloat16)
    grad_out = refold(matmul(attended.T, d_branch))
    grad_out_bias = jnp.sum(d_branch.astype(jnp.float32), axis=0)
    d_attended_flat = matmul(d_branch, back_out.T).astype(jnp.bfloat16)
    d_attended = d_attended_flat.reshape(row_count, head_count, HD)
    scores = make_scores()
    probs = jnp.exp(scores - log_total)
    d_probs = jnp.einsum(
        "qhd,khd->hqk", d_attended, value_heads, preferred_element_type=jnp.float32
    )
    delta_rows = jnp.sum(probs * d_probs, axis=-1, keepdims=True)
    d_scores = (probs * (d_probs - delta_rows)).astype(jnp.bfloat16)
    d_query = (
        jnp.einsum("hqk,khd->qhd", d_scores, key_heads, preferred_element_type=jnp.float32)
        * score_scale
    ).reshape(row_count, model_width)
    probs_again = probs.astype(jnp.bfloat16)
    d_key_all = (
        jnp.einsum("hqk,qhd->khd", d_scores, query_heads, preferred_element_type=jnp.float32)
        * score_scale
    ).reshape(key_count, model_width)
    d_value_all = jnp.einsum(
        "hqk,qhd->khd", probs_again, d_attended, preferred_element_type=jnp.float32
    ).reshape(key_count, model_width)
    d_key, d_value = (
        lax.psum_scatter(
            d_key_all.astype(jnp.bfloat16), "ctx", scatter_dimension=0, tiled=True
        ).astype(jnp.float32),
        lax.psum_scatter(
            d_value_all.astype(jnp.bfloat16), "ctx", scatter_dimension=0, tiled=True
        ).astype(jnp.float32),
    )
    d_query_low = d_query.astype(jnp.bfloat16)
    d_value_low = d_value.astype(jnp.bfloat16)
    d_joined = jnp.concatenate([d_query_low, d_key.astype(jnp.bfloat16), d_value_low], axis=1)
    grad_qkv = refold(matmul(normed1.T, d_joined))
    grad_query_bias = jnp.sum(d_query_low.astype(jnp.float32), axis=0)
    grad_value_bias = jnp.sum(d_value_low.astype(jnp.float32), axis=0)
    d_normed1 = matmul(d_joined, back_qkv.T)
    first_value, first_pull = jax.vjp(layer_norm, values_in, first_gain, first_shift)
    d_input_norm, grad_gain_one, grad_shift_one = first_pull(d_normed1)
    input_grad = d_middle + d_input_norm
    partial_sums = (
        lax.psum_scatter(
            grad_qkv.astype(jnp.bfloat16), "dp", scatter_dimension=0, tiled=True
        ).astype(jnp.float32),
        lax.psum_scatter(
            grad_query_bias.astype(jnp.bfloat16), "dp", scatter_dimension=0, tiled=True
        ).astype(jnp.float32),
        lax.psum_scatter(
            grad_value_bias.astype(jnp.bfloat16), "dp", scatter_dimension=0, tiled=True
        ).astype(jnp.float32),
        lax.psum_scatter(
            grad_out.astype(jnp.bfloat16), "dp", scatter_dimension=0, tiled=True
        ).astype(jnp.float32),
        lax.psum_scatter(
            grad_out_bias.astype(jnp.bfloat16), "dp", scatter_dimension=0, tiled=True
        ).astype(jnp.float32),
        lax.psum_scatter(
            grad_gain_one.astype(jnp.bfloat16), "dp", scatter_dimension=0, tiled=True
        ).astype(jnp.float32),
        lax.psum_scatter(
            grad_shift_one.astype(jnp.bfloat16), "dp", scatter_dimension=0, tiled=True
        ).astype(jnp.float32),
        lax.psum_scatter(
            grad_gain_two.astype(jnp.bfloat16), "dp", scatter_dimension=0, tiled=True
        ).astype(jnp.float32),
        lax.psum_scatter(
            grad_shift_two.astype(jnp.bfloat16), "dp", scatter_dimension=0, tiled=True
        ).astype(jnp.float32),
        lax.psum_scatter(
            grad_up.astype(jnp.bfloat16), "dp", scatter_dimension=0, tiled=True
        ).astype(jnp.float32),
        lax.psum_scatter(
            grad_up_bias.astype(jnp.bfloat16), "dp", scatter_dimension=0, tiled=True
        ).astype(jnp.float32),
        lax.psum_scatter(
            grad_down.astype(jnp.bfloat16), "dp", scatter_dimension=0, tiled=True
        ).astype(jnp.float32),
        lax.psum_scatter(
            grad_down_bias.astype(jnp.bfloat16), "dp", scatter_dimension=0, tiled=True
        ).astype(jnp.float32),
    )
    all_sums = (
        lax.psum_scatter(
            partial_sums[0].astype(jnp.bfloat16), "ctx", scatter_dimension=0, tiled=True
        ).astype(jnp.float32),
        lax.psum_scatter(
            partial_sums[1].astype(jnp.bfloat16), "ctx", scatter_dimension=0, tiled=True
        ).astype(jnp.float32),
        lax.psum_scatter(
            partial_sums[2].astype(jnp.bfloat16), "ctx", scatter_dimension=0, tiled=True
        ).astype(jnp.float32),
        lax.psum_scatter(
            partial_sums[3].astype(jnp.bfloat16), "ctx", scatter_dimension=0, tiled=True
        ).astype(jnp.float32),
        lax.psum_scatter(
            partial_sums[4].astype(jnp.bfloat16), "ctx", scatter_dimension=0, tiled=True
        ).astype(jnp.float32),
        lax.psum_scatter(
            partial_sums[5].astype(jnp.bfloat16), "ctx", scatter_dimension=0, tiled=True
        ).astype(jnp.float32),
        lax.psum_scatter(
            partial_sums[6].astype(jnp.bfloat16), "ctx", scatter_dimension=0, tiled=True
        ).astype(jnp.float32),
        lax.psum_scatter(
            partial_sums[7].astype(jnp.bfloat16), "ctx", scatter_dimension=0, tiled=True
        ).astype(jnp.float32),
        lax.psum_scatter(
            partial_sums[8].astype(jnp.bfloat16), "ctx", scatter_dimension=0, tiled=True
        ).astype(jnp.float32),
        lax.psum_scatter(
            partial_sums[9].astype(jnp.bfloat16), "ctx", scatter_dimension=0, tiled=True
        ).astype(jnp.float32),
        lax.psum_scatter(
            partial_sums[10].astype(jnp.bfloat16), "ctx", scatter_dimension=0, tiled=True
        ).astype(jnp.float32),
        lax.psum_scatter(
            partial_sums[11].astype(jnp.bfloat16), "ctx", scatter_dimension=0, tiled=True
        ).astype(jnp.float32),
        lax.psum_scatter(
            partial_sums[12].astype(jnp.bfloat16), "ctx", scatter_dimension=0, tiled=True
        ).astype(jnp.float32),
    )
    (
        sum_qkv,
        sum_query_bias,
        sum_value_bias,
        sum_out,
        sum_out_bias,
        sum_gain_one,
        sum_shift_one,
        sum_gain_two,
        sum_shift_two,
        sum_up,
        sum_up_bias,
        sum_down,
        sum_down_bias,
    ) = all_sums
    return (
        outputs,
        input_grad,
        sum_qkv,
        sum_query_bias,
        sum_value_bias,
        sum_out,
        sum_out_bias,
        sum_gain_one,
        sum_shift_one,
        sum_gain_two,
        sum_shift_two,
        sum_up,
        sum_up_bias,
        sum_down,
        sum_down_bias,
    )


def solution(mesh):
    placed = (
        P(("dp", "ctx"), None),
        P(("dp", "ctx"), None),
        P(("dp", "ctx")),
        P(("dp", "ctx"), None),
        P(("dp", "ctx")),
        P(("dp", "ctx")),
        P(("dp", "ctx"), None),
        P(("dp", "ctx")),
        P(("dp", "ctx")),
        P(("dp", "ctx")),
        P(("dp", "ctx")),
        P(("dp", "ctx")),
        P(("dp", "ctx"), None),
        P(("dp", "ctx")),
        P(("dp", "ctx"), None),
        P(("dp", "ctx")),
    )
    return jax.shard_map(
        on_device,
        mesh=mesh,
        in_specs=placed,
        out_specs=(
            P(("dp", "ctx"), None),
            P(("dp", "ctx"), None),
            P(("dp", "ctx"), None),
            P(("dp", "ctx")),
            P(("dp", "ctx")),
            P(("dp", "ctx"), None),
            P(("dp", "ctx")),
            P(("dp", "ctx")),
            P(("dp", "ctx")),
            P(("dp", "ctx")),
            P(("dp", "ctx")),
            P(("dp", "ctx"), None),
            P(("dp", "ctx")),
            P(("dp", "ctx"), None),
            P(("dp", "ctx")),
        ),
        check_vma=False,
    )
```

profile of v0, /device:TPU:0, one launch (start us, length us, event | category | flops | bytes accessed | tf_op | source)
XLA Modules:
  0.0 956.8 jit_solution(2025521680493168756)
XLA Ops:
  15.4 42.4 %all-reduce.27 = (bf16[1024]{0:T(1024)(128)(2,1)S(1)}, bf16[1024]{0:T(1024)(128)(2,1)S(1)}, bf16[1024]{0:T(1024)(128)(2,1)S(1)}, bf16[1024]{0:T(1024)(128)(2,1)S...) all-reduce(bf16[1024]{0:T(1024)(128)(2,1)S(1)} %dynamic-update-slic, ...), channel_id=1, replica_groups=mesh['dp'=16,'ctx'=2] {'dp','ctx'}, use_global_device_ids=true, to_apply=%add.1 | all-reduce | flops 8192 | bytes 32768
  61.7 21.5 %all-gather.8.cloned.1.call-done = bf16[8192,384]{1,0:T(8,128)(2,1)} async-done(((bf16[256,384]{1,0:T(8,128)(2,1)}), bf16[8192,384]{1,0:T(8,128)(2,1)}) %all-gather.8.cloned.1.call-update) | async-done | bytes 6291472 | tf_op jit(solution)/shard_map/all_gather | solution.py:55
  83.2 10.4 %reshape.180 = bf16[1024,3072]{1,0:T(8,128)(2,1)} reshape(bf16[8192,384]{1,0:T(8,128)(2,1)} %all-gather.8.cloned.1.call-done) | data formatting | bytes 12582912 | tf_op jit(solution)/shard_map/reshape | solution.py:29
  93.7 6.6 fusion.44
  100.3 2.9 copy-done.11
  104.5 4.1 fusion.27
  112.1 4.9 all-reduce.3
  117.0 64.7 %all-gather = bf16[32,1,128]{2,1,0:T(2,128)(2,1)S(1)} all-gather(bf16[1,1,128]{2,1,0:T(2,128)(2,1)S(1)} %bitcast.63), channel_id=1, replica_groups=mesh['dp'=16,'ctx'=2] {'dp','ctx'}, dimensions={0}, use_global_device_ids=true | all-gather | bytes 8448 | tf_op jit(solution)/shard_map/all_gather | solution.py:65
  182.2 4.1 reshape.184
  187.8 3.1 copy.45
  190.9 22.3 %fusion.55 = (f32[16,584]{1,0:T(8,128)S(1)}, f32[16,584,1168]{2,1,0:T(8,128)}) fusion(bf16[584,16,64]{0,2,1:T(8,128)(2,1)} %bitcast.51, bf16[1168,16,64]{0,2,1:T(8,128)(2,1)S(1)} %bitcast.49, pred[584,1168]{1,0:T(8,128)(4,1)S(1)} %broadcast_compare_fusion), kind=kOutput, calls=%fused_computation.105 | convolution fusion | flops 1429697408 | bytes 47962752 | tf_op jit(solution)/shard_map/qhd,khd->hqk/dot_general | solution.py:119
  213.2 15.5 %fusion = f32[16,584]{1,0:T(8,128)S(1)} fusion(f32[16,584,1168]{2,1,0:T(8,128)} %get-tuple-element.62, f32[16,584]{1,0:T(8,128)S(1)} %get-tuple-element.61), kind=kLoop, calls=%fused_computation.6 | loop fusion | flops 21818240 | bytes 43729920 | tf_op jit(solution)/shard_map/reduce_sum | solution.py:127
  228.8 3.0 copy.43
  231.8 19.3 %fusion.31 = bf16[16,64,584]{2,1,0:T(8,128)(2,1)S(1)} fusion(bf16[1168,16,64]{0,2,1:T(8,128)(2,1)S(1)} %bitcast.55, f32[16,584,1168]{2,1,0:T(8,128)} %get-tuple-element.62, f32[16,584]{1,0:T(8,128)S(1)} %fusion, f32[16,584]{1,0:T(8,128)S(1)} %get-tuple-element.61), kind=kOutput, calls=%fused_computation.68 | convolution fusion | flops 1430304768 | bytes 47318016 | tf_op jit(solution)/shard_map/hqk,khd->qhd/dot_general | solution.py:130
  253.2 44.8 %all-gather.16.cloned.1.call-done = bf16[8192,512]{1,0:T(8,128)(2,1)} async-done(((bf16[256,512]{1,0:T(8,128)(2,1)}), bf16[8192,512]{1,0:T(8,128)(2,1)}) %all-gather.16.cloned.1.call-update) | async-done | bytes 8388624 | tf_op jit(solution)/shard_map/all_gather | solution.py:64
  297.9 13.6 %reshape.185 = bf16[1024,4096]{1,0:T(8,128)(2,1)} reshape(bf16[8192,512]{1,0:T(8,128)(2,1)} %all-gather.16.cloned.1.call-done) | data formatting | bytes 16777216 | tf_op jit(solution)/shard_map/reshape | solution.py:29
  311.5 31.4 %multiply_convert_fusion.1 = (bf16[584,4096]{1,0:T(8,128)(2,1)}, f32[584,4096]{1,0:T(8,128)}, f32[584,4096]{1,0:T(8,128)}) fusion(f32[4096]{0:T(1024)S(1)} %bitcast.61, bf16[1024,4096]{1,0:T(8,128)(2,1)} %reshape.185, f32[584,1024]{1,0:T(8,128)S(1)} %get-tuple-element.64, f32[1024]{0:T(1024)S(1)} %convert_element_type.257, ...), kind=kOutput, calls=%fused_computation.14 | convolution fusion | flops 5059813376 | bytes 34730560 | tf_op jit(solution)/shard_map/dot_general | solution.py:25
  342.9 34.1 %all-gather.18.cloned.1.call-done = bf16[32768,128]{1,0:T(8,128)(2,1)} async-done(((bf16[1024,128]{1,0:T(8,128)(2,1)}), bf16[32768,128]{1,0:T(8,128)(2,1)}) %all-gather.18.cloned.1.call-update) | async-done | bytes 8388624 | tf_op jit(solution)/shard_map/all_gather | solution.py:66
  376.9 13.3 %reshape.186 = bf16[4096,1024]{1,0:T(8,128)(2,1)} reshape(bf16[32768,128]{1,0:T(8,128)(2,1)} %all-gather.18.cloned.1.call-done) | data formatting | bytes 16777216 | tf_op jit(solution)/shard_map/reshape | solution.py:29
  390.2 17.3 %fusion.58 = (bf16[4096]{0:T(1024)(128)(2,1)}, bf16[584,4096]{1,0:T(8,128)(2,1)}) fusion(f32[584,4096]{1,0:T(8,128)} %get-tuple-element.53, bf16[4096,1024]{1,0:T(8,128)(2,1)} %reshape.186, bf16[584,1024]{1,0:T(8,128)(2,1)} %param.17, f32[584]{0:T(1024)S(1)} %copy-done.23, f32[584,4096]{1,0:T(8,128)} %get-tuple-element.65, f32[4096]{0:T(1024)S(1)} %bitcast.62), kind=kOutput, calls=%fused_computation.108 | convolution fusion | flops 4939010048 | bytes 33532192 | tf_op jit(solution)/shard_map/dot_general | solution.py:25
  407.5 10.5 %multiply_reduce_fusion.1 = (bf16[1024]{0:T(1024)(128)(2,1)}, f32[584]{0:T(1024)S(1)}, bf16[1024]{0:T(1024)(128)(2,1)}, f32[584,1024]{1,0:T(8,128)S(1)}) fusion(f32[584,1024]{1,0:T(8,128)S(1)} %get-tuple-element.64, f32[584]{0:T(1024)S(1)} %fusion.34, f32[584]{0:T(1024)S(1)} %broadcast_multiply_fusion, f32[1024]{0:T(1024)S(1)} %convert_element_type.256, ...), kind=kOutput, calls=%fused_computation.57 | convolution fusion | flops 4903728640 | bytes 17972064 | tf_op jit(solution)/shard_map/dot_general | solution.py:25
  421.4 2.5 convolution_convert_fusion.4
  429.7 20.1 %fusion.12 = bf16[16,64,1168]{2,1,0:T(8,128)(2,1)} fusion(bf16[584,16,64]{0,2,1:T(8,128)(2,1)S(1)} %bitcast.53, f32[16,584,1168]{2,1,0:T(8,128)} %get-tuple-element.62, f32[16,584]{1,0:T(8,128)S(1)} %log_add_fusion), kind=kOutput, calls=%fused_computation.33 | convolution fusion | flops 1419988992 | bytes 47280640 | tf_op jit(solution)/shard_map/hqk,qhd->khd/dot_general | solution.py:175
  449.8 4.4 copy.49
  454.2 33.7 %multiply_reduce_fusion = (f32[16,584]{1,0:T(8,128)S(1)}, f32[16,584,1168]{2,1,0:T(8,128)}) fusion(f32[16,584,1168]{2,1,0:T(8,128)} %get-tuple-element.62, f32[16,584]{1,0:T(8,128)S(1)} %log_add_fusion, bf16[584,16,64]{0,2,1:T(8,128)(2,1)S(1)} %bitcast.54, bf16[1168,16,64]{0,2,1:T(8,128)(2,1)} %bitcast.56), kind=kOutput, calls=%fused_computation.1 | convolution fusion | flops 1429697408 | bytes 90973184 | tf_op jit(solution)/shard_map/qhd,khd->hqk/dot_general | solution.py:161
  488.0 39.4 %multiply_convert_fusion = bf16[16,584,1168]{2,1,0:T(8,128)(2,1)} fusion(f32[16,584,1168]{2,1,0:T(8,128)} %get-tuple-element.68, f32[16,584,1168]{2,1,0:T(8,128)} %get-tuple-element.62, f32[16,584]{1,0:T(8,128)S(1)} %get-tuple-element.67, f32[16,584]{1,0:T(8,128)S(1)} %log_add_fusion), kind=kLoop, calls=%fused_computation | loop fusion | flops 43655168 | bytes 109212672 | tf_op jit(solution)/shard_map/convert_element_type | solution.py:165
  527.4 13.9 %multiply_convert_fusion.2 = bf16[16,64,1168]{2,1,0:T(8,128)(2,1)} fusion(bf16[584,16,64]{0,2,1:T(8,128)(2,1)S(1)} %bitcast.52, bf16[16,584,1168]{2,1,0:T(8,128)(2,1)} %multiply_convert_fusion), kind=kOutput, calls=%fused_computation.31 | convolution fusion | flops 1399357440 | bytes 25415680 | tf_op jit(solution)/shard_map/hqk,qhd->khd/dot_general | solution.py:172
  541.3 4.6 copy.47
  546.1 11.6 %convolution_convert_fusion = bf16[1024,4096]{1,0:T(8,128)(2,1)} fusion(bf16[584,4096]{1,0:T(8,128)(2,1)} %get-tuple-element.73, f32[584,1024]{1,0:T(8,128)S(1)} %copy-done.10, f32[1024]{0:T(1024)S(1)} %copy-done.35, f32[1024]{0:T(1024)S(1)} %convert_element_type.256, f32[584]{0:T(1024)S(1)} %fusion.34, f32[584]{0:T(1024)S(1)} %broadcast_multiply_fusion), kind=kOutput, calls=%fused_computation.28 | convolution fusion | flops 4906131456 | bytes 15577664 | tf_op jit(solution)/shard_map/dot_general | solution.py:25
  557.7 13.5 %convert_element_type.298 = bf16[8192,512]{1,0:T(8,128)(2,1)} reshape(bf16[1024,4096]{1,0:T(8,128)(2,1)} %convolution_convert_fusion) | data formatting | bytes 16777216 | tf_op jit(solution)/shard_map/convert_element_type | solution.py:225
  572.5 11.9 %convolution_convert_fusion.1 = bf16[4096,1024]{1,0:T(8,128)(2,1)} fusion(bf16[584,4096]{1,0:T(8,128)(2,1)} %get-tuple-element.52, bf16[584,1024]{1,0:T(8,128)(2,1)S(1)} %copy-done.13, f32[584]{0:T(1024)S(1)} %copy-done.23), kind=kOutput, calls=%fused_computation.29 | convolution fusion | flops 4904935424 | bytes 14371104 | tf_op jit(solution)/shard_map/dot_general | solution.py:25
  584.4 13.7 %convert_element_type.302 = bf16[32768,128]{1,0:T(8,128)(2,1)} reshape(bf16[4096,1024]{1,0:T(8,128)(2,1)} %convolution_convert_fusion.1) | data formatting | bytes 16777216 | tf_op jit(solution)/shard_map/convert_element_type | solution.py:231
  600.1 14.5 %fusion.57 = (bf16[16,64]{1,0:T(8,128)(2,1)S(1)}, bf16[16,64,584]{2,1,0:T(8,128)(2,1)}) fusion(bf16[1168,16,64]{0,2,1:T(8,128)(2,1)S(1)} %bitcast.50, bf16[16,584,1168]{2,1,0:T(8,128)(2,1)} %multiply_convert_fusion), kind=kOutput, calls=%fused_computation.107 | convolution fusion | flops 1398758400 | bytes 25417728 | tf_op jit(solution)/shard_map/hqk,khd->qhd/dot_general | solution.py:167
  614.7 2.8 copy.50
  619.9 9.9 %convolution_convert_fusion.2 = bf16[1024,3072]{1,0:T(8,128)(2,1)} fusion(bf16[584,1024]{0,1:T(8,128)(2,1)} %copy.50, bf16[584,1024]{0,1:T(8,128)(2,1)} %copy.48, bf16[584,1024]{0,1:T(8,128)(2,1)S(1)} %bitcast.59, bf16[584,1024]{1,0:T(8,128)(2,1)S(1)} %copy-done.6, f32[1024]{0:T(1024)S(1)} %copy-done.33, f32[1024]{0:T(1024)S(1)} %copy-done.20, ...), kind=kOutput, calls=%fused_computation.30 | convolution fusion | flops 3691708416 | bytes 11088448 | tf_op jit(solution)/shard_map/dot_general | solution.py:25
  629.9 10.5 %convert_element_type.281 = bf16[8192,384]{1,0:T(8,128)(2,1)} reshape(bf16[1024,3072]{1,0:T(8,128)(2,1)} %convolution_convert_fusion.2) | data formatting | bytes 12582912 | tf_op jit(solution)/shard_map/convert_element_type | solution.py:198
  644.3 44.5 %reduce-scatter.23.cloned.1.call-done = bf16[512,512]{1,0:T(8,128)(2,1)} async-done(((bf16[8192,512]{1,0:T(8,128)(2,1)}), bf16[512,512]{1,0:T(8,128)(2,1)}) %reduce-scatter.23.cloned.1.call-update) | async-done | bytes 524304 | tf_op jit(solution)/shard_map/reduce_scatter | solution.py:224
  688.8 10.1 %add_convert_fusion.1 = bf16[584,1024]{1,0:T(8,128)(2,1)} fusion(f32[584,1024]{1,0:T(8,128)} %copy-done.9, bf16[584,4096]{1,0:T(8,128)(2,1)} %get-tuple-element.52, bf16[4096,1024]{1,0:T(8,128)(2,1)} %reshape.186, f32[1024]{0:T(1024)S(1)} %convert_element_type.261), kind=kOutput, calls=%fused_computation.63 | convolution fusion | flops 4900741120 | bytes 16764928 | tf_op jit(solution)/shard_map/dot_general | solution.py:25
  702.6 107.6 %reduce-scatter.27.cloned.1.call-done = bf16[2048,128]{1,0:T(8,128)(2,1)} async-done(((bf16[32768,128]{1,0:T(8,128)(2,1)}), bf16[2048,128]{1,0:T(8,128)(2,1)}) %reduce-scatter.27.cloned.1.call-update) | async-done | bytes 524304 | tf_op jit(solution)/shard_map/reduce_scatter | solution.py:230
  810.5 9.4 fusion.48
  821.6 3.4 fusion.23
  825.1 61.6 %all-reduce.28 = (bf16[1024]{0:T(1024)(128)(2,1)S(1)}, bf16[1024]{0:T(1024)(128)(2,1)S(1)}, bf16[1024]{0:T(1024)(128)(2,1)S(1)}, bf16[1024]{0:T(1024)(128)(2,1)S...) all-reduce(bf16[1024]{0:T(1024)(128)(2,1)S(1)} %reduce_sum.216, ...), channel_id=6, replica_groups=mesh['dp'=16,'ctx'=2] {'dp'}, use_global_device_ids=true, to_apply=%region_16.17.clone | all-reduce | flops 12288 | bytes 49152
  887.4 5.0 all-reduce.29
  894.7 5.5 reduce-scatter.15.cloned.1.call-done
  900.8 4.1 add_add_fusion.2
  904.9 11.2 %reduce-scatter.25.cloned.1.call-done = bf16[256,512]{1,0:T(8,128)(2,1)} async-done(((bf16[512,512]{1,0:T(8,128)(2,1)}), bf16[256,512]{1,0:T(8,128)(2,1)}) %reduce-scatter.25.cloned.1.call-update) | async-done | bytes 262160 | tf_op jit(solution)/shard_map/reduce_scatter | solution.py:265
  917.9 15.0 %reduce-scatter.29.cloned.1.call-done = bf16[1024,128]{1,0:T(8,128)(2,1)} async-done(((bf16[2048,128]{1,0:T(8,128)(2,1)}), bf16[1024,128]{1,0:T(8,128)(2,1)}) %reduce-scatter.29.cloned.1.call-update) | async-done | bytes 262160 | tf_op jit(solution)/shard_map/reduce_scatter | solution.py:271
  934.6 13.5 %reduce-scatter.17.cloned.1.call-done = bf16[256,384]{1,0:T(8,128)(2,1)} async-done(((bf16[512,384]{1,0:T(8,128)(2,1)}), bf16[256,384]{1,0:T(8,128)(2,1)}) %reduce-scatter.17.cloned.1.call-update) | async-done | bytes 196624 | tf_op jit(solution)/shard_map/reduce_scatter | solution.py:238
  (200 shorter events, 51.0 us)
Async XLA Ops:
  7.2 76.1 %all-gather.8.cloned.1.call-start = ((), (), s32[]{:S(2)}) async-start(), calls=%async_computation.10 | async-start | bytes 6488064 | tf_op jit(solution)/shard_map/all_gather | solution.py:55
  7.9 174.3 %all-gather.14.cloned.1.call-start = ((), (), s32[]{:S(2)}) async-start(), calls=%async_computation.13 | async-start | bytes 2162688 | tf_op jit(solution)/shard_map/all_gather | solution.py:58
  8.7 179.1 %all-gather.12.cloned.1.call-start = ((), (), s32[]{:S(2)}) async-start(), calls=%async_computation.12 | async-start | bytes 3588096 | tf_op jit(solution)/shard_map/all_gather | solution.py:105
  57.8 35.8 %copy-start.32 = (f32[1024]{0:T(1024)}, f32[1024]{0:T(1024)S(1)}, u32[]{:S(2)}) copy-start(f32[1024]{0:T(1024)S(1)} %convert_element_type.242) | copy-start | bytes 12292
  57.8 35.8 %copy-start.19 = (f32[1024]{0:T(1024)}, f32[1024]{0:T(1024)S(1)}, u32[]{:S(2)}) copy-start(f32[1024]{0:T(1024)S(1)} %convert_element_type.241) | copy-start | bytes 12292
  59.4 34.3 %copy-start.17 = (f32[584]{0:T(1024)}, f32[584]{0:T(1024)S(1)}, u32[]{:S(2)}) copy-start(f32[584]{0:T(1024)S(1)} %broadcast_multiply_fusion.1) | copy-start | bytes 7012
  61.7 31.9 %copy-start.21 = (f32[584]{0:T(1024)}, f32[584]{0:T(1024)S(1)}, u32[]{:S(2)}) copy-start(f32[584]{0:T(1024)S(1)} %fusion.33) | copy-start | bytes 7012
  61.7 31.9 %copy-start.4 = (bf16[584,1024]{1,0:T(8,128)(2,1)S(1)}, bf16[584,1024]{1,0:T(8,128)(2,1)}, u32[]{:S(2)}) copy-start(bf16[584,1024]{1,0:T(8,128)(2,1)} %param.16) | copy-start | bytes 3588100
  104.4 124.4 %all-gather.10.cloned.1.call-start = ((), (), s32[]{:S(2)}) async-start(), calls=%async_computation.11 | async-start | bytes 3588096 | tf_op jit(solution)/shard_map/all_gather | solution.py:106
  104.5 5.4 copy-start.28
  104.5 6.1 copy-start.39
  104.5 12.5 %copy-start.40 = (bf16[128]{0:T(256)(128)(2,1)S(1)}, bf16[128]{0:T(256)(128)(2,1)}, u32[]{:S(2)}) copy-start(bf16[128]{0:T(256)(128)(2,1)} %param.29) | copy-start | bytes 772
  108.7 189.2 %all-gather.16.cloned.1.call-start = ((), (), s32[]{:S(2)}) async-start(), calls=%async_computation.14 | async-start | bytes 8650752 | tf_op jit(solution)/shard_map/all_gather | solution.py:64
  109.3 267.6 %all-gather.18.cloned.1.call-start = ((), (), s32[]{:S(2)}) async-start(), calls=%async_computation.15 | async-start | bytes 8650752 | tf_op jit(solution)/shard_map/all_gather | solution.py:66
  109.9 461.5 %reduce-scatter.19.cloned.1.call-start = ((), (), s32[]{:S(2)}) async-start(), calls=%async_computation.18 | async-start | bytes 2228224 | tf_op jit(solution)/shard_map/reduce_scatter | solution.py:206
  110.5 200.9 %copy-start.34 = (f32[1024]{0:T(1024)}, f32[1024]{0:T(1024)S(1)}, u32[]{:S(2)}) copy-start(f32[1024]{0:T(1024)S(1)} %convert_element_type.257) | copy-start | bytes 12292
  190.9 22.3 %copy-start = (bf16[1168,1024]{0,1:T(8,128)(2,1)}, bf16[1168,1024]{0,1:T(8,128)(2,1)S(1)}, u32[]{:S(2)}) copy-start(bf16[1168,1024]{0,1:T(8,128)(2,1)S(1)} %copy.45) | copy-start | bytes 7176196
  231.7 19.3 %copy-start.8 = (bf16[1168,1024]{0,1:T(8,128)(2,1)}, bf16[1168,1024]{0,1:T(8,128)(2,1)S(1)}, u32[]{:S(2)}) copy-start(bf16[1168,1024]{0,1:T(8,128)(2,1)S(1)} %copy.43) | copy-start | bytes 7176196
  231.8 19.3 %copy-start.5 = (bf16[584,1024]{1,0:T(8,128)(2,1)S(1)}, bf16[584,1024]{1,0:T(8,128)(2,1)}, u32[]{:S(2)}) copy-start(bf16[584,1024]{1,0:T(8,128)(2,1)} %param.16) | copy-start | bytes 3588100
  231.8 19.3 %copy-start.15 = (bf16[1024,1024]{1,0:T(8,128)(2,1)S(1)}, bf16[1024,1024]{1,0:T(8,128)(2,1)}, u32[]{:S(2)}) copy-start(bf16[1024,1024]{1,0:T(8,128)(2,1)} %reshape.184) | copy-start | bytes 6291460
  252.7 165.3 %copy-start.9 = (f32[584,1024]{1,0:T(8,128)}, f32[584,1024]{1,0:T(8,128)S(1)}, u32[]{:S(2)}) copy-start(f32[584,1024]{1,0:T(8,128)S(1)} %get-tuple-element.64) | copy-start | bytes 7176196
  342.8 47.4 %copy-start.23 = (f32[584]{0:T(1024)S(1)}, f32[584]{0:T(1024)}, u32[]{:S(2)}) copy-start(f32[584]{0:T(1024)} %compare_convert_fusion) | copy-start | bytes 7012
  418.8 5.0 copy-start.2
  418.9 5.0 copy-start.24
  429.7 185.0 %reduce-scatter.33.cloned.1.call-start = ((), (), s32[]{:S(2)}) async-start(), calls=%async_computation.25 | async-start | bytes 3588096
  487.9 129.6 %reduce-scatter.31.cloned.1.call-start = ((), (), s32[]{:S(2)}) async-start(), calls=%async_computation.24 | async-start | bytes 3588096
  488.0 39.4 %copy-start.7 = (bf16[584,1024]{0,1:T(8,128)(2,1)S(1)}, bf16[584,1024]{0,1:T(8,128)(2,1)}, u32[]{:S(2)}) copy-start(bf16[584,1024]{0,1:T(8,128)(2,1)} %copy.44) | copy-start | bytes 3588100
  546.0 142.8 %reduce-scatter.23.cloned.1.call-start = ((), (), s32[]{:S(2)}) async-start(), calls=%async_computation.20 | async-start | bytes 8912896 | tf_op jit(solution)/shard_map/reduce_scatter | solution.py:224
  571.2 129.9 %reduce-scatter.21.cloned.1.call-start = ((), (), s32[]{:S(2)}) async-start(), calls=%async_computation.19 | async-start | bytes 196608 | tf_op jit(solution)/shard_map/reduce_scatter | solution.py:247
  572.0 238.2 %reduce-scatter.27.cloned.1.call-start = ((), (), s32[]{:S(2)}) async-start(), calls=%async_computation.22 | async-start | bytes 8912896 | tf_op jit(solution)/shard_map/reduce_scatter | solution.py:230
  598.1 302.1 %reduce-scatter.15.cloned.1.call-start = ((), (), s32[]{:S(2)}) async-start(), calls=%async_computation.16 | async-start | bytes 6684672 | tf_op jit(solution)/shard_map/reduce_scatter | solution.py:197
  614.6 5.3 copy-start.6
  614.6 5.3 copy-start.14
  614.6 5.3 copy-start.18
  614.6 5.3 copy-start.20
  614.6 5.3 copy-start.22
  614.7 5.3 copy-start.33
  640.3 275.7 %reduce-scatter.25.cloned.1.call-start = ((), (), s32[]{:S(2)}) async-start(), calls=%async_computation.21 | async-start | bytes 786432 | tf_op jit(solution)/shard_map/reduce_scatter | solution.py:265
  688.8 244.1 %reduce-scatter.29.cloned.1.call-start = ((), (), s32[]{:S(2)}) async-start(), calls=%async_computation.23 | async-start | bytes 786432 | tf_op jit(solution)/shard_map/reduce_scatter | solution.py:271
  810.2 11.4 %copy-start.27 = (f32[584]{0:T(1024)S(1)}, f32[584]{0:T(1024)}, u32[]{:S(2)}) copy-start(f32[584]{0:T(1024)} %copy-done.26) | copy-start | bytes 7012
  810.2 137.9 %reduce-scatter.17.cloned.1.call-start = ((), (), s32[]{:S(2)}) async-start(), calls=%async_computation.17 | async-start | bytes 589824 | tf_op jit(solution)/shard_map/reduce_scatter | solution.py:238
  819.9 5.1 copy-start.29
  819.9 5.1 copy-start.30
  819.9 5.1 copy-start.31
  819.9 5.1 copy-start.37
  819.9 5.1 copy-start.38
  819.9 80.9 %copy-start.3 = (f32[584,1024]{1,0:T(8,128)S(1)}, f32[584,1024]{1,0:T(8,128)}, u32[]{:S(2)}) copy-start(f32[584,1024]{1,0:T(8,128)} %copy-done.2) | copy-start | bytes 7176196
  819.9 80.9 %copy-start.25 = (f32[584]{0:T(1024)S(1)}, f32[584]{0:T(1024)}, u32[]{:S(2)}) copy-start(f32[584]{0:T(1024)} %copy-done.24) | copy-start | bytes 7012
  (12 other events, 28.7 us)
Sparse Core Ops, SparseCore 0:
  10.9 72.2 all-gather.7
  86.3 55.0 all-gather.13
  143.5 35.4 all-gather.11
  180.9 36.4 all-gather.9
  220.4 77.4 all-gather.15
  300.9 76.0 all-gather.17
  429.8 60.1 reduce-scatter.18
  492.3 34.0 reduce-scatter.32
  546.1 33.5 reduce-scatter.30
  584.1 104.6 reduce-scatter.22
  691.1 9.9 reduce-scatter.20
  705.6 104.5 reduce-scatter.26
  814.7 85.4 reduce-scatter.14
  902.3 13.7 reduce-scatter.24
  918.3 14.5 reduce-scatter.28
  935.0 13.1 reduce-scatter.16
where the time goes:
time: 965 us; the launch traced here: 957 us
  waiting for transfers between devices  303 us (31%)
  matrix products  248 us (26%)
  blocking collectives  179 us (19%)
  local copies, waits for them, and re-layouts  123 us (13%)
  other arithmetic  84.7 us (9%)
  between operations  18.3 us (2%)
    dot_general x12, matrix products, matmul(): return jnp.dot(left, right, preferred_element_type=jnp.float32)  125 us
    unnamed x4, blocking collectives  114 us
    reduce_scatter x1, waiting for transfers between devices, on_device(): lax.psum_scatter(grad_down.astype(jnp.bfloat16), 'dp', scatter_dimension=...  108 us
    all_gather x1, blocking collectives, on_device(): lax.all_gather(b_up, ('dp', 'ctx'), axis=0, tiled=True)  64.7 us
    all_gather x1, waiting for transfers between devices, on_device(): lax.all_gather(w_up, ('dp', 'ctx'), axis=0, tiled=True)  44.8 us
    reduce_scatter x1, waiting for transfers between devices, on_device(): lax.psum_scatter(grad_up.astype(jnp.bfloat16), 'dp', scatter_dimension=0,...  44.5 us
    reshape x4, local copies, waits for them, and re-layouts, unfold(): return stored.reshape(stored.shape[0] // 8, stored.shape[1] * 8)  41.4 us
    convert_element_type x1, other arithmetic, on_device(): d_scores = (probs * (d_probs - delta_rows)).astype(jnp.bfloat16)  39.4 us
  transfers between devices with their start and end apart: 16, of which 10 were waited for; matrix products, arithmetic and copies ran while one was open for 41% of the time, Pallas kernels for 0%

commit v1 on v0

--- a/solution.py
+++ b/solution.py
@@ -3,6 +3,8 @@
 import jax
 import jax.numpy as jnp
 from jax import lax
+from jax.experimental import pallas as pl
+from jax.experimental.pallas import tpu as pltpu
 from jax.sharding import PartitionSpec as P
 
 HD = 64
@@ -309,45 +311,374 @@
     )
 
 
+SEQ = 577
+IMAGES = 2
+PAIR = 2 * HD
+CHUNK = 256
+
+
+def round_up(count, unit):
+    return -(-count // unit) * unit
+
+
+def chunks_of(count):
+    return [(start, min(CHUNK, count - start)) for start in range(0, count, CHUNK)]
+
+
+def nt_dot(left, right):
+    return lax.dot_general(
+        left, right, (((1,), (1,)), ((), ())), preferred_element_type=jnp.float32
+    )
+
+
+def half_mask(rows):
+    return lax.broadcasted_iota(jnp.int32, (rows, PAIR), 1) < HD
+
+
+def forward_kernel(query_ref, key_ref, value_ref, bias_ref, attended_ref, log_ref):
+    rows = query_ref.shape[0]
+    first = half_mask(rows)
+    zero = jnp.zeros((rows, PAIR), jnp.bfloat16)
+    key = key_ref[...]
+    key_sides = (jnp.where(first, key, zero), jnp.where(first, zero, key))
+    value_t = value_ref[...].astype(jnp.float32).T.astype(jnp.bfloat16)
+    scale = jnp.bfloat16(1.0 / math.sqrt(HD))
+    for start, size in chunks_of(rows):
+        query = query_ref[start : start + size, :] * scale
+        bias = bias_ref[:, start : start + size]
+        outs = []
+        for side in range(2):
+            scores = nt_dot(key_sides[side], query) + bias
+            top = jnp.max(scores, axis=0, keepdims=True)
+            expo = jnp.exp(scores - top)
+            total = jnp.sum(expo, axis=0, keepdims=True)
+            probs_low = (expo * (1.0 / total)).astype(jnp.bfloat16)
+            outs.append(matmul(value_t[side * HD : (side + 1) * HD, :], probs_low))
+            log_ref[0, side : side + 1, start : start + size] = top + jnp.log(total)
+        mixed = jnp.concatenate(outs, axis=0)
+        attended_ref[start : start + size, :] = mixed.T.astype(jnp.bfloat16)
+
+
+def backward_kernel(
+    query_ref, key_ref, value_ref, d_ref, log_ref, bias_ref, dq_ref, dk_ref, dv_ref, dk_sum, dv_sum
+):
+    rows = query_ref.shape[0]
+    first = half_mask(rows)
+    zero = jnp.zeros((rows, PAIR), jnp.bfloat16)
+    key = key_ref[...]
+    value = value_ref[...]
+    key_sides = (jnp.where(first, key, zero), jnp.where(first, zero, key))
+    value_sides = (jnp.where(first, value, zero), jnp.where(first, zero, value))
+    key_t = key.astype(jnp.float32).T.astype(jnp.bfloat16)
+    scale = jnp.bfloat16(1.0 / math.sqrt(HD))
+    for start, size in chunks_of(rows):
+        query = query_ref[start : start + size, :] * scale
+        d_rows = d_ref[start : start + size, :]
+        bias = bias_ref[:, start : start + size]
+        outs = []
+        for side in range(2):
+            scores = nt_dot(key_sides[side], query) + bias
+            probs = jnp.exp(scores - log_ref[0, side : side + 1, start : start + size])
+            d_probs = nt_dot(value_sides[side], d_rows)
+            product = probs * d_probs
+            delta = jnp.sum(product, axis=0, keepdims=True)
+            d_scores = (product - probs * delta).astype(jnp.bfloat16)
+            d_value = matmul(probs.astype(jnp.bfloat16), d_rows)
+            d_key = matmul(d_scores, query)
+            if start == 0:
+                dv_sum[side] = d_value
+                dk_sum[side] = d_key
+            else:
+                dv_sum[side] += d_value
+                dk_sum[side] += d_key
+            outs.append(matmul(key_t[side * HD : (side + 1) * HD, :], d_scores))
+        d_query = jnp.concatenate(outs, axis=0) * (1.0 / math.sqrt(HD))
+        dq_ref[start : start + size, :] = d_query.T.astype(jnp.bfloat16)
+    dk_ref[...] = jnp.where(first, dk_sum[0], dk_sum[1]).astype(jnp.bfloat16)
+    dv_ref[...] = jnp.where(first, dv_sum[0], dv_sum[1]).astype(jnp.bfloat16)
+
+
+def attention_forward(joined, bias):
+    rows, width = joined.shape[0], joined.shape[1] // 3
+    pairs = width // PAIR
+    flops = 4 * rows * rows * width
+    return pl.pallas_call(
+        forward_kernel,
+        grid=(pairs,),
+        in_specs=[
+            pl.BlockSpec((rows, PAIR), lambda i: (0, i)),
+            pl.BlockSpec((rows, PAIR), lambda i: (0, pairs + i)),
+            pl.BlockSpec((rows, PAIR), lambda i: (0, 2 * pairs + i)),
+            pl.BlockSpec((rows, rows), lambda i: (0, 0)),
+        ],
+        out_specs=[
+            pl.BlockSpec((rows, PAIR), lambda i: (0, i)),
+            pl.BlockSpec((1, 2, rows), lambda i: (i, 0, 0)),
+        ],
+        out_shape=[
+            jax.ShapeDtypeStruct((rows, width), jnp.bfloat16),
+            jax.ShapeDtypeStruct((pairs, 2, rows), jnp.float32),
+        ],
+        compiler_params=pltpu.CompilerParams(vmem_limit_bytes=40 * 2**20),
+        cost_estimate=pl.CostEstimate(
+            flops=4 * flops, bytes_accessed=8 * rows * width, transcendentals=rows * rows * 16
+        ),
+        name="attention_forward",
+    )(joined, joined, joined, bias)
+
+
+def attention_backward(joined, d_attended, log_total, bias):
+    rows, width = d_attended.shape
+    pairs = width // PAIR
+    flops = 10 * rows * rows * width
+    block = jax.ShapeDtypeStruct((rows, width), jnp.bfloat16)
+    return pl.pallas_call(
+        backward_kernel,
+        grid=(pairs,),
+        in_specs=[
+            pl.BlockSpec((rows, PAIR), lambda i: (0, i)),
+            pl.BlockSpec((rows, PAIR), lambda i: (0, pairs + i)),
+            pl.BlockSpec((rows, PAIR), lambda i: (0, 2 * pairs + i)),
+            pl.BlockSpec((rows, PAIR), lambda i: (0, i)),
+            pl.BlockSpec((1, 2, rows), lambda i: (i, 0, 0)),
+            pl.BlockSpec((rows, rows), lambda i: (0, 0)),
+        ],
+        out_specs=[pl.BlockSpec((rows, PAIR), lambda i: (0, i))] * 3,
+        out_shape=[block] * 3,
+        scratch_shapes=[pltpu.VMEM((2, rows, PAIR), jnp.float32)] * 2,
+        compiler_params=pltpu.CompilerParams(vmem_limit_bytes=40 * 2**20),
+        cost_estimate=pl.CostEstimate(
+            flops=4 * flops, bytes_accessed=14 * rows * width, transcendentals=rows * rows * 16
+        ),
+        name="attention_backward",
+    )(joined, joined, joined, d_attended, log_total, bias)
+
+
+def standardize(value):
+    center = value - jnp.mean(value, axis=-1, keepdims=True)
+    variance = jnp.mean(center * center, axis=-1, keepdims=True)
+    scale = lax.rsqrt(variance + EPSILON)
+    return center * scale, scale
+
+
+def norm_backward(d_normed, normal, scale, gain):
+    scaled = d_normed * gain
+    mean = jnp.mean(scaled, axis=-1, keepdims=True)
+    along = jnp.mean(scaled * normal, axis=-1, keepdims=True)
+    return (scaled - mean - normal * along) * scale
+
+
+def gelu_slope(value):
+    phi = 0.5 * (1.0 + lax.erf(value * math.sqrt(0.5)))
+    return phi + value * jnp.exp(-0.5 * value * value) * (1.0 / math.sqrt(2.0 * math.pi))
+
+
+def by_core(array, axis, chips):
+    shape = array.shape
+    cut = shape[:axis] + (chips, 2, shape[axis] // (2 * chips)) + shape[axis + 1 :]
+    return jnp.swapaxes(array.reshape(cut), axis, axis + 1).reshape(shape)
+
+
+def by_chip(array, axis, chips):
+    shape = array.shape
+    cut = shape[:axis] + (2, chips, shape[axis] // (2 * chips)) + shape[axis + 1 :]
+    return jnp.swapaxes(array.reshape(cut), axis, axis + 1).reshape(shape)
+
+
+def gather_rows(shard):
+    near = lax.all_gather(shard, ("chip", "ctx"), axis=0, tiled=True)
+    return lax.all_gather(near, "core", axis=0, tiled=True)
+
+
+def scatter_rows(matrix):
+    near = lax.psum_scatter(
+        matrix.astype(jnp.bfloat16), "core", scatter_dimension=0, tiled=True
+    )
+    return lax.psum_scatter(near, ("chip", "ctx"), scatter_dimension=0, tiled=True)
+
+
+def column_sums(array):
+    return jnp.sum(array.astype(jnp.float32), axis=0)
+
+
+def by_image(chips):
+    def on_device(
+        inputs,
+        cotangent,
+        segment,
+        w_qkv,
+        b_query,
+        b_value,
+        w_out,
+        b_out,
+        norm1_gain,
+        norm1_shift,
+        norm2_gain,
+        norm2_shift,
+        w_up,
+        b_up,
+        w_down,
+        b_down,
+    ):
+        place = lax.axis_index("ctx")
+        swap = lambda array: lax.ppermute(array, "ctx", [(0, 1), (1, 0)])
+        slots, width = inputs.shape
+        pads = 2 * slots - IMAGES * SEQ
+        rows = round_up(SEQ + pads, 16)
+        near_width = w_up.shape[0] // 8
+
+        segment_far = swap(segment)
+        inputs_far = swap(inputs)
+        small = jnp.concatenate(
+            [b_query, b_value, b_out, norm1_gain, norm1_shift, norm2_gain, norm2_shift, b_down, b_up]
+        )
+        small_all = lax.all_gather(small, ("chip", "core", "ctx"), axis=0, tiled=False)
+        qkv_weight = gather_rows(unfold(w_qkv))
+        out_weight = by_chip(gather_rows(by_core(unfold(w_out), 1, chips)), 0, chips)
+        up_weight = gather_rows(by_core(unfold(w_up), 1, chips))
+        down_weight = gather_rows(by_core(unfold(w_down), 1, chips))
+        cotangent_far = swap(cotangent)
+
+        small_all = small_all.astype(jnp.float32)
+        small_core = by_core(small_all, 0, chips)
+        piece = lambda table, index: table[:, index * near_width : (index + 1) * near_width].reshape(-1)
+        query_bias = piece(small_all, 0)
+        value_bias = piece(small_all, 1)
+        out_bias, first_gain, first_shift, second_gain, second_shift, down_bias = (
+            piece(small_core, index) for index in range(2, 8)
+        )
+        up_bias = small_core[:, 8 * near_width :].reshape(-1)
+
+        slot = jnp.arange(slots)
+        earlier = slot[:, None] < slot[None, :]
+
+        def ranks(own, far, far_first):
+            inside = jnp.sum((own[:, None] == own[None, :]) & earlier, axis=0)
+            outside = jnp.sum(far[:, None] == own[None, :], axis=0)
+            return inside + jnp.where(far_first, outside, 0)
+
+        rank_near = ranks(segment, segment_far, place == 1)
+        rank_far = ranks(segment_far, segment, place == 0)
+
+        def positions(ids, rank, image):
+            return jnp.where(ids == image, rank, jnp.where(ids < 0, SEQ + rank, -1))
+
+        row = jnp.arange(rows)
+        pick_near = (positions(segment, rank_near, place)[None, :] == row[:, None])
+        pick_far = (positions(segment_far, rank_far, place)[None, :] == row[:, None])
+        pick_near, pick_far = pick_near.astype(jnp.bfloat16), pick_far.astype(jnp.bfloat16)
+        give_near = (positions(segment, rank_near, place)[:, None] == row[None, :])
+        other_image = jnp.where(segment == 1 - place, rank_near, -1)
+        give_far = other_image[:, None] == row[None, :]
+        give_near, give_far = give_near.astype(jnp.bfloat16), give_far.astype(jnp.bfloat16)
+        column = jnp.arange(width)
+        order = by_core(column, 0, chips)
+        to_core = (column[:, None] == order[None, :]).astype(jnp.bfloat16)
+
+        def take(near, far):
+            picked = matmul(pick_near, near) + matmul(pick_far, far)
+            return matmul(picked.astype(jnp.bfloat16), to_core)
+
+        def give(array):
+            natural = nt_dot(array.astype(jnp.bfloat16), to_core).astype(jnp.bfloat16)
+            return matmul(give_near, natural) + matmul(give_far, swap(natural))
+
+        kind = (row >= SEQ).astype(jnp.int32) + (row >= SEQ + pads).astype(jnp.int32)
+        bias = jnp.where(kind[:, None] == kind[None, :], 0.0, -1e30).astype(jnp.float32)
+
+        values_in = take(inputs, inputs_far)
+        normal1, scale1 = standardize(values_in)
+        normed1 = (normal1 * first_gain + first_shift).astype(jnp.bfloat16)
+        joined_bias = jnp.concatenate([query_bias, jnp.zeros_like(query_bias), value_bias])
+        joined = (matmul(normed1, qkv_weight) + joined_bias).astype(jnp.bfloat16)
+        attended, log_total = attention_forward(joined, bias)
+        middle = values_in + matmul(attended, out_weight) + out_bias
+        normal2, scale2 = standardize(middle)
+        normed2 = (normal2 * second_gain + second_shift).astype(jnp.bfloat16)
+        hidden = matmul(normed2, up_weight) + up_bias
+        active = gelu_exact(hidden).astype(jnp.bfloat16)
+        slope = gelu_slope(hidden).astype(jnp.bfloat16)
+        outputs = give(middle + matmul(active, down_weight) + down_bias).astype(jnp.bfloat16)
+
+        live = (row < SEQ).astype(jnp.float32)[:, None]
+        d_out = take(cotangent, cotangent_far) * live
+        d_out_low = d_out.astype(jnp.bfloat16)
+        sum_down = scatter_rows(matmul(active.T, d_out_low))
+        d_hidden = (matmul(d_out_low, down_weight.T) * slope.astype(jnp.float32)).astype(jnp.bfloat16)
+        sum_up = scatter_rows(matmul(normed2.T, d_hidden))
+        d_normed2 = matmul(d_hidden, up_weight.T)
+        d_middle = d_out + norm_backward(d_normed2, normal2, scale2, second_gain)
+        d_branch = d_middle.astype(jnp.bfloat16)
+        sum_out = scatter_rows(by_core(matmul(attended.T, d_branch).astype(jnp.bfloat16), 0, chips))
+        d_attended = matmul(d_branch, out_weight.T).astype(jnp.bfloat16)
+        d_query, d_key, d_value = attention_backward(joined, d_attended, log_total, bias)
+        d_joined = jnp.concatenate([d_query, d_key, d_value], axis=1)
+        sum_qkv = scatter_rows(matmul(normed1.T, d_joined))
+        d_normed1 = matmul(d_joined, qkv_weight.T)
+        input_grad = give(d_middle + norm_backward(d_normed1, normal1, scale1, first_gain))
+
+        part = lambda vector: vector.reshape(2 * chips * 2, -1)
+        core_sums = jnp.concatenate(
+            [
+                part(vector)
+                for vector in (
+                    column_sums(d_branch),
+                    column_sums(d_normed1 * normal1),
+                    column_sums(d_normed1),
+                    column_sums(d_normed2 * normal2),
+                    column_sums(d_normed2),
+                    column_sums(d_out_low),
+                    column_sums(d_hidden),
+                )
+            ],
+            axis=1,
+        )
+        chip_sums = jnp.concatenate([part(column_sums(d_query)), part(column_sums(d_value))], axis=1)
+        small_sums = jnp.concatenate([chip_sums, by_chip(core_sums, 0, chips)], axis=1)
+        small_sums = lax.psum_scatter(
+            small_sums, ("chip", "core", "ctx"), scatter_dimension=0, tiled=True
+        )[0]
+        own = lambda index: small_sums[index * near_width : (index + 1) * near_width]
+        back = lambda matrix: refold(by_chip(matrix, 1, chips).astype(jnp.float32))
+        return (
+            outputs,
+            input_grad,
+            refold(sum_qkv.astype(jnp.float32)),
+            own(0),
+            own(1),
+            back(sum_out),
+            own(2),
+            own(3),
+            own(4),
+            own(5),
+            own(6),
+            back(sum_up),
+            small_sums[8 * near_width :],
+            back(sum_down),
+            own(7),
+        )
+
+    return on_device
+
+
 def solution(mesh):
-    placed = (
-        P(("dp", "ctx"), None),
-        P(("dp", "ctx"), None),
-        P(("dp", "ctx")),
-        P(("dp", "ctx"), None),
-        P(("dp", "ctx")),
-        P(("dp", "ctx")),
-        P(("dp", "ctx"), None),
-        P(("dp", "ctx")),
-        P(("dp", "ctx")),
-        P(("dp", "ctx")),
-        P(("dp", "ctx")),
-        P(("dp", "ctx")),
-        P(("dp", "ctx"), None),
-        P(("dp", "ctx")),
-        P(("dp", "ctx"), None),
-        P(("dp", "ctx")),
-    )
+    if mesh.shape["ctx"] == IMAGES and mesh.shape["dp"] % 2 == 0:
+        chips = mesh.shape["dp"] // 2
+        mesh = jax.sharding.Mesh(
+            mesh.devices.reshape(chips, 2, IMAGES), ("chip", "core", "ctx")
+        )
+        body, axes = by_image(chips), ("chip", "core", "ctx")
+    else:
+        body, axes = on_device, ("dp", "ctx")
+    matrix, vector = P(axes, None), P(axes)
     return jax.shard_map(
-        on_device,
+        body,
         mesh=mesh,
-        in_specs=placed,
-        out_specs=(
-            P(("dp", "ctx"), None),
-            P(("dp", "ctx"), None),
-            P(("dp", "ctx"), None),
-            P(("dp", "ctx")),
-            P(("dp", "ctx")),
-            P(("dp", "ctx"), None),
-            P(("dp", "ctx")),
-            P(("dp", "ctx")),
-            P(("dp", "ctx")),
-            P(("dp", "ctx")),
-            P(("dp", "ctx")),
-            P(("dp", "ctx"), None),
-            P(("dp", "ctx")),
-            P(("dp", "ctx"), None),
-            P(("dp", "ctx")),
-        ),
+        in_specs=(matrix, matrix, vector, matrix, vector, vector, matrix)
+        + (vector,) * 5
+        + (matrix, vector, matrix, vector),
+        out_specs=(matrix, matrix, matrix, vector, vector, matrix)
+        + (vector,) * 5
+        + (matrix, vector, matrix, vector),
         check_vma=False,
     )

time: 965 us -> 989 us (1.025)
  waiting for transfers between devices: 303 us -> 500 us
  local copies, waits for them, and re-layouts: 123 us -> 27.6 us
  matrix products: 248 us -> 156 us
  other arithmetic: 84.7 us -> 9.03 us
  Pallas kernels: 0 us -> 55.1 us
  blocking collectives: 179 us -> 212 us
    dot_general x6 -> x2, matrix products: 124 us -> 16.1 us  [nt_dot(): lax.dot_general(left, right, (((1,), (1,)), ((), ())), preferred_element_...]
    all_gather x6 -> x8, waiting for transfers between devices: 100 us -> 203 us  [the longest x4 203 us: gather_rows(): near = lax.all_gather(shard, ('chip', 'ctx'), axis=0, tiled=True)]
    reduce_scatter x8, waiting for transfers between devices: 199 us -> 295 us  [the longest x4 270 us: scatter_rows(): lax.psum_scatter(near, ('chip', 'ctx'), scatter_dimension=0, tiled=True)]
    pallas_call x0 -> x2, Pallas kernels: none -> 55.1 us  [the longest x1 27.8 us: attention_backward(): pl.pallas_call(backward_kernel, grid=(pairs,), in_specs=[pl.BlockSpec((ro...]
    all_gather x1, blocking collectives: 64.7 us -> 119 us  [on_device(): lax.all_gather(small, ('chip', 'core', 'ctx'), axis=0, tiled=False)]
    convert_element_type x23 -> x2, other arithmetic: 53.9 us -> 0.13 us  [the longest x1 0.13 us: on_device(): small_all = small_all.astype(jnp.float32)]
    reshape x4 -> x1, local copies, waits for them, and re-layouts: 41.4 us -> 1.7 us  [unfold(): return stored.reshape(stored.shape[0] // 8, stored.shape[1] * 8)]
    convert_element_type x6, local copies, waits for them, and re-layouts: 43.2 us -> 5.2 us  [on_device(): back = lambda matrix: refold(by_chip(matrix, 1, chips).astype(jnp.float32))]
  transfers between devices with their start and end apart: 16 -> 21, of which waited for: 10 -> 8; matrix products, arithmetic and copies ran while one was open for 41% -> 16% of each run, Pallas kernels for 0% -> 6%
where the time goes in v1:
time: 989 us; the launch traced here: 981 us
  waiting for transfers between devices  500 us (51%)
  blocking collectives  212 us (21%)
  matrix products  156 us (16%)
  Pallas kernels  55.1 us (6%)
  local copies, waits for them, and re-layouts  27.6 us (3%)
  between operations  15.3 us (2%)
    reduce_scatter x4, waiting for transfers between devices, scatter_rows(): lax.psum_scatter(near, ('chip', 'ctx'), scatter_dimension=0, tiled=True)  270 us
    all_gather x4, waiting for transfers between devices, gather_rows(): near = lax.all_gather(shard, ('chip', 'ctx'), axis=0, tiled=True)  203 us
    dot_general x19, matrix products, matmul(): return jnp.dot(left, right, preferred_element_type=jnp.float32)  139 us
    all_gather x1, blocking collectives, on_device(): lax.all_gather(small, ('chip', 'core', 'ctx'), axis=0, tiled=False)  119 us
    unnamed x1, blocking collectives  92.9 us
    pallas_call x1, Pallas kernels, attention_backward(): pl.pallas_call(backward_kernel, grid=(pairs,), in_specs=[pl.BlockSpec((ro...  27.8 us
    pallas_call x1, Pallas kernels, attention_forward(): pl.pallas_call(forward_kernel, grid=(pairs,), in_specs=[pl.BlockSpec((row...  27.2 us
    reduce_scatter x4, waiting for transfers between devices, scatter_rows(): lax.psum_scatter(matrix.astype(jnp.bfloat16), 'core', scatter_dimension=0...  25.5 us
  transfers between devices with their start and end apart: 21, of which 8 were waited for; matrix products, arithmetic and copies ran while one was open for 16% of the time, Pallas kernels for 6%

profile of v1, /device:TPU:0, one launch (start us, length us, event | category | flops | bytes accessed | tf_op | source)
XLA Modules:
  0.0 981.0 jit_solution(12908975108375870028)
XLA Ops:
  9.1 1.7 reshape.297
  10.9 1.7 copy.67
  12.7 56.6 %all-gather.15.cloned.1.call-done = bf16[512,1024]{1,0:T(8,128)(2,1)} async-done(((bf16[32,1024]{1,0:T(8,128)(2,1)}), bf16[512,1024]{1,0:T(8,128)(2,1)}) %all-gather.15.cloned.1.call-update) | async-done | bytes 1048592 | tf_op jit(solution)/shard_map/all_gather | solution.py:489
  69.7 1.1 copy.59
  70.8 68.9 %all-gather.11.cloned.1.call-done = bf16[512,3072]{1,0:T(8,128)(2,1)} async-done(((bf16[32,3072]{1,0:T(8,128)(2,1)}), bf16[512,3072]{1,0:T(8,128)(2,1)}) %all-gather.11.cloned.1.call-update) | async-done | bytes 3145744 | tf_op jit(solution)/shard_map/all_gather | solution.py:489
  139.9 77.6 %all-gather.19.cloned.1.call-done = bf16[512,4096]{1,0:T(8,128)(2,1)} async-done(((bf16[32,4096]{1,0:T(8,128)(2,1)}), bf16[512,4096]{1,0:T(8,128)(2,1)}) %all-gather.19.cloned.1.call-update) | async-done | bytes 4194320 | tf_op jit(solution)/shard_map/all_gather | solution.py:489
  217.6 1.5 collective-permute-start
  219.7 1.5 collective-permute-start.3
  221.4 118.8 %all-gather.1 = bf16[32,1,384]{2,1,0:T(2,128)(2,1)S(1)} all-gather(bf16[1,1,384]{2,1,0:T(2,128)(2,1)S(1)} %reshape.323), channel_id=2, replica_groups=mesh['chip'=8,'core'=2,'ctx'=2] {'chip','core','ctx'}, dimensions={0}, use_global_device_ids=true | all-gather | bytes 25344 | tf_op jit(solution)/shard_map/all_gather | solution.py:535
  343.3 3.8 fusion.25
  347.1 3.9 fusion.26
  351.0 5.9 fusion.50
  356.9 2.5 multiply_reduce_fusion.5
  359.4 7.5 convert_reduce_fusion.1
  366.9 3.1 copy.58
  370.4 7.5 add_convert_fusion.query_ref.key_ref.value_ref
  378.0 27.2 %attention_forward.1 = (bf16[592,1024]{1,0:T(8,128)(2,1)S(1)}, f32[8,2,592]{2,1,0:T(2,128)S(1)}) custom-call(bf16[592,3072]{1,0:T(8,128)(2,1)S(1)} %add_convert_fusion.query_ref.key_ref.value_ref, bf16[592,3072]{1,0:T(8,128)(2,1)S(1)} %add_convert_fusion.query_ref.key_ref.value_ref, bf16[592,3072]{1,0:T(8,128)(2,1)S(1)} %add_convert_fusion.query_ref.key_ref.value_ref, ...), custom_call_target="tpu_custom_call" | custom-call | flops 5742002176 | bytes 4849664 | tf_op jit(solution)/shard_map/attention_forward/pallas_call | solution.py:405
  405.3 2.9 fusion.51
  408.2 2.1 multiply_reduce_fusion.4
  410.3 30.9 %fusion.2 = (bf16[592,4096]{1,0:T(8,128)(2,1)}, f32[592,4096]{1,0:T(8,128)}) fusion(f32[4096]{0:T(1024)S(1)} %slice_bitcast_fusion, bf16[1024,4096]{1,0:T(8,128)(2,1)} %all-gather.21.cloned.1.call-done, f32[592,1024]{1,0:T(8,128)} %get-tuple-element.62, f32[1024]{0:T(1024)S(1)} %add.179, f32[1024]{0:T(1024)S(1)} %mul.147, f32[592]{0:T(1024)S(1)} %add_rsqrt_fusion, ...), kind=kOutput, calls=%fused_computation.4 | convolution fusion | flops 5129125888 | bytes 25391744 | tf_op jit(solution)/shard_map/dot_general | solution.py:27
  441.2 12.5 %convert_reduce_fusion = (f32[4096]{0:T(1024)S(1)}, bf16[592,4096]{1,0:T(8,128)(2,1)S(1)}) fusion(f32[592,4096]{1,0:T(8,128)} %get-tuple-element.64, f32[4096]{0:T(1024)S(1)} %slice_bitcast_fusion, bf16[592,1024]{1,0:T(8,128)(2,1)S(1)} %copy-done.42, bf16[4096,1024]{0,1:T(8,128)(2,1)} %all-gather.25.cloned.1.call-done), kind=kOutput, calls=%fused_computation.10 | convolution fusion | flops 5002424320 | bytes 24182784 | tf_op jit(solution)/shard_map/dot_general | solution.py:27
  453.8 9.1 multiply_reduce_fusion
  463.0 2.4 convert_reduce_fusion.2
  465.4 1.8 convolution_convert_fusion.3
  467.2 1.5 copy.61
  469.7 3.6 convolution_convert_fusion.4.d_ref
  473.5 27.8 %attention_backward.1 = (bf16[592,1024]{1,0:T(8,128)(2,1)S(1)}, bf16[592,1024]{1,0:T(8,128)(2,1)S(1)}, bf16[592,1024]{1,0:T(8,128)(2,1)S(1)}) custom-call(bf16[592,3072]{1,0:T(8,128)(2,1)S(1)} %copy-done.3, bf16[592,3072]{1,0:T(8,128)(2,1)S(1)} %copy-done.3, bf16[592,3072]{1,0:T(8,128)(2,1)S(1)} %copy-done.3, ...), custom_call_target="tpu_custom_call" | custom-call | flops 14355005440 | bytes 8486912 | tf_op jit(solution)/shard_map/attention_backward/pallas_call | solution.py:435
  501.7 1.8 copy-done.12
  504.3 7.2 convolution_convert_fusion.2
  511.6 12.4 %convolution_convert_fusion = bf16[1024,4096]{1,0:T(8,128)(2,1)} fusion(bf16[592,4096]{1,0:T(8,128)(2,1)} %copy-done.41, f32[592,1024]{1,0:T(8,128)} %get-tuple-element.62, f32[1024]{0:T(1024)S(1)} %add.179, f32[1024]{0:T(1024)S(1)} %mul.147, f32[592]{0:T(1024)S(1)} %add_rsqrt_fusion, f32[592]{0:T(1024)S(1)} %broadcast_multiply_fusion.4), kind=kOutput, calls=%fused_computation.27 | convolution fusion | flops 4973281280 | bytes 15676032 | tf_op jit(solution)/shard_map/dot_general | solution.py:27
  524.1 11.5 %convolution_convert_fusion.1 = bf16[4096,1024]{1,0:T(8,128)(2,1)} fusion(bf16[592,4096]{1,0:T(8,128)(2,1)} %get-tuple-element.63, bf16[592,1024]{1,0:T(8,128)(2,1)} %get-tuple-element.38), kind=kOutput, calls=%fused_computation.28 | convolution fusion | flops 4970250240 | bytes 14450688 | tf_op jit(solution)/shard_map/dot_general | solution.py:27
  537.0 5.4 reduce-scatter.17.cloned.1.call-done
  542.7 20.1 %reduce-scatter.21.cloned.1.call-done = bf16[2048,1024]{1,0:T(8,128)(2,1)} async-done(((bf16[4096,1024]{1,0:T(8,128)(2,1)}), bf16[2048,1024]{1,0:T(8,128)(2,1)}) %reduce-scatter.21.cloned.1.call-update) | async-done | bytes 4194320 | tf_op jit(solution)/shard_map/reduce_scatter | solution.py:494
  563.0 13.1 %fusion.23 = bf16[592,1024]{1,0:T(8,128)(2,1)} fusion(s32[1024]{0:T(1024)S(1)} %copy-done.20, f32[592,1024]{1,0:T(8,128)} %get-tuple-element.62, bf16[592,4096]{1,0:T(8,128)(2,1)} %get-tuple-element.63, bf16[4096,1024]{0,1:T(8,128)(2,1)} %all-gather.25.cloned.1.call-done, f32[1024]{0:T(1024)S(1)} %add.186), kind=kOutput, calls=%fused_computation.67 | convolution fusion | flops 6211043328 | bytes 16883712 | tf_op jit(solution)/shard_map/dot_general | solution.py:329
  576.1 1.8 collective-permute-start.2
  577.9 9.0 multiply_reduce_fusion.1
  587.0 3.0 fusion.24
  591.7 92.9 %all-reduce = f32[32,384]{1,0:T(8,128)S(1)} all-reduce(f32[32,384]{1,0:T(8,128)S(1)} %pad_maximum_fusion), channel_id=5, replica_groups=mesh['chip'=8,'core'=2,'ctx'=2] {'chip','core','ctx'}, use_global_device_ids=true, to_apply=%region_23.24.clone | all-reduce | flops 12288 | bytes 98304
  685.8 2.5 fusion.28
  688.4 1.1 fusion.27
  689.5 3.5 add_convert_fusion.7
  693.0 2.6 convolution_add_fusion
  697.6 79.9 %reduce-scatter.11.cloned.1.call-done = bf16[32,3072]{1,0:T(8,128)(2,1)} async-done(((bf16[512,3072]{1,0:T(8,128)(2,1)}), bf16[32,3072]{1,0:T(8,128)(2,1)}) %reduce-scatter.11.cloned.1.call-update) | async-done | bytes 196624 | tf_op jit(solution)/shard_map/reduce_scatter | solution.py:497
  777.4 1.8 reshape.313
  779.2 95.4 %reduce-scatter.19.cloned.1.call-done = bf16[32,4096]{1,0:T(8,128)(2,1)} async-done(((bf16[512,4096]{1,0:T(8,128)(2,1)}), bf16[32,4096]{1,0:T(8,128)(2,1)}) %reduce-scatter.19.cloned.1.call-update) | async-done | bytes 262160 | tf_op jit(solution)/shard_map/reduce_scatter | solution.py:497
  874.5 1.8 copy.68
  876.3 94.4 %reduce-scatter.23.cloned.1.call-done = bf16[128,1024]{1,0:T(8,128)(2,1)} async-done(((bf16[2048,1024]{1,0:T(8,128)(2,1)}), bf16[128,1024]{1,0:T(8,128)(2,1)}) %reduce-scatter.23.cloned.1.call-update) | async-done | bytes 262160 | tf_op jit(solution)/shard_map/reduce_scatter | solution.py:497
  972.6 1.4 reshape.316
  (195 shorter events, 17.5 us)
Async XLA Ops:
  7.2 62.2 %copy-start.13 = (bf16[1024,128]{1,0:T(8,128)(2,1)S(1)}, bf16[1024,128]{1,0:T(8,128)(2,1)}, u32[]{:S(2)}) copy-start(bf16[1024,128]{1,0:T(8,128)(2,1)} %param.30) | copy-start | bytes 786436
  7.2 62.1 %all-gather.15.cloned.1.call-start = ((), (), s32[]{:S(2)}) async-start(), calls=%async_computation.10 | async-start | bytes 1114112 | tf_op jit(solution)/shard_map/all_gather | solution.py:489
  9.0 130.7 %all-gather.11.cloned.1.call-start = ((), (), s32[]{:S(2)}) async-start(), calls=%async_computation.8 | async-start | bytes 3342336 | tf_op jit(solution)/shard_map/all_gather | solution.py:489
  10.8 206.7 %all-gather.19.cloned.1.call-start = ((), (), s32[]{:S(2)}) async-start(), calls=%async_computation.12 | async-start | bytes 4456448 | tf_op jit(solution)/shard_map/all_gather | solution.py:489
  12.6 354.3 %all-gather.17.cloned.1.call-start = ((), (), s32[]{:S(2)}) async-start(), calls=%async_computation.11 | async-start | bytes 3145728 | tf_op jit(solution)/shard_map/all_gather | solution.py:490
  69.3 300.7 %all-gather.23.cloned.1.call-start = ((), (), s32[]{:S(2)}) async-start(), calls=%async_computation.14 | async-start | bytes 4456448 | tf_op jit(solution)/shard_map/all_gather | solution.py:489
  70.8 299.6 %all-gather.13.cloned.1.call-start = ((), (), s32[]{:S(2)}) async-start(), calls=%async_computation.9 | async-start | bytes 9437184 | tf_op jit(solution)/shard_map/all_gather | solution.py:490
  139.8 77.8 %copy-start.15 = (s32[584]{0:T(1024)S(1)}, s32[584]{0:T(1024)}, u32[]{:S(2)}) copy-start(s32[584]{0:T(1024)} %param.18) | copy-start | bytes 7012
  139.8 81.4 %copy-start.30 = (bf16[32]{0:T(256)(128)(2,1)S(1)}, bf16[32]{0:T(256)(128)(2,1)}, u32[]{:S(2)}) copy-start(bf16[32]{0:T(256)(128)(2,1)} %param.20) | copy-start | bytes 196
  139.8 81.4 %copy-start.31 = (bf16[32]{0:T(256)(128)(2,1)S(1)}, bf16[32]{0:T(256)(128)(2,1)}, u32[]{:S(2)}) copy-start(bf16[32]{0:T(256)(128)(2,1)} %param.21) | copy-start | bytes 196
  139.8 81.4 %copy-start.32 = (bf16[32]{0:T(256)(128)(2,1)S(1)}, bf16[32]{0:T(256)(128)(2,1)}, u32[]{:S(2)}) copy-start(bf16[32]{0:T(256)(128)(2,1)} %param.23) | copy-start | bytes 196
  139.8 81.4 %copy-start.33 = (bf16[32]{0:T(256)(128)(2,1)S(1)}, bf16[32]{0:T(256)(128)(2,1)}, u32[]{:S(2)}) copy-start(bf16[32]{0:T(256)(128)(2,1)} %param.24) | copy-start | bytes 196
  139.8 81.4 %copy-start.34 = (bf16[32]{0:T(256)(128)(2,1)S(1)}, bf16[32]{0:T(256)(128)(2,1)}, u32[]{:S(2)}) copy-start(bf16[32]{0:T(256)(128)(2,1)} %param.25) | copy-start | bytes 196
  139.8 81.4 %copy-start.35 = (bf16[32]{0:T(256)(128)(2,1)S(1)}, bf16[32]{0:T(256)(128)(2,1)}, u32[]{:S(2)}) copy-start(bf16[32]{0:T(256)(128)(2,1)} %param.26) | copy-start | bytes 196
  139.8 81.4 %copy-start.36 = (bf16[32]{0:T(256)(128)(2,1)S(1)}, bf16[32]{0:T(256)(128)(2,1)}, u32[]{:S(2)}) copy-start(bf16[32]{0:T(256)(128)(2,1)} %param.27) | copy-start | bytes 196
  139.9 81.4 %copy-start.37 = (bf16[32]{0:T(256)(128)(2,1)S(1)}, bf16[32]{0:T(256)(128)(2,1)}, u32[]{:S(2)}) copy-start(bf16[32]{0:T(256)(128)(2,1)} %param.31) | copy-start | bytes 196
  139.9 81.4 %copy-start.38 = (bf16[128]{0:T(256)(128)(2,1)S(1)}, bf16[128]{0:T(256)(128)(2,1)}, u32[]{:S(2)}) copy-start(bf16[128]{0:T(256)(128)(2,1)} %param.29) | copy-start | bytes 772
  139.9 270.4 %all-gather.21.cloned.1.call-start = ((), (), s32[]{:S(2)}) async-start(), calls=%async_computation.13 | async-start | bytes 12582912 | tf_op jit(solution)/shard_map/all_gather | solution.py:490
  217.6 223.7 %all-gather.25.cloned.1.call-start = ((), (), s32[]{:S(2)}) async-start(), calls=%async_computation.15 | async-start | bytes 12582912 | tf_op jit(solution)/shard_map/all_gather | solution.py:490
  217.6 124.4 %collective-permute-start = (s32[584]{0:T(1024)S(1)}, s32[584]{0:T(1024)S(1)}, u32[]{:S(2)}, u32[]{:S(2)}) collective-permute-start(s32[584]{0:T(1024)S(1)} %copy-done.15), channel_id=1, source_target_pairs={{0,1},{1,0},{2,3},{3,2},{4,5},{5,4},{6,7},{7,6},{8,9},{9,8},{10,11... | collective-permute-start | bytes 7016 | tf_op jit(solution)/shard_map/ppermute | solution.py:524
  219.2 131.8 %collective-permute-start.1 = (bf16[584,1024]{1,0:T(8,128)(2,1)}, bf16[584,1024]{1,0:T(8,128)(2,1)}, u32[]{:S(2)}, u32[]{:S(2)}) collective-permute-start(bf16[584,1024]{1,0:T(8,128)(2,1)} %param.16), channel_id=1, source_target_pairs={{0,1},{1,0},{2,3},{3,2},{4,5},{5,4},{6,7},{7,6},{8,9},{9,8},{10,11... | collective-permute-start | bytes 3588104 | tf_op jit(solution)/shard_map/ppermute | solution.py:524
  219.7 139.7 %collective-permute-start.3 = (bf16[584,1024]{1,0:T(8,128)(2,1)}, bf16[584,1024]{1,0:T(8,128)(2,1)}, u32[]{:S(2)}, u32[]{:S(2)}) collective-permute-start(bf16[584,1024]{1,0:T(8,128)(2,1)} %param.17), channel_id=1, source_target_pairs={{0,1},{1,0},{2,3},{3,2},{4,5},{5,4},{6,7},{7,6},{8,9},{9,8},{10,11... | collective-permute-start | bytes 3588104 | tf_op jit(solution)/shard_map/ppermute | solution.py:524
  341.5 36.4 %copy-start = (f32[592,592]{1,0:T(8,128)}, f32[592,592]{1,0:T(8,128)S(1)}, u32[]{:S(2)}) copy-start(f32[592,592]{1,0:T(8,128)S(1)} %compare_select_fusion.bias_ref) | copy-start | bytes 4205572
  341.6 17.8 %copy-start.19 = (s32[1024]{0:T(1024)}, s32[1024]{0:T(1024)S(1)}, u32[]{:S(2)}) copy-start(s32[1024]{0:T(1024)S(1)} %reshape.294) | copy-start | bytes 12292
  341.7 28.6 %copy-start.21 = (f32[1024]{0:T(1024)}, f32[1024]{0:T(1024)S(1)}, u32[]{:S(2)}) copy-start(f32[1024]{0:T(1024)S(1)} %mul.141) | copy-start | bytes 12292
  341.9 28.5 %copy-start.24 = (f32[1024]{0:T(1024)}, f32[1024]{0:T(1024)S(1)}, u32[]{:S(2)}) copy-start(f32[1024]{0:T(1024)S(1)} %add.168) | copy-start | bytes 12292
  356.9 13.5 %copy-start.16 = (f32[592]{0:T(1024)}, f32[592]{0:T(1024)S(1)}, u32[]{:S(2)}) copy-start(f32[592]{0:T(1024)S(1)} %broadcast_multiply_fusion.5) | copy-start | bytes 7108
  359.3 11.0 %copy-start.26 = (f32[592]{0:T(1024)}, f32[592]{0:T(1024)S(1)}, u32[]{:S(2)}) copy-start(f32[592]{0:T(1024)S(1)} %add_rsqrt_fusion.1) | copy-start | bytes 7108
  370.1 165.6 %reduce-scatter.13.cloned.1.call-start = ((), (), s32[]{:S(2)}) async-start(), calls=%async_computation.18 | async-start | bytes 3145728 | tf_op jit(solution)/shard_map/reduce_scatter | solution.py:494
  377.9 27.3 %copy-start.2 = (bf16[592,3072]{1,0:T(8,128)(2,1)}, bf16[592,3072]{1,0:T(8,128)(2,1)S(1)}, u32[]{:S(2)}) copy-start(bf16[592,3072]{1,0:T(8,128)(2,1)S(1)} %add_convert_fusion.query_ref.key_ref.value_ref) | copy-start | bytes 10911748
  378.0 27.3 %copy-start.8 = (f32[592,1024]{1,0:T(8,128)S(1)}, f32[592,1024]{1,0:T(8,128)}, u32[]{:S(2)}) copy-start(f32[592,1024]{1,0:T(8,128)} %get-tuple-element.60) | copy-start | bytes 7274500
  378.0 27.3 %copy-start.11 = (bf16[2,8,64,1024]{3,2,0,1:T(8,128)(2,1)S(1)}, bf16[2,8,64,1024]{3,2,0,1:T(8,128)(2,1)}, u32[]{:S(2)}) copy-start(bf16[2,8,64,1024]{3,2,0,1:T(8,128)(2,1)} %copy.58) | copy-start | bytes 6291460
  410.3 30.9 %copy-start.42 = (bf16[592,1024]{1,0:T(8,128)(2,1)S(1)}, bf16[592,1024]{1,0:T(8,128)(2,1)}, u32[]{:S(2)}) copy-start(bf16[592,1024]{1,0:T(8,128)(2,1)} %get-tuple-element.38) | copy-start | bytes 3637252
  441.2 12.6 %copy-start.39 = (bf16[1024,4096]{1,0:T(8,128)(2,1)S(1)}, bf16[1024,4096]{1,0:T(8,128)(2,1)}, u32[]{:S(2)}) copy-start(bf16[1024,4096]{1,0:T(8,128)(2,1)} %all-gather.21.cloned.1.call-done) | copy-start | bytes 25165828
  468.8 67.6 %reduce-scatter.9.cloned.1.call-start = ((), (), s32[]{:S(2)}) async-start(), calls=%async_computation.16 | async-start | bytes 9437184 | tf_op jit(solution)/shard_map/reduce_scatter | solution.py:494
  511.6 30.8 %reduce-scatter.17.cloned.1.call-start = ((), (), s32[]{:S(2)}) async-start(), calls=%async_computation.20 | async-start | bytes 12582912 | tf_op jit(solution)/shard_map/reduce_scatter | solution.py:494
  524.0 38.8 %reduce-scatter.21.cloned.1.call-start = ((), (), s32[]{:S(2)}) async-start(), calls=%async_computation.22 | async-start | bytes 12582912 | tf_op jit(solution)/shard_map/reduce_scatter | solution.py:494
  535.6 160.0 %reduce-scatter.15.cloned.1.call-start = ((), (), s32[]{:S(2)}) async-start(), calls=%async_computation.19 | async-start | bytes 1114112 | tf_op jit(solution)/shard_map/reduce_scatter | solution.py:497
  536.3 241.1 %reduce-scatter.11.cloned.1.call-start = ((), (), s32[]{:S(2)}) async-start(), calls=%async_computation.17 | async-start | bytes 3342336 | tf_op jit(solution)/shard_map/reduce_scatter | solution.py:497
  536.9 337.6 %reduce-scatter.19.cloned.1.call-start = ((), (), s32[]{:S(2)}) async-start(), calls=%async_computation.21 | async-start | bytes 4456448 | tf_op jit(solution)/shard_map/reduce_scatter | solution.py:497
  542.4 20.4 %copy-start.14 = (f32[32,32]{1,0:T(8,128)S(1)}, f32[32,32]{1,0:T(8,128)}, u32[]{:S(2)}) copy-start(f32[32,32]{1,0:T(8,128)} %get-tuple-element.49) | copy-start | bytes 12292
  542.4 20.5 %copy-start.23 = (f32[1024]{0:T(1024)S(1)}, f32[1024]{0:T(1024)}, u32[]{:S(2)}) copy-start(f32[1024]{0:T(1024)} %get-tuple-element.37) | copy-start | bytes 12292
  542.4 20.5 %copy-start.20 = (s32[1024]{0:T(1024)S(1)}, s32[1024]{0:T(1024)}, u32[]{:S(2)}) copy-start(s32[1024]{0:T(1024)} %copy-done.19) | copy-start | bytes 12292
  542.4 428.3 %reduce-scatter.23.cloned.1.call-start = ((), (), s32[]{:S(2)}) async-start(), calls=%async_computation.23 | async-start | bytes 4456448 | tf_op jit(solution)/shard_map/reduce_scatter | solution.py:497
  576.1 10.9 %copy-start.10 = (f32[592,1024]{1,0:T(8,128)S(1)}, f32[592,1024]{1,0:T(8,128)}, u32[]{:S(2)}) copy-start(f32[592,1024]{1,0:T(8,128)} %get-tuple-element.60) | copy-start | bytes 7274500
  576.1 113.4 %collective-permute-start.2 = (bf16[592,1024]{1,0:T(8,128)(2,1)}, bf16[592,1024]{1,0:T(8,128)(2,1)}, u32[]{:S(2)}, u32[]{:S(2)}) collective-permute-start(bf16[592,1024]{1,0:T(8,128)(2,1)} %fusion.23), channel_id=1, source_target_pairs={{0,1},{1,0},{2,3},{3,2},{4,5},{5,4},{6,7},{7,6},{8,9},{9,8},{10,11... | collective-permute-start | bytes 3637256 | tf_op jit(solution)/shard_map/ppermute | solution.py:524
  589.9 95.9 %copy-start.29 = (s32[584]{0:T(1024)S(1)}, s32[584]{0:T(1024)}, u32[]{:S(2)}) copy-start(s32[584]{0:T(1024)} %copy-done.28) | copy-start | bytes 7012
  591.2 101.8 %collective-permute-start.4 = (bf16[592,1024]{1,0:T(8,128)(2,1)}, bf16[592,1024]{1,0:T(8,128)(2,1)S(1)}, u32[]{:S(2)}, u32[]{:S(2)}) collective-permute-start(bf16[592,1024]{1,0:T(8,128)(2,1)} %fusion.24), channel_id=1, source_target_pairs={{0,1},{1,0},{2,3},{3,2},{4,5},{5,4},{6,7},{7,6},{8,9},{9,8},{10,11... | collective-permute-start | bytes 3637256 | tf_op jit(solution)/shard_map/ppermute | solution.py:524
  (16 other events, 64.6 us)
Sparse Core Ops, SparseCore 0:
  11.4 57.9 all-gather.14
  72.8 66.9 all-gather.10
  143.1 74.4 all-gather.18
  218.9 9.1 all-gather.16
  231.3 99.4 all-gather.22
  332.1 14.9 all-gather.12
  348.6 21.0 all-gather.20
  371.2 21.0 all-gather.24
  468.9 5.7 reduce-scatter.12
  511.7 10.3 reduce-scatter.8
  524.4 17.9 reduce-scatter.16
  544.6 18.0 reduce-scatter.20
  565.0 79.7 reduce-scatter.14
  650.4 126.9 reduce-scatter.10
  779.7 94.8 reduce-scatter.18
  876.8 93.9 reduce-scatter.22

commit v2 on v1

--- a/solution.py
+++ b/solution.py
@@ -473,35 +473,106 @@
     return phi + value * jnp.exp(-0.5 * value * value) * (1.0 / math.sqrt(2.0 * math.pi))
 
 
-def by_core(array, axis, chips):
+def to_local(array, axis, far):
     shape = array.shape
-    cut = shape[:axis] + (chips, 2, shape[axis] // (2 * chips)) + shape[axis + 1 :]
-    return jnp.swapaxes(array.reshape(cut), axis, axis + 1).reshape(shape)
-
-
-def by_chip(array, axis, chips):
+    cut = shape[:axis] + (far, 2, 2, 2, shape[axis] // (8 * far)) + shape[axis + 1 :]
+    spots = [axis + 2, axis + 1, axis + 3, axis]
+    spots = list(range(axis)) + spots + list(range(axis + 4, len(cut)))
+    return array.reshape(cut).transpose(spots).reshape(shape)
+
+
+def to_natural(array, axis, far):
     shape = array.shape
-    cut = shape[:axis] + (2, chips, shape[axis] // (2 * chips)) + shape[axis + 1 :]
-    return jnp.swapaxes(array.reshape(cut), axis, axis + 1).reshape(shape)
-
-
-def gather_rows(shard):
-    near = lax.all_gather(shard, ("chip", "ctx"), axis=0, tiled=True)
-    return lax.all_gather(near, "core", axis=0, tiled=True)
-
-
-def scatter_rows(matrix):
-    near = lax.psum_scatter(
-        matrix.astype(jnp.bfloat16), "core", scatter_dimension=0, tiled=True
-    )
-    return lax.psum_scatter(near, ("chip", "ctx"), scatter_dimension=0, tiled=True)
+    cut = shape[:axis] + (2, 2, 2, far, shape[axis] // (8 * far)) + shape[axis + 1 :]
+    spots = [axis + 3, axis + 1, axis, axis + 2]
+    spots = list(range(axis)) + spots + list(range(axis + 4, len(cut)))
+    return array.reshape(cut).transpose(spots).reshape(shape)
+
+
+def assemble_kernel(index_ref, *refs):
+    *pieces, whole, arrived = refs
+    copies = []
+    for number, piece in enumerate(pieces):
+        size = piece.shape[0]
+        start = pl.multiple_of(index_ref[number] * size, 16)
+        copies.append(
+            pltpu.make_async_copy(piece, whole.at[pl.ds(start, size)], arrived.at[number])
+        )
+    for copy in copies:
+        copy.start()
+    for copy in copies:
+        copy.wait()
+
+
+def assemble(pieces, indices):
+    size, width = pieces[0].shape
+    count = len(pieces)
+    return pl.pallas_call(
+        assemble_kernel,
+        in_specs=[pl.BlockSpec(memory_space=pltpu.SMEM)]
+        + [pl.BlockSpec(memory_space=pl.ANY)] * count,
+        out_specs=pl.BlockSpec(memory_space=pl.ANY),
+        out_shape=jax.ShapeDtypeStruct((count * size, width), pieces[0].dtype),
+        scratch_shapes=[pltpu.SemaphoreType.DMA((count,))],
+        cost_estimate=pl.CostEstimate(
+            flops=0, bytes_accessed=4 * count * size * width, transcendentals=0
+        ),
+        name="assemble",
+    )(jnp.stack(indices).astype(jnp.int32), *pieces)
+
+
+def trade(array, axis):
+    return lax.ppermute(array, axis, [(0, 1), (1, 0)])
+
+
+def after(array, other):
+    return lax.optimization_barrier((array, other))[0]
+
+
+def gather_far(shard, far):
+    place = lax.axis_index("z")
+    pieces, indices = [shard], [place]
+    for step in range(1, far):
+        pieces.append(lax.ppermute(shard, "z", [(i, (i + step) % far) for i in range(far)]))
+        indices.append((place - step) % far)
+    return assemble(pieces, indices)
+
+
+def gather_near(block):
+    own = 4 * lax.axis_index("core") + 2 * lax.axis_index("x") + lax.axis_index("ctx")
+    blocks = [block]
+    for axis in ("ctx", "x", "core"):
+        blocks = blocks + [trade(one, axis) for one in blocks]
+    return assemble(blocks, [own ^ number for number in range(8)])
+
+
+def scatter_rows(matrix, far):
+    for axis in ("core", "x", "ctx"):
+        half = matrix.shape[0] // 2
+        place = lax.axis_index(axis)
+        kept = lax.dynamic_slice_in_dim(matrix, place * half, half)
+        sent = lax.dynamic_slice_in_dim(matrix, (1 - place) * half, half)
+        total = kept.astype(jnp.float32) + trade(sent, axis).astype(jnp.float32)
+        matrix = total.astype(matrix.dtype)
+    size = matrix.shape[0] // far
+    place = lax.axis_index("z")
+    total = lax.dynamic_slice_in_dim(matrix, place * size, size).astype(jnp.float32)
+    for step in range(1, far):
+        sent = lax.dynamic_slice_in_dim(matrix, ((place + step) % far) * size, size)
+        got = lax.ppermute(sent, "z", [(i, (i + step) % far) for i in range(far)])
+        total = total + got.astype(jnp.float32)
+    return total
+
+
+def scatter_low(matrix, far):
+    return scatter_rows(matrix.astype(jnp.bfloat16), far)
 
 
 def column_sums(array):
     return jnp.sum(array.astype(jnp.float32), axis=0)
 
 
-def by_image(chips):
+def by_image(far):
     def on_device(
         inputs,
         cotangent,
@@ -521,7 +592,7 @@
         b_down,
     ):
         place = lax.axis_index("ctx")
-        swap = lambda array: lax.ppermute(array, "ctx", [(0, 1), (1, 0)])
+        swap = lambda array: trade(array, "ctx")
         slots, width = inputs.shape
         pads = 2 * slots - IMAGES * SEQ
         rows = round_up(SEQ + pads, 16)
@@ -532,15 +603,18 @@
         small = jnp.concatenate(
             [b_query, b_value, b_out, norm1_gain, norm1_shift, norm2_gain, norm2_shift, b_down, b_up]
         )
-        small_all = lax.all_gather(small, ("chip", "core", "ctx"), axis=0, tiled=False)
-        qkv_weight = gather_rows(unfold(w_qkv))
-        out_weight = by_chip(gather_rows(by_core(unfold(w_out), 1, chips)), 0, chips)
-        up_weight = gather_rows(by_core(unfold(w_up), 1, chips))
-        down_weight = gather_rows(by_core(unfold(w_down), 1, chips))
-        cotangent_far = swap(cotangent)
+        small_all = lax.all_gather(small, ("z", "x", "core", "ctx"), axis=0, tiled=False)
+        far_qkv = gather_far(unfold(w_qkv), far)
+        qkv_weight = gather_near(far_qkv)
+        far_out = gather_far(to_local(after(unfold(w_out), far_qkv), 1, far), far)
+        far_up = gather_far(to_local(after(unfold(w_up), far_qkv), 1, far), far)
+        far_down = gather_far(to_local(after(unfold(w_down), far_up), 1, far), far)
+        out_weight = to_natural(gather_near(far_out), 0, far)
+        up_weight = gather_near(far_up)
+        down_weight = gather_near(far_down)
 
         small_all = small_all.astype(jnp.float32)
-        small_core = by_core(small_all, 0, chips)
+        small_core = to_local(small_all, 0, far)
         piece = lambda table, index: table[:, index * near_width : (index + 1) * near_width].reshape(-1)
         query_bias = piece(small_all, 0)
         value_bias = piece(small_all, 1)
@@ -572,7 +646,7 @@
         give_far = other_image[:, None] == row[None, :]
         give_near, give_far = give_near.astype(jnp.bfloat16), give_far.astype(jnp.bfloat16)
         column = jnp.arange(width)
-        order = by_core(column, 0, chips)
+        order = to_local(column, 0, far)
         to_core = (column[:, None] == order[None, :]).astype(jnp.bfloat16)
 
         def take(near, far):
@@ -601,23 +675,26 @@
         outputs = give(middle + matmul(active, down_weight) + down_bias).astype(jnp.bfloat16)
 
         live = (row < SEQ).astype(jnp.float32)[:, None]
+        cotangent_far = swap(after(cotangent, joined))
         d_out = take(cotangent, cotangent_far) * live
         d_out_low = d_out.astype(jnp.bfloat16)
-        sum_down = scatter_rows(matmul(active.T, d_out_low))
+        sum_down = scatter_low(matmul(active.T, d_out_low), far)
         d_hidden = (matmul(d_out_low, down_weight.T) * slope.astype(jnp.float32)).astype(jnp.bfloat16)
-        sum_up = scatter_rows(matmul(normed2.T, d_hidden))
+        sum_up = scatter_low(matmul(normed2.T, d_hidden), far)
         d_normed2 = matmul(d_hidden, up_weight.T)
         d_middle = d_out + norm_backward(d_normed2, normal2, scale2, second_gain)
         d_branch = d_middle.astype(jnp.bfloat16)
-        sum_out = scatter_rows(by_core(matmul(attended.T, d_branch).astype(jnp.bfloat16), 0, chips))
+        sum_out = scatter_low(
+            to_local(matmul(attended.T, d_branch).astype(jnp.bfloat16), 0, far), far
+        )
         d_attended = matmul(d_branch, out_weight.T).astype(jnp.bfloat16)
         d_query, d_key, d_value = attention_backward(joined, d_attended, log_total, bias)
         d_joined = jnp.concatenate([d_query, d_key, d_value], axis=1)
-        sum_qkv = scatter_rows(matmul(normed1.T, d_joined))
+        sum_qkv = scatter_low(matmul(normed1.T, d_joined), far)
         d_normed1 = matmul(d_joined, qkv_weight.T)
         input_grad = give(d_middle + norm_backward(d_normed1, normal1, scale1, first_gain))
 
-        part = lambda vector: vector.reshape(2 * chips * 2, -1)
+        part = lambda vector: vector.reshape(8 * far, -1)
         core_sums = jnp.concatenate(
             [
                 part(vector)
@@ -634,16 +711,14 @@
             axis=1,
         )
         chip_sums = jnp.concatenate([part(column_sums(d_query)), part(column_sums(d_value))], axis=1)
-        small_sums = jnp.concatenate([chip_sums, by_chip(core_sums, 0, chips)], axis=1)
-        small_sums = lax.psum_scatter(
-            small_sums, ("chip", "core", "ctx"), scatter_dimension=0, tiled=True
-        )[0]
+        small_sums = jnp.concatenate([to_local(chip_sums, 0, far), core_sums], axis=1)
+        small_sums = scatter_rows(small_sums, far)[0]
         own = lambda index: small_sums[index * near_width : (index + 1) * near_width]
-        back = lambda matrix: refold(by_chip(matrix, 1, chips).astype(jnp.float32))
+        back = lambda matrix: refold(to_natural(matrix, 1, far))
         return (
             outputs,
             input_grad,
-            refold(sum_qkv.astype(jnp.float32)),
+            refold(sum_qkv),
             own(0),
             own(1),
             back(sum_out),
@@ -662,12 +737,10 @@
 
 
 def solution(mesh):
-    if mesh.shape["ctx"] == IMAGES and mesh.shape["dp"] % 2 == 0:
-        chips = mesh.shape["dp"] // 2
-        mesh = jax.sharding.Mesh(
-            mesh.devices.reshape(chips, 2, IMAGES), ("chip", "core", "ctx")
-        )
-        body, axes = by_image(chips), ("chip", "core", "ctx")
+    if mesh.shape["ctx"] == IMAGES and mesh.shape["dp"] % 4 == 0:
+        far, axes = mesh.shape["dp"] // 4, ("z", "x", "core", "ctx")
+        mesh = jax.sharding.Mesh(mesh.devices.reshape(far, 2, 2, IMAGES), axes)
+        body = by_image(far)
     else:
         body, axes = on_device, ("dp", "ctx")
     matrix, vector = P(axes, None), P(axes)

time: 989 us -> 1560 us (1.58)
  Pallas kernels: 55.1 us -> 928 us
  waiting for transfers between devices: 500 us -> 239 us
  blocking collectives: 212 us -> 67.4 us
  starting transfers between devices: 7 us -> 79.5 us
  local copies, waits for them, and re-layouts: 27.6 us -> 56.6 us
  other arithmetic: 9.03 us -> 31.8 us
    pallas_call x0 -> x8, Pallas kernels: none -> 872 us  [assemble(): pl.pallas_call(assemble_kernel, in_specs=[pl.BlockSpec(memory_space=pltpu...]
    reduce_scatter x8 -> x0, waiting for transfers between devices: 295 us -> none  [the longest x4 270 us: scatter_rows(): lax.psum_scatter(near, ('chip', 'ctx'), scatter_dimension=0, tiled=True)]
    ppermute x5 -> x75, waiting for transfers between devices: 0.01 us -> 239 us  [the longest x48 190 us: trade(): return lax.ppermute(array, axis, [(0, 1), (1, 0)])]
    all_gather x8 -> x0, waiting for transfers between devices: 203 us -> none  [the longest x4 203 us: gather_rows(): near = lax.all_gather(shard, ('chip', 'ctx'), axis=0, tiled=True)]
    unnamed x1 -> x0, blocking collectives: 92.9 us -> none
    ppermute x5 -> x75, starting transfers between devices: 5.77 us -> 79.5 us  [the longest x15 32.7 us: scatter_rows(): got = lax.ppermute(sent, 'z', [(i, (i + step) % far) for i in range(far)])]
    all_gather x1, blocking collectives: 119 us -> 67.4 us  [on_device(): lax.all_gather(small, ('z', 'x', 'core', 'ctx'), axis=0, tiled=False)]
    convert_element_type x0 -> x12, other arithmetic: none -> 22.1 us  [scatter_rows(): matrix = total.astype(matrix.dtype)]
  transfers between devices with their start and end apart: 21 -> 75, of which waited for: 8 -> 19; matrix products, arithmetic and copies ran while one was open for 16% -> 14% of each run, Pallas kernels for 6% -> 58%
where the time goes in v2:
time: 1560 us; the launch traced here: 1550 us
  Pallas kernels  928 us (59%)
  waiting for transfers between devices  239 us (15%)
  matrix products  148 us (9%)
  starting transfers between devices  79.5 us (5%)
  blocking collectives  67.4 us (4%)
  local copies, waits for them, and re-layouts  56.6 us (4%)
  other arithmetic  31.8 us (2%)
    pallas_call x8, Pallas kernels, assemble(): pl.pallas_call(assemble_kernel, in_specs=[pl.BlockSpec(memory_space=pltpu...  872 us
    ppermute x48, waiting for transfers between devices, trade(): return lax.ppermute(array, axis, [(0, 1), (1, 0)])  190 us
    dot_general x19, matrix products, matmul(): return jnp.dot(left, right, preferred_element_type=jnp.float32)  130 us
    all_gather x1, blocking collectives, on_device(): lax.all_gather(small, ('z', 'x', 'core', 'ctx'), axis=0, tiled=False)  67.4 us
    ppermute x15, starting transfers between devices, scatter_rows(): got = lax.ppermute(sent, 'z', [(i, (i + step) % far) for i in range(far)])  32.7 us
  transfers between devices with their start and end apart: 75, of which 19 were waited for; matrix products, arithmetic and copies ran while one was open for 14% of the time, Pallas kernels for 58%

profile of v2, /device:TPU:0, one launch (start us, length us, event | category | flops | bytes accessed | tf_op | source)
XLA Modules:
  0.0 1553.4 jit_solution(182946401915731623)
XLA Ops:
  1.7 5.1 collective-permute-start.4
  7.8 6.1 concatenate.20
  13.9 67.4 %all-gather.1 = bf16[32,1,384]{2,1,0:T(2,128)(2,1)S(1)} all-gather(bf16[1,1,384]{2,1,0:T(2,128)(2,1)S(1)} %reshape.402), channel_id=2, replica_groups=mesh['z'=4,'x'=2,'core'=2,'ctx'=2] {'z','x','core','ctx'}, dimensions={0}, use_global_device_ids=true | all-gather | bytes 25344 | tf_op jit(solution)/shard_map/all_gather | solution.py:606
  85.0 25.6 %assemble.8.refs_0_ = bf16[128,3072]{1,0:T(8,128)(2,1)} custom-call(s32[4]{0:T(128)} %pad_add_fusion.index_ref, bf16[32,3072]{1,0:T(8,128)(2,1)} %copy-done.20, bf16[32,3072]{1,0:T(8,128)(2,1)} %copy-done.33, bf16[32,3072]{1,0:T(8,128)(2,1)} %copy-done.32, bf16[32,3072]{1,0:T(8,128)(2,1)} %copy-done.31), custom_call_target="tpu_custom_call" | custom-call | bytes 1572864 | tf_op jit(solution)/shard_map/assemble/pallas_call | solution.py:510
  113.2 4.2 collective-permute-start.14
  118.1 4.6 collective-permute-done.14.refs_3_
  122.8 6.0 collective-permute-done.13.refs_2_
  132.0 9.7 assemble.10.refs_0_
  144.9 33.6 %assemble.12.refs_0_ = bf16[128,4096]{1,0:T(8,128)(2,1)} custom-call(s32[4]{0:T(128)} %pad_add_fusion.index_ref, bf16[32,4096]{1,0:T(8,128)(2,1)} %copy-done.17, bf16[32,4096]{1,0:T(8,128)(2,1)} %collective-permute-done.22.refs_1_, bf16[32,4096]{1,0:T(8,128)(2,1)} %copy-done.22, bf16[32,4096]{1,0:T(8,128)(2,1)} %copy-done.21), custom_call_target="tpu_custom_call" | custom-call | bytes 2097152 | tf_op jit(solution)/shard_map/assemble/pallas_call | solution.py:510
  191.1 14.4 collective-permute-done.33.refs_2_
  207.7 3.8 fusion.26
  215.1 3.9 fusion.25
  219.0 33.6 %assemble.14.refs_0_ = bf16[512,1024]{1,0:T(8,128)(2,1)} custom-call(s32[4]{0:T(128)} %pad_add_fusion.index_ref, bf16[128,1024]{1,0:T(8,128)(2,1)} %copy-done.18, bf16[128,1024]{1,0:T(8,128)(2,1)} %copy-done.25, bf16[128,1024]{1,0:T(8,128)(2,1)} %copy-done.24, bf16[128,1024]{1,0:T(8,128)(2,1)} %copy-done.23), custom_call_target="tpu_custom_call" | custom-call | bytes 2097152 | tf_op jit(solution)/shard_map/assemble/pallas_call | solution.py:510
  254.8 65.4 %assemble.11 = bf16[1024,1024]{1,0:T(8,128)(2,1)} custom-call(s32[8]{0:T(128)} %stack.36.index_ref, bf16[128,1024]{1,0:T(8,128)(2,1)} %assemble.10.refs_0_, bf16[128,1024]{1,0:T(8,128)(2,1)} %collective-permute-done.15.refs_1_, bf16[128,1024]{1,0:T(8,128)(2,1)} %collective-permute-done.16.refs_2_, bf16[128,1024]{1,0:T(8,128)(2,1)} %collective-permute-done.17.refs_3_, ...), custom_call_target="tpu_custom_call" | custom-call | bytes 4194304 | tf_op jit(solution)/shard_map/assemble/pallas_call | solution.py:510
  324.0 5.9 fusion.55
  336.6 192.4 %assemble.9 = bf16[1024,3072]{1,0:T(8,128)(2,1)} custom-call(s32[8]{0:T(128)} %stack.36.index_ref, bf16[128,3072]{1,0:T(8,128)(2,1)} %assemble.8.refs_0_, bf16[128,3072]{1,0:T(8,128)(2,1)} %collective-permute-done.5.refs_1_, bf16[128,3072]{1,0:T(8,128)(2,1)} %copy-done.19, bf16[128,3072]{1,0:T(8,128)(2,1)} %collective-permute-done.7.refs_3_, ...), custom_call_target="tpu_custom_call" | custom-call | bytes 12582912 | tf_op jit(solution)/shard_map/assemble/pallas_call | solution.py:510
  529.0 7.5 add_convert_fusion.2.query_ref.key_ref.value_ref
  536.6 27.8 %attention_forward.1 = (bf16[592,1024]{1,0:T(8,128)(2,1)S(1)}, f32[8,2,592]{2,1,0:T(2,128)S(1)}) custom-call(bf16[592,3072]{1,0:T(8,128)(2,1)S(1)} %add_convert_fusion.2.query_ref.key_ref.value_ref, bf16[592,3072]{1,0:T(8,128)(2,1)S(1)} %add_convert_fusion.2.query_ref.key_ref.value_ref, bf16[592,3072]{1,0:T(8,128)(2,1)S(1)} %add_convert_fusion.2.query_ref.key_ref.value_ref, ...), custom_call_target="tpu_custom_call" | custom-call | flops 5742002176 | bytes 4849664 | tf_op jit(solution)/shard_map/attention_forward/pallas_call | solution.py:405
  569.9 20.6 %collective-permute-done.37.refs_3_ = bf16[512,1024]{1,0:T(8,128)(2,1)} collective-permute-done((bf16[512,1024]{1,0:T(8,128)(2,1)}, bf16[512,1024]{1,0:T(8,128)(2,1)}, u32[]{:S(2)}, u32[]{:S(2)}) %collective-permute-start.37) | collective-permute-done | bytes 1048608 | tf_op jit(solution)/shard_map/ppermute | solution.py:525
  592.1 256.0 %assemble.13 = bf16[1024,4096]{1,0:T(8,128)(2,1)} custom-call(s32[8]{0:T(128)} %stack.36.index_ref, bf16[128,4096]{1,0:T(8,128)(2,1)} %assemble.12.refs_0_, bf16[128,4096]{1,0:T(8,128)(2,1)} %collective-permute-done.25.refs_1_, bf16[128,4096]{1,0:T(8,128)(2,1)} %collective-permute-done.26.refs_2_, bf16[128,4096]{1,0:T(8,128)(2,1)} %collective-permute-done.27.refs_3_, ...), custom_call_target="tpu_custom_call" | custom-call | bytes 16777216 | tf_op jit(solution)/shard_map/assemble/pallas_call | solution.py:510
  848.1 30.8 %fusion.2 = (bf16[592,4096]{1,0:T(8,128)(2,1)}, f32[592,4096]{1,0:T(8,128)}) fusion(f32[4096]{0:T(1024)S(1)} %slice_bitcast_fusion, bf16[1024,4096]{1,0:T(8,128)(2,1)} %assemble.13, f32[592,1024]{1,0:T(8,128)} %copy-done.6, f32[1024]{0:T(1024)S(1)} %add.455, f32[1024]{0:T(1024)S(1)} %mul.259, f32[592]{0:T(1024)S(1)} %add_rsqrt_fusion, ...), kind=kOutput, calls=%fused_computation.4 | convolution fusion | flops 5129125888 | bytes 25391744 | tf_op jit(solution)/shard_map/dot_general | solution.py:27
  878.9 6.3 convert_reduce_fusion.1
  885.2 10.9 convolution_convert_fusion.1
  896.2 4.8 constant_dynamic-slice_fusion.5
  901.5 256.0 %assemble.15 = bf16[4096,1024]{1,0:T(8,128)(2,1)} custom-call(s32[8]{0:T(128)} %stack.36.index_ref, bf16[512,1024]{1,0:T(8,128)(2,1)} %assemble.14.refs_0_, bf16[512,1024]{1,0:T(8,128)(2,1)} %collective-permute-done.35.refs_1_, bf16[512,1024]{1,0:T(8,128)(2,1)} %collective-permute-done.36.refs_2_, bf16[512,1024]{1,0:T(8,128)(2,1)} %collective-permute-done.37.refs_3_, ...), custom_call_target="tpu_custom_call" | custom-call | bytes 16777216 | tf_op jit(solution)/shard_map/assemble/pallas_call | solution.py:510
  1157.4 12.5 convert_reduce_fusion
  1169.9 8.8 multiply_reduce_fusion
  1185.0 9.5 convolution_convert_fusion
  1194.5 28.2 %attention_backward.1 = (bf16[592,1024]{1,0:T(8,128)(2,1)S(1)}, bf16[592,1024]{1,0:T(8,128)(2,1)S(1)}, bf16[592,1024]{1,0:T(8,128)(2,1)S(1)}) custom-call(bf16[592,3072]{1,0:T(8,128)(2,1)S(1)} %copy-done.1, bf16[592,3072]{1,0:T(8,128)(2,1)S(1)} %copy-done.1, bf16[592,3072]{1,0:T(8,128)(2,1)S(1)} %copy-done.1, ...), custom_call_target="tpu_custom_call" | custom-call | flops 14355005440 | bytes 8486912 | tf_op jit(solution)/shard_map/attention_backward/pallas_call | solution.py:435
  1225.0 5.7 multiply_reduce_fusion.1
  1230.7 7.5 convolution_convert_fusion.2
  1238.2 12.4 fusion.23
  1254.8 5.2 fusion.24
  1269.4 19.5 %collective-permute-done.53 = f32[4,384]{1,0:T(4,128)S(1)} collective-permute-done((f32[4,384]{1,0:T(4,128)S(1)}, f32[4,384]{1,0:T(4,128)S(1)}, u32[]{:S(2)}, u32[]{:S(2)}) %collective-permute-start.53) | collective-permute-done | bytes 6176 | tf_op jit(solution)/shard_map/ppermute | solution.py:525
  1288.9 9.3 collective-permute-start.54
  1298.2 4.0 fusion.28
  1305.9 4.4 collective-permute-done.55
  1311.7 10.5 collective-permute-done.58
  1327.2 26.7 %collective-permute-done.59 = bf16[128,1024]{1,0:T(8,128)(2,1)S(1)} collective-permute-done((bf16[128,1024]{1,0:T(8,128)(2,1)S(1)}, bf16[128,1024]{1,0:T(8,128)(2,1)S(1)}, u32[]{:S(2)}, u32[]{:S(2)}) %collective-permute-start.59) | collective-permute-done | bytes 262176 | tf_op jit(solution)/shard_map/ppermute | solution.py:525
  1364.3 4.1 add_convert_fusion
  1371.9 5.0 add_convert_fusion.1
  1389.1 12.5 collective-permute-done.46
  1404.1 42.5 %collective-permute-done.70 = bf16[1024,1024]{0,1:T(8,128)(2,1)} collective-permute-done((bf16[1024,1024]{0,1:T(8,128)(2,1)}, bf16[1024,1024]{0,1:T(8,128)(2,1)}, u32[]{:S(2)}, u32[]{:S(2)}) %collective-permute-start.70) | collective-permute-done | bytes 2097184 | tf_op jit(solution)/shard_map/ppermute | solution.py:525
  1449.8 36.8 %collective-permute-done.64 = bf16[256,4096]{1,0:T(8,128)(2,1)} collective-permute-done((bf16[256,4096]{1,0:T(8,128)(2,1)}, bf16[256,4096]{1,0:T(8,128)(2,1)}, u32[]{:S(2)}, u32[]{:S(2)}) %collective-permute-start.64) | collective-permute-done | bytes 2097184 | tf_op jit(solution)/shard_map/ppermute | solution.py:525
  1495.4 14.0 collective-permute-done.65
  1513.6 5.3 collective-permute-done.49
  1519.9 11.5 collective-permute-start.67
  1532.3 9.2 collective-permute-done.73
  (379 shorter events, 143.4 us)
Async XLA Ops:
  1.7 81.9 %collective-permute-start.4 = (bf16[32,3072]{1,0:T(8,128)(2,1)S(1)}, bf16[32,3072]{1,0:T(8,128)(2,1)S(1)}, u32[]{:S(2)}, u32[]{:S(2)}) collective-permute-start(bf16[32,3072]{1,0:T(8,128)(2,1)S(1)} %reshape.369.refs_0_), channel_id=1, source_target_pairs={{0,24},{8,0},{16,8},{24,16},{1,25},{9,1},{17,9},{25,17},{2,26},{10... | collective-permute-start | bytes 589832 | tf_op jit(solution)/shard_map/ppermute | solution.py:536
  6.8 76.8 %collective-permute-start.3 = (bf16[32,3072]{1,0:T(8,128)(2,1)S(1)}, bf16[32,3072]{1,0:T(8,128)(2,1)S(1)}, u32[]{:S(2)}, u32[]{:S(2)}) collective-permute-start(bf16[32,3072]{1,0:T(8,128)(2,1)S(1)} %reshape.369.refs_0_), channel_id=1, source_target_pairs={{0,16},{8,24},{16,0},{24,8},{1,17},{9,25},{17,1},{25,9},{2,18},{10... | collective-permute-start | bytes 589832 | tf_op jit(solution)/shard_map/ppermute | solution.py:536
  6.8 76.8 %collective-permute-start.2 = (bf16[32,3072]{1,0:T(8,128)(2,1)S(1)}, bf16[32,3072]{1,0:T(8,128)(2,1)S(1)}, u32[]{:S(2)}, u32[]{:S(2)}) collective-permute-start(bf16[32,3072]{1,0:T(8,128)(2,1)S(1)} %reshape.369.refs_0_), channel_id=1, source_target_pairs={{0,8},{8,16},{16,24},{24,0},{1,9},{9,17},{17,25},{25,1},{2,10},{10... | collective-permute-start | bytes 589832 | tf_op jit(solution)/shard_map/ppermute | solution.py:536
  111.1 30.7 %collective-permute-start.24 = (bf16[32,4096]{1,0:T(8,128)(2,1)S(1)}, bf16[32,4096]{1,0:T(8,128)(2,1)S(1)}, u32[]{:S(2)}, u32[]{:S(2)}) collective-permute-start(bf16[32,4096]{1,0:T(8,128)(2,1)S(1)} %reshape.379.refs_0_), channel_id=1, source_target_pairs={{0,24},{8,0},{16,8},{24,16},{1,25},{9,1},{17,9},{25,17},{2,26},{10... | collective-permute-start | bytes 786440 | tf_op jit(solution)/shard_map/ppermute | solution.py:536
  111.2 30.7 %collective-permute-start.23 = (bf16[32,4096]{1,0:T(8,128)(2,1)S(1)}, bf16[32,4096]{1,0:T(8,128)(2,1)S(1)}, u32[]{:S(2)}, u32[]{:S(2)}) collective-permute-start(bf16[32,4096]{1,0:T(8,128)(2,1)S(1)} %reshape.379.refs_0_), channel_id=1, source_target_pairs={{0,16},{8,24},{16,0},{24,8},{1,17},{9,25},{17,1},{25,9},{2,18},{10... | collective-permute-start | bytes 786440 | tf_op jit(solution)/shard_map/ppermute | solution.py:536
  122.8 84.5 %collective-permute-start.5 = (bf16[128,3072]{1,0:T(8,128)(2,1)S(1)}, bf16[128,3072]{1,0:T(8,128)(2,1)}, u32[]{:S(2)}, u32[]{:S(2)}) collective-permute-start(bf16[128,3072]{1,0:T(8,128)(2,1)S(1)} %copy-done.9), channel_id=1, source_target_pairs={{0,1},{1,0},{2,3},{3,2},{4,5},{5,4},{6,7},{7,6},{8,9},{9,8},{10,11... | collective-permute-start | bytes 2359304 | tf_op jit(solution)/shard_map/ppermute | solution.py:525
  141.7 37.8 %collective-permute-start.18 = (bf16[128,1024]{1,0:T(8,128)(2,1)}, bf16[128,1024]{1,0:T(8,128)(2,1)}, u32[]{:S(2)}, u32[]{:S(2)}) collective-permute-start(bf16[128,1024]{1,0:T(8,128)(2,1)} %assemble.10.refs_0_), channel_id=1, source_target_pairs={{0,2},{2,0},{1,3},{3,1},{4,6},{6,4},{5,7},{7,5},{8,10},{10,8},{9,1... | collective-permute-start | bytes 786440 | tf_op jit(solution)/shard_map/ppermute | solution.py:525
  141.8 41.1 %collective-permute-start.16 = (bf16[128,1024]{1,0:T(8,128)(2,1)}, bf16[128,1024]{1,0:T(8,128)(2,1)}, u32[]{:S(2)}, u32[]{:S(2)}) collective-permute-start(bf16[128,1024]{1,0:T(8,128)(2,1)} %assemble.10.refs_0_), channel_id=1, source_target_pairs={{0,4},{4,0},{1,5},{5,1},{2,6},{6,2},{3,7},{7,3},{8,12},{12,8},{9,1... | collective-permute-start | bytes 786440 | tf_op jit(solution)/shard_map/ppermute | solution.py:525
  141.9 41.3 %collective-permute-start.15 = (bf16[128,1024]{1,0:T(8,128)(2,1)}, bf16[128,1024]{1,0:T(8,128)(2,1)}, u32[]{:S(2)}, u32[]{:S(2)}) collective-permute-start(bf16[128,1024]{1,0:T(8,128)(2,1)} %assemble.10.refs_0_), channel_id=1, source_target_pairs={{0,1},{1,0},{2,3},{3,2},{4,5},{5,4},{6,7},{7,6},{8,9},{9,8},{10,11... | collective-permute-start | bytes 786440 | tf_op jit(solution)/shard_map/ppermute | solution.py:525
  142.8 36.1 %collective-permute-start = (s32[584]{0:T(1024)S(1)}, s32[584]{0:T(1024)S(1)}, u32[]{:S(2)}, u32[]{:S(2)}) collective-permute-start(s32[584]{0:T(1024)S(1)} %copy-done.38), channel_id=1, source_target_pairs={{0,1},{1,0},{2,3},{3,2},{4,5},{5,4},{6,7},{7,6},{8,9},{9,8},{10,11... | collective-permute-start | bytes 7016 | tf_op jit(solution)/shard_map/ppermute | solution.py:525
  178.8 144.6 %collective-permute-start.1 = (bf16[584,1024]{1,0:T(8,128)(2,1)}, bf16[584,1024]{1,0:T(8,128)(2,1)}, u32[]{:S(2)}, u32[]{:S(2)}) collective-permute-start(bf16[584,1024]{1,0:T(8,128)(2,1)} %param.16), channel_id=1, source_target_pairs={{0,1},{1,0},{2,3},{3,2},{4,5},{5,4},{6,7},{7,6},{8,9},{9,8},{10,11... | collective-permute-start | bytes 3588104 | tf_op jit(solution)/shard_map/ppermute | solution.py:525
  189.7 133.7 %collective-permute-start.6 = (bf16[128,3072]{1,0:T(8,128)(2,1)S(1)}, bf16[128,3072]{1,0:T(8,128)(2,1)S(1)}, u32[]{:S(2)}, u32[]{:S(2)}) collective-permute-start(bf16[128,3072]{1,0:T(8,128)(2,1)S(1)} %copy-done.9), channel_id=1, source_target_pairs={{0,4},{4,0},{1,5},{5,1},{2,6},{6,2},{3,7},{7,3},{8,12},{12,8},{9,1... | collective-permute-start | bytes 2359304 | tf_op jit(solution)/shard_map/ppermute | solution.py:525
  207.3 116.6 %collective-permute-start.7 = (bf16[128,3072]{1,0:T(8,128)(2,1)}, bf16[128,3072]{1,0:T(8,128)(2,1)}, u32[]{:S(2)}, u32[]{:S(2)}) collective-permute-start(bf16[128,3072]{1,0:T(8,128)(2,1)} %collective-permute-done.5.refs_1_), channel_id=1, source_target_pairs={{0,4},{4,0},{1,5},{5,1},{2,6},{6,2},{3,7},{7,3},{8,12},{12,8},{9,1... | collective-permute-start | bytes 2359304 | tf_op jit(solution)/shard_map/ppermute | solution.py:525
  211.5 41.1 %collective-permute-start.19 = (bf16[128,1024]{1,0:T(8,128)(2,1)}, bf16[128,1024]{1,0:T(8,128)(2,1)S(1)}, u32[]{:S(2)}, u32[]{:S(2)}) collective-permute-start(bf16[128,1024]{1,0:T(8,128)(2,1)} %collective-permute-done.15.refs_1_), channel_id=1, source_target_pairs={{0,2},{2,0},{1,3},{3,1},{4,6},{6,4},{5,7},{7,5},{8,10},{10,8},{9,1... | collective-permute-start | bytes 786440 | tf_op jit(solution)/shard_map/ppermute | solution.py:525
  215.0 38.1 %collective-permute-start.21 = (bf16[128,1024]{1,0:T(8,128)(2,1)}, bf16[128,1024]{1,0:T(8,128)(2,1)}, u32[]{:S(2)}, u32[]{:S(2)}) collective-permute-start(bf16[128,1024]{1,0:T(8,128)(2,1)} %collective-permute-done.17.refs_3_), channel_id=1, source_target_pairs={{0,2},{2,0},{1,3},{3,1},{4,6},{6,4},{5,7},{7,5},{8,10},{10,8},{9,1... | collective-permute-start | bytes 786440 | tf_op jit(solution)/shard_map/ppermute | solution.py:525
  252.6 79.4 %collective-permute-start.8 = (bf16[128,3072]{1,0:T(8,128)(2,1)S(1)}, bf16[128,3072]{1,0:T(8,128)(2,1)}, u32[]{:S(2)}, u32[]{:S(2)}) collective-permute-start(bf16[128,3072]{1,0:T(8,128)(2,1)S(1)} %copy-done.9), channel_id=1, source_target_pairs={{0,2},{2,0},{1,3},{3,1},{4,6},{6,4},{5,7},{7,5},{8,10},{10,8},{9,1... | collective-permute-start | bytes 2359304 | tf_op jit(solution)/shard_map/ppermute | solution.py:525
  253.2 79.3 %collective-permute-start.25 = (bf16[128,4096]{1,0:T(8,128)(2,1)}, bf16[128,4096]{1,0:T(8,128)(2,1)}, u32[]{:S(2)}, u32[]{:S(2)}) collective-permute-start(bf16[128,4096]{1,0:T(8,128)(2,1)} %assemble.12.refs_0_), channel_id=1, source_target_pairs={{0,1},{1,0},{2,3},{3,2},{4,5},{5,4},{6,7},{7,6},{8,9},{9,8},{10,11... | collective-permute-start | bytes 3145736 | tf_op jit(solution)/shard_map/ppermute | solution.py:525
  332.0 232.4 %collective-permute-start.28 = (bf16[128,4096]{1,0:T(8,128)(2,1)}, bf16[128,4096]{1,0:T(8,128)(2,1)}, u32[]{:S(2)}, u32[]{:S(2)}) collective-permute-start(bf16[128,4096]{1,0:T(8,128)(2,1)} %assemble.12.refs_0_), channel_id=1, source_target_pairs={{0,2},{2,0},{1,3},{3,1},{4,6},{6,4},{5,7},{7,5},{8,10},{10,8},{9,1... | collective-permute-start | bytes 3145736 | tf_op jit(solution)/shard_map/ppermute | solution.py:525
  332.5 232.0 %collective-permute-start.26 = (bf16[128,4096]{1,0:T(8,128)(2,1)}, bf16[128,4096]{1,0:T(8,128)(2,1)}, u32[]{:S(2)}, u32[]{:S(2)}) collective-permute-start(bf16[128,4096]{1,0:T(8,128)(2,1)} %assemble.12.refs_0_), channel_id=1, source_target_pairs={{0,4},{4,0},{1,5},{5,1},{2,6},{6,2},{3,7},{7,3},{8,12},{12,8},{9,1... | collective-permute-start | bytes 3145736 | tf_op jit(solution)/shard_map/ppermute | solution.py:525
  334.2 234.6 %collective-permute-start.36 = (bf16[512,1024]{1,0:T(8,128)(2,1)}, bf16[512,1024]{1,0:T(8,128)(2,1)}, u32[]{:S(2)}, u32[]{:S(2)}) collective-permute-start(bf16[512,1024]{1,0:T(8,128)(2,1)} %assemble.14.refs_0_), channel_id=1, source_target_pairs={{0,4},{4,0},{1,5},{5,1},{2,6},{6,2},{3,7},{7,3},{8,12},{12,8},{9,1... | collective-permute-start | bytes 3145736 | tf_op jit(solution)/shard_map/ppermute | solution.py:525
  334.5 230.5 %collective-permute-start.35 = (bf16[512,1024]{1,0:T(8,128)(2,1)}, bf16[512,1024]{1,0:T(8,128)(2,1)}, u32[]{:S(2)}, u32[]{:S(2)}) collective-permute-start(bf16[512,1024]{1,0:T(8,128)(2,1)} %assemble.14.refs_0_), channel_id=1, source_target_pairs={{0,1},{1,0},{2,3},{3,2},{4,5},{5,4},{6,7},{7,6},{8,9},{9,8},{10,11... | collective-permute-start | bytes 3145736 | tf_op jit(solution)/shard_map/ppermute | solution.py:525
  334.9 230.5 %collective-permute-start.27 = (bf16[128,4096]{1,0:T(8,128)(2,1)}, bf16[128,4096]{1,0:T(8,128)(2,1)}, u32[]{:S(2)}, u32[]{:S(2)}) collective-permute-start(bf16[128,4096]{1,0:T(8,128)(2,1)} %collective-permute-done.25.refs_1_), channel_id=1, source_target_pairs={{0,4},{4,0},{1,5},{5,1},{2,6},{6,2},{3,7},{7,3},{8,12},{12,8},{9,1... | collective-permute-start | bytes 3145736 | tf_op jit(solution)/shard_map/ppermute | solution.py:525
  565.0 25.5 %collective-permute-start.37 = (bf16[512,1024]{1,0:T(8,128)(2,1)}, bf16[512,1024]{1,0:T(8,128)(2,1)}, u32[]{:S(2)}, u32[]{:S(2)}) collective-permute-start(bf16[512,1024]{1,0:T(8,128)(2,1)} %collective-permute-done.35.refs_1_), channel_id=1, source_target_pairs={{0,4},{4,0},{1,5},{5,1},{2,6},{6,2},{3,7},{7,3},{8,12},{12,8},{9,1... | collective-permute-start | bytes 3145736 | tf_op jit(solution)/shard_map/ppermute | solution.py:525
  565.4 26.8 %collective-permute-start.31 = (bf16[128,4096]{1,0:T(8,128)(2,1)}, bf16[128,4096]{1,0:T(8,128)(2,1)}, u32[]{:S(2)}, u32[]{:S(2)}) collective-permute-start(bf16[128,4096]{1,0:T(8,128)(2,1)} %collective-permute-done.27.refs_3_), channel_id=1, source_target_pairs={{0,2},{2,0},{1,3},{3,1},{4,6},{6,4},{5,7},{7,5},{8,10},{10,8},{9,1... | collective-permute-start | bytes 3145736 | tf_op jit(solution)/shard_map/ppermute | solution.py:525
  568.8 332.6 %collective-permute-start.38 = (bf16[512,1024]{1,0:T(8,128)(2,1)}, bf16[512,1024]{1,0:T(8,128)(2,1)}, u32[]{:S(2)}, u32[]{:S(2)}) collective-permute-start(bf16[512,1024]{1,0:T(8,128)(2,1)} %assemble.14.refs_0_), channel_id=1, source_target_pairs={{0,2},{2,0},{1,3},{3,1},{4,6},{6,4},{5,7},{7,5},{8,10},{10,8},{9,1... | collective-permute-start | bytes 3145736 | tf_op jit(solution)/shard_map/ppermute | solution.py:525
  569.4 332.1 %collective-permute-start.39 = (bf16[512,1024]{1,0:T(8,128)(2,1)}, bf16[512,1024]{1,0:T(8,128)(2,1)}, u32[]{:S(2)}, u32[]{:S(2)}) collective-permute-start(bf16[512,1024]{1,0:T(8,128)(2,1)} %collective-permute-done.35.refs_1_), channel_id=1, source_target_pairs={{0,2},{2,0},{1,3},{3,1},{4,6},{6,4},{5,7},{7,5},{8,10},{10,8},{9,1... | collective-permute-start | bytes 3145736 | tf_op jit(solution)/shard_map/ppermute | solution.py:525
  569.5 332.0 %collective-permute-start.40 = (bf16[512,1024]{1,0:T(8,128)(2,1)}, bf16[512,1024]{1,0:T(8,128)(2,1)}, u32[]{:S(2)}, u32[]{:S(2)}) collective-permute-start(bf16[512,1024]{1,0:T(8,128)(2,1)} %collective-permute-done.36.refs_2_), channel_id=1, source_target_pairs={{0,2},{2,0},{1,3},{3,1},{4,6},{6,4},{5,7},{7,5},{8,10},{10,8},{9,1... | collective-permute-start | bytes 3145736 | tf_op jit(solution)/shard_map/ppermute | solution.py:525
  590.5 288.5 %collective-permute-start.43 = (bf16[584,1024]{1,0:T(8,128)(2,1)}, bf16[584,1024]{1,0:T(8,128)(2,1)}, u32[]{:S(2)}, u32[]{:S(2)}) collective-permute-start(bf16[584,1024]{1,0:T(8,128)(2,1)} %param.17), channel_id=1, source_target_pairs={{0,1},{1,0},{2,3},{3,2},{4,5},{5,4},{6,7},{7,6},{8,9},{9,8},{10,11... | collective-permute-start | bytes 3588104 | tf_op jit(solution)/shard_map/ppermute | solution.py:525
  592.1 309.3 %collective-permute-start.41 = (bf16[512,1024]{1,0:T(8,128)(2,1)}, bf16[512,1024]{1,0:T(8,128)(2,1)}, u32[]{:S(2)}, u32[]{:S(2)}) collective-permute-start(bf16[512,1024]{1,0:T(8,128)(2,1)} %collective-permute-done.37.refs_3_), channel_id=1, source_target_pairs={{0,2},{2,0},{1,3},{3,1},{4,6},{6,4},{5,7},{7,5},{8,10},{10,8},{9,1... | collective-permute-start | bytes 3145736 | tf_op jit(solution)/shard_map/ppermute | solution.py:525
  901.0 463.0 %collective-permute-start.69 = (bf16[2048,1024]{0,1:T(8,128)(2,1)}, bf16[2048,1024]{0,1:T(8,128)(2,1)}, u32[]{:S(2)}, u32[]{:S(2)}) collective-permute-start(bf16[2048,1024]{0,1:T(8,128)(2,1)} %constant_dynamic-slice_fusion.5), channel_id=1, source_target_pairs={{0,2},{2,0},{1,3},{3,1},{4,6},{6,4},{5,7},{7,5},{8,10},{10,8},{9,1... | collective-permute-start | bytes 12582920 | tf_op jit(solution)/shard_map/ppermute | solution.py:525
  1254.0 48.2 %collective-permute-start.57 = (bf16[512,1024]{1,0:T(8,128)(2,1)}, bf16[512,1024]{1,0:T(8,128)(2,1)}, u32[]{:S(2)}, u32[]{:S(2)}) collective-permute-start(bf16[512,1024]{1,0:T(8,128)(2,1)} %constant_dynamic-slice_fusion.17), channel_id=1, source_target_pairs={{0,2},{2,0},{1,3},{3,1},{4,6},{6,4},{5,7},{7,5},{8,10},{10,8},{9,1... | collective-permute-start | bytes 3145736 | tf_op jit(solution)/shard_map/ppermute | solution.py:525
  1260.0 62.8 %collective-permute-start.44 = (bf16[592,1024]{1,0:T(8,128)(2,1)S(1)}, bf16[592,1024]{1,0:T(8,128)(2,1)S(1)}, u32[]{:S(2)}, u32[]{:S(2)}) collective-permute-start(bf16[592,1024]{1,0:T(8,128)(2,1)S(1)} %fusion.24), channel_id=1, source_target_pairs={{0,1},{1,0},{2,3},{3,2},{4,5},{5,4},{6,7},{7,6},{8,9},{9,8},{10,11... | collective-permute-start | bytes 3637256 | tf_op jit(solution)/shard_map/ppermute | solution.py:525
  1262.6 93.4 %collective-permute-start.45 = (bf16[512,3072]{1,0:T(8,128)(2,1)S(1)}, bf16[512,3072]{1,0:T(8,128)(2,1)S(1)}, u32[]{:S(2)}, u32[]{:S(2)}) collective-permute-start(bf16[512,3072]{1,0:T(8,128)(2,1)S(1)} %constant_dynamic-slice_fusion.32), channel_id=1, source_target_pairs={{0,2},{2,0},{1,3},{3,1},{4,6},{6,4},{5,7},{7,5},{8,10},{10,8},{9,1... | collective-permute-start | bytes 9437192 | tf_op jit(solution)/shard_map/ppermute | solution.py:525
  1302.2 68.0 %collective-permute-start.63 = (bf16[512,4096]{1,0:T(8,128)(2,1)S(1)}, bf16[512,4096]{1,0:T(8,128)(2,1)}, u32[]{:S(2)}, u32[]{:S(2)}) collective-permute-start(bf16[512,4096]{1,0:T(8,128)(2,1)S(1)} %constant_dynamic-slice_fusion.11), channel_id=1, source_target_pairs={{0,2},{2,0},{1,3},{3,1},{4,6},{6,4},{5,7},{7,5},{8,10},{10,8},{9,1... | collective-permute-start | bytes 12582920 | tf_op jit(solution)/shard_map/ppermute | solution.py:525
  1322.3 56.1 %collective-permute-start.42 = (bf16[592,1024]{1,0:T(8,128)(2,1)}, bf16[592,1024]{1,0:T(8,128)(2,1)}, u32[]{:S(2)}, u32[]{:S(2)}) collective-permute-start(bf16[592,1024]{1,0:T(8,128)(2,1)} %fusion.23), channel_id=1, source_target_pairs={{0,1},{1,0},{2,3},{3,2},{4,5},{5,4},{6,7},{7,6},{8,9},{9,8},{10,11... | collective-permute-start | bytes 3637256 | tf_op jit(solution)/shard_map/ppermute | solution.py:525
  1322.8 31.1 %collective-permute-start.59 = (bf16[128,1024]{1,0:T(8,128)(2,1)S(1)}, bf16[128,1024]{1,0:T(8,128)(2,1)S(1)}, u32[]{:S(2)}, u32[]{:S(2)}) collective-permute-start(bf16[128,1024]{1,0:T(8,128)(2,1)S(1)} %constant_dynamic-slice_fusion.15), channel_id=1, source_target_pairs={{0,1},{1,0},{2,3},{3,2},{4,5},{5,4},{6,7},{7,6},{8,9},{9,8},{10,11... | collective-permute-start | bytes 786440 | tf_op jit(solution)/shard_map/ppermute | solution.py:525
  1357.6 26.2 %collective-permute-start.62 = (bf16[32,1024]{1,0:T(8,128)(2,1)S(1)}, bf16[32,1024]{1,0:T(8,128)(2,1)S(1)}, u32[]{:S(2)}, u32[]{:S(2)}) collective-permute-start(bf16[32,1024]{1,0:T(8,128)(2,1)S(1)} %get-tuple-element.59), channel_id=1, source_target_pairs={{0,24},{8,0},{16,8},{24,16},{1,25},{9,1},{17,9},{25,17},{2,26},{10... | collective-permute-start | bytes 196616 | tf_op jit(solution)/shard_map/ppermute | solution.py:562
  1364.0 37.6 %collective-permute-start.46 = (bf16[256,3072]{1,0:T(8,128)(2,1)}, bf16[256,3072]{1,0:T(8,128)(2,1)}, u32[]{:S(2)}, u32[]{:S(2)}) collective-permute-start(bf16[256,3072]{1,0:T(8,128)(2,1)} %constant_dynamic-slice_fusion.31), channel_id=1, source_target_pairs={{0,4},{4,0},{1,5},{5,1},{2,6},{6,2},{3,7},{7,3},{8,12},{12,8},{9,1... | collective-permute-start | bytes 4718600 | tf_op jit(solution)/shard_map/ppermute | solution.py:525
  1370.1 76.5 %collective-permute-start.70 = (bf16[1024,1024]{0,1:T(8,128)(2,1)}, bf16[1024,1024]{0,1:T(8,128)(2,1)}, u32[]{:S(2)}, u32[]{:S(2)}) collective-permute-start(bf16[1024,1024]{0,1:T(8,128)(2,1)} %constant_dynamic-slice_fusion.4), channel_id=1, source_target_pairs={{0,4},{4,0},{1,5},{5,1},{2,6},{6,2},{3,7},{7,3},{8,12},{12,8},{9,1... | collective-permute-start | bytes 6291464 | tf_op jit(solution)/shard_map/ppermute | solution.py:525
  1378.4 108.2 %collective-permute-start.64 = (bf16[256,4096]{1,0:T(8,128)(2,1)}, bf16[256,4096]{1,0:T(8,128)(2,1)}, u32[]{:S(2)}, u32[]{:S(2)}) collective-permute-start(bf16[256,4096]{1,0:T(8,128)(2,1)} %constant_dynamic-slice_fusion.10), channel_id=1, source_target_pairs={{0,4},{4,0},{1,5},{5,1},{2,6},{6,2},{3,7},{7,3},{8,12},{12,8},{9,1... | collective-permute-start | bytes 6291464 | tf_op jit(solution)/shard_map/ppermute | solution.py:525
  1403.7 85.7 %collective-permute-start.47 = (bf16[128,3072]{1,0:T(8,128)(2,1)S(1)}, bf16[128,3072]{1,0:T(8,128)(2,1)S(1)}, u32[]{:S(2)}, u32[]{:S(2)}) collective-permute-start(bf16[128,3072]{1,0:T(8,128)(2,1)S(1)} %constant_dynamic-slice_fusion.30), channel_id=1, source_target_pairs={{0,1},{1,0},{2,3},{3,2},{4,5},{5,4},{6,7},{7,6},{8,9},{9,8},{10,11... | collective-permute-start | bytes 2359304 | tf_op jit(solution)/shard_map/ppermute | solution.py:525
  1449.5 44.1 %collective-permute-start.71 = (bf16[512,1024]{0,1:T(8,128)(2,1)S(1)}, bf16[512,1024]{0,1:T(8,128)(2,1)S(1)}, u32[]{:S(2)}, u32[]{:S(2)}) collective-permute-start(bf16[512,1024]{0,1:T(8,128)(2,1)S(1)} %constant_dynamic-slice_fusion.3), channel_id=1, source_target_pairs={{0,1},{1,0},{2,3},{3,2},{4,5},{5,4},{6,7},{7,6},{8,9},{9,8},{10,11... | collective-permute-start | bytes 3145736 | tf_op jit(solution)/shard_map/ppermute | solution.py:525
  1493.6 25.4 %collective-permute-start.49 = (bf16[32,3072]{1,0:T(8,128)(2,1)S(1)}, bf16[32,3072]{1,0:T(8,128)(2,1)S(1)}, u32[]{:S(2)}, u32[]{:S(2)}) collective-permute-start(bf16[32,3072]{1,0:T(8,128)(2,1)S(1)} %get-tuple-element.57), channel_id=1, source_target_pairs={{0,16},{8,24},{16,0},{24,8},{1,17},{9,25},{17,1},{25,9},{2,18},{10... | collective-permute-start | bytes 589832 | tf_op jit(solution)/shard_map/ppermute | solution.py:562
  1494.8 24.4 %collective-permute-start.72 = (bf16[128,1024]{0,1:T(8,128)(2,1)S(1)}, bf16[128,1024]{0,1:T(8,128)(2,1)S(1)}, u32[]{:S(2)}, u32[]{:S(2)}) collective-permute-start(bf16[128,1024]{0,1:T(8,128)(2,1)S(1)} %get-tuple-element.49), channel_id=1, source_target_pairs={{0,8},{8,16},{16,24},{24,0},{1,9},{9,17},{17,25},{25,1},{2,10},{10... | collective-permute-start | bytes 786440 | tf_op jit(solution)/shard_map/ppermute | solution.py:562
  1511.5 30.1 %collective-permute-start.73 = (bf16[128,1024]{0,1:T(8,128)(2,1)S(1)}, bf16[128,1024]{0,1:T(8,128)(2,1)}, u32[]{:S(2)}, u32[]{:S(2)}) collective-permute-start(bf16[128,1024]{0,1:T(8,128)(2,1)S(1)} %get-tuple-element.51), channel_id=1, source_target_pairs={{0,16},{8,24},{16,0},{24,8},{1,17},{9,25},{17,1},{25,9},{2,18},{10... | collective-permute-start | bytes 786440 | tf_op jit(solution)/shard_map/ppermute | solution.py:562
  1513.3 35.9 %collective-permute-start.66 = (bf16[32,4096]{1,0:T(8,128)(2,1)}, bf16[32,4096]{1,0:T(8,128)(2,1)}, u32[]{:S(2)}, u32[]{:S(2)}) collective-permute-start(bf16[32,4096]{1,0:T(8,128)(2,1)} %get-tuple-element.52), channel_id=1, source_target_pairs={{0,8},{8,16},{16,24},{24,0},{1,9},{9,17},{17,25},{25,1},{2,10},{10... | collective-permute-start | bytes 786440 | tf_op jit(solution)/shard_map/ppermute | solution.py:562
  1519.0 30.2 %collective-permute-start.68 = (bf16[32,4096]{1,0:T(8,128)(2,1)}, bf16[32,4096]{1,0:T(8,128)(2,1)}, u32[]{:S(2)}, u32[]{:S(2)}) collective-permute-start(bf16[32,4096]{1,0:T(8,128)(2,1)} %get-tuple-element.53), channel_id=1, source_target_pairs={{0,24},{8,0},{16,8},{24,16},{1,25},{9,1},{17,9},{25,17},{2,26},{10... | collective-permute-start | bytes 786440 | tf_op jit(solution)/shard_map/ppermute | solution.py:562
  1519.9 30.1 %collective-permute-start.67 = (bf16[32,4096]{1,0:T(8,128)(2,1)}, bf16[32,4096]{1,0:T(8,128)(2,1)}, u32[]{:S(2)}, u32[]{:S(2)}) collective-permute-start(bf16[32,4096]{1,0:T(8,128)(2,1)} %get-tuple-element.54), channel_id=1, source_target_pairs={{0,16},{8,24},{16,0},{24,8},{1,17},{9,25},{17,1},{25,9},{2,18},{10... | collective-permute-start | bytes 786440 | tf_op jit(solution)/shard_map/ppermute | solution.py:562
  (87 other events, 2484.5 us)

commit v3 on v2

--- a/solution.py
+++ b/solution.py
@@ -490,35 +490,55 @@
 
 
 def assemble_kernel(index_ref, *refs):
-    *pieces, whole, arrived = refs
-    copies = []
+    pieces, (*wholes, stage, arrived, left) = refs[: index_ref.shape[0]], refs[index_ref.shape[0] :]
+    incoming = [
+        pltpu.make_async_copy(piece, stage.at[number], arrived.at[number])
+        for number, piece in enumerate(pieces)
+    ]
+    for copy in incoming:
+        copy.start()
+    outgoing = []
     for number, piece in enumerate(pieces):
+        incoming[number].wait()
         size = piece.shape[0]
         start = pl.multiple_of(index_ref[number] * size, 16)
-        copies.append(
-            pltpu.make_async_copy(piece, whole.at[pl.ds(start, size)], arrived.at[number])
-        )
-    for copy in copies:
-        copy.start()
-    for copy in copies:
+        column = 0
+        for part, whole in enumerate(wholes):
+            width = whole.shape[1]
+            copy = pltpu.make_async_copy(
+                stage.at[number, :, pl.ds(column, width)],
+                whole.at[pl.ds(start, size)],
+                left.at[part, number],
+            )
+            copy.start()
+            outgoing.append(copy)
+            column += width
+    for copy in outgoing:
         copy.wait()
 
 
-def assemble(pieces, indices):
+def assemble(pieces, indices, extra=0):
     size, width = pieces[0].shape
     count = len(pieces)
-    return pl.pallas_call(
+    widths = (width - extra, extra) if extra else (width,)
+    anywhere = pl.BlockSpec(memory_space=pl.ANY)
+    wholes = pl.pallas_call(
         assemble_kernel,
-        in_specs=[pl.BlockSpec(memory_space=pltpu.SMEM)]
-        + [pl.BlockSpec(memory_space=pl.ANY)] * count,
-        out_specs=pl.BlockSpec(memory_space=pl.ANY),
-        out_shape=jax.ShapeDtypeStruct((count * size, width), pieces[0].dtype),
-        scratch_shapes=[pltpu.SemaphoreType.DMA((count,))],
+        in_specs=[pl.BlockSpec(memory_space=pltpu.SMEM)] + [anywhere] * count,
+        out_specs=[anywhere] * len(widths),
+        out_shape=[jax.ShapeDtypeStruct((count * size, one), pieces[0].dtype) for one in widths],
+        scratch_shapes=[
+            pltpu.VMEM((count, size, width), pieces[0].dtype),
+            pltpu.SemaphoreType.DMA((count,)),
+            pltpu.SemaphoreType.DMA((len(widths), count)),
+        ],
+        compiler_params=pltpu.CompilerParams(vmem_limit_bytes=16 * 2**20),
         cost_estimate=pl.CostEstimate(
             flops=0, bytes_accessed=4 * count * size * width, transcendentals=0
         ),
         name="assemble",
     )(jnp.stack(indices).astype(jnp.int32), *pieces)
+    return wholes if extra else wholes[0]
 
 
 def trade(array, axis):
@@ -538,34 +558,46 @@
     return assemble(pieces, indices)
 
 
-def gather_near(block):
-    own = 4 * lax.axis_index("core") + 2 * lax.axis_index("x") + lax.axis_index("ctx")
-    blocks = [block]
-    for axis in ("ctx", "x", "core"):
-        blocks = blocks + [trade(one, axis) for one in blocks]
-    return assemble(blocks, [own ^ number for number in range(8)])
-
-
-def scatter_rows(matrix, far):
-    for axis in ("core", "x", "ctx"):
-        half = matrix.shape[0] // 2
-        place = lax.axis_index(axis)
-        kept = lax.dynamic_slice_in_dim(matrix, place * half, half)
-        sent = lax.dynamic_slice_in_dim(matrix, (1 - place) * half, half)
-        total = kept.astype(jnp.float32) + trade(sent, axis).astype(jnp.float32)
-        matrix = total.astype(matrix.dtype)
+SPOT = {"core": 4, "x": 2, "ctx": 1}
+
+
+def spread(blocks, axis):
+    return blocks | {key ^ SPOT[axis]: trade(block, axis) for key, block in blocks.items()}
+
+
+def order_blocks(blocks, extra=0):
+    own = sum(spot * lax.axis_index(axis) for axis, spot in SPOT.items())
+    return assemble(list(blocks.values()), [own ^ key for key in blocks], extra)
+
+
+def send_half(matrix, axis, outer=1):
+    rows, width = matrix.shape
+    place = lax.axis_index(axis)
+    blocks = matrix.reshape(outer, 2, rows // (2 * outer), width)
+    kept = lax.dynamic_index_in_dim(blocks, place, 1, False).reshape(rows // 2, width)
+    sent = lax.dynamic_index_in_dim(blocks, 1 - place, 1, False).reshape(rows // 2, width)
+    return kept, trade(sent, axis)
+
+
+def add_half(halves, follow=None):
+    kept, got = halves
+    if follow is not None:
+        got = after(got, follow)
+    return (kept.astype(jnp.float32) + got.astype(jnp.float32)).astype(kept.dtype)
+
+
+def send_far(matrix, far):
     size = matrix.shape[0] // far
     place = lax.axis_index("z")
-    total = lax.dynamic_slice_in_dim(matrix, place * size, size).astype(jnp.float32)
+    arrays = [lax.dynamic_slice_in_dim(matrix, place * size, size)]
     for step in range(1, far):
         sent = lax.dynamic_slice_in_dim(matrix, ((place + step) % far) * size, size)
-        got = lax.ppermute(sent, "z", [(i, (i + step) % far) for i in range(far)])
-        total = total + got.astype(jnp.float32)
-    return total
-
-
-def scatter_low(matrix, far):
-    return scatter_rows(matrix.astype(jnp.bfloat16), far)
+        arrays.append(lax.ppermute(sent, "z", [(i, (i + step) % far) for i in range(far)]))
+    return arrays
+
+
+def add_far(arrays):
+    return sum(array.astype(jnp.float32) for array in arrays)
 
 
 def column_sums(array):
@@ -603,18 +635,32 @@
         small = jnp.concatenate(
             [b_query, b_value, b_out, norm1_gain, norm1_shift, norm2_gain, norm2_shift, b_down, b_up]
         )
-        small_all = lax.all_gather(small, ("z", "x", "core", "ctx"), axis=0, tiled=False)
-        far_qkv = gather_far(unfold(w_qkv), far)
-        qkv_weight = gather_near(far_qkv)
+        shard_qkv = unfold(w_qkv)
+        shard_rows = shard_qkv.shape[0]
+        small = small.reshape(shard_rows, -1)
+        small_width = small.shape[1]
+        extra = round_up(small_width, 128)
+        small = jnp.pad(small, ((0, 0), (0, extra - small_width)))
+        far_qkv = gather_far(jnp.concatenate([shard_qkv, small], axis=1), far)
         far_out = gather_far(to_local(after(unfold(w_out), far_qkv), 1, far), far)
-        far_up = gather_far(to_local(after(unfold(w_up), far_qkv), 1, far), far)
-        far_down = gather_far(to_local(after(unfold(w_down), far_up), 1, far), far)
-        out_weight = to_natural(gather_near(far_out), 0, far)
-        up_weight = gather_near(far_up)
-        down_weight = gather_near(far_down)
-
-        small_all = small_all.astype(jnp.float32)
-        small_core = to_local(small_all, 0, far)
+        far_down = gather_far(to_local(after(unfold(w_down), far_qkv), 1, far), far)
+        far_up = gather_far(to_local(after(unfold(w_up), far_down), 1, far), far)
+        far_qkv = after(far_qkv, inputs_far)
+        qkv_blocks = spread(spread({0: far_qkv}, "x"), "ctx")
+        out_blocks = spread(spread({0: far_out}, "ctx"), "x")
+        down_blocks = spread({0: far_down}, "x")
+        up_blocks = spread({0: after(far_up, qkv_blocks[3])}, "ctx")
+        up_blocks = spread(up_blocks, "x")
+        down_blocks = spread(
+            {key: after(block, up_blocks[1]) for key, block in down_blocks.items()}, "ctx"
+        )
+        qkv_weight, small_local = order_blocks(spread(qkv_blocks, "core"), extra)
+        out_weight = to_natural(order_blocks(spread(out_blocks, "core")), 0, far)
+        up_blocks = spread(up_blocks, "core")
+        down_blocks = spread(down_blocks, "core")
+
+        small_core = small_local[:, :small_width].astype(jnp.float32).reshape(8 * far, -1)
+        small_all = to_natural(small_core, 0, far)
         piece = lambda table, index: table[:, index * near_width : (index + 1) * near_width].reshape(-1)
         query_bias = piece(small_all, 0)
         value_bias = piece(small_all, 1)
@@ -653,9 +699,13 @@
             picked = matmul(pick_near, near) + matmul(pick_far, far)
             return matmul(picked.astype(jnp.bfloat16), to_core)
 
-        def give(array):
+        def to_give(array):
             natural = nt_dot(array.astype(jnp.bfloat16), to_core).astype(jnp.bfloat16)
-            return matmul(give_near, natural) + matmul(give_far, swap(natural))
+            return natural, swap(natural)
+
+        def give(both, follow):
+            near, far_rows = both
+            return matmul(give_near, near) + matmul(give_far, after(far_rows, follow))
 
         kind = (row >= SEQ).astype(jnp.int32) + (row >= SEQ + pads).astype(jnp.int32)
         bias = jnp.where(kind[:, None] == kind[None, :], 0.0, -1e30).astype(jnp.float32)
@@ -669,30 +719,57 @@
         middle = values_in + matmul(attended, out_weight) + out_bias
         normal2, scale2 = standardize(middle)
         normed2 = (normal2 * second_gain + second_shift).astype(jnp.bfloat16)
+        up_weight = order_blocks(up_blocks)
         hidden = matmul(normed2, up_weight) + up_bias
         active = gelu_exact(hidden).astype(jnp.bfloat16)
         slope = gelu_slope(hidden).astype(jnp.bfloat16)
-        outputs = give(middle + matmul(active, down_weight) + down_bias).astype(jnp.bfloat16)
+        down_weight = order_blocks(down_blocks)
 
         live = (row < SEQ).astype(jnp.float32)[:, None]
         cotangent_far = swap(after(cotangent, joined))
         d_out = take(cotangent, cotangent_far) * live
         d_out_low = d_out.astype(jnp.bfloat16)
-        sum_down = scatter_low(matmul(active.T, d_out_low), far)
-        d_hidden = (matmul(d_out_low, down_weight.T) * slope.astype(jnp.float32)).astype(jnp.bfloat16)
-        sum_up = scatter_low(matmul(normed2.T, d_hidden), far)
-        d_normed2 = matmul(d_hidden, up_weight.T)
+        grad_down = matmul(active.T, d_out_low).astype(jnp.bfloat16)
+        down_core = send_half(grad_down, "core")
+        last = middle + matmul(after(active, grad_down), down_weight) + down_bias
+        last_given = to_give(last)
+        d_hidden = (
+            matmul(after(d_out_low, last_given[0]), down_weight.T) * slope.astype(jnp.float32)
+        ).astype(jnp.bfloat16)
+        grad_up = matmul(normed2.T, d_hidden).astype(jnp.bfloat16)
+        up_core = send_half(grad_up, "core")
+        down_x = send_half(add_half(down_core, grad_up), "x")
+        d_normed2 = matmul(after(d_hidden, down_x[0]), up_weight.T)
         d_middle = d_out + norm_backward(d_normed2, normal2, scale2, second_gain)
         d_branch = d_middle.astype(jnp.bfloat16)
-        sum_out = scatter_low(
-            to_local(matmul(attended.T, d_branch).astype(jnp.bfloat16), 0, far), far
+        up_y = send_half(add_half(up_core, d_branch), "ctx", 2)
+        grad_out = to_local(matmul(attended.T, after(d_branch, up_y[0])).astype(jnp.bfloat16), 0, far)
+        out_core = send_half(grad_out, "core")
+        d_attended = matmul(d_branch, out_weight.T).astype(jnp.bfloat16)
+        out_x = send_half(add_half(out_core, d_attended), "x")
+        d_query, d_key, d_value = attention_backward(
+            joined, after(d_attended, out_x[0]), log_total, bias
         )
-        d_attended = matmul(d_branch, out_weight.T).astype(jnp.bfloat16)
-        d_query, d_key, d_value = attention_backward(joined, d_attended, log_total, bias)
+        outputs = give(last_given, d_query).astype(jnp.bfloat16)
         d_joined = jnp.concatenate([d_query, d_key, d_value], axis=1)
-        sum_qkv = scatter_low(matmul(normed1.T, d_joined), far)
-        d_normed1 = matmul(d_joined, qkv_weight.T)
-        input_grad = give(d_middle + norm_backward(d_normed1, normal1, scale1, first_gain))
+        out_y = send_half(add_half(out_x, d_joined), "ctx")
+        grad_qkv = matmul(normed1.T, d_joined).astype(jnp.bfloat16)
+        qkv_core = send_half(grad_qkv, "core")
+        down_y = send_half(add_half(down_x, grad_qkv), "ctx")
+        d_normed1 = matmul(after(d_joined, grad_qkv), qkv_weight.T)
+        d_last = d_middle + norm_backward(d_normed1, normal1, scale1, first_gain)
+        d_last_given = to_give(d_last)
+        qkv_x = send_half(add_half(qkv_core, d_last_given[0]), "x")
+        up_x = send_half(add_half(up_y, qkv_x[0]), "x")
+        out_far = send_far(add_half(out_y, up_x[0]), far)
+        down_far = send_far(add_half(down_y, out_far[0]), far)
+        up_far = send_far(add_half(up_x, down_far[0]), far)
+        qkv_y = send_half(add_half(qkv_x, up_far[0]), "ctx")
+        qkv_far = send_far(add_half(qkv_y), far)
+        sum_down, sum_up, sum_out, sum_qkv = (
+            add_far(arrays) for arrays in (down_far, up_far, out_far, qkv_far)
+        )
+        input_grad = give(d_last_given, qkv_far[0])
 
         part = lambda vector: vector.reshape(8 * far, -1)
         core_sums = jnp.concatenate(
@@ -712,7 +789,9 @@
         )
         chip_sums = jnp.concatenate([part(column_sums(d_query)), part(column_sums(d_value))], axis=1)
         small_sums = jnp.concatenate([to_local(chip_sums, 0, far), core_sums], axis=1)
-        small_sums = scatter_rows(small_sums, far)[0]
+        for axis in ("core", "x", "ctx"):
+            small_sums = add_half(send_half(small_sums, axis))
+        small_sums = add_far(send_far(small_sums, far))[0]
         own = lambda index: small_sums[index * near_width : (index + 1) * near_width]
         back = lambda matrix: refold(to_natural(matrix, 1, far))
         return (

time: 1560 us -> 628 us (0.40)
  Pallas kernels: 928 us -> 73.3 us
  blocking collectives: 67.4 us -> 0 us
  waiting for transfers between devices: 239 us -> 178 us
  starting transfers between devices: 79.5 us -> 117 us
    pallas_call x8, Pallas kernels: 872 us -> 18 us  [assemble(): pl.pallas_call(assemble_kernel, in_specs=[pl.BlockSpec(memory_space=pltpu...]
    ppermute x48, waiting for transfers between devices: 190 us -> 122 us  [trade(): return lax.ppermute(array, axis, [(0, 1), (1, 0)])]
    all_gather x1 -> x0, blocking collectives: 67.4 us -> none  [on_device(): lax.all_gather(small, ('z', 'x', 'core', 'ctx'), axis=0, tiled=False)]
    ppermute x15, starting transfers between devices: 32.7 us -> 56.1 us  [send_far(): lax.ppermute(sent, 'z', [(i, (i + step) % far) for i in range(far)])]
    reshape x6 -> x17, local copies, waits for them, and re-layouts: 0.42 us -> 17.1 us  [the longest x12 13.5 us: send_half(): lax.dynamic_index_in_dim(blocks, 1 - place, 1, False)]
  transfers between devices with their start and end apart: 75 -> 75, of which waited for: 19 -> 22; matrix products, arithmetic and copies ran while one was open for 14% -> 34% of each run, Pallas kernels for 58% -> 11%
where the time goes in v3:
time: 628 us; the launch traced here: 620 us
  waiting for transfers between devices  178 us (28%)
  matrix products  151 us (24%)
  starting transfers between devices  117 us (19%)
  Pallas kernels  73.3 us (12%)
  local copies, waits for them, and re-layouts  59.2 us (9%)
  other arithmetic  39 us (6%)
    dot_general x19, matrix products, matmul(): return jnp.dot(left, right, preferred_element_type=jnp.float32)  132 us
    ppermute x48, waiting for transfers between devices, trade(): return lax.ppermute(array, axis, [(0, 1), (1, 0)])  122 us
    ppermute x15, starting transfers between devices, send_far(): lax.ppermute(sent, 'z', [(i, (i + step) % far) for i in range(far)])  56.1 us
    ppermute x12, waiting for transfers between devices, gather_far(): lax.ppermute(shard, 'z', [(i, (i + step) % far) for i in range(far)])  37.9 us
    ppermute x48, starting transfers between devices, trade(): return lax.ppermute(array, axis, [(0, 1), (1, 0)])  34.7 us
    pallas_call x1, Pallas kernels, attention_backward(): pl.pallas_call(backward_kernel, grid=(pairs,), in_specs=[pl.BlockSpec((ro...  27.8 us
    pallas_call x1, Pallas kernels, attention_forward(): pl.pallas_call(forward_kernel, grid=(pairs,), in_specs=[pl.BlockSpec((row...  27.4 us
    ppermute x12, starting transfers between devices, gather_far(): lax.ppermute(shard, 'z', [(i, (i + step) % far) for i in range(far)])  25.9 us
  transfers between devices with their start and end apart: 75, of which 22 were waited for; matrix products, arithmetic and copies ran while one was open for 34% of the time, Pallas kernels for 11%

profile of v3, /device:TPU:0, one launch (start us, length us, event | category | flops | bytes accessed | tf_op | source)
XLA Modules:
  0.0 619.8 jit_solution(9847715828874175760)
XLA Ops:
  4.7 6.1 concatenate.40
  20.9 7.4 %collective-permute-done.3.refs_2_ = bf16[32,3200]{1,0:T(8,128)(2,1)S(1)} collective-permute-done((bf16[32,3200]{1,0:T(8,128)(2,1)S(1)}, bf16[32,3200]{1,0:T(8,128)(2,1)S(1)}, u32[]{:S(2)}, u32[]{:S(2)}) %collective-permute-start.3) | collective-permute-done | bytes 204832 | tf_op jit(solution)/shard_map/ppermute | solution.py:556
  31.4 4.9 collective-permute-start.22
  43.4 11.9 %collective-permute-done.12.refs_1_ = bf16[32,1024]{1,0:T(8,128)(2,1)S(1)} collective-permute-done((bf16[32,1024]{1,0:T(8,128)(2,1)S(1)}, bf16[32,1024]{1,0:T(8,128)(2,1)S(1)}, u32[]{:S(2)}, u32[]{:S(2)}) %collective-permute-start.12) | collective-permute-done | bytes 65568 | tf_op jit(solution)/shard_map/ppermute | solution.py:556
  55.3 7.2 %collective-permute-start.13 = (bf16[32,1024]{1,0:T(8,128)(2,1)S(1)}, bf16[32,1024]{1,0:T(8,128)(2,1)S(1)}, u32[]{:S(2)}, u32[]{:S(2)}) collective-permute-start(bf16[32,1024]{1,0:T(8,128)(2,1)S(1)} %reshape.535.refs_0_), channel_id=1, source_target_pairs={{0,16},{8,24},{16,0},{24,8},{1,17},{9,25},{17,1},{25,9},{2,18},{10... | collective-permute-start | bytes 196616 | tf_op jit(solution)/shard_map/ppermute | solution.py:556
  65.7 4.3 collective-permute-done.14.refs_3_
  83.5 4.1 collective-permute-done.25.refs_1_
  89.7 4.0 fusion.32
  93.6 4.8 collective-permute-done.26.refs_2_
  108.9 15.8 %collective-permute-done.7.refs_3_ = bf16[128,3200]{1,0:T(8,128)(2,1)} collective-permute-done((bf16[128,3200]{1,0:T(8,128)(2,1)}, bf16[128,3200]{1,0:T(8,128)(2,1)}, u32[]{:S(2)}, u32[]{:S(2)}) %collective-permute-start.7) | collective-permute-done | bytes 819232 | tf_op jit(solution)/shard_map/ppermute | solution.py:545
  124.7 5.9 fusion.67
  134.1 3.6 assemble.9
  141.6 7.7 %add_convert_fusion.query_ref.key_ref.value_ref = bf16[592,3072]{1,0:T(8,128)(2,1)S(1)} fusion(bf16[1024,3072]{1,0:T(8,128)(2,1)} %copy-done.5, f32[3072]{0:T(1024)S(1)} %pad_maximum_fusion, f32[592,1024]{1,0:T(8,128)} %get-tuple-element.154, f32[1024]{0:T(1024)S(1)} %add.439, f32[1024]{0:T(1024)S(1)} %mul.187, f32[592]{0:T(1024)S(1)} %add_rsqrt_fusion.1, ...), kind=kOutput, calls=%fused_computation.33 | convolution fusion | flops 3731210240 | bytes 12378752 | tf_op jit(solution)/shard_map/dot_general | solution.py:27
  150.7 8.2 %collective-permute-done.28.refs_1_ = bf16[128,4096]{1,0:T(8,128)(2,1)} collective-permute-done((bf16[128,4096]{1,0:T(8,128)(2,1)S(1)}, bf16[128,4096]{1,0:T(8,128)(2,1)}, u32[]{:S(2)}, u32[]{:S(2)}) %collective-permute-start.28) | collective-permute-done | bytes 1048608 | tf_op jit(solution)/shard_map/ppermute | solution.py:545
  159.4 27.4 %attention_forward.1 = (bf16[592,1024]{1,0:T(8,128)(2,1)S(1)}, f32[8,2,592]{2,1,0:T(2,128)S(1)}) custom-call(bf16[592,3072]{1,0:T(8,128)(2,1)S(1)} %add_convert_fusion.query_ref.key_ref.value_ref, bf16[592,3072]{1,0:T(8,128)(2,1)S(1)} %add_convert_fusion.query_ref.key_ref.value_ref, bf16[592,3072]{1,0:T(8,128)(2,1)S(1)} %add_convert_fusion.query_ref.key_ref.value_ref, ...), custom_call_target="tpu_custom_call" | custom-call | flops 5742002176 | bytes 4849664 | tf_op jit(solution)/shard_map/attention_forward/pallas_call | solution.py:405
  194.8 6.3 %convert_reduce_fusion.1 = (f32[1024]{0:T(1024)S(1)}, bf16[592,1024]{1,0:T(8,128)(2,1)}, f32[592,1024]{1,0:T(8,128)}) fusion(f32[592]{0:T(1024)S(1)} %fusion.60, s32[1024]{0:T(1024)S(1)} %reshape.586, f32[592,1024]{1,0:T(8,128)} %fusion.31, bf16[584,1024]{1,0:T(8,128)(2,1)} %copy-done.42, s32[584]{0:T(1024)S(1)} %select_select_fusion), kind=kOutput, calls=%fused_computation.48 | convolution fusion | flops 1954595456 | bytes 7271008 | tf_op jit(solution)/shard_map/dot_general | solution.py:27
  201.1 15.1 %collective-permute-done.38.refs_3_ = bf16[512,1024]{1,0:T(8,128)(2,1)S(1)} collective-permute-done((bf16[512,1024]{1,0:T(8,128)(2,1)}, bf16[512,1024]{1,0:T(8,128)(2,1)S(1)}, u32[]{:S(2)}, u32[]{:S(2)}) %collective-permute-start.38) | collective-permute-done | bytes 1048608 | tf_op jit(solution)/shard_map/ppermute | solution.py:545
  216.2 20.6 %collective-permute-done.37.refs_2_ = bf16[512,1024]{1,0:T(8,128)(2,1)} collective-permute-done((bf16[512,1024]{1,0:T(8,128)(2,1)S(1)}, bf16[512,1024]{1,0:T(8,128)(2,1)}, u32[]{:S(2)}, u32[]{:S(2)}) %collective-permute-start.37) | collective-permute-done | bytes 1048608 | tf_op jit(solution)/shard_map/ppermute | solution.py:545
  237.4 3.9 assemble.14
  241.3 30.7 %fusion.2 = (bf16[592,4096]{1,0:T(8,128)(2,1)S(1)}, f32[592,4096]{1,0:T(8,128)}) fusion(f32[4096]{0:T(1024)S(1)} %slice_bitcast_fusion, bf16[1024,4096]{1,0:T(8,128)(2,1)S(1)} %assemble.14, f32[592,1024]{1,0:T(8,128)} %get-tuple-element.156, f32[1024]{0:T(1024)S(1)} %add.450, f32[1024]{0:T(1024)S(1)} %mul.193, f32[592]{0:T(1024)S(1)} %add_rsqrt_fusion, ...), kind=kOutput, calls=%fused_computation.4 | convolution fusion | flops 5129125888 | bytes 25391744 | tf_op jit(solution)/shard_map/dot_general | solution.py:27
  272.1 9.5 %convolution_convert_fusion.1 = bf16[4096,1024]{1,0:T(8,128)(2,1)} fusion(bf16[592,4096]{1,0:T(8,128)(2,1)S(1)} %get-tuple-element.58, bf16[592,1024]{1,0:T(8,128)(2,1)S(1)} %copy-done.45), kind=kOutput, calls=%fused_computation.32 | convolution fusion | flops 4970250240 | bytes 14450688 | tf_op jit(solution)/shard_map/dot_general | solution.py:27
  287.7 13.0 %fusion.29 = bf16[592,1024]{1,0:T(8,128)(2,1)} fusion(s32[1024]{0:T(1024)S(1)} %reshape.586, f32[592,1024]{1,0:T(8,128)} %get-tuple-element.156, bf16[592,4096]{1,0:T(8,128)(2,1)} %copy-done.47, bf16[4096,1024]{1,0:T(8,128)(2,1)} %copy-done.1, f32[1024]{0:T(1024)S(1)} %add.458), kind=kOutput, calls=%fused_computation.90 | convolution fusion | flops 6211043328 | bytes 16883712 | tf_op jit(solution)/shard_map/dot_general | solution.py:329
  300.8 4.9 dynamic-slice_bitcast_fusion.1
  306.9 10.6 %convert_reduce_fusion = (f32[4096]{0:T(1024)S(1)}, bf16[592,4096]{1,0:T(8,128)(2,1)S(1)}) fusion(f32[592,4096]{1,0:T(8,128)} %get-tuple-element.158, f32[4096]{0:T(1024)S(1)} %slice_bitcast_fusion, bf16[592,1024]{1,0:T(8,128)(2,1)S(1)} %copy-done.46, bf16[4096,1024]{1,0:T(8,128)(2,1)S(1)} %copy-done.2), kind=kOutput, calls=%fused_computation.10 | convolution fusion | flops 5002424320 | bytes 24182784 | tf_op jit(solution)/shard_map/dot_general | solution.py:27
  317.5 10.9 %convolution_convert_fusion = bf16[1024,4096]{1,0:T(8,128)(2,1)S(1)} fusion(bf16[592,4096]{1,0:T(8,128)(2,1)S(1)} %get-tuple-element.63, f32[592,1024]{1,0:T(8,128)} %get-tuple-element.156, f32[1024]{0:T(1024)S(1)} %add.450, f32[1024]{0:T(1024)S(1)} %mul.193, f32[592]{0:T(1024)S(1)} %add_rsqrt_fusion, f32[592]{0:T(1024)S(1)} %broadcast_multiply_fusion.4), kind=kOutput, calls=%fused_computation.31 | convolution fusion | flops 4973281280 | bytes 15676032 | tf_op jit(solution)/shard_map/dot_general | solution.py:27
  334.2 4.0 fusion.34
  338.2 5.7 fusion.16
  346.4 7.6 %multiply_reduce_fusion = (f32[1024]{0:T(1024)S(1)}, f32[592]{0:T(1024)S(1)}, f32[592]{0:T(1024)S(1)}, f32[1024]{0:T(1024)S(1)}, f32[592,1024]{1,0:T(8,128)S(1)}) fusion(f32[592,1024]{1,0:T(8,128)} %get-tuple-element.156, f32[592]{0:T(1024)S(1)} %add_rsqrt_fusion, f32[592]{0:T(1024)S(1)} %broadcast_multiply_fusion.4, f32[1024]{0:T(1024)S(1)} %mul.193, ...), kind=kOutput, calls=%fused_computation.49 | convolution fusion | flops 4971508736 | bytes 18109696 | tf_op jit(solution)/shard_map/dot_general | solution.py:27
  354.0 3.9 convert_reduce_fusion.2
  361.8 5.7 fusion.15
  369.3 3.6 convolution_convert_fusion.4.d_ref
  378.2 27.8 %attention_backward.1 = (bf16[592,1024]{1,0:T(8,128)(2,1)S(1)}, bf16[592,1024]{1,0:T(8,128)(2,1)S(1)}, bf16[592,1024]{1,0:T(8,128)(2,1)S(1)}) custom-call(bf16[592,3072]{1,0:T(8,128)(2,1)S(1)} %copy-done.9, bf16[592,3072]{1,0:T(8,128)(2,1)S(1)} %copy-done.9, bf16[592,3072]{1,0:T(8,128)(2,1)S(1)} %copy-done.9, ...), custom_call_target="tpu_custom_call" | custom-call | flops 14355005440 | bytes 8486912 | tf_op jit(solution)/shard_map/attention_backward/pallas_call | solution.py:435
  407.9 5.9 convolution_convert_fusion.2
  417.4 5.7 multiply_reduce_fusion.1
  425.1 6.3 %fusion.30 = bf16[592,1024]{1,0:T(8,128)(2,1)} fusion(s32[1024]{0:T(1024)S(1)} %reshape.586, f32[592,1024]{1,0:T(8,128)} %get-tuple-element.107, f32[592,1024]{1,0:T(8,128)} %get-tuple-element.161, f32[592,1024]{1,0:T(8,128)} %get-tuple-element.154, f32[592]{0:T(1024)S(1)} %broadcast_multiply_fusion, f32[592]{0:T(1024)S(1)} %broadcast_multiply_fusion.1, ...), kind=kOutput, calls=%fused_computation.91 | convolution fusion | flops 1248624640 | bytes 8504576 | tf_op jit(solution)/shard_map/dot_general | solution.py:329
  432.8 5.9 collective-permute-done.54
  448.2 31.9 %collective-permute-done.50 = bf16[256,4096]{1,0:T(8,128)(2,1)S(1)} collective-permute-done((bf16[256,4096]{1,0:T(8,128)(2,1)S(1)}, bf16[256,4096]{1,0:T(8,128)(2,1)S(1)}, u32[]{:S(2)}, u32[]{:S(2)}) %collective-permute-start.50) | collective-permute-done | bytes 2097184 | tf_op jit(solution)/shard_map/ppermute | solution.py:545
  482.1 3.6 collective-permute-done.55
  485.8 11.3 %collective-permute-start.67 = (bf16[32,1024]{1,0:T(8,128)(2,1)S(1)}, bf16[32,1024]{1,0:T(8,128)(2,1)S(1)}, u32[]{:S(2)}, u32[]{:S(2)}) collective-permute-start(bf16[32,1024]{1,0:T(8,128)(2,1)S(1)} %get-tuple-element.131), channel_id=1, source_target_pairs={{0,16},{8,24},{16,0},{24,8},{1,17},{9,25},{17,1},{25,9},{2,18},{10... | collective-permute-start | bytes 196616 | tf_op jit(solution)/shard_map/ppermute | solution.py:595
  502.1 4.8 collective-permute-done.53
  508.5 11.3 %collective-permute-start.73 = (bf16[128,1024]{1,0:T(8,128)(2,1)S(1)}, bf16[128,1024]{1,0:T(8,128)(2,1)}, u32[]{:S(2)}, u32[]{:S(2)}) collective-permute-start(bf16[128,1024]{1,0:T(8,128)(2,1)S(1)} %get-tuple-element.123), channel_id=1, source_target_pairs={{0,16},{8,24},{16,0},{24,8},{1,17},{9,25},{17,1},{25,9},{2,18},{10... | collective-permute-start | bytes 786440 | tf_op jit(solution)/shard_map/ppermute | solution.py:595
  527.2 5.6 collective-permute-done.73
  536.6 9.2 %collective-permute-start.69 = (bf16[32,4096]{1,0:T(8,128)(2,1)S(1)}, bf16[32,4096]{1,0:T(8,128)(2,1)S(1)}, u32[]{:S(2)}, u32[]{:S(2)}) collective-permute-start(bf16[32,4096]{1,0:T(8,128)(2,1)S(1)} %get-tuple-element.118), channel_id=1, source_target_pairs={{0,8},{8,16},{16,24},{24,0},{1,9},{9,17},{17,25},{25,1},{2,10},{10... | collective-permute-start | bytes 786440 | tf_op jit(solution)/shard_map/ppermute | solution.py:595
  556.1 9.4 %collective-permute-done.70 = bf16[32,4096]{1,0:T(8,128)(2,1)S(1)} collective-permute-done((bf16[32,4096]{1,0:T(8,128)(2,1)S(1)}, bf16[32,4096]{1,0:T(8,128)(2,1)S(1)}, u32[]{:S(2)}, u32[]{:S(2)}) %collective-permute-start.70) | collective-permute-done | bytes 262176 | tf_op jit(solution)/shard_map/ppermute | solution.py:595
  568.7 6.1 collective-permute-start.63
  579.0 3.8 fusion.33
  583.5 13.4 %collective-permute-done.56 = bf16[128,3072]{1,0:T(8,128)(2,1)S(1)} collective-permute-done((bf16[128,3072]{1,0:T(8,128)(2,1)S(1)}, bf16[128,3072]{1,0:T(8,128)(2,1)S(1)}, u32[]{:S(2)}, u32[]{:S(2)}) %collective-permute-start.56) | collective-permute-done | bytes 786464 | tf_op jit(solution)/shard_map/ppermute | solution.py:545
  614.9 4.6 convolution_add_fusion
  (380 shorter events, 171.4 us)
Async XLA Ops:
  0.6 40.0 %collective-permute-start.1 = (bf16[584,1024]{1,0:T(8,128)(2,1)}, bf16[584,1024]{1,0:T(8,128)(2,1)}, u32[]{:S(2)}, u32[]{:S(2)}) collective-permute-start(bf16[584,1024]{1,0:T(8,128)(2,1)} %param.16), channel_id=1, source_target_pairs={{0,1},{1,0},{2,3},{3,2},{4,5},{5,4},{6,7},{7,6},{8,9},{9,8},{10,11... | collective-permute-start | bytes 3588104 | tf_op jit(solution)/shard_map/ppermute | solution.py:545
  31.4 40.9 %collective-permute-start.22 = (bf16[128,1024]{1,0:T(8,128)(2,1)S(1)}, bf16[128,1024]{1,0:T(8,128)(2,1)S(1)}, u32[]{:S(2)}, u32[]{:S(2)}) collective-permute-start(bf16[128,1024]{1,0:T(8,128)(2,1)S(1)} %copy.66.refs_0_), channel_id=1, source_target_pairs={{0,8},{8,16},{16,24},{24,0},{1,9},{9,17},{17,25},{25,1},{2,10},{10... | collective-permute-start | bytes 786440 | tf_op jit(solution)/shard_map/ppermute | solution.py:556
  36.3 37.4 %collective-permute-start.23 = (bf16[128,1024]{1,0:T(8,128)(2,1)S(1)}, bf16[128,1024]{1,0:T(8,128)(2,1)S(1)}, u32[]{:S(2)}, u32[]{:S(2)}) collective-permute-start(bf16[128,1024]{1,0:T(8,128)(2,1)S(1)} %copy.66.refs_0_), channel_id=1, source_target_pairs={{0,16},{8,24},{16,0},{24,8},{1,17},{9,25},{17,1},{25,9},{2,18},{10... | collective-permute-start | bytes 786440 | tf_op jit(solution)/shard_map/ppermute | solution.py:556
  37.9 37.3 %collective-permute-start.24 = (bf16[128,1024]{1,0:T(8,128)(2,1)S(1)}, bf16[128,1024]{1,0:T(8,128)(2,1)S(1)}, u32[]{:S(2)}, u32[]{:S(2)}) collective-permute-start(bf16[128,1024]{1,0:T(8,128)(2,1)S(1)} %copy.66.refs_0_), channel_id=1, source_target_pairs={{0,24},{8,0},{16,8},{24,16},{1,25},{9,1},{17,9},{25,17},{2,26},{10... | collective-permute-start | bytes 786440 | tf_op jit(solution)/shard_map/ppermute | solution.py:556
  40.6 47.7 %collective-permute-start.5 = (bf16[128,3200]{1,0:T(8,128)(2,1)S(1)}, bf16[128,3200]{1,0:T(8,128)(2,1)}, u32[]{:S(2)}, u32[]{:S(2)}) collective-permute-start(bf16[128,3200]{1,0:T(8,128)(2,1)S(1)} %assemble.8.refs_0_), channel_id=1, source_target_pairs={{0,4},{4,0},{1,5},{5,1},{2,6},{6,2},{3,7},{7,3},{8,12},{12,8},{9,1... | collective-permute-start | bytes 2457608 | tf_op jit(solution)/shard_map/ppermute | solution.py:545
  79.1 19.4 %collective-permute-start.26 = (bf16[32,4096]{1,0:T(8,128)(2,1)S(1)}, bf16[32,4096]{1,0:T(8,128)(2,1)S(1)}, u32[]{:S(2)}, u32[]{:S(2)}) collective-permute-start(bf16[32,4096]{1,0:T(8,128)(2,1)S(1)} %reshape.543.refs_0_), channel_id=1, source_target_pairs={{0,16},{8,24},{16,0},{24,8},{1,17},{9,25},{17,1},{25,9},{2,18},{10... | collective-permute-start | bytes 786440 | tf_op jit(solution)/shard_map/ppermute | solution.py:556
  80.8 17.7 %collective-permute-start.27 = (bf16[32,4096]{1,0:T(8,128)(2,1)S(1)}, bf16[32,4096]{1,0:T(8,128)(2,1)S(1)}, u32[]{:S(2)}, u32[]{:S(2)}) collective-permute-start(bf16[32,4096]{1,0:T(8,128)(2,1)S(1)} %reshape.543.refs_0_), channel_id=1, source_target_pairs={{0,24},{8,0},{16,8},{24,16},{1,25},{9,1},{17,9},{25,17},{2,26},{10... | collective-permute-start | bytes 786440 | tf_op jit(solution)/shard_map/ppermute | solution.py:556
  82.9 16.1 %collective-permute-start.17 = (bf16[128,1024]{1,0:T(8,128)(2,1)}, bf16[128,1024]{1,0:T(8,128)(2,1)S(1)}, u32[]{:S(2)}, u32[]{:S(2)}) collective-permute-start(bf16[128,1024]{1,0:T(8,128)(2,1)} %collective-permute-done.15.refs_1_), channel_id=1, source_target_pairs={{0,4},{4,0},{1,5},{5,1},{2,6},{6,2},{3,7},{7,3},{8,12},{12,8},{9,1... | collective-permute-start | bytes 786440 | tf_op jit(solution)/shard_map/ppermute | solution.py:545
  87.6 21.3 %collective-permute-start.6 = (bf16[128,3200]{1,0:T(8,128)(2,1)S(1)}, bf16[128,3200]{1,0:T(8,128)(2,1)}, u32[]{:S(2)}, u32[]{:S(2)}) collective-permute-start(bf16[128,3200]{1,0:T(8,128)(2,1)S(1)} %assemble.8.refs_0_), channel_id=1, source_target_pairs={{0,1},{1,0},{2,3},{3,2},{4,5},{5,4},{6,7},{7,6},{8,9},{9,8},{10,11... | collective-permute-start | bytes 2457608 | tf_op jit(solution)/shard_map/ppermute | solution.py:545
  88.3 36.4 %collective-permute-start.7 = (bf16[128,3200]{1,0:T(8,128)(2,1)}, bf16[128,3200]{1,0:T(8,128)(2,1)}, u32[]{:S(2)}, u32[]{:S(2)}) collective-permute-start(bf16[128,3200]{1,0:T(8,128)(2,1)} %collective-permute-done.5.refs_1_), channel_id=1, source_target_pairs={{0,1},{1,0},{2,3},{3,2},{4,5},{5,4},{6,7},{7,6},{8,9},{9,8},{10,11... | collective-permute-start | bytes 2457608 | tf_op jit(solution)/shard_map/ppermute | solution.py:545
  102.6 87.2 %collective-permute-start.36 = (bf16[512,1024]{1,0:T(8,128)(2,1)S(1)}, bf16[512,1024]{1,0:T(8,128)(2,1)}, u32[]{:S(2)}, u32[]{:S(2)}) collective-permute-start(bf16[512,1024]{1,0:T(8,128)(2,1)S(1)} %assemble.12.refs_0_), channel_id=1, source_target_pairs={{0,4},{4,0},{1,5},{5,1},{2,6},{6,2},{3,7},{7,3},{8,12},{12,8},{9,1... | collective-permute-start | bytes 3145736 | tf_op jit(solution)/shard_map/ppermute | solution.py:545
  106.7 26.1 %collective-permute-start.8 = (bf16[128,3200]{1,0:T(8,128)(2,1)S(1)}, bf16[128,3200]{1,0:T(8,128)(2,1)}, u32[]{:S(2)}, u32[]{:S(2)}) collective-permute-start(bf16[128,3200]{1,0:T(8,128)(2,1)S(1)} %assemble.8.refs_0_), channel_id=1, source_target_pairs={{0,2},{2,0},{1,3},{3,1},{4,6},{6,4},{5,7},{7,5},{8,10},{10,8},{9,1... | collective-permute-start | bytes 2457608 | tf_op jit(solution)/shard_map/ppermute | solution.py:545
  106.8 27.2 %collective-permute-start.9 = (bf16[128,3200]{1,0:T(8,128)(2,1)}, bf16[128,3200]{1,0:T(8,128)(2,1)}, u32[]{:S(2)}, u32[]{:S(2)}) collective-permute-start(bf16[128,3200]{1,0:T(8,128)(2,1)} %collective-permute-done.5.refs_1_), channel_id=1, source_target_pairs={{0,2},{2,0},{1,3},{3,1},{4,6},{6,4},{5,7},{7,5},{8,10},{10,8},{9,1... | collective-permute-start | bytes 2457608 | tf_op jit(solution)/shard_map/ppermute | solution.py:545
  108.9 24.6 %collective-permute-start.10 = (bf16[128,3200]{1,0:T(8,128)(2,1)}, bf16[128,3200]{1,0:T(8,128)(2,1)}, u32[]{:S(2)}, u32[]{:S(2)}) collective-permute-start(bf16[128,3200]{1,0:T(8,128)(2,1)} %collective-permute-done.6.refs_2_), channel_id=1, source_target_pairs={{0,2},{2,0},{1,3},{3,1},{4,6},{6,4},{5,7},{7,5},{8,10},{10,8},{9,1... | collective-permute-start | bytes 2457608 | tf_op jit(solution)/shard_map/ppermute | solution.py:545
  132.8 26.1 %collective-permute-start.28 = (bf16[128,4096]{1,0:T(8,128)(2,1)S(1)}, bf16[128,4096]{1,0:T(8,128)(2,1)}, u32[]{:S(2)}, u32[]{:S(2)}) collective-permute-start(bf16[128,4096]{1,0:T(8,128)(2,1)S(1)} %assemble.13.refs_0_), channel_id=1, source_target_pairs={{0,1},{1,0},{2,3},{3,2},{4,5},{5,4},{6,7},{7,6},{8,9},{9,8},{10,11... | collective-permute-start | bytes 3145736 | tf_op jit(solution)/shard_map/ppermute | solution.py:545
  133.5 57.0 %collective-permute-start.29 = (bf16[128,4096]{1,0:T(8,128)(2,1)S(1)}, bf16[128,4096]{1,0:T(8,128)(2,1)}, u32[]{:S(2)}, u32[]{:S(2)}) collective-permute-start(bf16[128,4096]{1,0:T(8,128)(2,1)S(1)} %assemble.13.refs_0_), channel_id=1, source_target_pairs={{0,4},{4,0},{1,5},{5,1},{2,6},{6,2},{3,7},{7,3},{8,12},{12,8},{9,1... | collective-permute-start | bytes 3145736 | tf_op jit(solution)/shard_map/ppermute | solution.py:545
  134.1 57.8 %collective-permute-start.31 = (bf16[128,4096]{1,0:T(8,128)(2,1)S(1)}, bf16[128,4096]{1,0:T(8,128)(2,1)}, u32[]{:S(2)}, u32[]{:S(2)}) collective-permute-start(bf16[128,4096]{1,0:T(8,128)(2,1)S(1)} %assemble.13.refs_0_), channel_id=1, source_target_pairs={{0,2},{2,0},{1,3},{3,1},{4,6},{6,4},{5,7},{7,5},{8,10},{10,8},{9,1... | collective-permute-start | bytes 3145736 | tf_op jit(solution)/shard_map/ppermute | solution.py:545
  149.3 42.6 %collective-permute-start.35 = (bf16[584,1024]{1,0:T(8,128)(2,1)S(1)}, bf16[584,1024]{1,0:T(8,128)(2,1)S(1)}, u32[]{:S(2)}, u32[]{:S(2)}) collective-permute-start(bf16[584,1024]{1,0:T(8,128)(2,1)S(1)} %copy-done.41), channel_id=1, source_target_pairs={{0,1},{1,0},{2,3},{3,2},{4,5},{5,4},{6,7},{7,6},{8,9},{9,8},{10,11... | collective-permute-start | bytes 3588104 | tf_op jit(solution)/shard_map/ppermute | solution.py:545
  158.9 33.5 %collective-permute-start.30 = (bf16[128,4096]{1,0:T(8,128)(2,1)}, bf16[128,4096]{1,0:T(8,128)(2,1)}, u32[]{:S(2)}, u32[]{:S(2)}) collective-permute-start(bf16[128,4096]{1,0:T(8,128)(2,1)} %collective-permute-done.28.refs_1_), channel_id=1, source_target_pairs={{0,4},{4,0},{1,5},{5,1},{2,6},{6,2},{3,7},{7,3},{8,12},{12,8},{9,1... | collective-permute-start | bytes 3145736 | tf_op jit(solution)/shard_map/ppermute | solution.py:545
  189.8 26.4 %collective-permute-start.38 = (bf16[512,1024]{1,0:T(8,128)(2,1)}, bf16[512,1024]{1,0:T(8,128)(2,1)S(1)}, u32[]{:S(2)}, u32[]{:S(2)}) collective-permute-start(bf16[512,1024]{1,0:T(8,128)(2,1)} %collective-permute-done.36.refs_1_), channel_id=1, source_target_pairs={{0,1},{1,0},{2,3},{3,2},{4,5},{5,4},{6,7},{7,6},{8,9},{9,8},{10,11... | collective-permute-start | bytes 3145736 | tf_op jit(solution)/shard_map/ppermute | solution.py:545
  190.6 46.2 %collective-permute-start.37 = (bf16[512,1024]{1,0:T(8,128)(2,1)S(1)}, bf16[512,1024]{1,0:T(8,128)(2,1)}, u32[]{:S(2)}, u32[]{:S(2)}) collective-permute-start(bf16[512,1024]{1,0:T(8,128)(2,1)S(1)} %assemble.12.refs_0_), channel_id=1, source_target_pairs={{0,1},{1,0},{2,3},{3,2},{4,5},{5,4},{6,7},{7,6},{8,9},{9,8},{10,11... | collective-permute-start | bytes 3145736 | tf_op jit(solution)/shard_map/ppermute | solution.py:545
  191.9 44.9 %collective-permute-start.32 = (bf16[128,4096]{1,0:T(8,128)(2,1)}, bf16[128,4096]{1,0:T(8,128)(2,1)}, u32[]{:S(2)}, u32[]{:S(2)}) collective-permute-start(bf16[128,4096]{1,0:T(8,128)(2,1)} %collective-permute-done.28.refs_1_), channel_id=1, source_target_pairs={{0,2},{2,0},{1,3},{3,1},{4,6},{6,4},{5,7},{7,5},{8,10},{10,8},{9,1... | collective-permute-start | bytes 3145736 | tf_op jit(solution)/shard_map/ppermute | solution.py:545
  191.9 45.4 %collective-permute-start.33 = (bf16[128,4096]{1,0:T(8,128)(2,1)}, bf16[128,4096]{1,0:T(8,128)(2,1)}, u32[]{:S(2)}, u32[]{:S(2)}) collective-permute-start(bf16[128,4096]{1,0:T(8,128)(2,1)} %collective-permute-done.29.refs_2_), channel_id=1, source_target_pairs={{0,2},{2,0},{1,3},{3,1},{4,6},{6,4},{5,7},{7,5},{8,10},{10,8},{9,1... | collective-permute-start | bytes 3145736 | tf_op jit(solution)/shard_map/ppermute | solution.py:545
  192.4 44.9 %collective-permute-start.34 = (bf16[128,4096]{1,0:T(8,128)(2,1)}, bf16[128,4096]{1,0:T(8,128)(2,1)}, u32[]{:S(2)}, u32[]{:S(2)}) collective-permute-start(bf16[128,4096]{1,0:T(8,128)(2,1)} %collective-permute-done.30.refs_3_), channel_id=1, source_target_pairs={{0,2},{2,0},{1,3},{3,1},{4,6},{6,4},{5,7},{7,5},{8,10},{10,8},{9,1... | collective-permute-start | bytes 3145736 | tf_op jit(solution)/shard_map/ppermute | solution.py:545
  216.2 65.4 %collective-permute-start.40 = (bf16[512,1024]{1,0:T(8,128)(2,1)}, bf16[512,1024]{1,0:T(8,128)(2,1)S(1)}, u32[]{:S(2)}, u32[]{:S(2)}) collective-permute-start(bf16[512,1024]{1,0:T(8,128)(2,1)} %collective-permute-done.36.refs_1_), channel_id=1, source_target_pairs={{0,2},{2,0},{1,3},{3,1},{4,6},{6,4},{5,7},{7,5},{8,10},{10,8},{9,1... | collective-permute-start | bytes 3145736 | tf_op jit(solution)/shard_map/ppermute | solution.py:545
  236.8 44.8 %collective-permute-start.39 = (bf16[512,1024]{1,0:T(8,128)(2,1)S(1)}, bf16[512,1024]{1,0:T(8,128)(2,1)S(1)}, u32[]{:S(2)}, u32[]{:S(2)}) collective-permute-start(bf16[512,1024]{1,0:T(8,128)(2,1)S(1)} %assemble.12.refs_0_), channel_id=1, source_target_pairs={{0,2},{2,0},{1,3},{3,1},{4,6},{6,4},{5,7},{7,5},{8,10},{10,8},{9,1... | collective-permute-start | bytes 3145736 | tf_op jit(solution)/shard_map/ppermute | solution.py:545
  236.8 44.8 %collective-permute-start.42 = (bf16[512,1024]{1,0:T(8,128)(2,1)S(1)}, bf16[512,1024]{1,0:T(8,128)(2,1)S(1)}, u32[]{:S(2)}, u32[]{:S(2)}) collective-permute-start(bf16[512,1024]{1,0:T(8,128)(2,1)S(1)} %collective-permute-done.38.refs_3_), channel_id=1, source_target_pairs={{0,2},{2,0},{1,3},{3,1},{4,6},{6,4},{5,7},{7,5},{8,10},{10,8},{9,1... | collective-permute-start | bytes 3145736 | tf_op jit(solution)/shard_map/ppermute | solution.py:545
  237.3 44.3 %collective-permute-start.41 = (bf16[512,1024]{1,0:T(8,128)(2,1)}, bf16[512,1024]{1,0:T(8,128)(2,1)S(1)}, u32[]{:S(2)}, u32[]{:S(2)}) collective-permute-start(bf16[512,1024]{1,0:T(8,128)(2,1)} %collective-permute-done.37.refs_2_), channel_id=1, source_target_pairs={{0,2},{2,0},{1,3},{3,1},{4,6},{6,4},{5,7},{7,5},{8,10},{10,8},{9,1... | collective-permute-start | bytes 3145736 | tf_op jit(solution)/shard_map/ppermute | solution.py:545
  305.7 32.5 %collective-permute-start.44 = (bf16[2048,1024]{1,0:T(8,128)(2,1)}, bf16[2048,1024]{1,0:T(8,128)(2,1)}, u32[]{:S(2)}, u32[]{:S(2)}) collective-permute-start(bf16[2048,1024]{1,0:T(8,128)(2,1)} %dynamic-slice_bitcast_fusion.1), channel_id=1, source_target_pairs={{0,2},{2,0},{1,3},{3,1},{4,6},{6,4},{5,7},{7,5},{8,10},{10,8},{9,1... | collective-permute-start | bytes 12582920 | tf_op jit(solution)/shard_map/ppermute | solution.py:545
  332.9 27.3 %collective-permute-start.45 = (bf16[512,4096]{1,0:T(8,128)(2,1)}, bf16[512,4096]{1,0:T(8,128)(2,1)}, u32[]{:S(2)}, u32[]{:S(2)}) collective-permute-start(bf16[512,4096]{1,0:T(8,128)(2,1)} %dynamic-slice_bitcast_fusion), channel_id=1, source_target_pairs={{0,2},{2,0},{1,3},{3,1},{4,6},{6,4},{5,7},{7,5},{8,10},{10,8},{9,1... | collective-permute-start | bytes 12582920 | tf_op jit(solution)/shard_map/ppermute | solution.py:545
  333.4 98.1 %collective-permute-start.43 = (bf16[592,1024]{1,0:T(8,128)(2,1)}, bf16[592,1024]{1,0:T(8,128)(2,1)}, u32[]{:S(2)}, u32[]{:S(2)}) collective-permute-start(bf16[592,1024]{1,0:T(8,128)(2,1)} %fusion.29), channel_id=1, source_target_pairs={{0,1},{1,0},{2,3},{3,2},{4,5},{5,4},{6,7},{7,6},{8,9},{9,8},{10,11... | collective-permute-start | bytes 3637256 | tf_op jit(solution)/shard_map/ppermute | solution.py:545
  367.8 72.6 %collective-permute-start.52 = (bf16[1024,1024]{1,0:T(8,128)(2,1)}, bf16[1024,1024]{1,0:T(8,128)(2,1)}, u32[]{:S(2)}, u32[]{:S(2)}) collective-permute-start(bf16[1024,1024]{1,0:T(8,128)(2,1)} %get-tuple-element.110), channel_id=1, source_target_pairs={{0,4},{4,0},{1,5},{5,1},{2,6},{6,2},{3,7},{7,3},{8,12},{12,8},{9,1... | collective-permute-start | bytes 6291464 | tf_op jit(solution)/shard_map/ppermute | solution.py:545
  417.3 26.4 %collective-permute-start.48 = (bf16[512,3072]{1,0:T(8,128)(2,1)}, bf16[512,3072]{1,0:T(8,128)(2,1)}, u32[]{:S(2)}, u32[]{:S(2)}) collective-permute-start(bf16[512,3072]{1,0:T(8,128)(2,1)} %dynamic-slice_bitcast_fusion.2), channel_id=1, source_target_pairs={{0,2},{2,0},{1,3},{3,1},{4,6},{6,4},{5,7},{7,5},{8,10},{10,8},{9,1... | collective-permute-start | bytes 9437192 | tf_op jit(solution)/shard_map/ppermute | solution.py:545
  431.5 48.6 %collective-permute-start.50 = (bf16[256,4096]{1,0:T(8,128)(2,1)S(1)}, bf16[256,4096]{1,0:T(8,128)(2,1)S(1)}, u32[]{:S(2)}, u32[]{:S(2)}) collective-permute-start(bf16[256,4096]{1,0:T(8,128)(2,1)S(1)} %bitcast.197), channel_id=1, source_target_pairs={{0,1},{1,0},{2,3},{3,2},{4,5},{5,4},{6,7},{7,6},{8,9},{9,8},{10,11... | collective-permute-start | bytes 6291464 | tf_op jit(solution)/shard_map/ppermute | solution.py:545
  439.0 46.7 %collective-permute-start.55 = (bf16[128,1024]{1,0:T(8,128)(2,1)S(1)}, bf16[128,1024]{1,0:T(8,128)(2,1)S(1)}, u32[]{:S(2)}, u32[]{:S(2)}) collective-permute-start(bf16[128,1024]{1,0:T(8,128)(2,1)S(1)} %dynamic-slice_bitcast_fusion.14), channel_id=1, source_target_pairs={{0,1},{1,0},{2,3},{3,2},{4,5},{5,4},{6,7},{7,6},{8,9},{9,8},{10,11... | collective-permute-start | bytes 786440 | tf_op jit(solution)/shard_map/ppermute | solution.py:545
  443.0 63.9 %collective-permute-start.53 = (bf16[512,1024]{1,0:T(8,128)(2,1)S(1)}, bf16[512,1024]{1,0:T(8,128)(2,1)S(1)}, u32[]{:S(2)}, u32[]{:S(2)}) collective-permute-start(bf16[512,1024]{1,0:T(8,128)(2,1)S(1)} %dynamic-slice_bitcast_fusion.7), channel_id=1, source_target_pairs={{0,1},{1,0},{2,3},{3,2},{4,5},{5,4},{6,7},{7,6},{8,9},{9,8},{10,11... | collective-permute-start | bytes 3145736 | tf_op jit(solution)/shard_map/ppermute | solution.py:545
  485.8 16.2 %collective-permute-start.67 = (bf16[32,1024]{1,0:T(8,128)(2,1)S(1)}, bf16[32,1024]{1,0:T(8,128)(2,1)S(1)}, u32[]{:S(2)}, u32[]{:S(2)}) collective-permute-start(bf16[32,1024]{1,0:T(8,128)(2,1)S(1)} %get-tuple-element.131), channel_id=1, source_target_pairs={{0,16},{8,24},{16,0},{24,8},{1,17},{9,25},{17,1},{25,9},{2,18},{10... | collective-permute-start | bytes 196616 | tf_op jit(solution)/shard_map/ppermute | solution.py:595
  500.0 22.8 %collective-permute-start.61 = (f32[8,384]{1,0:T(8,128)S(1)}, f32[8,384]{1,0:T(8,128)S(1)}, u32[]{:S(2)}, u32[]{:S(2)}) collective-permute-start(f32[8,384]{1,0:T(8,128)S(1)} %fusion.56), channel_id=1, source_target_pairs={{0,4},{4,0},{1,5},{5,1},{2,6},{6,2},{3,7},{7,3},{8,12},{12,8},{9,1... | collective-permute-start | bytes 36872 | tf_op jit(solution)/shard_map/ppermute | solution.py:545
  501.5 33.4 %collective-permute-start.51 = (bf16[128,4096]{1,0:T(8,128)(2,1)}, bf16[128,4096]{1,0:T(8,128)(2,1)}, u32[]{:S(2)}, u32[]{:S(2)}) collective-permute-start(bf16[128,4096]{1,0:T(8,128)(2,1)} %get-tuple-element.117), channel_id=1, source_target_pairs={{0,4},{4,0},{1,5},{5,1},{2,6},{6,2},{3,7},{7,3},{8,12},{12,8},{9,1... | collective-permute-start | bytes 3145736 | tf_op jit(solution)/shard_map/ppermute | solution.py:545
  508.4 17.2 %collective-permute-start.72 = (bf16[128,1024]{1,0:T(8,128)(2,1)S(1)}, bf16[128,1024]{1,0:T(8,128)(2,1)}, u32[]{:S(2)}, u32[]{:S(2)}) collective-permute-start(bf16[128,1024]{1,0:T(8,128)(2,1)S(1)} %get-tuple-element.121), channel_id=1, source_target_pairs={{0,8},{8,16},{16,24},{24,0},{1,9},{9,17},{17,25},{25,1},{2,10},{10... | collective-permute-start | bytes 786440 | tf_op jit(solution)/shard_map/ppermute | solution.py:595
  508.5 24.3 %collective-permute-start.73 = (bf16[128,1024]{1,0:T(8,128)(2,1)S(1)}, bf16[128,1024]{1,0:T(8,128)(2,1)}, u32[]{:S(2)}, u32[]{:S(2)}) collective-permute-start(bf16[128,1024]{1,0:T(8,128)(2,1)S(1)} %get-tuple-element.123), channel_id=1, source_target_pairs={{0,16},{8,24},{16,0},{24,8},{1,17},{9,25},{17,1},{25,9},{2,18},{10... | collective-permute-start | bytes 786440 | tf_op jit(solution)/shard_map/ppermute | solution.py:595
  524.2 28.6 %collective-permute-start.62 = (f32[4,384]{1,0:T(4,128)S(1)}, f32[4,384]{1,0:T(4,128)S(1)}, u32[]{:S(2)}, u32[]{:S(2)}) collective-permute-start(f32[4,384]{1,0:T(4,128)S(1)} %fusion.59), channel_id=1, source_target_pairs={{0,1},{1,0},{2,3},{3,2},{4,5},{5,4},{6,7},{7,6},{8,9},{9,8},{10,11... | collective-permute-start | bytes 18440 | tf_op jit(solution)/shard_map/ppermute | solution.py:545
  525.7 40.8 %collective-permute-start.49 = (bf16[256,3072]{1,0:T(8,128)(2,1)}, bf16[256,3072]{1,0:T(8,128)(2,1)S(1)}, u32[]{:S(2)}, u32[]{:S(2)}) collective-permute-start(bf16[256,3072]{1,0:T(8,128)(2,1)} %get-tuple-element.115), channel_id=1, source_target_pairs={{0,4},{4,0},{1,5},{5,1},{2,6},{6,2},{3,7},{7,3},{8,12},{12,8},{9,1... | collective-permute-start | bytes 4718600 | tf_op jit(solution)/shard_map/ppermute | solution.py:545
  536.6 19.5 %collective-permute-start.69 = (bf16[32,4096]{1,0:T(8,128)(2,1)S(1)}, bf16[32,4096]{1,0:T(8,128)(2,1)S(1)}, u32[]{:S(2)}, u32[]{:S(2)}) collective-permute-start(bf16[32,4096]{1,0:T(8,128)(2,1)S(1)} %get-tuple-element.118), channel_id=1, source_target_pairs={{0,8},{8,16},{16,24},{24,0},{1,9},{9,17},{17,25},{25,1},{2,10},{10... | collective-permute-start | bytes 786440 | tf_op jit(solution)/shard_map/ppermute | solution.py:595
  545.8 19.7 %collective-permute-start.70 = (bf16[32,4096]{1,0:T(8,128)(2,1)S(1)}, bf16[32,4096]{1,0:T(8,128)(2,1)S(1)}, u32[]{:S(2)}, u32[]{:S(2)}) collective-permute-start(bf16[32,4096]{1,0:T(8,128)(2,1)S(1)} %get-tuple-element.120), channel_id=1, source_target_pairs={{0,16},{8,24},{16,0},{24,8},{1,17},{9,25},{17,1},{25,9},{2,18},{10... | collective-permute-start | bytes 786440 | tf_op jit(solution)/shard_map/ppermute | solution.py:595
  549.3 16.2 %collective-permute-start.71 = (bf16[32,4096]{1,0:T(8,128)(2,1)S(1)}, bf16[32,4096]{1,0:T(8,128)(2,1)S(1)}, u32[]{:S(2)}, u32[]{:S(2)}) collective-permute-start(bf16[32,4096]{1,0:T(8,128)(2,1)S(1)} %get-tuple-element.119), channel_id=1, source_target_pairs={{0,24},{8,0},{16,8},{24,16},{1,25},{9,1},{17,9},{25,17},{2,26},{10... | collective-permute-start | bytes 786440 | tf_op jit(solution)/shard_map/ppermute | solution.py:595
  552.8 61.3 %collective-permute-start.47 = (bf16[592,1024]{1,0:T(8,128)(2,1)}, bf16[592,1024]{1,0:T(8,128)(2,1)}, u32[]{:S(2)}, u32[]{:S(2)}) collective-permute-start(bf16[592,1024]{1,0:T(8,128)(2,1)} %fusion.30), channel_id=1, source_target_pairs={{0,1},{1,0},{2,3},{3,2},{4,5},{5,4},{6,7},{7,6},{8,9},{9,8},{10,11... | collective-permute-start | bytes 3637256 | tf_op jit(solution)/shard_map/ppermute | solution.py:545
  567.1 29.7 %collective-permute-start.56 = (bf16[128,3072]{1,0:T(8,128)(2,1)S(1)}, bf16[128,3072]{1,0:T(8,128)(2,1)S(1)}, u32[]{:S(2)}, u32[]{:S(2)}) collective-permute-start(bf16[128,3072]{1,0:T(8,128)(2,1)S(1)} %dynamic-slice_bitcast_fusion.11), channel_id=1, source_target_pairs={{0,1},{1,0},{2,3},{3,2},{4,5},{5,4},{6,7},{7,6},{8,9},{9,8},{10,11... | collective-permute-start | bytes 2359304 | tf_op jit(solution)/shard_map/ppermute | solution.py:545
  (85 other events, 1074.7 us)

commit v4 on v3

--- a/solution.py
+++ b/solution.py
@@ -481,10 +481,26 @@
     return array.reshape(cut).transpose(spots).reshape(shape)
 
 
+def hidden_to_local(array, axis, far):
+    shape = array.shape
+    cut = shape[:axis] + (far, 2, 2, 2, shape[axis] // (8 * far)) + shape[axis + 1 :]
+    spots = [axis + 2, axis + 1, axis, axis + 3]
+    spots = list(range(axis)) + spots + list(range(axis + 4, len(cut)))
+    return array.reshape(cut).transpose(spots).reshape(shape)
+
+
 def to_natural(array, axis, far):
     shape = array.shape
     cut = shape[:axis] + (2, 2, 2, far, shape[axis] // (8 * far)) + shape[axis + 1 :]
     spots = [axis + 3, axis + 1, axis, axis + 2]
+    spots = list(range(axis)) + spots + list(range(axis + 4, len(cut)))
+    return array.reshape(cut).transpose(spots).reshape(shape)
+
+
+def hidden_to_natural(array, axis, far):
+    shape = array.shape
+    cut = shape[:axis] + (2, 2, far, 2, shape[axis] // (8 * far)) + shape[axis + 1 :]
+    spots = [axis + 2, axis + 1, axis, axis + 3]
     spots = list(range(axis)) + spots + list(range(axis + 4, len(cut)))
     return array.reshape(cut).transpose(spots).reshape(shape)
 
@@ -558,16 +574,26 @@
     return assemble(pieces, indices)
 
 
-SPOT = {"core": 4, "x": 2, "ctx": 1}
-
-
 def spread(blocks, axis):
-    return blocks | {key ^ SPOT[axis]: trade(block, axis) for key, block in blocks.items()}
-
-
-def order_blocks(blocks, extra=0):
-    own = sum(spot * lax.axis_index(axis) for axis, spot in SPOT.items())
-    return assemble(list(blocks.values()), [own ^ key for key in blocks], extra)
+    return blocks | {key | {axis}: trade(block, axis) for key, block in blocks.items()}
+
+
+def order_blocks(blocks, axes, extra=0):
+    indices = []
+    for key in blocks:
+        index = 0
+        for axis in axes:
+            place = lax.axis_index(axis)
+            index = 2 * index + (1 - place if axis in key else place)
+        indices.append(index)
+    return assemble(list(blocks.values()), indices, extra)
+
+
+def tie_blocks(blocks, other):
+    return {key: after(block, other) for key, block in blocks.items()}
+
+
+OWN = frozenset()
 
 
 def send_half(matrix, axis, outer=1):
@@ -596,8 +622,11 @@
     return arrays
 
 
-def add_far(arrays):
-    return sum(array.astype(jnp.float32) for array in arrays)
+def add_far(arrays, follow=None):
+    own, *got = arrays
+    if follow is not None:
+        got = [after(array, follow) for array in got]
+    return sum(array.astype(jnp.float32) for array in [own, *got])
 
 
 def column_sums(array):
@@ -642,22 +671,21 @@
         extra = round_up(small_width, 128)
         small = jnp.pad(small, ((0, 0), (0, extra - small_width)))
         far_qkv = gather_far(jnp.concatenate([shard_qkv, small], axis=1), far)
-        far_out = gather_far(to_local(after(unfold(w_out), far_qkv), 1, far), far)
-        far_down = gather_far(to_local(after(unfold(w_down), far_qkv), 1, far), far)
-        far_up = gather_far(to_local(after(unfold(w_up), far_down), 1, far), far)
-        far_qkv = after(far_qkv, inputs_far)
-        qkv_blocks = spread(spread({0: far_qkv}, "x"), "ctx")
-        out_blocks = spread(spread({0: far_out}, "ctx"), "x")
-        down_blocks = spread({0: far_down}, "x")
-        up_blocks = spread({0: after(far_up, qkv_blocks[3])}, "ctx")
-        up_blocks = spread(up_blocks, "x")
-        down_blocks = spread(
-            {key: after(block, up_blocks[1]) for key, block in down_blocks.items()}, "ctx"
+        shard_up = jnp.concatenate(
+            [hidden_to_local(unfold(w_up), 1, far), to_local(unfold(w_out), 1, far)], axis=1
         )
-        qkv_weight, small_local = order_blocks(spread(qkv_blocks, "core"), extra)
-        out_weight = to_natural(order_blocks(spread(out_blocks, "core")), 0, far)
-        up_blocks = spread(up_blocks, "core")
-        down_blocks = spread(down_blocks, "core")
+        far_up = gather_far(after(shard_up, far_qkv), far)
+        qkv_blocks = spread({OWN: after(far_qkv, inputs_far)}, "x")
+        far_x = qkv_blocks[frozenset({"x"})]
+        qkv_blocks = spread(qkv_blocks, "ctx")
+        up_blocks = spread({OWN: after(far_up, far_x)}, "x")
+        shard_down = after(to_local(unfold(w_down), 1, far), far_up)
+        near_down = order_blocks(spread({OWN: shard_down}, "ctx"), ["ctx"])
+        qkv_weight, small_local = order_blocks(
+            spread(qkv_blocks, "core"), ["core", "x", "ctx"], extra
+        )
+        up_blocks = spread(tie_blocks(up_blocks, qkv_blocks[frozenset({"x", "ctx"})]), "ctx")
+        far_down = gather_far(near_down, far)
 
         small_core = small_local[:, :small_width].astype(jnp.float32).reshape(8 * far, -1)
         small_all = to_natural(small_core, 0, far)
@@ -667,7 +695,7 @@
         out_bias, first_gain, first_shift, second_gain, second_shift, down_bias = (
             piece(small_core, index) for index in range(2, 8)
         )
-        up_bias = small_core[:, 8 * near_width :].reshape(-1)
+        up_bias = hidden_to_local(small_all[:, 8 * near_width :].reshape(-1), 0, far)
 
         slot = jnp.arange(slots)
         earlier = slot[:, None] < slot[None, :]
@@ -715,15 +743,21 @@
         normed1 = (normal1 * first_gain + first_shift).astype(jnp.bfloat16)
         joined_bias = jnp.concatenate([query_bias, jnp.zeros_like(query_bias), value_bias])
         joined = (matmul(normed1, qkv_weight) + joined_bias).astype(jnp.bfloat16)
-        attended, log_total = attention_forward(joined, bias)
+        up_near = order_blocks(up_blocks, ["x", "ctx"])
+        attended, log_total = attention_forward(after(joined, near_down), bias)
+        down_blocks = spread({OWN: after(far_down, attended)}, "x")
+        up_weight, out_rows = order_blocks(
+            spread({OWN: after(up_near, attended)}, "core"), ["core"], width
+        )
+        out_weight = to_natural(out_rows, 0, far)
         middle = values_in + matmul(attended, out_weight) + out_bias
         normal2, scale2 = standardize(middle)
         normed2 = (normal2 * second_gain + second_shift).astype(jnp.bfloat16)
-        up_weight = order_blocks(up_blocks)
         hidden = matmul(normed2, up_weight) + up_bias
         active = gelu_exact(hidden).astype(jnp.bfloat16)
         slope = gelu_slope(hidden).astype(jnp.bfloat16)
-        down_weight = order_blocks(down_blocks)
+        down_blocks = tie_blocks(down_blocks, active)
+        down_weight = order_blocks(spread(down_blocks, "core"), ["core", "x"])
 
         live = (row < SEQ).astype(jnp.float32)[:, None]
         cotangent_far = swap(after(cotangent, joined))
@@ -731,45 +765,44 @@
         d_out_low = d_out.astype(jnp.bfloat16)
         grad_down = matmul(active.T, d_out_low).astype(jnp.bfloat16)
         down_core = send_half(grad_down, "core")
-        last = middle + matmul(after(active, grad_down), down_weight) + down_bias
+        last = middle + matmul(after(active, down_core[0]), down_weight) + down_bias
         last_given = to_give(last)
+        down_x = send_half(add_half(down_core, last_given[0]), "x")
         d_hidden = (
-            matmul(after(d_out_low, last_given[0]), down_weight.T) * slope.astype(jnp.float32)
+            matmul(after(d_out_low, down_x[0]), down_weight.T) * slope.astype(jnp.float32)
         ).astype(jnp.bfloat16)
         grad_up = matmul(normed2.T, d_hidden).astype(jnp.bfloat16)
         up_core = send_half(grad_up, "core")
-        down_x = send_half(add_half(down_core, grad_up), "x")
-        d_normed2 = matmul(after(d_hidden, down_x[0]), up_weight.T)
+        d_normed2 = matmul(after(d_hidden, up_core[0]), up_weight.T)
         d_middle = d_out + norm_backward(d_normed2, normal2, scale2, second_gain)
         d_branch = d_middle.astype(jnp.bfloat16)
+        outputs = give(last_given, d_branch).astype(jnp.bfloat16)
         up_y = send_half(add_half(up_core, d_branch), "ctx", 2)
         grad_out = to_local(matmul(attended.T, after(d_branch, up_y[0])).astype(jnp.bfloat16), 0, far)
         out_core = send_half(grad_out, "core")
         d_attended = matmul(d_branch, out_weight.T).astype(jnp.bfloat16)
+        down_far = send_far(add_half(down_x, d_attended), far)
         out_x = send_half(add_half(out_core, d_attended), "x")
-        d_query, d_key, d_value = attention_backward(
-            joined, after(d_attended, out_x[0]), log_total, bias
-        )
-        outputs = give(last_given, d_query).astype(jnp.bfloat16)
+        d_attended = after(after(d_attended, out_x[0]), down_far[0])
+        d_query, d_key, d_value = attention_backward(joined, d_attended, log_total, bias)
         d_joined = jnp.concatenate([d_query, d_key, d_value], axis=1)
         out_y = send_half(add_half(out_x, d_joined), "ctx")
-        grad_qkv = matmul(normed1.T, d_joined).astype(jnp.bfloat16)
+        up_x = send_half(add_half(up_y, d_joined), "x")
+        grad_qkv = matmul(normed1.T, after(after(d_joined, out_y[0]), up_x[0])).astype(jnp.bfloat16)
         qkv_core = send_half(grad_qkv, "core")
-        down_y = send_half(add_half(down_x, grad_qkv), "ctx")
-        d_normed1 = matmul(after(d_joined, grad_qkv), qkv_weight.T)
+        d_normed1 = matmul(after(d_joined, qkv_core[0]), qkv_weight.T)
         d_last = d_middle + norm_backward(d_normed1, normal1, scale1, first_gain)
-        d_last_given = to_give(d_last)
-        qkv_x = send_half(add_half(qkv_core, d_last_given[0]), "x")
-        up_x = send_half(add_half(up_y, qkv_x[0]), "x")
-        out_far = send_far(add_half(out_y, up_x[0]), far)
-        down_far = send_far(add_half(down_y, out_far[0]), far)
-        up_far = send_far(add_half(up_x, down_far[0]), far)
+        qkv_x = send_half(add_half(qkv_core, d_last), "x")
+        out_far = send_far(add_half(out_y, d_last), far)
+        down_y = send_half(add_far(down_far, d_last).astype(jnp.bfloat16), "ctx")
+        d_last_given = to_give(after(after(d_last, qkv_x[0]), down_y[0]))
+        up_far = send_far(add_half(up_x, d_last_given[0]), far)
         qkv_y = send_half(add_half(qkv_x, up_far[0]), "ctx")
+        sum_down = add_half(down_y, qkv_y[0]).astype(jnp.float32)
+        sum_up, sum_out = add_far(up_far, qkv_y[0]), add_far(out_far, qkv_y[0])
         qkv_far = send_far(add_half(qkv_y), far)
-        sum_down, sum_up, sum_out, sum_qkv = (
-            add_far(arrays) for arrays in (down_far, up_far, out_far, qkv_far)
-        )
         input_grad = give(d_last_given, qkv_far[0])
+        sum_qkv = add_far(qkv_far)
 
         part = lambda vector: vector.reshape(8 * far, -1)
         core_sums = jnp.concatenate(
@@ -782,13 +815,15 @@
                     column_sums(d_normed2 * normal2),
                     column_sums(d_normed2),
                     column_sums(d_out_low),
-                    column_sums(d_hidden),
                 )
             ],
             axis=1,
         )
         chip_sums = jnp.concatenate([part(column_sums(d_query)), part(column_sums(d_value))], axis=1)
-        small_sums = jnp.concatenate([to_local(chip_sums, 0, far), core_sums], axis=1)
+        up_sums = part(hidden_to_natural(column_sums(d_hidden), 0, far))
+        small_sums = jnp.concatenate(
+            [to_local(chip_sums, 0, far), core_sums, to_local(up_sums, 0, far)], axis=1
+        )
         for axis in ("core", "x", "ctx"):
             small_sums = add_half(send_half(small_sums, axis))
         small_sums = add_far(send_far(small_sums, far))[0]
@@ -806,7 +841,7 @@
             own(4),
             own(5),
             own(6),
-            back(sum_up),
+            refold(hidden_to_natural(sum_up, 1, far)),
             small_sums[8 * near_width :],
             back(sum_down),
             own(7),

time: 628 us -> 635 us (1.011)
  waiting for transfers between devices: 178 us -> 202 us
  starting transfers between devices: 117 us -> 95.5 us
  local copies, waits for them, and re-layouts: 59.2 us -> 71.3 us
  matrix products: 151 us -> 142 us
    ppermute x15, starting transfers between devices: 56.1 us -> 44.8 us  [send_far(): lax.ppermute(sent, 'z', [(i, (i + step) % far) for i in range(far)])]
    ppermute x12 -> x9, waiting for transfers between devices: 37.9 us -> 47.5 us  [gather_far(): lax.ppermute(shard, 'z', [(i, (i + step) % far) for i in range(far)])]
    ppermute x48 -> x35, waiting for transfers between devices: 122 us -> 130 us  [trade(): return lax.ppermute(array, axis, [(0, 1), (1, 0)])]
    reshape x12 -> x14, local copies, waits for them, and re-layouts: 13.5 us -> 21.5 us  [send_half(): lax.dynamic_index_in_dim(blocks, 1 - place, 1, False)]
    ppermute x48 -> x35, starting transfers between devices: 34.7 us -> 27.1 us  [trade(): return lax.ppermute(array, axis, [(0, 1), (1, 0)])]
    unnamed x118 -> x116, local copies, waits for them, and re-layouts: 14.2 us -> 17.5 us
    ppermute x12 -> x9, starting transfers between devices: 25.9 us -> 23.6 us  [gather_far(): lax.ppermute(shard, 'z', [(i, (i + step) % far) for i in range(far)])]
    convert_element_type x12 -> x11, other arithmetic: 22.8 us -> 23.3 us  [add_half(): (kept.astype(jnp.float32) + got.astype(jnp.float32)).astype(kept.dtype)]
  transfers between devices with their start and end apart: 75 -> 59, of which waited for: 22 -> 19; matrix products, arithmetic and copies ran while one was open for 34% -> 36% of each run, Pallas kernels for 11% -> 12%
where the time goes in v4:
time: 635 us; the launch traced here: 629 us
  waiting for transfers between devices  202 us (32%)
  matrix products  142 us (22%)
  starting transfers between devices  95.5 us (15%)
  Pallas kernels  78.3 us (12%)
  local copies, waits for them, and re-layouts  71.3 us (11%)
  other arithmetic  37.9 us (6%)
    ppermute x35, waiting for transfers between devices, trade(): return lax.ppermute(array, axis, [(0, 1), (1, 0)])  130 us
    dot_general x19, matrix products, matmul(): return jnp.dot(left, right, preferred_element_type=jnp.float32)  126 us
    ppermute x9, waiting for transfers between devices, gather_far(): lax.ppermute(shard, 'z', [(i, (i + step) % far) for i in range(far)])  47.5 us
    ppermute x15, starting transfers between devices, send_far(): lax.ppermute(sent, 'z', [(i, (i + step) % far) for i in range(far)])  44.8 us
    pallas_call x1, Pallas kernels, attention_backward(): pl.pallas_call(backward_kernel, grid=(pairs,), in_specs=[pl.BlockSpec((ro...  28 us
    pallas_call x1, Pallas kernels, attention_forward(): pl.pallas_call(forward_kernel, grid=(pairs,), in_specs=[pl.BlockSpec((row...  27.2 us
    ppermute x35, starting transfers between devices, trade(): return lax.ppermute(array, axis, [(0, 1), (1, 0)])  27.1 us
    ppermute x15, waiting for transfers between devices, send_far(): lax.ppermute(sent, 'z', [(i, (i + step) % far) for i in range(far)])  23.9 us
  transfers between devices with their start and end apart: 59, of which 19 were waited for; matrix products, arithmetic and copies ran while one was open for 36% of the time, Pallas kernels for 12%

profile of v4, /device:TPU:0, one launch (start us, length us, event | category | flops | bytes accessed | tf_op | source)
XLA Modules:
  0.0 628.8 jit_solution(3110334463393480299)
XLA Ops:
  4.7 6.1 concatenate.43
  20.9 7.4 %collective-permute-done.3.refs_2_ = bf16[32,3200]{1,0:T(8,128)(2,1)S(1)} collective-permute-done((bf16[32,3200]{1,0:T(8,128)(2,1)S(1)}, bf16[32,3200]{1,0:T(8,128)(2,1)S(1)}, u32[]{:S(2)}, u32[]{:S(2)}) %collective-permute-start.3) | collective-permute-done | bytes 204832 | tf_op jit(solution)/shard_map/ppermute | solution.py:572
  35.8 4.9 collective-permute-start.12
  43.6 7.7 %collective-permute-done.5.refs_1_ = bf16[128,3200]{1,0:T(8,128)(2,1)} collective-permute-done((bf16[128,3200]{1,0:T(8,128)(2,1)S(1)}, bf16[128,3200]{1,0:T(8,128)(2,1)}, u32[]{:S(2)}, u32[]{:S(2)}) %collective-permute-start.5) | collective-permute-done | bytes 819232 | tf_op jit(solution)/shard_map/ppermute | solution.py:561
  53.1 9.1 %collective-permute-done.13.refs_2_ = bf16[32,5120]{1,0:T(8,128)(2,1)S(1)} collective-permute-done((bf16[32,5120]{1,0:T(8,128)(2,1)S(1)}, bf16[32,5120]{1,0:T(8,128)(2,1)S(1)}, u32[]{:S(2)}, u32[]{:S(2)}) %collective-permute-start.13) | collective-permute-done | bytes 327712 | tf_op jit(solution)/shard_map/ppermute | solution.py:572
  64.6 3.8 fusion.27
  68.9 16.7 %collective-permute-done.15.refs_1_ = bf16[128,1024]{1,0:T(8,128)(2,1)S(1)} collective-permute-done((bf16[128,1024]{1,0:T(8,128)(2,1)S(1)}, bf16[128,1024]{1,0:T(8,128)(2,1)S(1)}, u32[]{:S(2)}, u32[]{:S(2)}) %collective-permute-start.15) | collective-permute-done | bytes 262176 | tf_op jit(solution)/shard_map/ppermute | solution.py:561
  87.4 5.9 fusion.58
  108.0 7.6 %add_convert_fusion.2.query_ref.key_ref.value_ref = bf16[592,3072]{1,0:T(8,128)(2,1)S(1)} fusion(bf16[1024,3072]{1,0:T(8,128)(2,1)} %copy-done.5, f32[3072]{0:T(1024)S(1)} %pad_maximum_fusion.1, f32[592,1024]{1,0:T(8,128)} %get-tuple-element.200, f32[1024]{0:T(1024)S(1)} %add.490, f32[1024]{0:T(1024)S(1)} %mul.219, f32[592]{0:T(1024)S(1)} %add_rsqrt_fusion.1, ...), kind=kOutput, calls=%fused_computation.31 | convolution fusion | flops 3731210240 | bytes 12378752 | tf_op jit(solution)/shard_map/dot_general | solution.py:27
  115.7 27.2 %attention_forward.1 = (bf16[592,1024]{1,0:T(8,128)(2,1)S(1)}, f32[8,2,592]{2,1,0:T(2,128)S(1)}) custom-call(bf16[592,3072]{1,0:T(8,128)(2,1)S(1)} %add_convert_fusion.2.query_ref.key_ref.value_ref, bf16[592,3072]{1,0:T(8,128)(2,1)S(1)} %add_convert_fusion.2.query_ref.key_ref.value_ref, bf16[592,3072]{1,0:T(8,128)(2,1)S(1)} %add_convert_fusion.2.query_ref.key_ref.value_ref, ...), custom_call_target="tpu_custom_call" | custom-call | flops 5742002176 | bytes 4849664 | tf_op jit(solution)/shard_map/attention_forward/pallas_call | solution.py:405
  143.0 13.4 %collective-permute-done.18.refs_3_ = bf16[128,5120]{1,0:T(8,128)(2,1)} collective-permute-done((bf16[128,5120]{1,0:T(8,128)(2,1)}, bf16[128,5120]{1,0:T(8,128)(2,1)}, u32[]{:S(2)}, u32[]{:S(2)}) %collective-permute-start.18) | collective-permute-done | bytes 1310752 | tf_op jit(solution)/shard_map/ppermute | solution.py:561
  156.4 4.4 assemble.12.refs_0_
  162.5 8.3 %collective-permute-start.21 = (bf16[256,1024]{1,0:T(8,128)(2,1)S(1)}, bf16[256,1024]{1,0:T(8,128)(2,1)S(1)}, u32[]{:S(2)}, u32[]{:S(2)}) collective-permute-start(bf16[256,1024]{1,0:T(8,128)(2,1)S(1)} %assemble.11.refs_0_), channel_id=1, source_target_pairs={{0,8},{8,16},{16,24},{24,0},{1,9},{9,17},{17,25},{25,1},{2,10},{10... | collective-permute-start | bytes 1572872 | tf_op jit(solution)/shard_map/ppermute | solution.py:572
  173.3 3.9 fusion.26
  177.2 6.6 %collective-permute-done.21.refs_1_ = bf16[256,1024]{1,0:T(8,128)(2,1)S(1)} collective-permute-done((bf16[256,1024]{1,0:T(8,128)(2,1)S(1)}, bf16[256,1024]{1,0:T(8,128)(2,1)S(1)}, u32[]{:S(2)}, u32[]{:S(2)}) %collective-permute-start.21) | collective-permute-done | bytes 524320 | tf_op jit(solution)/shard_map/ppermute | solution.py:572
  183.7 22.0 %collective-permute-done.22.refs_2_ = bf16[256,1024]{1,0:T(8,128)(2,1)S(1)} collective-permute-done((bf16[256,1024]{1,0:T(8,128)(2,1)S(1)}, bf16[256,1024]{1,0:T(8,128)(2,1)S(1)}, u32[]{:S(2)}, u32[]{:S(2)}) %collective-permute-start.22) | collective-permute-done | bytes 524320 | tf_op jit(solution)/shard_map/ppermute | solution.py:572
  207.6 6.3 convert_reduce_fusion.1
  213.8 5.6 assemble.13
  226.1 28.2 %fusion.2 = (bf16[592,4096]{1,0:T(8,128)(2,1)S(1)}, f32[592,4096]{1,0:T(8,128)}) fusion(f32[4096]{0:T(1024)S(1)} %bitcast.223, bf16[1024,4096]{1,0:T(8,128)(2,1)S(1)} %get-tuple-element.81, f32[592,1024]{1,0:T(8,128)S(1)} %get-tuple-element.202, f32[1024]{0:T(1024)S(1)} %add.505, f32[1024]{0:T(1024)S(1)} %mul.227, f32[592]{0:T(1024)S(1)} %add_rsqrt_fusion, ...), kind=kOutput, calls=%fused_computation.4 | convolution fusion | flops 5129125888 | bytes 25391744 | tf_op jit(solution)/shard_map/dot_general | solution.py:27
  254.4 7.0 %convolution_convert_fusion.1 = bf16[4096,1024]{1,0:T(8,128)(2,1)S(1)} fusion(bf16[592,4096]{1,0:T(8,128)(2,1)S(1)} %get-tuple-element.83, bf16[592,1024]{1,0:T(8,128)(2,1)S(1)} %copy-done.51), kind=kOutput, calls=%fused_computation.30 | convolution fusion | flops 4970250240 | bytes 14450688 | tf_op jit(solution)/shard_map/dot_general | solution.py:27
  261.4 4.3 dynamic-slice_bitcast_fusion.2
  266.4 12.8 %collective-permute-done.26.refs_3_ = bf16[1024,1024]{1,0:T(8,128)(2,1)} collective-permute-done((bf16[1024,1024]{1,0:T(8,128)(2,1)}, bf16[1024,1024]{1,0:T(8,128)(2,1)}, u32[]{:S(2)}, u32[]{:S(2)}) %collective-permute-start.26) | collective-permute-done | bytes 2097184 | tf_op jit(solution)/shard_map/ppermute | solution.py:561
  279.2 3.8 assemble.15
  286.4 13.2 %fusion.24 = bf16[592,1024]{1,0:T(8,128)(2,1)} fusion(s32[1024]{0:T(1024)S(1)} %reshape.573, f32[592,1024]{1,0:T(8,128)} %copy-done.14, bf16[592,4096]{1,0:T(8,128)(2,1)} %copy-done.52, bf16[4096,1024]{1,0:T(8,128)(2,1)} %copy-done, f32[1024]{0:T(1024)S(1)} %add.514), kind=kOutput, calls=%fused_computation.87 | convolution fusion | flops 6211043328 | bytes 16883712 | tf_op jit(solution)/shard_map/dot_general | solution.py:329
  300.4 5.6 add_convert_fusion.1
  310.9 12.1 %convert_reduce_fusion = (f32[4096]{0:T(1024)S(1)}, bf16[592,4096]{1,0:T(8,128)(2,1)}) fusion(f32[592,4096]{1,0:T(8,128)} %get-tuple-element.204, f32[4096]{0:T(1024)S(1)} %bitcast.224, bf16[592,1024]{1,0:T(8,128)(2,1)} %get-tuple-element.88, bf16[4096,1024]{1,0:T(8,128)(2,1)S(1)} %copy-done.1), kind=kOutput, calls=%fused_computation.10 | convolution fusion | flops 5002424320 | bytes 24182784 | tf_op jit(solution)/shard_map/dot_general | solution.py:27
  323.0 12.0 %convolution_convert_fusion = bf16[1024,4096]{1,0:T(8,128)(2,1)} fusion(bf16[592,4096]{1,0:T(8,128)(2,1)} %get-tuple-element.89, f32[592,1024]{1,0:T(8,128)} %copy-done.14, f32[1024]{0:T(1024)S(1)} %add.505, f32[1024]{0:T(1024)S(1)} %mul.227, f32[592]{0:T(1024)S(1)} %add_rsqrt_fusion, f32[592]{0:T(1024)S(1)} %broadcast_multiply_fusion.4), kind=kOutput, calls=%fused_computation.29 | convolution fusion | flops 4973281280 | bytes 15676032 | tf_op jit(solution)/shard_map/dot_general | solution.py:27
  335.1 8.0 %dynamic-slice_bitcast_fusion = (bf16[512,4096]{1,0:T(8,128)(2,1)}, bf16[512,4096]{1,0:T(8,128)(2,1)}) fusion(bf16[1,2,512,4096]{3,2,1,0:T(8,128)(2,1)} %bitcast.199, s32[]{:T(128)S(6)} %select_n.216, s32[]{:T(128)S(6)} %select_n.214), kind=kLoop, calls=%fused_computation.36 | loop fusion | bytes 16777224 | tf_op jit(solution)/shard_map/reshape | solution.py:604
  344.6 8.1 %multiply_reduce_fusion = (f32[1024]{0:T(1024)S(1)}, f32[592]{0:T(1024)S(1)}, f32[592]{0:T(1024)S(1)}, f32[1024]{0:T(1024)S(1)}, f32[592,1024]{1,0:T(8,128)S(1)}) fusion(f32[592,1024]{1,0:T(8,128)S(1)} %copy-done.15, f32[592]{0:T(1024)S(1)} %add_rsqrt_fusion, f32[592]{0:T(1024)S(1)} %broadcast_multiply_fusion.4, f32[1024]{0:T(1024)S(1)} %mul.227, ...), kind=kOutput, calls=%fused_computation.49 | convolution fusion | flops 4971508736 | bytes 18109696 | tf_op jit(solution)/shard_map/dot_general | solution.py:27
  358.7 3.8 fusion.29
  363.4 4.4 add_convert_fusion.12
  371.8 20.1 %collective-permute-done.31 = bf16[1024,1024]{1,0:T(8,128)(2,1)} collective-permute-done((bf16[1024,1024]{1,0:T(8,128)(2,1)}, bf16[1024,1024]{1,0:T(8,128)(2,1)}, u32[]{:S(2)}, u32[]{:S(2)}) %collective-permute-start.31) | collective-permute-done | bytes 2097184 | tf_op jit(solution)/shard_map/ppermute | solution.py:561
  397.4 3.7 add_convert_fusion
  405.1 28.0 %attention_backward.1 = (bf16[592,1024]{1,0:T(8,128)(2,1)S(1)}, bf16[592,1024]{1,0:T(8,128)(2,1)S(1)}, bf16[592,1024]{1,0:T(8,128)(2,1)S(1)}) custom-call(bf16[592,3072]{1,0:T(8,128)(2,1)S(1)} %copy-done.10, bf16[592,3072]{1,0:T(8,128)(2,1)S(1)} %copy-done.10, bf16[592,3072]{1,0:T(8,128)(2,1)S(1)} %copy-done.10, ...), custom_call_target="tpu_custom_call" | custom-call | flops 14355005440 | bytes 8486912 | tf_op jit(solution)/shard_map/attention_backward/pallas_call | solution.py:435
  435.5 11.7 %collective-permute-start.35 = (bf16[256,1024]{1,0:T(8,128)(2,1)}, bf16[256,1024]{1,0:T(8,128)(2,1)}, u32[]{:S(2)}, u32[]{:S(2)}) collective-permute-start(bf16[256,1024]{1,0:T(8,128)(2,1)} %get-tuple-element.158), channel_id=1, source_target_pairs={{0,8},{8,16},{16,24},{24,0},{1,9},{9,17},{17,25},{25,1},{2,10},{10... | collective-permute-start | bytes 1572872 | tf_op jit(solution)/shard_map/ppermute | solution.py:621
  457.4 5.6 convolution_convert_fusion.2
  465.2 4.4 multiply_reduce_fusion.1
  471.5 11.3 %collective-permute-done.36 = bf16[256,1024]{1,0:T(8,128)(2,1)} collective-permute-done((bf16[256,1024]{1,0:T(8,128)(2,1)}, bf16[256,1024]{1,0:T(8,128)(2,1)}, u32[]{:S(2)}, u32[]{:S(2)}) %collective-permute-start.36) | collective-permute-done | bytes 524320 | tf_op jit(solution)/shard_map/ppermute | solution.py:621
  491.9 20.7 %collective-permute-done.46 = f32[8,384]{1,0:T(8,128)S(1)} collective-permute-done((f32[8,384]{1,0:T(8,128)S(1)}, f32[8,384]{1,0:T(8,128)S(1)}, u32[]{:S(2)}, u32[]{:S(2)}) %collective-permute-start.46) | collective-permute-done | bytes 12320 | tf_op jit(solution)/shard_map/ppermute | solution.py:561
  515.7 11.7 %collective-permute-start.52 = (bf16[32,1024]{1,0:T(8,128)(2,1)}, bf16[32,1024]{1,0:T(8,128)(2,1)S(1)}, u32[]{:S(2)}, u32[]{:S(2)}) collective-permute-start(bf16[32,1024]{1,0:T(8,128)(2,1)} %get-tuple-element.175), channel_id=1, source_target_pairs={{0,8},{8,16},{16,24},{24,0},{1,9},{9,17},{17,25},{25,1},{2,10},{10... | collective-permute-start | bytes 196616 | tf_op jit(solution)/shard_map/ppermute | solution.py:621
  538.2 28.4 %collective-permute-done.39 = bf16[256,3072]{1,0:T(8,128)(2,1)S(1)} collective-permute-done((bf16[256,3072]{1,0:T(8,128)(2,1)S(1)}, bf16[256,3072]{1,0:T(8,128)(2,1)S(1)}, u32[]{:S(2)}, u32[]{:S(2)}) %collective-permute-start.39) | collective-permute-done | bytes 1572896 | tf_op jit(solution)/shard_map/ppermute | solution.py:561
  572.6 4.7 collective-permute-start.56
  577.3 3.8 fusion.28
  581.2 6.9 %collective-permute-done.41 = bf16[128,3072]{1,0:T(8,128)(2,1)S(1)} collective-permute-done((bf16[128,3072]{1,0:T(8,128)(2,1)S(1)}, bf16[128,3072]{1,0:T(8,128)(2,1)S(1)}, u32[]{:S(2)}, u32[]{:S(2)}) %collective-permute-start.41) | collective-permute-done | bytes 786464 | tf_op jit(solution)/shard_map/ppermute | solution.py:561
  588.7 4.1 collective-permute-start.54
  593.7 3.9 collective-permute-done.57
  617.2 5.8 collective-permute-done.43
  624.0 4.6 convolution_add_fusion
  (347 shorter events, 157.2 us)
Async XLA Ops:
  0.7 30.4 %collective-permute-start.1 = (bf16[584,1024]{1,0:T(8,128)(2,1)}, bf16[584,1024]{1,0:T(8,128)(2,1)}, u32[]{:S(2)}, u32[]{:S(2)}) collective-permute-start(bf16[584,1024]{1,0:T(8,128)(2,1)} %param.16), channel_id=1, source_target_pairs={{0,1},{1,0},{2,3},{3,2},{4,5},{5,4},{6,7},{7,6},{8,9},{9,8},{10,11... | collective-permute-start | bytes 3588104 | tf_op jit(solution)/shard_map/ppermute | solution.py:561
  12.6 15.7 %collective-permute-start.3 = (bf16[32,3200]{1,0:T(8,128)(2,1)S(1)}, bf16[32,3200]{1,0:T(8,128)(2,1)S(1)}, u32[]{:S(2)}, u32[]{:S(2)}) collective-permute-start(bf16[32,3200]{1,0:T(8,128)(2,1)S(1)} %fusion.43.refs_0_), channel_id=1, source_target_pairs={{0,16},{8,24},{16,0},{24,8},{1,17},{9,25},{17,1},{25,9},{2,18},{10... | collective-permute-start | bytes 614408 | tf_op jit(solution)/shard_map/ppermute | solution.py:572
  16.5 26.6 %collective-permute-start = (s32[584]{0:T(1024)}, s32[584]{0:T(1024)S(1)}, u32[]{:S(2)}, u32[]{:S(2)}) collective-permute-start(s32[584]{0:T(1024)} %param.18), channel_id=1, source_target_pairs={{0,1},{1,0},{2,3},{3,2},{4,5},{5,4},{6,7},{7,6},{8,9},{9,8},{10,11... | collective-permute-start | bytes 7016 | tf_op jit(solution)/shard_map/ppermute | solution.py:561
  31.0 20.2 %collective-permute-start.5 = (bf16[128,3200]{1,0:T(8,128)(2,1)S(1)}, bf16[128,3200]{1,0:T(8,128)(2,1)}, u32[]{:S(2)}, u32[]{:S(2)}) collective-permute-start(bf16[128,3200]{1,0:T(8,128)(2,1)S(1)} %assemble.8.refs_0_), channel_id=1, source_target_pairs={{0,4},{4,0},{1,5},{5,1},{2,6},{6,2},{3,7},{7,3},{8,12},{12,8},{9,1... | collective-permute-start | bytes 2457608 | tf_op jit(solution)/shard_map/ppermute | solution.py:561
  35.8 17.3 %collective-permute-start.12 = (bf16[32,5120]{1,0:T(8,128)(2,1)S(1)}, bf16[32,5120]{1,0:T(8,128)(2,1)S(1)}, u32[]{:S(2)}, u32[]{:S(2)}) collective-permute-start(bf16[32,5120]{1,0:T(8,128)(2,1)S(1)} %pad_maximum_fusion.refs_0_), channel_id=1, source_target_pairs={{0,8},{8,16},{16,24},{24,0},{1,9},{9,17},{17,25},{25,1},{2,10},{10... | collective-permute-start | bytes 983048 | tf_op jit(solution)/shard_map/ppermute | solution.py:572
  40.7 21.5 %collective-permute-start.13 = (bf16[32,5120]{1,0:T(8,128)(2,1)S(1)}, bf16[32,5120]{1,0:T(8,128)(2,1)S(1)}, u32[]{:S(2)}, u32[]{:S(2)}) collective-permute-start(bf16[32,5120]{1,0:T(8,128)(2,1)S(1)} %pad_maximum_fusion.refs_0_), channel_id=1, source_target_pairs={{0,16},{8,24},{16,0},{24,8},{1,17},{9,25},{17,1},{25,9},{2,18},{10... | collective-permute-start | bytes 983048 | tf_op jit(solution)/shard_map/ppermute | solution.py:572
  42.3 19.9 %collective-permute-start.14 = (bf16[32,5120]{1,0:T(8,128)(2,1)S(1)}, bf16[32,5120]{1,0:T(8,128)(2,1)S(1)}, u32[]{:S(2)}, u32[]{:S(2)}) collective-permute-start(bf16[32,5120]{1,0:T(8,128)(2,1)S(1)} %pad_maximum_fusion.refs_0_), channel_id=1, source_target_pairs={{0,24},{8,0},{16,8},{24,16},{1,25},{9,1},{17,9},{25,17},{2,26},{10... | collective-permute-start | bytes 983048 | tf_op jit(solution)/shard_map/ppermute | solution.py:572
  43.1 43.8 %collective-permute-start.6 = (bf16[128,3200]{1,0:T(8,128)(2,1)S(1)}, bf16[128,3200]{1,0:T(8,128)(2,1)}, u32[]{:S(2)}, u32[]{:S(2)}) collective-permute-start(bf16[128,3200]{1,0:T(8,128)(2,1)S(1)} %assemble.8.refs_0_), channel_id=1, source_target_pairs={{0,1},{1,0},{2,3},{3,2},{4,5},{5,4},{6,7},{7,6},{8,9},{9,8},{10,11... | collective-permute-start | bytes 2457608 | tf_op jit(solution)/shard_map/ppermute | solution.py:561
  51.3 35.7 %collective-permute-start.7 = (bf16[128,3200]{1,0:T(8,128)(2,1)}, bf16[128,3200]{1,0:T(8,128)(2,1)}, u32[]{:S(2)}, u32[]{:S(2)}) collective-permute-start(bf16[128,3200]{1,0:T(8,128)(2,1)} %collective-permute-done.5.refs_1_), channel_id=1, source_target_pairs={{0,1},{1,0},{2,3},{3,2},{4,5},{5,4},{6,7},{7,6},{8,9},{9,8},{10,11... | collective-permute-start | bytes 2457608 | tf_op jit(solution)/shard_map/ppermute | solution.py:561
  64.0 21.6 %collective-permute-start.15 = (bf16[128,1024]{1,0:T(8,128)(2,1)S(1)}, bf16[128,1024]{1,0:T(8,128)(2,1)S(1)}, u32[]{:S(2)}, u32[]{:S(2)}) collective-permute-start(bf16[128,1024]{1,0:T(8,128)(2,1)S(1)} %copy.78.refs_0_), channel_id=1, source_target_pairs={{0,1},{1,0},{2,3},{3,2},{4,5},{5,4},{6,7},{7,6},{8,9},{9,8},{10,11... | collective-permute-start | bytes 786440 | tf_op jit(solution)/shard_map/ppermute | solution.py:561
  68.4 30.4 %collective-permute-start.16 = (bf16[128,5120]{1,0:T(8,128)(2,1)S(1)}, bf16[128,5120]{1,0:T(8,128)(2,1)}, u32[]{:S(2)}, u32[]{:S(2)}) collective-permute-start(bf16[128,5120]{1,0:T(8,128)(2,1)S(1)} %assemble.10.refs_0_), channel_id=1, source_target_pairs={{0,4},{4,0},{1,5},{5,1},{2,6},{6,2},{3,7},{7,3},{8,12},{12,8},{9,1... | collective-permute-start | bytes 3932168 | tf_op jit(solution)/shard_map/ppermute | solution.py:561
  86.3 14.0 %collective-permute-start.8 = (bf16[128,3200]{1,0:T(8,128)(2,1)S(1)}, bf16[128,3200]{1,0:T(8,128)(2,1)S(1)}, u32[]{:S(2)}, u32[]{:S(2)}) collective-permute-start(bf16[128,3200]{1,0:T(8,128)(2,1)S(1)} %assemble.8.refs_0_), channel_id=1, source_target_pairs={{0,2},{2,0},{1,3},{3,1},{4,6},{6,4},{5,7},{7,5},{8,10},{10,8},{9,1... | collective-permute-start | bytes 2457608 | tf_op jit(solution)/shard_map/ppermute | solution.py:561
  86.4 14.5 %collective-permute-start.9 = (bf16[128,3200]{1,0:T(8,128)(2,1)}, bf16[128,3200]{1,0:T(8,128)(2,1)}, u32[]{:S(2)}, u32[]{:S(2)}) collective-permute-start(bf16[128,3200]{1,0:T(8,128)(2,1)} %collective-permute-done.5.refs_1_), channel_id=1, source_target_pairs={{0,2},{2,0},{1,3},{3,1},{4,6},{6,4},{5,7},{7,5},{8,10},{10,8},{9,1... | collective-permute-start | bytes 2457608 | tf_op jit(solution)/shard_map/ppermute | solution.py:561
  86.9 13.9 %collective-permute-start.10 = (bf16[128,3200]{1,0:T(8,128)(2,1)}, bf16[128,3200]{1,0:T(8,128)(2,1)}, u32[]{:S(2)}, u32[]{:S(2)}) collective-permute-start(bf16[128,3200]{1,0:T(8,128)(2,1)} %collective-permute-done.6.refs_2_), channel_id=1, source_target_pairs={{0,2},{2,0},{1,3},{3,1},{4,6},{6,4},{5,7},{7,5},{8,10},{10,8},{9,1... | collective-permute-start | bytes 2457608 | tf_op jit(solution)/shard_map/ppermute | solution.py:561
  98.8 44.2 %collective-permute-start.17 = (bf16[128,5120]{1,0:T(8,128)(2,1)S(1)}, bf16[128,5120]{1,0:T(8,128)(2,1)}, u32[]{:S(2)}, u32[]{:S(2)}) collective-permute-start(bf16[128,5120]{1,0:T(8,128)(2,1)S(1)} %assemble.10.refs_0_), channel_id=1, source_target_pairs={{0,1},{1,0},{2,3},{3,2},{4,5},{5,4},{6,7},{7,6},{8,9},{9,8},{10,11... | collective-permute-start | bytes 3932168 | tf_op jit(solution)/shard_map/ppermute | solution.py:561
  100.3 56.1 %collective-permute-start.18 = (bf16[128,5120]{1,0:T(8,128)(2,1)}, bf16[128,5120]{1,0:T(8,128)(2,1)}, u32[]{:S(2)}, u32[]{:S(2)}) collective-permute-start(bf16[128,5120]{1,0:T(8,128)(2,1)} %collective-permute-done.16.refs_1_), channel_id=1, source_target_pairs={{0,1},{1,0},{2,3},{3,2},{4,5},{5,4},{6,7},{7,6},{8,9},{9,8},{10,11... | collective-permute-start | bytes 3932168 | tf_op jit(solution)/shard_map/ppermute | solution.py:561
  160.9 53.0 %collective-permute-start.19 = (bf16[512,5120]{1,0:T(8,128)(2,1)}, bf16[512,5120]{1,0:T(8,128)(2,1)}, u32[]{:S(2)}, u32[]{:S(2)}) collective-permute-start(bf16[512,5120]{1,0:T(8,128)(2,1)} %assemble.12.refs_0_), channel_id=1, source_target_pairs={{0,2},{2,0},{1,3},{3,1},{4,6},{6,4},{5,7},{7,5},{8,10},{10,8},{9,1... | collective-permute-start | bytes 15728648 | tf_op jit(solution)/shard_map/ppermute | solution.py:561
  161.0 46.6 %collective-permute-start.20 = (bf16[584,1024]{1,0:T(8,128)(2,1)}, bf16[584,1024]{1,0:T(8,128)(2,1)}, u32[]{:S(2)}, u32[]{:S(2)}) collective-permute-start(bf16[584,1024]{1,0:T(8,128)(2,1)} %param.17), channel_id=1, source_target_pairs={{0,1},{1,0},{2,3},{3,2},{4,5},{5,4},{6,7},{7,6},{8,9},{9,8},{10,11... | collective-permute-start | bytes 3588104 | tf_op jit(solution)/shard_map/ppermute | solution.py:561
  162.5 21.3 %collective-permute-start.21 = (bf16[256,1024]{1,0:T(8,128)(2,1)S(1)}, bf16[256,1024]{1,0:T(8,128)(2,1)S(1)}, u32[]{:S(2)}, u32[]{:S(2)}) collective-permute-start(bf16[256,1024]{1,0:T(8,128)(2,1)S(1)} %assemble.11.refs_0_), channel_id=1, source_target_pairs={{0,8},{8,16},{16,24},{24,0},{1,9},{9,17},{17,25},{25,1},{2,10},{10... | collective-permute-start | bytes 1572872 | tf_op jit(solution)/shard_map/ppermute | solution.py:572
  170.8 35.0 %collective-permute-start.22 = (bf16[256,1024]{1,0:T(8,128)(2,1)S(1)}, bf16[256,1024]{1,0:T(8,128)(2,1)S(1)}, u32[]{:S(2)}, u32[]{:S(2)}) collective-permute-start(bf16[256,1024]{1,0:T(8,128)(2,1)S(1)} %assemble.11.refs_0_), channel_id=1, source_target_pairs={{0,16},{8,24},{16,0},{24,8},{1,17},{9,25},{17,1},{25,9},{2,18},{10... | collective-permute-start | bytes 1572872 | tf_op jit(solution)/shard_map/ppermute | solution.py:572
  171.5 34.3 %collective-permute-start.23 = (bf16[256,1024]{1,0:T(8,128)(2,1)S(1)}, bf16[256,1024]{1,0:T(8,128)(2,1)S(1)}, u32[]{:S(2)}, u32[]{:S(2)}) collective-permute-start(bf16[256,1024]{1,0:T(8,128)(2,1)S(1)} %assemble.11.refs_0_), channel_id=1, source_target_pairs={{0,24},{8,0},{16,8},{24,16},{1,25},{9,1},{17,9},{25,17},{2,26},{10... | collective-permute-start | bytes 1572872 | tf_op jit(solution)/shard_map/ppermute | solution.py:572
  206.7 59.0 %collective-permute-start.24 = (bf16[1024,1024]{1,0:T(8,128)(2,1)S(1)}, bf16[1024,1024]{1,0:T(8,128)(2,1)}, u32[]{:S(2)}, u32[]{:S(2)}) collective-permute-start(bf16[1024,1024]{1,0:T(8,128)(2,1)S(1)} %assemble.14.refs_0_), channel_id=1, source_target_pairs={{0,4},{4,0},{1,5},{5,1},{2,6},{6,2},{3,7},{7,3},{8,12},{12,8},{9,1... | collective-permute-start | bytes 6291464 | tf_op jit(solution)/shard_map/ppermute | solution.py:561
  265.7 34.7 %collective-permute-start.28 = (bf16[2048,1024]{1,0:T(8,128)(2,1)}, bf16[2048,1024]{1,0:T(8,128)(2,1)}, u32[]{:S(2)}, u32[]{:S(2)}) collective-permute-start(bf16[2048,1024]{1,0:T(8,128)(2,1)} %get-tuple-element.146), channel_id=1, source_target_pairs={{0,2},{2,0},{1,3},{3,1},{4,6},{6,4},{5,7},{7,5},{8,10},{10,8},{9,1... | collective-permute-start | bytes 12582920 | tf_op jit(solution)/shard_map/ppermute | solution.py:561
  299.6 63.8 %collective-permute-start.27 = (bf16[592,1024]{1,0:T(8,128)(2,1)}, bf16[592,1024]{1,0:T(8,128)(2,1)}, u32[]{:S(2)}, u32[]{:S(2)}) collective-permute-start(bf16[592,1024]{1,0:T(8,128)(2,1)} %fusion.24), channel_id=1, source_target_pairs={{0,1},{1,0},{2,3},{3,2},{4,5},{5,4},{6,7},{7,6},{8,9},{9,8},{10,11... | collective-permute-start | bytes 3637256 | tf_op jit(solution)/shard_map/ppermute | solution.py:561
  343.0 52.8 %collective-permute-start.29 = (bf16[512,4096]{1,0:T(8,128)(2,1)}, bf16[512,4096]{1,0:T(8,128)(2,1)}, u32[]{:S(2)}, u32[]{:S(2)}) collective-permute-start(bf16[512,4096]{1,0:T(8,128)(2,1)} %get-tuple-element.144), channel_id=1, source_target_pairs={{0,2},{2,0},{1,3},{3,1},{4,6},{6,4},{5,7},{7,5},{8,10},{10,8},{9,1... | collective-permute-start | bytes 12582920 | tf_op jit(solution)/shard_map/ppermute | solution.py:561
  343.1 48.8 %collective-permute-start.31 = (bf16[1024,1024]{1,0:T(8,128)(2,1)}, bf16[1024,1024]{1,0:T(8,128)(2,1)}, u32[]{:S(2)}, u32[]{:S(2)}) collective-permute-start(bf16[1024,1024]{1,0:T(8,128)(2,1)} %get-tuple-element.152), channel_id=1, source_target_pairs={{0,4},{4,0},{1,5},{5,1},{2,6},{6,2},{3,7},{7,3},{8,12},{12,8},{9,1... | collective-permute-start | bytes 6291464 | tf_op jit(solution)/shard_map/ppermute | solution.py:561
  371.1 62.4 %collective-permute-start.32 = (bf16[256,1024]{1,0:T(8,128)(2,1)S(1)}, bf16[256,1024]{1,0:T(8,128)(2,1)S(1)}, u32[]{:S(2)}, u32[]{:S(2)}) collective-permute-start(bf16[256,1024]{1,0:T(8,128)(2,1)S(1)} %get-tuple-element.166), channel_id=1, source_target_pairs={{0,4},{4,0},{1,5},{5,1},{2,6},{6,2},{3,7},{7,3},{8,12},{12,8},{9,1... | collective-permute-start | bytes 1572872 | tf_op jit(solution)/shard_map/ppermute | solution.py:561
  403.6 48.5 %collective-permute-start.33 = (bf16[256,4096]{1,0:T(8,128)(2,1)}, bf16[256,4096]{1,0:T(8,128)(2,1)}, u32[]{:S(2)}, u32[]{:S(2)}) collective-permute-start(bf16[256,4096]{1,0:T(8,128)(2,1)} %bitcast.58), channel_id=1, source_target_pairs={{0,1},{1,0},{2,3},{3,2},{4,5},{5,4},{6,7},{7,6},{8,9},{9,8},{10,11... | collective-permute-start | bytes 6291464 | tf_op jit(solution)/shard_map/ppermute | solution.py:561
  435.5 35.9 %collective-permute-start.35 = (bf16[256,1024]{1,0:T(8,128)(2,1)}, bf16[256,1024]{1,0:T(8,128)(2,1)}, u32[]{:S(2)}, u32[]{:S(2)}) collective-permute-start(bf16[256,1024]{1,0:T(8,128)(2,1)} %get-tuple-element.158), channel_id=1, source_target_pairs={{0,8},{8,16},{16,24},{24,0},{1,9},{9,17},{17,25},{25,1},{2,10},{10... | collective-permute-start | bytes 1572872 | tf_op jit(solution)/shard_map/ppermute | solution.py:621
  447.2 35.5 %collective-permute-start.36 = (bf16[256,1024]{1,0:T(8,128)(2,1)}, bf16[256,1024]{1,0:T(8,128)(2,1)}, u32[]{:S(2)}, u32[]{:S(2)}) collective-permute-start(bf16[256,1024]{1,0:T(8,128)(2,1)} %get-tuple-element.160), channel_id=1, source_target_pairs={{0,16},{8,24},{16,0},{24,8},{1,17},{9,25},{17,1},{25,9},{2,18},{10... | collective-permute-start | bytes 1572872 | tf_op jit(solution)/shard_map/ppermute | solution.py:621
  449.1 33.6 %collective-permute-start.37 = (bf16[256,1024]{1,0:T(8,128)(2,1)}, bf16[256,1024]{1,0:T(8,128)(2,1)}, u32[]{:S(2)}, u32[]{:S(2)}) collective-permute-start(bf16[256,1024]{1,0:T(8,128)(2,1)} %get-tuple-element.159), channel_id=1, source_target_pairs={{0,24},{8,0},{16,8},{24,16},{1,25},{9,1},{17,9},{25,17},{2,26},{10... | collective-permute-start | bytes 1572872 | tf_op jit(solution)/shard_map/ppermute | solution.py:621
  449.6 39.9 %collective-permute-start.51 = (bf16[128,1024]{1,0:T(8,128)(2,1)}, bf16[128,1024]{1,0:T(8,128)(2,1)}, u32[]{:S(2)}, u32[]{:S(2)}) collective-permute-start(bf16[128,1024]{1,0:T(8,128)(2,1)} %get-tuple-element.173), channel_id=1, source_target_pairs={{0,1},{1,0},{2,3},{3,2},{4,5},{5,4},{6,7},{7,6},{8,9},{9,8},{10,11... | collective-permute-start | bytes 786440 | tf_op jit(solution)/shard_map/ppermute | solution.py:561
  465.1 63.1 %collective-permute-start.34 = (bf16[512,3072]{1,0:T(8,128)(2,1)}, bf16[512,3072]{1,0:T(8,128)(2,1)}, u32[]{:S(2)}, u32[]{:S(2)}) collective-permute-start(bf16[512,3072]{1,0:T(8,128)(2,1)} %get-tuple-element.148), channel_id=1, source_target_pairs={{0,2},{2,0},{1,3},{3,1},{4,6},{6,4},{5,7},{7,5},{8,10},{10,8},{9,1... | collective-permute-start | bytes 9437192 | tf_op jit(solution)/shard_map/ppermute | solution.py:561
  486.5 49.1 %collective-permute-start.40 = (bf16[128,4096]{1,0:T(8,128)(2,1)}, bf16[128,4096]{1,0:T(8,128)(2,1)}, u32[]{:S(2)}, u32[]{:S(2)}) collective-permute-start(bf16[128,4096]{1,0:T(8,128)(2,1)} %get-tuple-element.156), channel_id=1, source_target_pairs={{0,4},{4,0},{1,5},{5,1},{2,6},{6,2},{3,7},{7,3},{8,12},{12,8},{9,1... | collective-permute-start | bytes 3145736 | tf_op jit(solution)/shard_map/ppermute | solution.py:561
  488.0 100.6 %collective-permute-start.58 = (bf16[128,1024]{1,0:T(8,128)(2,1)}, bf16[128,1024]{1,0:T(8,128)(2,1)}, u32[]{:S(2)}, u32[]{:S(2)}) collective-permute-start(bf16[128,1024]{1,0:T(8,128)(2,1)} %get-tuple-element.171), channel_id=1, source_target_pairs={{0,1},{1,0},{2,3},{3,2},{4,5},{5,4},{6,7},{7,6},{8,9},{9,8},{10,11... | collective-permute-start | bytes 786440 | tf_op jit(solution)/shard_map/ppermute | solution.py:561
  489.5 23.0 %collective-permute-start.46 = (f32[8,384]{1,0:T(8,128)S(1)}, f32[8,384]{1,0:T(8,128)S(1)}, u32[]{:S(2)}, u32[]{:S(2)}) collective-permute-start(f32[8,384]{1,0:T(8,128)S(1)} %fusion.47), channel_id=1, source_target_pairs={{0,4},{4,0},{1,5},{5,1},{2,6},{6,2},{3,7},{7,3},{8,12},{12,8},{9,1... | collective-permute-start | bytes 36872 | tf_op jit(solution)/shard_map/ppermute | solution.py:561
  512.6 14.9 %collective-permute-start.47 = (f32[4,384]{1,0:T(4,128)S(1)}, f32[4,384]{1,0:T(4,128)S(1)}, u32[]{:S(2)}, u32[]{:S(2)}) collective-permute-start(f32[4,384]{1,0:T(4,128)S(1)} %fusion.50), channel_id=1, source_target_pairs={{0,1},{1,0},{2,3},{3,2},{4,5},{5,4},{6,7},{7,6},{8,9},{9,8},{10,11... | collective-permute-start | bytes 18440 | tf_op jit(solution)/shard_map/ppermute | solution.py:561
  515.7 91.5 %collective-permute-start.52 = (bf16[32,1024]{1,0:T(8,128)(2,1)}, bf16[32,1024]{1,0:T(8,128)(2,1)S(1)}, u32[]{:S(2)}, u32[]{:S(2)}) collective-permute-start(bf16[32,1024]{1,0:T(8,128)(2,1)} %get-tuple-element.175), channel_id=1, source_target_pairs={{0,8},{8,16},{16,24},{24,0},{1,9},{9,17},{17,25},{25,1},{2,10},{10... | collective-permute-start | bytes 196616 | tf_op jit(solution)/shard_map/ppermute | solution.py:621
  527.5 43.4 %collective-permute-start.48 = (f32[1,384]{1,0:T(1,128)S(1)}, f32[1,384]{1,0:T(1,128)S(1)}, u32[]{:S(2)}, u32[]{:S(2)}) collective-permute-start(f32[1,384]{1,0:T(1,128)S(1)} %get-tuple-element.188), channel_id=1, source_target_pairs={{0,8},{8,16},{16,24},{24,0},{1,9},{9,17},{17,25},{25,1},{2,10},{10... | collective-permute-start | bytes 4616 | tf_op jit(solution)/shard_map/ppermute | solution.py:621
  531.5 35.1 %collective-permute-start.39 = (bf16[256,3072]{1,0:T(8,128)(2,1)S(1)}, bf16[256,3072]{1,0:T(8,128)(2,1)S(1)}, u32[]{:S(2)}, u32[]{:S(2)}) collective-permute-start(bf16[256,3072]{1,0:T(8,128)(2,1)S(1)} %get-tuple-element.154), channel_id=1, source_target_pairs={{0,4},{4,0},{1,5},{5,1},{2,6},{6,2},{3,7},{7,3},{8,12},{12,8},{9,1... | collective-permute-start | bytes 4718600 | tf_op jit(solution)/shard_map/ppermute | solution.py:561
  535.6 35.8 %collective-permute-start.49 = (f32[1,384]{1,0:T(1,128)S(1)}, f32[1,384]{1,0:T(1,128)S(1)}, u32[]{:S(2)}, u32[]{:S(2)}) collective-permute-start(f32[1,384]{1,0:T(1,128)S(1)} %get-tuple-element.190), channel_id=1, source_target_pairs={{0,16},{8,24},{16,0},{24,8},{1,17},{9,25},{17,1},{25,9},{2,18},{10... | collective-permute-start | bytes 4616 | tf_op jit(solution)/shard_map/ppermute | solution.py:621
  570.8 17.3 %collective-permute-start.41 = (bf16[128,3072]{1,0:T(8,128)(2,1)S(1)}, bf16[128,3072]{1,0:T(8,128)(2,1)S(1)}, u32[]{:S(2)}, u32[]{:S(2)}) collective-permute-start(bf16[128,3072]{1,0:T(8,128)(2,1)S(1)} %dynamic-slice_bitcast_fusion.13), channel_id=1, source_target_pairs={{0,1},{1,0},{2,3},{3,2},{4,5},{5,4},{6,7},{7,6},{8,9},{9,8},{10,11... | collective-permute-start | bytes 2359304 | tf_op jit(solution)/shard_map/ppermute | solution.py:561
  572.6 16.1 %collective-permute-start.55 = (bf16[32,4096]{1,0:T(8,128)(2,1)S(1)}, bf16[32,4096]{1,0:T(8,128)(2,1)S(1)}, u32[]{:S(2)}, u32[]{:S(2)}) collective-permute-start(bf16[32,4096]{1,0:T(8,128)(2,1)S(1)} %get-tuple-element.162), channel_id=1, source_target_pairs={{0,8},{8,16},{16,24},{24,0},{1,9},{9,17},{17,25},{25,1},{2,10},{10... | collective-permute-start | bytes 786440 | tf_op jit(solution)/shard_map/ppermute | solution.py:621
  572.6 20.2 %collective-permute-start.56 = (bf16[32,4096]{1,0:T(8,128)(2,1)S(1)}, bf16[32,4096]{1,0:T(8,128)(2,1)S(1)}, u32[]{:S(2)}, u32[]{:S(2)}) collective-permute-start(bf16[32,4096]{1,0:T(8,128)(2,1)S(1)} %get-tuple-element.164), channel_id=1, source_target_pairs={{0,16},{8,24},{16,0},{24,8},{1,17},{9,25},{17,1},{25,9},{2,18},{10... | collective-permute-start | bytes 786440 | tf_op jit(solution)/shard_map/ppermute | solution.py:621
  588.6 18.6 %collective-permute-start.53 = (bf16[32,1024]{1,0:T(8,128)(2,1)}, bf16[32,1024]{1,0:T(8,128)(2,1)}, u32[]{:S(2)}, u32[]{:S(2)}) collective-permute-start(bf16[32,1024]{1,0:T(8,128)(2,1)} %get-tuple-element.177), channel_id=1, source_target_pairs={{0,16},{8,24},{16,0},{24,8},{1,17},{9,25},{17,1},{25,9},{2,18},{10... | collective-permute-start | bytes 196616 | tf_op jit(solution)/shard_map/ppermute | solution.py:621
  588.7 18.5 %collective-permute-start.54 = (bf16[32,1024]{1,0:T(8,128)(2,1)S(1)}, bf16[32,1024]{1,0:T(8,128)(2,1)}, u32[]{:S(2)}, u32[]{:S(2)}) collective-permute-start(bf16[32,1024]{1,0:T(8,128)(2,1)S(1)} %get-tuple-element.176), channel_id=1, source_target_pairs={{0,24},{8,0},{16,8},{24,16},{1,25},{9,1},{17,9},{25,17},{2,26},{10... | collective-permute-start | bytes 196616 | tf_op jit(solution)/shard_map/ppermute | solution.py:621
  592.8 30.4 %collective-permute-start.38 = (bf16[592,1024]{1,0:T(8,128)(2,1)}, bf16[592,1024]{1,0:T(8,128)(2,1)}, u32[]{:S(2)}, u32[]{:S(2)}) collective-permute-start(bf16[592,1024]{1,0:T(8,128)(2,1)} %fusion.25), channel_id=1, source_target_pairs={{0,1},{1,0},{2,3},{3,2},{4,5},{5,4},{6,7},{7,6},{8,9},{9,8},{10,11... | collective-permute-start | bytes 3637256 | tf_op jit(solution)/shard_map/ppermute | solution.py:561
  608.8 14.3 %collective-permute-start.43 = (bf16[32,3072]{1,0:T(8,128)(2,1)S(1)}, bf16[32,3072]{1,0:T(8,128)(2,1)S(1)}, u32[]{:S(2)}, u32[]{:S(2)}) collective-permute-start(bf16[32,3072]{1,0:T(8,128)(2,1)S(1)} %get-tuple-element.170), channel_id=1, source_target_pairs={{0,16},{8,24},{16,0},{24,8},{1,17},{9,25},{17,1},{25,9},{2,18},{10... | collective-permute-start | bytes 589832 | tf_op jit(solution)/shard_map/ppermute | solution.py:621
  (68 other events, 1075.7 us)

commit v5 on v4

--- a/solution.py
+++ b/solution.py
@@ -1,3 +1,4 @@
+import functools
 import math
 
 import jax
@@ -315,10 +316,29 @@
 IMAGES = 2
 PAIR = 2 * HD
 CHUNK = 256
+BLOCK = 512
+HINT = pl.CostEstimate(flops=1, bytes_accessed=1, transcendentals=0)
+ERFC = (
+    0.09873409569263458,
+    0.09871950000524521,
+    0.09271052479743958,
+    0.08134904503822327,
+    0.056456614285707474,
+    0.07422702759504318,
+    -0.050631966441869736,
+    0.11820460855960846,
+    -0.09110676497220993,
+    0.021337319165468216,
+)
+ERFC_STEP = 0.35
 
 
 def round_up(count, unit):
     return -(-count // unit) * unit
+
+
+def limit(mebibytes):
+    return pltpu.CompilerParams(vmem_limit_bytes=mebibytes * 2**20)
 
 
 def chunks_of(count):
@@ -331,20 +351,26 @@
     )
 
 
+def tn_dot(left, right):
+    return lax.dot_general(
+        left, right, (((0,), (0,)), ((), ())), preferred_element_type=jnp.float32
+    )
+
+
 def half_mask(rows):
     return lax.broadcasted_iota(jnp.int32, (rows, PAIR), 1) < HD
 
 
 def forward_kernel(query_ref, key_ref, value_ref, bias_ref, attended_ref, log_ref):
-    rows = query_ref.shape[0]
+    rows = query_ref.shape[1]
     first = half_mask(rows)
     zero = jnp.zeros((rows, PAIR), jnp.bfloat16)
-    key = key_ref[...]
+    key = key_ref[0]
     key_sides = (jnp.where(first, key, zero), jnp.where(first, zero, key))
-    value_t = value_ref[...].astype(jnp.float32).T.astype(jnp.bfloat16)
+    value_t = value_ref[0].astype(jnp.float32).T.astype(jnp.bfloat16)
     scale = jnp.bfloat16(1.0 / math.sqrt(HD))
     for start, size in chunks_of(rows):
-        query = query_ref[start : start + size, :] * scale
+        query = query_ref[0, start : start + size, :] * scale
         bias = bias_ref[:, start : start + size]
         outs = []
         for side in range(2):
@@ -360,19 +386,19 @@
 
 
 def backward_kernel(
-    query_ref, key_ref, value_ref, d_ref, log_ref, bias_ref, dq_ref, dk_ref, dv_ref, dk_sum, dv_sum
+    query_ref, key_ref, value_ref, d_ref, log_ref, bias_ref, joined_ref, dk_sum, dv_sum
 ):
-    rows = query_ref.shape[0]
+    rows = query_ref.shape[1]
     first = half_mask(rows)
     zero = jnp.zeros((rows, PAIR), jnp.bfloat16)
-    key = key_ref[...]
-    value = value_ref[...]
+    key = key_ref[0]
+    value = value_ref[0]
     key_sides = (jnp.where(first, key, zero), jnp.where(first, zero, key))
     value_sides = (jnp.where(first, value, zero), jnp.where(first, zero, value))
     key_t = key.astype(jnp.float32).T.astype(jnp.bfloat16)
     scale = jnp.bfloat16(1.0 / math.sqrt(HD))
     for start, size in chunks_of(rows):
-        query = query_ref[start : start + size, :] * scale
+        query = query_ref[0, start : start + size, :] * scale
         d_rows = d_ref[start : start + size, :]
         bias = bias_ref[:, start : start + size]
         outs = []
@@ -393,24 +419,23 @@
                 dk_sum[side] += d_key
             outs.append(matmul(key_t[side * HD : (side + 1) * HD, :], d_scores))
         d_query = jnp.concatenate(outs, axis=0) * (1.0 / math.sqrt(HD))
-        dq_ref[start : start + size, :] = d_query.T.astype(jnp.bfloat16)
-    dk_ref[...] = jnp.where(first, dk_sum[0], dk_sum[1]).astype(jnp.bfloat16)
-    dv_ref[...] = jnp.where(first, dv_sum[0], dv_sum[1]).astype(jnp.bfloat16)
+        joined_ref[0, start : start + size, :] = d_query.T.astype(jnp.bfloat16)
+    joined_ref[1] = jnp.where(first, dk_sum[0], dk_sum[1]).astype(jnp.bfloat16)
+    joined_ref[2] = jnp.where(first, dv_sum[0], dv_sum[1]).astype(jnp.bfloat16)
+
+
+def pair_spec(rows, part):
+    return pl.BlockSpec((1, rows, PAIR), lambda i: (part, 0, i))
 
 
 def attention_forward(joined, bias):
-    rows, width = joined.shape[0], joined.shape[1] // 3
+    rows, width = joined.shape[1:]
     pairs = width // PAIR
-    flops = 4 * rows * rows * width
     return pl.pallas_call(
         forward_kernel,
         grid=(pairs,),
-        in_specs=[
-            pl.BlockSpec((rows, PAIR), lambda i: (0, i)),
-            pl.BlockSpec((rows, PAIR), lambda i: (0, pairs + i)),
-            pl.BlockSpec((rows, PAIR), lambda i: (0, 2 * pairs + i)),
-            pl.BlockSpec((rows, rows), lambda i: (0, 0)),
-        ],
+        in_specs=[pair_spec(rows, part) for part in range(3)]
+        + [pl.BlockSpec((rows, rows), lambda i: (0, 0))],
         out_specs=[
             pl.BlockSpec((rows, PAIR), lambda i: (0, i)),
             pl.BlockSpec((1, 2, rows), lambda i: (i, 0, 0)),
@@ -419,39 +444,234 @@
             jax.ShapeDtypeStruct((rows, width), jnp.bfloat16),
             jax.ShapeDtypeStruct((pairs, 2, rows), jnp.float32),
         ],
-        compiler_params=pltpu.CompilerParams(vmem_limit_bytes=40 * 2**20),
-        cost_estimate=pl.CostEstimate(
-            flops=4 * flops, bytes_accessed=8 * rows * width, transcendentals=rows * rows * 16
-        ),
+        compiler_params=limit(32),
+        cost_estimate=HINT,
         name="attention_forward",
     )(joined, joined, joined, bias)
 
 
-def attention_backward(joined, d_attended, log_total, bias):
-    rows, width = d_attended.shape
-    pairs = width // PAIR
-    flops = 10 * rows * rows * width
-    block = jax.ShapeDtypeStruct((rows, width), jnp.bfloat16)
+def attention_backward(joined, d_attended, first_pair, log_total, bias):
+    rows, width = joined.shape[1:]
     return pl.pallas_call(
         backward_kernel,
-        grid=(pairs,),
-        in_specs=[
-            pl.BlockSpec((rows, PAIR), lambda i: (0, i)),
-            pl.BlockSpec((rows, PAIR), lambda i: (0, pairs + i)),
-            pl.BlockSpec((rows, PAIR), lambda i: (0, 2 * pairs + i)),
-            pl.BlockSpec((rows, PAIR), lambda i: (0, i)),
+        grid=(width // PAIR,),
+        in_specs=[pair_spec(rows, part) for part in range(3)]
+        + [
+            pl.BlockSpec((rows, PAIR), lambda i: (0, first_pair + i)),
             pl.BlockSpec((1, 2, rows), lambda i: (i, 0, 0)),
             pl.BlockSpec((rows, rows), lambda i: (0, 0)),
         ],
-        out_specs=[pl.BlockSpec((rows, PAIR), lambda i: (0, i))] * 3,
-        out_shape=[block] * 3,
+        out_specs=pl.BlockSpec((3, rows, PAIR), lambda i: (0, 0, i)),
+        out_shape=jax.ShapeDtypeStruct((3, rows, width), jnp.bfloat16),
         scratch_shapes=[pltpu.VMEM((2, rows, PAIR), jnp.float32)] * 2,
-        compiler_params=pltpu.CompilerParams(vmem_limit_bytes=40 * 2**20),
-        cost_estimate=pl.CostEstimate(
-            flops=4 * flops, bytes_accessed=14 * rows * width, transcendentals=rows * rows * 16
-        ),
+        compiler_params=limit(32),
+        cost_estimate=HINT,
         name="attention_backward",
     )(joined, joined, joined, d_attended, log_total, bias)
+
+
+def whole_spec(shape):
+    return pl.BlockSpec(shape, lambda *_: (0,) * len(shape))
+
+
+def project_kernel(x_ref, weight_ref, bias_ref, out_ref):
+    out_ref[0] = (matmul(x_ref[...], weight_ref[...]) + bias_ref[...]).astype(out_ref.dtype)
+
+
+def project(x, weight, bias):
+    rows, depth = x.shape
+    width = weight.shape[1] // 3
+    return pl.pallas_call(
+        project_kernel,
+        grid=(3,),
+        in_specs=[
+            whole_spec(x.shape),
+            pl.BlockSpec((depth, width), lambda i: (0, i)),
+            pl.BlockSpec((1, width), lambda i: (0, i)),
+        ],
+        out_specs=pl.BlockSpec((1, rows, width), lambda i: (i, 0, 0)),
+        out_shape=jax.ShapeDtypeStruct((3, rows, width), jnp.bfloat16),
+        compiler_params=limit(24),
+        cost_estimate=HINT,
+        name="project",
+    )(x, weight, bias[None, :])
+
+
+def hidden_kernel(x_ref, weight_ref, bias_ref, active_ref, slope_ref):
+    hidden = matmul(x_ref[...], weight_ref[...]) + bias_ref[...]
+    share = 1.0 / (1.0 + (ERFC_STEP * math.sqrt(0.5)) * jnp.abs(hidden))
+    density = jnp.exp(-0.5 * hidden * hidden)
+    tail = jnp.full_like(share, ERFC[-1])
+    for factor in ERFC[-2::-1]:
+        tail = tail * share + factor
+    tail = tail * share * density
+    phi = jnp.where(hidden < 0.0, tail, 1.0 - tail)
+    active_ref[...] = (hidden * phi).astype(jnp.bfloat16)
+    slope = phi + hidden * density * (1.0 / math.sqrt(2.0 * math.pi))
+    slope_ref[...] = slope.astype(jnp.bfloat16)
+
+
+def hidden_layer(x, weight, bias):
+    rows, depth = x.shape
+    width = weight.shape[1]
+    block = pl.BlockSpec((rows, BLOCK), lambda i: (0, i))
+    return pl.pallas_call(
+        hidden_kernel,
+        grid=(width // BLOCK,),
+        in_specs=[
+            whole_spec(x.shape),
+            pl.BlockSpec((depth, BLOCK), lambda i: (0, i)),
+            pl.BlockSpec((1, BLOCK), lambda i: (0, i)),
+        ],
+        out_specs=[block, block],
+        out_shape=[jax.ShapeDtypeStruct((rows, width), jnp.bfloat16)] * 2,
+        compiler_params=limit(32),
+        cost_estimate=HINT,
+        name="hidden_layer",
+    )(x, weight, bias[None, :])
+
+
+def last_kernel(active_ref, weight_ref, middle_ref, bias_ref, out_ref, total):
+    step = pl.program_id(0)
+
+    @pl.when(step == 0)
+    def _():
+        total[...] = middle_ref[...] + bias_ref[...]
+
+    total[...] += matmul(active_ref[...], weight_ref[...])
+
+    @pl.when(step == pl.num_programs(0) - 1)
+    def _():
+        out_ref[...] = total[...].astype(out_ref.dtype)
+
+
+def last_layer(active, weight, middle, bias):
+    rows, depth = active.shape
+    width = weight.shape[1]
+    return pl.pallas_call(
+        last_kernel,
+        grid=(depth // BLOCK,),
+        in_specs=[
+            pl.BlockSpec((rows, BLOCK), lambda i: (0, i)),
+            pl.BlockSpec((BLOCK, width), lambda i: (i, 0)),
+            whole_spec((rows, width)),
+            whole_spec((1, width)),
+        ],
+        out_specs=whole_spec((rows, width)),
+        out_shape=jax.ShapeDtypeStruct((rows, width), jnp.bfloat16),
+        scratch_shapes=[pltpu.VMEM((rows, width), jnp.float32)],
+        compiler_params=limit(24),
+        cost_estimate=HINT,
+        name="last_layer",
+    )(active, weight, middle, bias[None, :])
+
+
+def d_hidden_kernel(d_ref, weight_ref, slope_ref, out_ref, sum_ref):
+    d_active = nt_dot(d_ref[...], weight_ref[...])
+    d_hidden = (d_active * slope_ref[...].astype(jnp.float32)).astype(jnp.bfloat16)
+    out_ref[...] = d_hidden
+    sum_ref[...] = jnp.sum(d_hidden.astype(jnp.float32), axis=0, keepdims=True)
+
+
+def d_hidden_layer(d_out, weight, slope):
+    rows, depth = d_out.shape
+    width = weight.shape[0]
+    block = pl.BlockSpec((rows, BLOCK), lambda i: (0, i))
+    return pl.pallas_call(
+        d_hidden_kernel,
+        grid=(width // BLOCK,),
+        in_specs=[
+            whole_spec(d_out.shape),
+            pl.BlockSpec((BLOCK, depth), lambda i: (i, 0)),
+            block,
+        ],
+        out_specs=[block, pl.BlockSpec((1, BLOCK), lambda i: (0, i))],
+        out_shape=[
+            jax.ShapeDtypeStruct((rows, width), jnp.bfloat16),
+            jax.ShapeDtypeStruct((1, width), jnp.float32),
+        ],
+        compiler_params=limit(24),
+        cost_estimate=HINT,
+        name="d_hidden_layer",
+    )(d_out, weight, slope)
+
+
+def d_normed_kernel(d_ref, weight_ref, *refs):
+    out_ref = refs[-1]
+    d_rows = d_ref[0] if len(d_ref.shape) == 3 else d_ref[...]
+    product = nt_dot(d_rows, weight_ref[...])
+    step = pl.program_id(0)
+
+    @pl.when(step == 0)
+    def _():
+        out_ref[...] = product + refs[0][...] if len(refs) == 2 else product
+
+    @pl.when(step > 0)
+    def _():
+        out_ref[...] += product
+
+
+def d_normed(d_rows, weight, base=None):
+    rows, depth = d_rows.shape[-2], weight.shape[0]
+    if d_rows.ndim == 3:
+        d_spec = pl.BlockSpec((1, rows, BLOCK), lambda i: (i, 0, 0))
+    else:
+        d_spec = pl.BlockSpec((rows, BLOCK), lambda i: (0, i))
+    extra = [] if base is None else [base]
+    return pl.pallas_call(
+        d_normed_kernel,
+        grid=(weight.shape[1] // BLOCK,),
+        in_specs=[d_spec, pl.BlockSpec((depth, BLOCK), lambda i: (0, i))]
+        + [whole_spec((rows, depth)) for _ in extra],
+        out_specs=whole_spec((rows, depth)),
+        out_shape=jax.ShapeDtypeStruct((rows, depth), jnp.float32),
+        compiler_params=limit(24),
+        cost_estimate=HINT,
+        name="d_normed",
+    )(d_rows, weight, *extra)
+
+
+def gradient_kernel(index_ref, x_ref, d_ref, *refs):
+    out_ref = refs[-1]
+    x = x_ref[...]
+    width = d_ref.shape[-1]
+    for part in range(out_ref.shape[1] // width):
+        columns = slice(part * width, (part + 1) * width)
+        product = tn_dot(x, d_ref[part] if len(d_ref.shape) == 3 else d_ref[...])
+        if len(refs) == 2:
+            product = product + refs[0][:, columns].astype(jnp.float32)
+        out_ref[:, columns] = product.astype(out_ref.dtype)
+
+
+def gradient(x, d_rows, half, column=0, columns=1, got=None):
+    rows, depth = x.shape
+    size = depth // 2
+    blocks = size // CHUNK
+    if d_rows.ndim == 3:
+        d_spec = pl.BlockSpec(d_rows.shape, lambda i, index: (0, 0, 0))
+        width = d_rows.shape[0] * d_rows.shape[2]
+    else:
+        width = d_rows.shape[1] // columns
+        d_spec = pl.BlockSpec((rows, width), lambda i, index: (0, column))
+    block = pl.BlockSpec((CHUNK, width), lambda i, index: (i, 0))
+    extra = [] if got is None else [got]
+    return pl.pallas_call(
+        gradient_kernel,
+        grid_spec=pltpu.PrefetchScalarGridSpec(
+            num_scalar_prefetch=1,
+            grid=(blocks,),
+            in_specs=[
+                pl.BlockSpec((rows, CHUNK), lambda i, index: (0, index[0] * blocks + i)),
+                d_spec,
+            ]
+            + [block for _ in extra],
+            out_specs=block,
+        ),
+        out_shape=jax.ShapeDtypeStruct((size, width), jnp.bfloat16),
+        compiler_params=limit(32),
+        cost_estimate=HINT,
+        name="gradient",
+    )(half.reshape(1).astype(jnp.int32), x, d_rows, *extra)
 
 
 def standardize(value):
@@ -461,124 +681,114 @@
     return center * scale, scale
 
 
-def norm_backward(d_normed, normal, scale, gain):
-    scaled = d_normed * gain
+def norm_backward(d_normed_rows, normal, scale, gain):
+    scaled = d_normed_rows * gain
     mean = jnp.mean(scaled, axis=-1, keepdims=True)
     along = jnp.mean(scaled * normal, axis=-1, keepdims=True)
     return (scaled - mean - normal * along) * scale
 
 
-def gelu_slope(value):
-    phi = 0.5 * (1.0 + lax.erf(value * math.sqrt(0.5)))
-    return phi + value * jnp.exp(-0.5 * value * value) * (1.0 / math.sqrt(2.0 * math.pi))
+def reorder(array, axis, sizes, spots):
+    shape = array.shape
+    count = math.prod(sizes)
+    cut = shape[:axis] + tuple(sizes) + (shape[axis] // count,) + shape[axis + 1 :]
+    spots = list(range(axis)) + [axis + spot for spot in spots]
+    return array.reshape(cut).transpose(spots + list(range(len(spots), len(cut)))).reshape(shape)
 
 
 def to_local(array, axis, far):
-    shape = array.shape
-    cut = shape[:axis] + (far, 2, 2, 2, shape[axis] // (8 * far)) + shape[axis + 1 :]
-    spots = [axis + 2, axis + 1, axis + 3, axis]
-    spots = list(range(axis)) + spots + list(range(axis + 4, len(cut)))
-    return array.reshape(cut).transpose(spots).reshape(shape)
+    return reorder(array, axis, (far, 2, 2, 2), (2, 1, 3, 0))
+
+
+def to_natural(array, axis, far):
+    return reorder(array, axis, (2, 2, 2, far), (3, 1, 0, 2))
 
 
 def hidden_to_local(array, axis, far):
-    shape = array.shape
-    cut = shape[:axis] + (far, 2, 2, 2, shape[axis] // (8 * far)) + shape[axis + 1 :]
-    spots = [axis + 2, axis + 1, axis, axis + 3]
-    spots = list(range(axis)) + spots + list(range(axis + 4, len(cut)))
-    return array.reshape(cut).transpose(spots).reshape(shape)
-
-
-def to_natural(array, axis, far):
-    shape = array.shape
-    cut = shape[:axis] + (2, 2, 2, far, shape[axis] // (8 * far)) + shape[axis + 1 :]
-    spots = [axis + 3, axis + 1, axis, axis + 2]
-    spots = list(range(axis)) + spots + list(range(axis + 4, len(cut)))
-    return array.reshape(cut).transpose(spots).reshape(shape)
+    return reorder(array, axis, (far, 2, 2, 2), (2, 1, 0, 3))
 
 
 def hidden_to_natural(array, axis, far):
-    shape = array.shape
-    cut = shape[:axis] + (2, 2, far, 2, shape[axis] // (8 * far)) + shape[axis + 1 :]
-    spots = [axis + 2, axis + 1, axis, axis + 3]
-    spots = list(range(axis)) + spots + list(range(axis + 4, len(cut)))
-    return array.reshape(cut).transpose(spots).reshape(shape)
-
-
-def assemble_kernel(index_ref, *refs):
-    pieces, (*wholes, stage, arrived, left) = refs[: index_ref.shape[0]], refs[index_ref.shape[0] :]
+    return reorder(array, axis, (2, 2, far, 2), (2, 1, 0, 3))
+
+
+def assemble_kernel(routes, index_ref, *refs):
+    count = len(routes)
+    pieces, stages = refs[:count], refs[-count - 2 : -2]
+    wholes, (arrived, left) = refs[count : -count - 2], refs[-2:]
     incoming = [
-        pltpu.make_async_copy(piece, stage.at[number], arrived.at[number])
-        for number, piece in enumerate(pieces)
+        pltpu.make_async_copy(piece, stage, arrived.at[number])
+        for number, (piece, stage) in enumerate(zip(pieces, stages))
     ]
     for copy in incoming:
         copy.start()
     outgoing = []
-    for number, piece in enumerate(pieces):
+    for number, route in enumerate(routes):
         incoming[number].wait()
-        size = piece.shape[0]
+        size = pieces[number].shape[0]
         start = pl.multiple_of(index_ref[number] * size, 16)
-        column = 0
-        for part, whole in enumerate(wholes):
-            width = whole.shape[1]
+        for part, (source, width, whole, target) in enumerate(route):
             copy = pltpu.make_async_copy(
-                stage.at[number, :, pl.ds(column, width)],
-                whole.at[pl.ds(start, size)],
+                stages[number].at[:, pl.ds(source, width)],
+                wholes[whole].at[pl.ds(start, size), pl.ds(target, width)],
                 left.at[part, number],
             )
             copy.start()
             outgoing.append(copy)
-            column += width
     for copy in outgoing:
         copy.wait()
 
 
-def assemble(pieces, indices, extra=0):
-    size, width = pieces[0].shape
+def assemble(pieces, indices, outs, routes=None):
+    if routes is None:
+        routes = [[(0, piece.shape[1], 0, 0)] for piece in pieces]
     count = len(pieces)
-    widths = (width - extra, extra) if extra else (width,)
     anywhere = pl.BlockSpec(memory_space=pl.ANY)
-    wholes = pl.pallas_call(
-        assemble_kernel,
+    kind = pieces[0].dtype
+    return pl.pallas_call(
+        functools.partial(assemble_kernel, routes),
         in_specs=[pl.BlockSpec(memory_space=pltpu.SMEM)] + [anywhere] * count,
-        out_specs=[anywhere] * len(widths),
-        out_shape=[jax.ShapeDtypeStruct((count * size, one), pieces[0].dtype) for one in widths],
-        scratch_shapes=[
-            pltpu.VMEM((count, size, width), pieces[0].dtype),
+        out_specs=[anywhere] * len(outs),
+        out_shape=[jax.ShapeDtypeStruct(shape, kind) for shape in outs],
+        scratch_shapes=[pltpu.VMEM(piece.shape, kind) for piece in pieces]
+        + [
             pltpu.SemaphoreType.DMA((count,)),
-            pltpu.SemaphoreType.DMA((len(widths), count)),
+            pltpu.SemaphoreType.DMA((max(len(route) for route in routes), count)),
         ],
-        compiler_params=pltpu.CompilerParams(vmem_limit_bytes=16 * 2**20),
-        cost_estimate=pl.CostEstimate(
-            flops=0, bytes_accessed=4 * count * size * width, transcendentals=0
-        ),
+        compiler_params=limit(16),
+        cost_estimate=HINT,
         name="assemble",
     )(jnp.stack(indices).astype(jnp.int32), *pieces)
-    return wholes if extra else wholes[0]
 
 
 def trade(array, axis):
     return lax.ppermute(array, axis, [(0, 1), (1, 0)])
 
 
-def after(array, other):
-    return lax.optimization_barrier((array, other))[0]
-
-
-def gather_far(shard, far):
+def after(array, *others):
+    return lax.optimization_barrier((array, *others))[0]
+
+
+def gather_far(shard, far, widths=None):
     place = lax.axis_index("z")
     pieces, indices = [shard], [place]
     for step in range(1, far):
         pieces.append(lax.ppermute(shard, "z", [(i, (i + step) % far) for i in range(far)]))
         indices.append((place - step) % far)
-    return assemble(pieces, indices)
+    rows, width = shard.shape
+    widths = widths or [width]
+    route, column = [], 0
+    for number, one in enumerate(widths):
+        route.append((column, one, number, 0))
+        column += one
+    return assemble(pieces, indices, [(far * rows, one) for one in widths], [route] * far)
 
 
 def spread(blocks, axis):
     return blocks | {key | {axis}: trade(block, axis) for key, block in blocks.items()}
 
 
-def order_blocks(blocks, axes, extra=0):
+def places(blocks, axes):
     indices = []
     for key in blocks:
         index = 0
@@ -586,14 +796,17 @@
             place = lax.axis_index(axis)
             index = 2 * index + (1 - place if axis in key else place)
         indices.append(index)
-    return assemble(list(blocks.values()), indices, extra)
-
-
-def tie_blocks(blocks, other):
-    return {key: after(block, other) for key, block in blocks.items()}
+    return indices
+
+
+def order_blocks(blocks, axes):
+    pieces = list(blocks.values())
+    rows, width = pieces[0].shape
+    return assemble(pieces, places(blocks, axes), [(len(pieces) * rows, width)])[0]
 
 
 OWN = frozenset()
+X, Y, XY = frozenset({"x"}), frozenset({"ctx"}), frozenset({"x", "ctx"})
 
 
 def send_half(matrix, axis, outer=1):
@@ -605,10 +818,9 @@
     return kept, trade(sent, axis)
 
 
-def add_half(halves, follow=None):
+def add_half(halves, *follow):
     kept, got = halves
-    if follow is not None:
-        got = after(got, follow)
+    got = after(got, *follow) if follow else got
     return (kept.astype(jnp.float32) + got.astype(jnp.float32)).astype(kept.dtype)
 
 
@@ -622,10 +834,10 @@
     return arrays
 
 
-def add_far(arrays, follow=None):
+def add_far(arrays, *follow):
     own, *got = arrays
-    if follow is not None:
-        got = [after(array, follow) for array in got]
+    if follow:
+        got = [after(array, *follow) for array in got]
     return sum(array.astype(jnp.float32) for array in [own, *got])
 
 
@@ -652,42 +864,57 @@
         w_down,
         b_down,
     ):
-        place = lax.axis_index("ctx")
+        place, core = lax.axis_index("ctx"), lax.axis_index("core")
         swap = lambda array: trade(array, "ctx")
         slots, width = inputs.shape
+        half_width = width // 2
         pads = 2 * slots - IMAGES * SEQ
         rows = round_up(SEQ + pads, 16)
         near_width = w_up.shape[0] // 8
 
+        inputs_far = swap(inputs)
         segment_far = swap(segment)
-        inputs_far = swap(inputs)
         small = jnp.concatenate(
             [b_query, b_value, b_out, norm1_gain, norm1_shift, norm2_gain, norm2_shift, b_down, b_up]
         )
-        shard_qkv = unfold(w_qkv)
-        shard_rows = shard_qkv.shape[0]
-        small = small.reshape(shard_rows, -1)
-        small_width = small.shape[1]
-        extra = round_up(small_width, 128)
-        small = jnp.pad(small, ((0, 0), (0, extra - small_width)))
-        far_qkv = gather_far(jnp.concatenate([shard_qkv, small], axis=1), far)
+        shard_rows = w_qkv.shape[0] // 8
+        small_count = small.shape[0]
+        small_rows = round_up(small_count, 128) // 128
+        small = jnp.pad(small, (0, shard_rows * 128 - small_count)).reshape(shard_rows, 128)
+        shard_qkv = unfold(w_qkv).reshape(shard_rows, 3, 2, half_width)
+        halves = [shard_qkv[:, :, side].reshape(shard_rows, 3 * half_width) for side in range(2)]
+        half_qkv = 3 * half_width
+        far_one, far_two = gather_far(
+            jnp.concatenate([halves[0], small, halves[1]], axis=1), far, [half_qkv + 128, half_qkv]
+        )
         shard_up = jnp.concatenate(
-            [hidden_to_local(unfold(w_up), 1, far), to_local(unfold(w_out), 1, far)], axis=1
-        )
-        far_up = gather_far(after(shard_up, far_qkv), far)
-        qkv_blocks = spread({OWN: after(far_qkv, inputs_far)}, "x")
-        far_x = qkv_blocks[frozenset({"x"})]
-        qkv_blocks = spread(qkv_blocks, "ctx")
-        up_blocks = spread({OWN: after(far_up, far_x)}, "x")
-        shard_down = after(to_local(unfold(w_down), 1, far), far_up)
+            [to_local(unfold(w_out), 1, far), hidden_to_local(unfold(w_up), 1, far)], axis=1
+        )
+        up_width = w_up.shape[1] * 8
+        up_cut = (width + up_width) // 2
+        far_up = gather_far(after(shard_up, far_one), far, [up_cut, up_cut])
+        far_one, far_two = after(far_one, inputs_far), after(far_two, inputs_far)
+        one = spread(spread({OWN: far_one}, "x"), "ctx")
+        two = spread(spread({OWN: far_two}, "ctx"), "x")
+        shard_down = after(to_local(unfold(w_down), 1, far), far_up[0])
         near_down = order_blocks(spread({OWN: shard_down}, "ctx"), ["ctx"])
-        qkv_weight, small_local = order_blocks(
-            spread(qkv_blocks, "core"), ["core", "x", "ctx"], extra
-        )
-        up_blocks = spread(tie_blocks(up_blocks, qkv_blocks[frozenset({"x", "ctx"})]), "ctx")
-        far_down = gather_far(near_down, far)
-
-        small_core = small_local[:, :small_width].astype(jnp.float32).reshape(8 * far, -1)
+        one_core, two_core = spread(one, "core"), spread(two, "core")
+        axes = ["core", "x", "ctx"]
+        routes = [[(0, half_qkv, 0, 0), (half_qkv, 128, 1, 0)]] * 8
+        qkv_one, small_local = assemble(
+            list(one_core.values()),
+            places(one_core, axes),
+            [(width, half_qkv), (width, 128)],
+            routes,
+        )
+        qkv_two = order_blocks(two_core, axes)
+        up_one = spread(spread({OWN: after(far_up[0], one[XY])}, "x"), "ctx")
+        up_two = spread(spread({OWN: after(far_up[1], two[XY])}, "ctx"), "x")
+        far_down = gather_far(near_down, far)[0]
+
+        devices = 8 * far
+        small_core = small_local.reshape(devices, shard_rows, 128)[:, :small_rows]
+        small_core = small_core.astype(jnp.float32).reshape(devices, -1)
         small_all = to_natural(small_core, 0, far)
         piece = lambda table, index: table[:, index * near_width : (index + 1) * near_width].reshape(-1)
         query_bias = piece(small_all, 0)
@@ -695,15 +922,16 @@
         out_bias, first_gain, first_shift, second_gain, second_shift, down_bias = (
             piece(small_core, index) for index in range(2, 8)
         )
-        up_bias = hidden_to_local(small_all[:, 8 * near_width :].reshape(-1), 0, far)
+        up_bias = small_all[:, 8 * near_width : small_count].reshape(-1)
+        up_bias = hidden_to_local(up_bias, 0, far)
 
         slot = jnp.arange(slots)
         earlier = slot[:, None] < slot[None, :]
 
-        def ranks(own, far, far_first):
+        def ranks(own, other, other_first):
             inside = jnp.sum((own[:, None] == own[None, :]) & earlier, axis=0)
-            outside = jnp.sum(far[:, None] == own[None, :], axis=0)
-            return inside + jnp.where(far_first, outside, 0)
+            outside = jnp.sum(other[:, None] == own[None, :], axis=0)
+            return inside + jnp.where(other_first, outside, 0)
 
         rank_near = ranks(segment, segment_far, place == 1)
         rank_far = ranks(segment_far, segment, place == 0)
@@ -712,28 +940,27 @@
             return jnp.where(ids == image, rank, jnp.where(ids < 0, SEQ + rank, -1))
 
         row = jnp.arange(rows)
-        pick_near = (positions(segment, rank_near, place)[None, :] == row[:, None])
-        pick_far = (positions(segment_far, rank_far, place)[None, :] == row[:, None])
-        pick_near, pick_far = pick_near.astype(jnp.bfloat16), pick_far.astype(jnp.bfloat16)
-        give_near = (positions(segment, rank_near, place)[:, None] == row[None, :])
-        other_image = jnp.where(segment == 1 - place, rank_near, -1)
-        give_far = other_image[:, None] == row[None, :]
-        give_near, give_far = give_near.astype(jnp.bfloat16), give_far.astype(jnp.bfloat16)
+        spot_near = positions(segment, rank_near, place)
+        spot_far = positions(segment_far, rank_far, place)
+        pick_near = (spot_near[None, :] == row[:, None]).astype(jnp.bfloat16)
+        pick_far = (spot_far[None, :] == row[:, None]).astype(jnp.bfloat16)
+        spot_other = jnp.where(segment == 1 - place, rank_near, -1)
+        give_near = (spot_near[:, None] == row[None, :]).astype(jnp.bfloat16)
+        give_far = (spot_other[:, None] == row[None, :]).astype(jnp.bfloat16)
         column = jnp.arange(width)
-        order = to_local(column, 0, far)
-        to_core = (column[:, None] == order[None, :]).astype(jnp.bfloat16)
-
-        def take(near, far):
-            picked = matmul(pick_near, near) + matmul(pick_far, far)
+        to_core = (column[:, None] == to_local(column, 0, far)[None, :]).astype(jnp.bfloat16)
+
+        def take(near, other):
+            picked = matmul(pick_near, near) + matmul(pick_far, other)
             return matmul(picked.astype(jnp.bfloat16), to_core)
 
         def to_give(array):
             natural = nt_dot(array.astype(jnp.bfloat16), to_core).astype(jnp.bfloat16)
             return natural, swap(natural)
 
-        def give(both, follow):
-            near, far_rows = both
-            return matmul(give_near, near) + matmul(give_far, after(far_rows, follow))
+        def give(both, *follow):
+            near, other = both
+            return matmul(give_near, near) + matmul(give_far, after(other, *follow))
 
         kind = (row >= SEQ).astype(jnp.int32) + (row >= SEQ + pads).astype(jnp.int32)
         bias = jnp.where(kind[:, None] == kind[None, :], 0.0, -1e30).astype(jnp.float32)
@@ -741,92 +968,134 @@
         values_in = take(inputs, inputs_far)
         normal1, scale1 = standardize(values_in)
         normed1 = (normal1 * first_gain + first_shift).astype(jnp.bfloat16)
-        joined_bias = jnp.concatenate([query_bias, jnp.zeros_like(query_bias), value_bias])
-        joined = (matmul(normed1, qkv_weight) + joined_bias).astype(jnp.bfloat16)
-        up_near = order_blocks(up_blocks, ["x", "ctx"])
-        attended, log_total = attention_forward(after(joined, near_down), bias)
-        down_blocks = spread({OWN: after(far_down, attended)}, "x")
-        up_weight, out_rows = order_blocks(
-            spread({OWN: after(up_near, attended)}, "core"), ["core"], width
+        joined_bias = [
+            jnp.concatenate(
+                [query_bias[cut], jnp.zeros((half_width,), jnp.float32), value_bias[cut]]
+            )
+            for cut in (slice(0, half_width), slice(half_width, width))
+        ]
+        joined_one = project(normed1, qkv_one, joined_bias[0])
+        attended_one, log_one = attention_forward(after(joined_one, near_down), bias)
+        joined_two = project(after(normed1, attended_one), qkv_two, joined_bias[1])
+        up_near = assemble(
+            list(up_one.values()) + list(up_two.values()),
+            places(up_one, ["x", "ctx"]) + places(up_two, ["x", "ctx"]),
+            [(half_width, width + up_width)],
+            [[(0, up_cut, 0, 0)]] * 4 + [[(0, up_cut, 0, up_cut)]] * 4,
+        )[0]
+        up_blocks = spread({OWN: up_near}, "core")
+        attended_two, log_two = attention_forward(joined_two, bias)
+        attended = jnp.concatenate([attended_one, attended_two], axis=1)
+        cotangent_far = swap(after(cotangent, up_near))
+        down_blocks = spread({OWN: after(far_down, up_near)}, "x")
+        out_rows, up_weight = assemble(
+            list(up_blocks.values()),
+            places(up_blocks, ["core"]),
+            [(width, width), (width, up_width)],
+            [[(0, width, 0, 0), (width, up_width, 1, 0)]] * 2,
         )
         out_weight = to_natural(out_rows, 0, far)
         middle = values_in + matmul(attended, out_weight) + out_bias
         normal2, scale2 = standardize(middle)
         normed2 = (normal2 * second_gain + second_shift).astype(jnp.bfloat16)
-        hidden = matmul(normed2, up_weight) + up_bias
-        active = gelu_exact(hidden).astype(jnp.bfloat16)
-        slope = gelu_slope(hidden).astype(jnp.bfloat16)
-        down_blocks = tie_blocks(down_blocks, active)
-        down_weight = order_blocks(spread(down_blocks, "core"), ["core", "x"])
+        active, slope = hidden_layer(normed2, up_weight, up_bias)
 
         live = (row < SEQ).astype(jnp.float32)[:, None]
-        cotangent_far = swap(after(cotangent, joined))
         d_out = take(cotangent, cotangent_far) * live
         d_out_low = d_out.astype(jnp.bfloat16)
-        grad_down = matmul(active.T, d_out_low).astype(jnp.bfloat16)
-        down_core = send_half(grad_down, "core")
-        last = middle + matmul(after(active, down_core[0]), down_weight) + down_bias
+        down_core = trade(gradient(active, d_out_low, 1 - core), "core")
+        down_blocks = {key: after(block, active) for key, block in down_blocks.items()}
+        down_weight = order_blocks(spread(down_blocks, "core"), ["core", "x"])
+        last = last_layer(active, down_weight, middle, down_bias)
         last_given = to_give(last)
-        down_x = send_half(add_half(down_core, last_given[0]), "x")
-        d_hidden = (
-            matmul(after(d_out_low, down_x[0]), down_weight.T) * slope.astype(jnp.float32)
-        ).astype(jnp.bfloat16)
-        grad_up = matmul(normed2.T, d_hidden).astype(jnp.bfloat16)
-        up_core = send_half(grad_up, "core")
-        d_normed2 = matmul(after(d_hidden, up_core[0]), up_weight.T)
+        down_x = send_half(
+            gradient(active, d_out_low, core, got=after(down_core, last_given[0])), "x"
+        )
+        d_hidden, up_sums = d_hidden_layer(after(d_out_low, down_x[0]), down_weight, slope)
+        up_core = [
+            trade(gradient(normed2, d_hidden, 1 - core, side, 2), "core") for side in range(2)
+        ]
+        d_normed2 = d_normed(d_hidden, up_weight)
         d_middle = d_out + norm_backward(d_normed2, normal2, scale2, second_gain)
         d_branch = d_middle.astype(jnp.bfloat16)
-        outputs = give(last_given, d_branch).astype(jnp.bfloat16)
-        up_y = send_half(add_half(up_core, d_branch), "ctx", 2)
-        grad_out = to_local(matmul(attended.T, after(d_branch, up_y[0])).astype(jnp.bfloat16), 0, far)
+        up_kept = [
+            gradient(normed2, d_hidden, core, side, 2, after(up_core[side], d_branch))
+            for side in range(2)
+        ]
+        up_one = send_half(up_kept[0], "ctx", 2)
+        up_two = send_half(up_kept[1], "x")
+        d_branch = after(d_branch, up_one[0], up_two[0])
+        grad_out = to_local(matmul(attended.T, d_branch).astype(jnp.bfloat16), 0, far)
         out_core = send_half(grad_out, "core")
         d_attended = matmul(d_branch, out_weight.T).astype(jnp.bfloat16)
+        outputs = give(last_given, d_attended).astype(jnp.bfloat16)
+        out_x = send_half(add_half(out_core, d_attended), "x")
         down_far = send_far(add_half(down_x, d_attended), far)
-        out_x = send_half(add_half(out_core, d_attended), "x")
-        d_attended = after(after(d_attended, out_x[0]), down_far[0])
-        d_query, d_key, d_value = attention_backward(joined, d_attended, log_total, bias)
-        d_joined = jnp.concatenate([d_query, d_key, d_value], axis=1)
-        out_y = send_half(add_half(out_x, d_joined), "ctx")
-        up_x = send_half(add_half(up_y, d_joined), "x")
-        grad_qkv = matmul(normed1.T, after(after(d_joined, out_y[0]), up_x[0])).astype(jnp.bfloat16)
-        qkv_core = send_half(grad_qkv, "core")
-        d_normed1 = matmul(after(d_joined, qkv_core[0]), qkv_weight.T)
+        d_attended = after(d_attended, out_x[0], down_far[0])
+        d_one = attention_backward(joined_one, d_attended, 0, log_one, bias)
+        one_core = trade(gradient(normed1, d_one, 1 - core), "core")
+        partial = d_normed(d_one, qkv_one)
+        d_two = attention_backward(
+            joined_two, after(d_attended, partial), half_width // PAIR, log_two, bias
+        )
+        two_core = trade(gradient(normed1, d_two, 1 - core), "core")
+        qkv_one_x = send_half(gradient(normed1, d_one, core, got=after(one_core, d_two)), "x")
+        up_one = send_half(add_half(up_one, d_two), "x")
+        up_two = send_half(add_half(up_two, d_two), "ctx")
+        out_y = send_half(add_half(out_x, d_two), "ctx")
+        d_two_tied = after(d_two, qkv_one_x[0], up_one[0], up_two[0], out_y[0])
+        d_normed1 = d_normed(d_two_tied, qkv_two, partial)
         d_last = d_middle + norm_backward(d_normed1, normal1, scale1, first_gain)
-        qkv_x = send_half(add_half(qkv_core, d_last), "x")
-        out_far = send_far(add_half(out_y, d_last), far)
-        down_y = send_half(add_far(down_far, d_last).astype(jnp.bfloat16), "ctx")
-        d_last_given = to_give(after(after(d_last, qkv_x[0]), down_y[0]))
-        up_far = send_far(add_half(up_x, d_last_given[0]), far)
-        qkv_y = send_half(add_half(qkv_x, up_far[0]), "ctx")
-        sum_down = add_half(down_y, qkv_y[0]).astype(jnp.float32)
-        sum_up, sum_out = add_far(up_far, qkv_y[0]), add_far(out_far, qkv_y[0])
-        qkv_far = send_far(add_half(qkv_y), far)
-        input_grad = give(d_last_given, qkv_far[0])
-        sum_qkv = add_far(qkv_far)
-
-        part = lambda vector: vector.reshape(8 * far, -1)
+        d_last_given = to_give(d_last)
+        qkv_two_y = send_half(
+            gradient(normed1, d_two, core, got=after(two_core, d_last_given[0])), "ctx", 2
+        )
+        down_y = send_half(add_far(down_far, d_last_given[0]).astype(jnp.bfloat16), "ctx")
+        up_one_far = send_far(add_half(up_one, qkv_two_y[0], down_y[0]), far)
+        qkv_one_y = send_half(add_half(qkv_one_x, up_one_far[0]), "ctx")
+        up_two_far = send_far(add_half(up_two, qkv_one_y[0]), far)
+        out_far = send_far(add_half(out_y, up_two_far[0]), far)
+        qkv_two_x = send_half(add_half(qkv_two_y, out_far[0]), "x")
+        qkv_one_far = send_far(add_half(qkv_one_y, qkv_two_x[0]), far)
+        qkv_two_far = send_far(add_half(qkv_two_x, qkv_one_far[0]), far)
+
+        part = lambda vector: vector.reshape(devices, -1)
         core_sums = jnp.concatenate(
             [
-                part(vector)
-                for vector in (
-                    column_sums(d_branch),
-                    column_sums(d_normed1 * normal1),
-                    column_sums(d_normed1),
-                    column_sums(d_normed2 * normal2),
-                    column_sums(d_normed2),
-                    column_sums(d_out_low),
+                part(column_sums(array))
+                for array in (
+                    d_branch,
+                    d_normed1 * normal1,
+                    d_normed1,
+                    d_normed2 * normal2,
+                    d_normed2,
+                    d_out_low,
                 )
             ],
             axis=1,
         )
-        chip_sums = jnp.concatenate([part(column_sums(d_query)), part(column_sums(d_value))], axis=1)
-        up_sums = part(hidden_to_natural(column_sums(d_hidden), 0, far))
+        joined_sums = [
+            part(jnp.concatenate([column_sums(d_one[index]), column_sums(d_two[index])]))
+            for index in (0, 2)
+        ]
+        joined_sums = jnp.concatenate(joined_sums, axis=1)
+        up_sums = part(hidden_to_natural(up_sums[0], 0, far))
         small_sums = jnp.concatenate(
-            [to_local(chip_sums, 0, far), core_sums, to_local(up_sums, 0, far)], axis=1
-        )
-        for axis in ("core", "x", "ctx"):
+            [to_local(joined_sums, 0, far), core_sums, to_local(up_sums, 0, far)], axis=1
+        )
+        for axis in axes:
             small_sums = add_half(send_half(small_sums, axis))
         small_sums = add_far(send_far(small_sums, far))[0]
+
+        sum_down = add_half(down_y).astype(jnp.float32)
+        sum_up = jnp.concatenate([add_far(up_one_far), add_far(up_two_far)], axis=1)
+        sum_out = add_far(out_far)
+        sum_qkv = [
+            add_far(arrays).reshape(shard_rows, 3, 1, half_width)
+            for arrays in (qkv_one_far, qkv_two_far)
+        ]
+        sum_qkv = jnp.concatenate(sum_qkv, axis=2).reshape(shard_rows, 3 * width)
+        input_grad = give(d_last_given, qkv_two_far[0])
         own = lambda index: small_sums[index * near_width : (index + 1) * near_width]
         back = lambda matrix: refold(to_natural(matrix, 1, far))
         return (

time: 635 us -> 630 us (level)
  Pallas kernels: 78.3 us -> 177 us
  matrix products: 142 us -> 48.8 us
  waiting for transfers between devices: 202 us -> 169 us
  local copies, waits for them, and re-layouts: 71.3 us -> 90.3 us
    pallas_call x10 -> x31, Pallas kernels: 78.3 us -> 177 us  [the longest x10 40.2 us: gradient(): pl.pallas_call(gradient_kernel, grid_spec=pltpu.PrefetchScalarGridSpec(nu...]
    dot_general x19 -> x11, matrix products: 126 us -> 43.3 us  [matmul(): return jnp.dot(left, right, preferred_element_type=jnp.float32)]
    unnamed x116 -> x244, local copies, waits for them, and re-layouts: 17.5 us -> 37.6 us
    ppermute x9, waiting for transfers between devices: 47.5 us -> 32.8 us  [gather_far(): lax.ppermute(shard, 'z', [(i, (i + step) % far) for i in range(far)])]
    convert_element_type x11 -> x12, other arithmetic: 23.3 us -> 11.9 us  [add_half(): (kept.astype(jnp.float32) + got.astype(jnp.float32)).astype(kept.dtype)]
    reshape x14 -> x13, local copies, waits for them, and re-layouts: 21.5 us -> 10.4 us  [send_half(): lax.dynamic_index_in_dim(blocks, 1 - place, 1, False)]
    ppermute x35 -> x51, waiting for transfers between devices: 130 us -> 119 us  [trade(): return lax.ppermute(array, axis, [(0, 1), (1, 0)])]
    dot_general x2, matrix products: 15.7 us -> 5.51 us  [nt_dot(): lax.dot_general(left, right, (((1,), (1,)), ((), ())), preferred_element_...]
  transfers between devices with their start and end apart: 59 -> 81, of which waited for: 19 -> 27; matrix products, arithmetic and copies ran while one was open for 36% -> 21% of each run, Pallas kernels for 12% -> 25%
where the time goes in v5:
time: 630 us; the launch traced here: 625 us
  Pallas kernels  177 us (28%)
  waiting for transfers between devices  169 us (27%)
  starting transfers between devices  101 us (16%)
  local copies, waits for them, and re-layouts  90.3 us (14%)
  matrix products  48.8 us (8%)
  other arithmetic  36.7 us (6%)
    ppermute x51, waiting for transfers between devices, trade(): return lax.ppermute(array, axis, [(0, 1), (1, 0)])  119 us
    dot_general x11, matrix products, matmul(): return jnp.dot(left, right, preferred_element_type=jnp.float32)  43.3 us
    ppermute x21, starting transfers between devices, send_far(): lax.ppermute(sent, 'z', [(i, (i + step) % far) for i in range(far)])  42.3 us
    pallas_call x10, Pallas kernels, gradient(): pl.pallas_call(gradient_kernel, grid_spec=pltpu.PrefetchScalarGridSpec(nu...  40.2 us
    unnamed x244, local copies, waits for them, and re-layouts  37.6 us
    ppermute x51, starting transfers between devices, trade(): return lax.ppermute(array, axis, [(0, 1), (1, 0)])  35.3 us
    ppermute x9, waiting for transfers between devices, gather_far(): lax.ppermute(shard, 'z', [(i, (i + step) % far) for i in range(far)])  32.8 us
    pallas_call x9, Pallas kernels, assemble(): pl.pallas_call(functools.partial(assemble_kernel, routes), in_specs=[pl.B...  27.8 us
  transfers between devices with their start and end apart: 81, of which 27 were waited for; matrix products, arithmetic and copies ran while one was open for 21% of the time, Pallas kernels for 25%

profile of v5, /device:TPU:0, one launch (start us, length us, event | category | flops | bytes accessed | tf_op | source)
XLA Modules:
  0.0 625.4 jit_solution(12852164808356433081)
XLA Ops:
  5.8 6.1 concatenate.63
  17.5 4.3 collective-permute-done.2.refs_1_
  21.9 7.4 %collective-permute-done.3.refs_2_ = bf16[32,3200]{1,0:T(8,128)(2,1)S(1)} collective-permute-done((bf16[32,3200]{1,0:T(8,128)(2,1)S(1)}, bf16[32,3200]{1,0:T(8,128)(2,1)S(1)}, u32[]{:S(2)}, u32[]{:S(2)}) %collective-permute-start.3) | collective-permute-done | bytes 204832 | tf_op jit(solution)/shard_map/ppermute | solution.py:776
  35.8 9.4 %collective-permute-done.16.refs_1_ = bf16[128,1536]{1,0:T(8,128)(2,1)} collective-permute-done((bf16[128,1536]{1,0:T(8,128)(2,1)}, bf16[128,1536]{1,0:T(8,128)(2,1)}, u32[]{:S(2)}, u32[]{:S(2)}) %collective-permute-start.16) | collective-permute-done | bytes 393248 | tf_op jit(solution)/shard_map/ppermute | solution.py:765
  46.4 5.0 collective-permute-start.12
  54.3 5.3 collective-permute-done.12.refs_1_
  59.6 10.6 %collective-permute-done.13.refs_2_ = bf16[32,5120]{1,0:T(8,128)(2,1)S(1)} collective-permute-done((bf16[32,5120]{1,0:T(8,128)(2,1)S(1)}, bf16[32,5120]{1,0:T(8,128)(2,1)S(1)}, u32[]{:S(2)}, u32[]{:S(2)}) %collective-permute-start.13) | collective-permute-done | bytes 327712 | tf_op jit(solution)/shard_map/ppermute | solution.py:776
  76.6 13.5 %collective-permute-done.26.refs_5_ = bf16[128,2560]{1,0:T(8,128)(2,1)S(1)} collective-permute-done((bf16[128,2560]{1,0:T(8,128)(2,1)S(1)}, bf16[128,2560]{1,0:T(8,128)(2,1)S(1)}, u32[]{:S(2)}, u32[]{:S(2)}) %collective-permute-start.26) | collective-permute-done | bytes 655392 | tf_op jit(solution)/shard_map/ppermute | solution.py:765
  93.8 11.9 %collective-permute-done.27.refs_6_ = bf16[128,2560]{1,0:T(8,128)(2,1)S(1)} collective-permute-done((bf16[128,2560]{1,0:T(8,128)(2,1)S(1)}, bf16[128,2560]{1,0:T(8,128)(2,1)S(1)}, u32[]{:S(2)}, u32[]{:S(2)}) %collective-permute-start.27) | collective-permute-done | bytes 655392 | tf_op jit(solution)/shard_map/ppermute | solution.py:765
  105.8 12.1 %collective-permute-done.28.refs_7_ = bf16[128,2560]{1,0:T(8,128)(2,1)} collective-permute-done((bf16[128,2560]{1,0:T(8,128)(2,1)S(1)}, bf16[128,2560]{1,0:T(8,128)(2,1)}, u32[]{:S(2)}, u32[]{:S(2)}) %collective-permute-start.28) | collective-permute-done | bytes 655392 | tf_op jit(solution)/shard_map/ppermute | solution.py:765
  117.9 4.2 assemble.14.refs_0_
  127.0 3.8 fusion.12
  133.1 3.8 fusion.11
  144.5 5.9 fusion.47
  160.2 7.6 %collective-permute-start.30 = (bf16[256,1024]{1,0:T(8,128)(2,1)S(1)}, bf16[256,1024]{1,0:T(8,128)(2,1)}, u32[]{:S(2)}, u32[]{:S(2)}) collective-permute-start(bf16[256,1024]{1,0:T(8,128)(2,1)S(1)} %assemble.12.refs_0_), channel_id=1, source_target_pairs={{0,8},{8,16},{16,24},{24,0},{1,9},{9,17},{17,25},{25,1},{2,10},{10... | collective-permute-start | bytes 1572872 | tf_op jit(solution)/shard_map/ppermute | solution.py:776
  182.3 13.4 %attention_forward.2 = (bf16[592,512]{1,0:T(8,128)(2,1)S(1)}, f32[4,2,592]{2,1,0:T(2,128)S(1)}) custom-call(bf16[3,592,512]{2,1,0:T(8,128)(2,1)S(1)} %project.2.query_ref.key_ref.value_ref, bf16[3,592,512]{2,1,0:T(8,128)(2,1)S(1)} %project.2.query_ref.key_ref.value_ref, bf16[3,592,512]{2,1,0:T(8,128)(2,1)S(1)} %project.2.query_ref.key_ref.value_ref, ...), custom_call_target="tpu_custom_call" | custom-call | flops 1 | bytes 1 | tf_op jit(solution)/shard_map/attention_forward/pallas_call | solution.py:434
  199.0 4.5 collective-permute-done.31.refs_2_
  206.6 13.4 %attention_forward.3 = (bf16[592,512]{1,0:T(8,128)(2,1)S(1)}, f32[4,2,592]{2,1,0:T(2,128)S(1)}) custom-call(bf16[3,592,512]{2,1,0:T(8,128)(2,1)S(1)} %project.3.query_ref.key_ref.value_ref, bf16[3,592,512]{2,1,0:T(8,128)(2,1)S(1)} %project.3.query_ref.key_ref.value_ref, bf16[3,592,512]{2,1,0:T(8,128)(2,1)S(1)} %project.3.query_ref.key_ref.value_ref, ...), custom_call_target="tpu_custom_call" | custom-call | flops 1 | bytes 1 | tf_op jit(solution)/shard_map/attention_forward/pallas_call | solution.py:434
  226.6 6.3 %convert_reduce_fusion = (f32[1024]{0:T(1024)S(1)}, bf16[592,1024]{1,0:T(8,128)(2,1)}, f32[592,1024]{1,0:T(8,128)}) fusion(f32[592]{0:T(1024)S(1)} %copy-done.102, s32[1024]{0:T(1024)S(1)} %copy-done.106, f32[592,1024]{1,0:T(8,128)} %fusion.11, bf16[584,1024]{1,0:T(8,128)(2,1)} %collective-permute-done.37, s32[584]{0:T(1024)S(1)} %copy-done.109), kind=kOutput, calls=%fused_computation.6 | convolution fusion | flops 1954595456 | bytes 7271008 | tf_op jit(solution)/shard_map/dot_general | solution.py:28
  232.9 5.8 assemble.15
  242.1 3.7 fusion.48
  247.3 18.1 %hidden_layer.1 = (bf16[592,4096]{1,0:T(8,128)(2,1)S(1)}, bf16[592,4096]{1,0:T(8,128)(2,1)S(1)}) custom-call(bf16[592,1024]{1,0:T(8,128)(2,1)S(1)} %add_convert_fusion.3.x_ref, bf16[1024,4096]{1,0:T(8,128)(2,1)S(1)} %get-tuple-element.87.weight_ref, f32[1,4096]{1,0:T(1,128)S(1)} %bitcast.204), custom_call_target="tpu_custom_call" | custom-call | flops 1 | bytes 1 | tf_op jit(solution)/shard_map/hidden_layer/pallas_call | solution.py:518
  265.5 7.6 %gradient.10 = bf16[2048,1024]{1,0:T(8,128)(2,1)} custom-call(s32[1]{0:T(128)} %bitcast.22.index_ref, bf16[592,4096]{1,0:T(8,128)(2,1)S(1)} %get-tuple-element.88.active_ref.x_ref, bf16[592,1024]{1,0:T(8,128)(2,1)S(1)} %copy-done.35), custom_call_target="tpu_custom_call" | custom-call | flops 1 | bytes 1 | tf_op jit(solution)/shard_map/gradient/pallas_call | solution.py:658
  273.8 9.8 %collective-permute-done.35.refs_3_ = bf16[1024,1024]{1,0:T(8,128)(2,1)} collective-permute-done((bf16[1024,1024]{1,0:T(8,128)(2,1)}, bf16[1024,1024]{1,0:T(8,128)(2,1)}, u32[]{:S(2)}, u32[]{:S(2)}) %collective-permute-start.35) | collective-permute-done | bytes 2097184 | tf_op jit(solution)/shard_map/ppermute | solution.py:765
  286.6 4.2 assemble.17.weight_ref
  294.1 3.4 copy-done.5
  301.6 7.1 %last_layer.1 = bf16[592,1024]{1,0:T(8,128)(2,1)S(1)} custom-call(bf16[592,4096]{1,0:T(8,128)(2,1)S(1)} %copy-done.14, bf16[4096,1024]{1,0:T(8,128)(2,1)S(1)} %copy-done.5, f32[592,1024]{1,0:T(8,128)S(1)} %copy-done.7, f32[1,1024]{1,0:T(1,128)S(1)} %broadcast_in_dim_reshape.5.bias_ref), custom_call_target="tpu_custom_call" | custom-call | flops 1 | bytes 1 | tf_op jit(solution)/shard_map/last_layer/pallas_call | solution.py:551
  311.3 8.3 %gradient.11 = bf16[2048,1024]{1,0:T(8,128)(2,1)S(1)} custom-call(s32[1]{0:T(128)} %bitcast.21.index_ref, bf16[592,4096]{1,0:T(8,128)(2,1)S(1)} %copy-done.15, bf16[592,1024]{1,0:T(8,128)(2,1)S(1)} %copy-done.36, bf16[2048,1024]{1,0:T(8,128)(2,1)} %collective-permute-done.38.refs_0_), custom_call_target="tpu_custom_call" | custom-call | flops 1 | bytes 1 | tf_op jit(solution)/shard_map/gradient/pallas_call | solution.py:658
  322.1 7.8 %d_hidden_layer.1 = (bf16[592,4096]{1,0:T(8,128)(2,1)S(1)}, f32[1,4096]{1,0:T(1,128)S(1)}) custom-call(bf16[592,1024]{1,0:T(8,128)(2,1)S(1)} %copy-done.36, bf16[4096,1024]{1,0:T(8,128)(2,1)S(1)} %bitcast.195, bf16[592,4096]{1,0:T(8,128)(2,1)S(1)} %bitcast.202), custom_call_target="tpu_custom_call" | custom-call | flops 1 | bytes 1 | tf_op jit(solution)/shard_map/d_hidden_layer/pallas_call | solution.py:580
  335.1 4.1 fusion.14
  339.2 3.4 copy-done.27
  342.7 9.8 %d_normed.3 = f32[592,1024]{1,0:T(8,128)S(1)} custom-call(bf16[592,4096]{1,0:T(8,128)(2,1)S(1)} %copy-done.1, bf16[1024,4096]{1,0:T(8,128)(2,1)S(1)} %copy-done.27), custom_call_target="tpu_custom_call" | custom-call | flops 1 | bytes 1 | tf_op jit(solution)/shard_map/d_normed/pallas_call | solution.py:621
  352.5 3.4 gradient.12
  358.8 4.8 fusion.44
  371.8 9.8 %collective-permute-done.42 = bf16[1024,1024]{1,0:T(8,128)(2,1)} collective-permute-done((bf16[1024,1024]{1,0:T(8,128)(2,1)}, bf16[1024,1024]{1,0:T(8,128)(2,1)}, u32[]{:S(2)}, u32[]{:S(2)}) %collective-permute-start.42) | collective-permute-done | bytes 2097184 | tf_op jit(solution)/shard_map/ppermute | solution.py:765
  395.3 11.7 %collective-permute-start.54 = (bf16[256,1024]{1,0:T(8,128)(2,1)}, bf16[256,1024]{1,0:T(8,128)(2,1)}, u32[]{:S(2)}, u32[]{:S(2)}) collective-permute-start(bf16[256,1024]{1,0:T(8,128)(2,1)} %get-tuple-element.161), channel_id=1, source_target_pairs={{0,8},{8,16},{16,24},{24,0},{1,9},{9,17},{17,25},{25,1},{2,10},{10... | collective-permute-start | bytes 1572872 | tf_op jit(solution)/shard_map/ppermute | solution.py:833
  408.7 3.4 add_convert_fusion.6
  414.8 13.3 %attention_backward.2.d_ref = bf16[3,592,512]{2,1,0:T(8,128)(2,1)S(1)} custom-call(bf16[3,592,512]{2,1,0:T(8,128)(2,1)S(1)} %copy-done.3, bf16[3,592,512]{2,1,0:T(8,128)(2,1)S(1)} %copy-done.3, bf16[3,592,512]{2,1,0:T(8,128)(2,1)S(1)} %copy-done.3, bf16[592,1024]{1,0:T(8,128)(2,1)S(1)} %convolution_convert_fusion.1.d_ref, f32[4,2,592]{2,1,0:T(2,128)S(1)} %copy-done.53, ...), custom_call_target="tpu_custom_call" | custom-call | flops 1 | bytes 1 | tf_op jit(solution)/shard_map/attention_backward/pallas_call | solution.py:455
  440.8 13.4 %attention_backward.3.d_ref = bf16[3,592,512]{2,1,0:T(8,128)(2,1)S(1)} custom-call(bf16[3,592,512]{2,1,0:T(8,128)(2,1)S(1)} %project.3.query_ref.key_ref.value_ref, bf16[3,592,512]{2,1,0:T(8,128)(2,1)S(1)} %project.3.query_ref.key_ref.value_ref, bf16[3,592,512]{2,1,0:T(8,128)(2,1)S(1)} %project.3.query_ref.key_ref.value_ref, ...), custom_call_target="tpu_custom_call" | custom-call | flops 1 | bytes 1 | tf_op jit(solution)/shard_map/attention_backward/pallas_call | solution.py:455
  481.0 3.6 d_normed.5
  493.7 3.8 fusion.13
  504.1 14.9 %collective-permute-done.66 = f32[8,384]{1,0:T(8,128)S(1)} collective-permute-done((f32[8,384]{1,0:T(8,128)S(1)}, f32[8,384]{1,0:T(8,128)S(1)}, u32[]{:S(2)}, u32[]{:S(2)}) %collective-permute-start.66) | collective-permute-done | bytes 12320 | tf_op jit(solution)/shard_map/ppermute | solution.py:765
  526.7 4.2 collective-permute-done.74
  548.0 4.2 collective-permute-done.77
  565.8 15.5 %collective-permute-done.49 = bf16[256,1536]{1,0:T(8,128)(2,1)S(1)} collective-permute-done((bf16[256,1536]{1,0:T(8,128)(2,1)S(1)}, bf16[256,1536]{1,0:T(8,128)(2,1)S(1)}, u32[]{:S(2)}, u32[]{:S(2)}) %collective-permute-start.49) | collective-permute-done | bytes 786464 | tf_op jit(solution)/shard_map/ppermute | solution.py:765
  582.3 6.3 %collective-permute-done.58 = bf16[128,1536]{1,0:T(8,128)(2,1)S(1)} collective-permute-done((bf16[128,1536]{1,0:T(8,128)(2,1)S(1)}, bf16[128,1536]{1,0:T(8,128)(2,1)S(1)}, u32[]{:S(2)}, u32[]{:S(2)}) %collective-permute-start.58) | collective-permute-done | bytes 393248 | tf_op jit(solution)/shard_map/ppermute | solution.py:765
  602.3 5.9 collective-permute-done.57
  621.3 3.8 convolution_add_fusion
  (555 shorter events, 259.0 us)
Async XLA Ops:
  0.7 31.1 %collective-permute-start.1 = (bf16[584,1024]{1,0:T(8,128)(2,1)}, bf16[584,1024]{1,0:T(8,128)(2,1)S(1)}, u32[]{:S(2)}, u32[]{:S(2)}) collective-permute-start(bf16[584,1024]{1,0:T(8,128)(2,1)} %param.16), channel_id=1, source_target_pairs={{0,1},{1,0},{2,3},{3,2},{4,5},{5,4},{6,7},{7,6},{8,9},{9,8},{10,11... | collective-permute-start | bytes 3588104 | tf_op jit(solution)/shard_map/ppermute | solution.py:765
  13.5 15.7 %collective-permute-start.3 = (bf16[32,3200]{1,0:T(8,128)(2,1)S(1)}, bf16[32,3200]{1,0:T(8,128)(2,1)S(1)}, u32[]{:S(2)}, u32[]{:S(2)}) collective-permute-start(bf16[32,3200]{1,0:T(8,128)(2,1)S(1)} %pad_maximum_fusion.3.refs_0_), channel_id=1, source_target_pairs={{0,16},{8,24},{16,0},{24,8},{1,17},{9,25},{17,1},{25,9},{2,18},{10... | collective-permute-start | bytes 614408 | tf_op jit(solution)/shard_map/ppermute | solution.py:776
  16.1 13.1 %collective-permute-start.4 = (bf16[32,3200]{1,0:T(8,128)(2,1)S(1)}, bf16[32,3200]{1,0:T(8,128)(2,1)S(1)}, u32[]{:S(2)}, u32[]{:S(2)}) collective-permute-start(bf16[32,3200]{1,0:T(8,128)(2,1)S(1)} %pad_maximum_fusion.3.refs_0_), channel_id=1, source_target_pairs={{0,24},{8,0},{16,8},{24,16},{1,25},{9,1},{17,9},{25,17},{2,26},{10... | collective-permute-start | bytes 614408 | tf_op jit(solution)/shard_map/ppermute | solution.py:776
  32.8 13.0 %collective-permute-start.5 = (bf16[128,1664]{1,0:T(8,128)(2,1)S(1)}, bf16[128,1664]{1,0:T(8,128)(2,1)S(1)}, u32[]{:S(2)}, u32[]{:S(2)}) collective-permute-start(bf16[128,1664]{1,0:T(8,128)(2,1)S(1)} %get-tuple-element.71.refs_0_), channel_id=1, source_target_pairs={{0,4},{4,0},{1,5},{5,1},{2,6},{6,2},{3,7},{7,3},{8,12},{12,8},{9,1... | collective-permute-start | bytes 1277960 | tf_op jit(solution)/shard_map/ppermute | solution.py:765
  45.3 27.1 %collective-permute-start.18 = (bf16[128,1536]{1,0:T(8,128)(2,1)}, bf16[128,1536]{1,0:T(8,128)(2,1)}, u32[]{:S(2)}, u32[]{:S(2)}) collective-permute-start(bf16[128,1536]{1,0:T(8,128)(2,1)} %collective-permute-done.16.refs_1_), channel_id=1, source_target_pairs={{0,4},{4,0},{1,5},{5,1},{2,6},{6,2},{3,7},{7,3},{8,12},{12,8},{9,1... | collective-permute-start | bytes 1179656 | tf_op jit(solution)/shard_map/ppermute | solution.py:765
  45.8 28.2 %collective-permute-start.7 = (bf16[128,1664]{1,0:T(8,128)(2,1)S(1)}, bf16[128,1664]{1,0:T(8,128)(2,1)S(1)}, u32[]{:S(2)}, u32[]{:S(2)}) collective-permute-start(bf16[128,1664]{1,0:T(8,128)(2,1)S(1)} %collective-permute-done.5.refs_1_), channel_id=1, source_target_pairs={{0,1},{1,0},{2,3},{3,2},{4,5},{5,4},{6,7},{7,6},{8,9},{9,8},{10,11... | collective-permute-start | bytes 1277960 | tf_op jit(solution)/shard_map/ppermute | solution.py:765
  46.4 13.3 %collective-permute-start.12 = (bf16[32,5120]{1,0:T(8,128)(2,1)S(1)}, bf16[32,5120]{1,0:T(8,128)(2,1)S(1)}, u32[]{:S(2)}, u32[]{:S(2)}) collective-permute-start(bf16[32,5120]{1,0:T(8,128)(2,1)S(1)} %pad_maximum_fusion.2.refs_0_), channel_id=1, source_target_pairs={{0,8},{8,16},{16,24},{24,0},{1,9},{9,17},{17,25},{25,1},{2,10},{10... | collective-permute-start | bytes 983048 | tf_op jit(solution)/shard_map/ppermute | solution.py:776
  51.4 18.9 %collective-permute-start.13 = (bf16[32,5120]{1,0:T(8,128)(2,1)S(1)}, bf16[32,5120]{1,0:T(8,128)(2,1)S(1)}, u32[]{:S(2)}, u32[]{:S(2)}) collective-permute-start(bf16[32,5120]{1,0:T(8,128)(2,1)S(1)} %pad_maximum_fusion.2.refs_0_), channel_id=1, source_target_pairs={{0,16},{8,24},{16,0},{24,8},{1,17},{9,25},{17,1},{25,9},{2,18},{10... | collective-permute-start | bytes 983048 | tf_op jit(solution)/shard_map/ppermute | solution.py:776
  51.6 19.3 %collective-permute-start.14 = (bf16[32,5120]{1,0:T(8,128)(2,1)S(1)}, bf16[32,5120]{1,0:T(8,128)(2,1)S(1)}, u32[]{:S(2)}, u32[]{:S(2)}) collective-permute-start(bf16[32,5120]{1,0:T(8,128)(2,1)S(1)} %pad_maximum_fusion.2.refs_0_), channel_id=1, source_target_pairs={{0,24},{8,0},{16,8},{24,16},{1,25},{9,1},{17,9},{25,17},{2,26},{10... | collective-permute-start | bytes 983048 | tf_op jit(solution)/shard_map/ppermute | solution.py:776
  72.4 17.7 %collective-permute-start.26 = (bf16[128,2560]{1,0:T(8,128)(2,1)S(1)}, bf16[128,2560]{1,0:T(8,128)(2,1)S(1)}, u32[]{:S(2)}, u32[]{:S(2)}) collective-permute-start(bf16[128,2560]{1,0:T(8,128)(2,1)S(1)} %get-tuple-element.85.refs_4_), channel_id=1, source_target_pairs={{0,1},{1,0},{2,3},{3,2},{4,5},{5,4},{6,7},{7,6},{8,9},{9,8},{10,11... | collective-permute-start | bytes 1966088 | tf_op jit(solution)/shard_map/ppermute | solution.py:765
  74.0 17.7 %collective-permute-start.23 = (bf16[128,2560]{1,0:T(8,128)(2,1)S(1)}, bf16[128,2560]{1,0:T(8,128)(2,1)S(1)}, u32[]{:S(2)}, u32[]{:S(2)}) collective-permute-start(bf16[128,2560]{1,0:T(8,128)(2,1)S(1)} %get-tuple-element.83.refs_0_), channel_id=1, source_target_pairs={{0,4},{4,0},{1,5},{5,1},{2,6},{6,2},{3,7},{7,3},{8,12},{12,8},{9,1... | collective-permute-start | bytes 1966088 | tf_op jit(solution)/shard_map/ppermute | solution.py:765
  75.5 30.2 %collective-permute-start.27 = (bf16[128,2560]{1,0:T(8,128)(2,1)S(1)}, bf16[128,2560]{1,0:T(8,128)(2,1)S(1)}, u32[]{:S(2)}, u32[]{:S(2)}) collective-permute-start(bf16[128,2560]{1,0:T(8,128)(2,1)S(1)} %get-tuple-element.85.refs_4_), channel_id=1, source_target_pairs={{0,4},{4,0},{1,5},{5,1},{2,6},{6,2},{3,7},{7,3},{8,12},{12,8},{9,1... | collective-permute-start | bytes 1966088 | tf_op jit(solution)/shard_map/ppermute | solution.py:765
  76.1 29.7 %collective-permute-start.24 = (bf16[128,2560]{1,0:T(8,128)(2,1)S(1)}, bf16[128,2560]{1,0:T(8,128)(2,1)}, u32[]{:S(2)}, u32[]{:S(2)}) collective-permute-start(bf16[128,2560]{1,0:T(8,128)(2,1)S(1)} %get-tuple-element.83.refs_0_), channel_id=1, source_target_pairs={{0,1},{1,0},{2,3},{3,2},{4,5},{5,4},{6,7},{7,6},{8,9},{9,8},{10,11... | collective-permute-start | bytes 1966088 | tf_op jit(solution)/shard_map/ppermute | solution.py:765
  90.1 27.8 %collective-permute-start.28 = (bf16[128,2560]{1,0:T(8,128)(2,1)S(1)}, bf16[128,2560]{1,0:T(8,128)(2,1)}, u32[]{:S(2)}, u32[]{:S(2)}) collective-permute-start(bf16[128,2560]{1,0:T(8,128)(2,1)S(1)} %collective-permute-done.26.refs_5_), channel_id=1, source_target_pairs={{0,4},{4,0},{1,5},{5,1},{2,6},{6,2},{3,7},{7,3},{8,12},{12,8},{9,1... | collective-permute-start | bytes 1966088 | tf_op jit(solution)/shard_map/ppermute | solution.py:765
  91.7 26.2 %collective-permute-start.25 = (bf16[128,2560]{1,0:T(8,128)(2,1)S(1)}, bf16[128,2560]{1,0:T(8,128)(2,1)}, u32[]{:S(2)}, u32[]{:S(2)}) collective-permute-start(bf16[128,2560]{1,0:T(8,128)(2,1)S(1)} %collective-permute-done.23.refs_1_), channel_id=1, source_target_pairs={{0,1},{1,0},{2,3},{3,2},{4,5},{5,4},{6,7},{7,6},{8,9},{9,8},{10,11... | collective-permute-start | bytes 1966088 | tf_op jit(solution)/shard_map/ppermute | solution.py:765
  93.2 32.6 %collective-permute-start = (s32[584]{0:T(1024)S(1)}, s32[584]{0:T(1024)S(1)}, u32[]{:S(2)}, u32[]{:S(2)}) collective-permute-start(s32[584]{0:T(1024)S(1)} %copy-done.93), channel_id=1, source_target_pairs={{0,1},{1,0},{2,3},{3,2},{4,5},{5,4},{6,7},{7,6},{8,9},{9,8},{10,11... | collective-permute-start | bytes 7016 | tf_op jit(solution)/shard_map/ppermute | solution.py:765
  122.1 110.8 %collective-permute-start.29 = (bf16[512,5120]{1,0:T(8,128)(2,1)}, bf16[512,5120]{1,0:T(8,128)(2,1)}, u32[]{:S(2)}, u32[]{:S(2)}) collective-permute-start(bf16[512,5120]{1,0:T(8,128)(2,1)} %assemble.14.refs_0_), channel_id=1, source_target_pairs={{0,2},{2,0},{1,3},{3,1},{4,6},{6,4},{5,7},{7,5},{8,10},{10,8},{9,1... | collective-permute-start | bytes 15728648 | tf_op jit(solution)/shard_map/ppermute | solution.py:765
  152.2 17.0 %collective-permute-start.9 = (bf16[128,1664]{1,0:T(8,128)(2,1)S(1)}, bf16[128,1664]{1,0:T(8,128)(2,1)S(1)}, u32[]{:S(2)}, u32[]{:S(2)}) collective-permute-start(bf16[128,1664]{1,0:T(8,128)(2,1)S(1)} %copy-done.47), channel_id=1, source_target_pairs={{0,2},{2,0},{1,3},{3,1},{4,6},{6,4},{5,7},{7,5},{8,10},{10,8},{9,1... | collective-permute-start | bytes 1277960 | tf_op jit(solution)/shard_map/ppermute | solution.py:765
  152.7 15.1 %collective-permute-start.10 = (bf16[128,1664]{1,0:T(8,128)(2,1)}, bf16[128,1664]{1,0:T(8,128)(2,1)S(1)}, u32[]{:S(2)}, u32[]{:S(2)}) collective-permute-start(bf16[128,1664]{1,0:T(8,128)(2,1)} %collective-permute-done.6.refs_2_), channel_id=1, source_target_pairs={{0,2},{2,0},{1,3},{3,1},{4,6},{6,4},{5,7},{7,5},{8,10},{10,8},{9,1... | collective-permute-start | bytes 1277960 | tf_op jit(solution)/shard_map/ppermute | solution.py:765
  152.8 17.6 %collective-permute-start.11 = (bf16[128,1664]{1,0:T(8,128)(2,1)}, bf16[128,1664]{1,0:T(8,128)(2,1)S(1)}, u32[]{:S(2)}, u32[]{:S(2)}) collective-permute-start(bf16[128,1664]{1,0:T(8,128)(2,1)} %copy-done.48), channel_id=1, source_target_pairs={{0,2},{2,0},{1,3},{3,1},{4,6},{6,4},{5,7},{7,5},{8,10},{10,8},{9,1... | collective-permute-start | bytes 1277960 | tf_op jit(solution)/shard_map/ppermute | solution.py:765
  160.2 38.8 %collective-permute-start.30 = (bf16[256,1024]{1,0:T(8,128)(2,1)S(1)}, bf16[256,1024]{1,0:T(8,128)(2,1)}, u32[]{:S(2)}, u32[]{:S(2)}) collective-permute-start(bf16[256,1024]{1,0:T(8,128)(2,1)S(1)} %assemble.12.refs_0_), channel_id=1, source_target_pairs={{0,8},{8,16},{16,24},{24,0},{1,9},{9,17},{17,25},{25,1},{2,10},{10... | collective-permute-start | bytes 1572872 | tf_op jit(solution)/shard_map/ppermute | solution.py:776
  167.8 35.7 %collective-permute-start.31 = (bf16[256,1024]{1,0:T(8,128)(2,1)S(1)}, bf16[256,1024]{1,0:T(8,128)(2,1)}, u32[]{:S(2)}, u32[]{:S(2)}) collective-permute-start(bf16[256,1024]{1,0:T(8,128)(2,1)S(1)} %assemble.12.refs_0_), channel_id=1, source_target_pairs={{0,16},{8,24},{16,0},{24,8},{1,17},{9,25},{17,1},{25,9},{2,18},{10... | collective-permute-start | bytes 1572872 | tf_op jit(solution)/shard_map/ppermute | solution.py:776
  169.2 34.3 %collective-permute-start.32 = (bf16[256,1024]{1,0:T(8,128)(2,1)S(1)}, bf16[256,1024]{1,0:T(8,128)(2,1)}, u32[]{:S(2)}, u32[]{:S(2)}) collective-permute-start(bf16[256,1024]{1,0:T(8,128)(2,1)S(1)} %assemble.12.refs_0_), channel_id=1, source_target_pairs={{0,24},{8,0},{16,8},{24,16},{1,25},{9,1},{17,9},{25,17},{2,26},{10... | collective-permute-start | bytes 1572872 | tf_op jit(solution)/shard_map/ppermute | solution.py:776
  174.8 51.8 %collective-permute-start.37 = (bf16[584,1024]{1,0:T(8,128)(2,1)}, bf16[584,1024]{1,0:T(8,128)(2,1)}, u32[]{:S(2)}, u32[]{:S(2)}) collective-permute-start(bf16[584,1024]{1,0:T(8,128)(2,1)} %param.17), channel_id=1, source_target_pairs={{0,1},{1,0},{2,3},{3,2},{4,5},{5,4},{6,7},{7,6},{8,9},{9,8},{10,11... | collective-permute-start | bytes 3588104 | tf_op jit(solution)/shard_map/ppermute | solution.py:765
  225.1 47.9 %collective-permute-start.33 = (bf16[1024,1024]{1,0:T(8,128)(2,1)}, bf16[1024,1024]{1,0:T(8,128)(2,1)}, u32[]{:S(2)}, u32[]{:S(2)}) collective-permute-start(bf16[1024,1024]{1,0:T(8,128)(2,1)} %assemble.16.refs_0_), channel_id=1, source_target_pairs={{0,4},{4,0},{1,5},{5,1},{2,6},{6,2},{3,7},{7,3},{8,12},{12,8},{9,1... | collective-permute-start | bytes 6291464 | tf_op jit(solution)/shard_map/ppermute | solution.py:765
  273.1 38.2 %collective-permute-start.38 = (bf16[2048,1024]{1,0:T(8,128)(2,1)}, bf16[2048,1024]{1,0:T(8,128)(2,1)}, u32[]{:S(2)}, u32[]{:S(2)}) collective-permute-start(bf16[2048,1024]{1,0:T(8,128)(2,1)} %gradient.10), channel_id=1, source_target_pairs={{0,2},{2,0},{1,3},{3,1},{4,6},{6,4},{5,7},{7,5},{8,10},{10,8},{9,1... | collective-permute-start | bytes 12582920 | tf_op jit(solution)/shard_map/ppermute | solution.py:765
  333.2 30.5 %collective-permute-start.40 = (bf16[512,2048]{1,0:T(8,128)(2,1)}, bf16[512,2048]{1,0:T(8,128)(2,1)}, u32[]{:S(2)}, u32[]{:S(2)}) collective-permute-start(bf16[512,2048]{1,0:T(8,128)(2,1)} %gradient.14), channel_id=1, source_target_pairs={{0,2},{2,0},{1,3},{3,1},{4,6},{6,4},{5,7},{7,5},{8,10},{10,8},{9,1... | collective-permute-start | bytes 6291464 | tf_op jit(solution)/shard_map/ppermute | solution.py:765
  333.3 48.2 %collective-permute-start.42 = (bf16[1024,1024]{1,0:T(8,128)(2,1)}, bf16[1024,1024]{1,0:T(8,128)(2,1)}, u32[]{:S(2)}, u32[]{:S(2)}) collective-permute-start(bf16[1024,1024]{1,0:T(8,128)(2,1)} %get-tuple-element.159), channel_id=1, source_target_pairs={{0,4},{4,0},{1,5},{5,1},{2,6},{6,2},{3,7},{7,3},{8,12},{12,8},{9,1... | collective-permute-start | bytes 6291464 | tf_op jit(solution)/shard_map/ppermute | solution.py:765
  334.5 72.5 %collective-permute-start.36 = (bf16[592,1024]{1,0:T(8,128)(2,1)}, bf16[592,1024]{1,0:T(8,128)(2,1)}, u32[]{:S(2)}, u32[]{:S(2)}) collective-permute-start(bf16[592,1024]{1,0:T(8,128)(2,1)} %fusion.9), channel_id=1, source_target_pairs={{0,1},{1,0},{2,3},{3,2},{4,5},{5,4},{6,7},{7,6},{8,9},{9,8},{10,11... | collective-permute-start | bytes 3637256 | tf_op jit(solution)/shard_map/ppermute | solution.py:765
  355.9 29.8 %collective-permute-start.39 = (bf16[512,2048]{1,0:T(8,128)(2,1)}, bf16[512,2048]{1,0:T(8,128)(2,1)}, u32[]{:S(2)}, u32[]{:S(2)}) collective-permute-start(bf16[512,2048]{1,0:T(8,128)(2,1)} %gradient.12), channel_id=1, source_target_pairs={{0,2},{2,0},{1,3},{3,1},{4,6},{6,4},{5,7},{7,5},{8,10},{10,8},{9,1... | collective-permute-start | bytes 6291464 | tf_op jit(solution)/shard_map/ppermute | solution.py:765
  385.0 27.2 %collective-permute-start.41 = (bf16[512,1024]{1,0:T(8,128)(2,1)S(1)}, bf16[512,1024]{1,0:T(8,128)(2,1)S(1)}, u32[]{:S(2)}, u32[]{:S(2)}) collective-permute-start(bf16[512,1024]{1,0:T(8,128)(2,1)S(1)} %dynamic-slice_bitcast_fusion.3), channel_id=1, source_target_pairs={{0,2},{2,0},{1,3},{3,1},{4,6},{6,4},{5,7},{7,5},{8,10},{10,8},{9,1... | collective-permute-start | bytes 3145736 | tf_op jit(solution)/shard_map/ppermute | solution.py:765
  385.1 69.1 %collective-permute-start.45 = (bf16[256,2048]{1,0:T(8,128)(2,1)}, bf16[256,2048]{1,0:T(8,128)(2,1)}, u32[]{:S(2)}, u32[]{:S(2)}) collective-permute-start(bf16[256,2048]{1,0:T(8,128)(2,1)} %get-tuple-element.165), channel_id=1, source_target_pairs={{0,4},{4,0},{1,5},{5,1},{2,6},{6,2},{3,7},{7,3},{8,12},{12,8},{9,1... | collective-permute-start | bytes 3145736 | tf_op jit(solution)/shard_map/ppermute | solution.py:765
  390.6 68.1 %collective-permute-start.44 = (bf16[256,2048]{1,0:T(8,128)(2,1)}, bf16[256,2048]{1,0:T(8,128)(2,1)}, u32[]{:S(2)}, u32[]{:S(2)}) collective-permute-start(bf16[256,2048]{1,0:T(8,128)(2,1)} %bitcast.55), channel_id=1, source_target_pairs={{0,1},{1,0},{2,3},{3,2},{4,5},{5,4},{6,7},{7,6},{8,9},{9,8},{10,11... | collective-permute-start | bytes 3145736 | tf_op jit(solution)/shard_map/ppermute | solution.py:765
  395.3 94.1 %collective-permute-start.54 = (bf16[256,1024]{1,0:T(8,128)(2,1)}, bf16[256,1024]{1,0:T(8,128)(2,1)}, u32[]{:S(2)}, u32[]{:S(2)}) collective-permute-start(bf16[256,1024]{1,0:T(8,128)(2,1)} %get-tuple-element.161), channel_id=1, source_target_pairs={{0,8},{8,16},{16,24},{24,0},{1,9},{9,17},{17,25},{25,1},{2,10},{10... | collective-permute-start | bytes 1572872 | tf_op jit(solution)/shard_map/ppermute | solution.py:833
  407.0 83.7 %collective-permute-start.55 = (bf16[256,1024]{1,0:T(8,128)(2,1)}, bf16[256,1024]{1,0:T(8,128)(2,1)}, u32[]{:S(2)}, u32[]{:S(2)}) collective-permute-start(bf16[256,1024]{1,0:T(8,128)(2,1)} %get-tuple-element.163), channel_id=1, source_target_pairs={{0,16},{8,24},{16,0},{24,8},{1,17},{9,25},{17,1},{25,9},{2,18},{10... | collective-permute-start | bytes 1572872 | tf_op jit(solution)/shard_map/ppermute | solution.py:833
  412.2 78.5 %collective-permute-start.56 = (bf16[256,1024]{1,0:T(8,128)(2,1)}, bf16[256,1024]{1,0:T(8,128)(2,1)}, u32[]{:S(2)}, u32[]{:S(2)}) collective-permute-start(bf16[256,1024]{1,0:T(8,128)(2,1)} %get-tuple-element.162), channel_id=1, source_target_pairs={{0,24},{8,0},{16,8},{24,16},{1,25},{9,1},{17,9},{25,17},{2,26},{10... | collective-permute-start | bytes 1572872 | tf_op jit(solution)/shard_map/ppermute | solution.py:833
  454.2 21.3 %collective-permute-start.43 = (bf16[512,1536]{1,0:T(8,128)(2,1)}, bf16[512,1536]{1,0:T(8,128)(2,1)}, u32[]{:S(2)}, u32[]{:S(2)}) collective-permute-start(bf16[512,1536]{1,0:T(8,128)(2,1)} %gradient.16), channel_id=1, source_target_pairs={{0,2},{2,0},{1,3},{3,1},{4,6},{6,4},{5,7},{7,5},{8,10},{10,8},{9,1... | collective-permute-start | bytes 4718600 | tf_op jit(solution)/shard_map/ppermute | solution.py:765
  458.7 14.5 %collective-permute-start.46 = (bf16[256,1024]{1,0:T(8,128)(2,1)}, bf16[256,1024]{1,0:T(8,128)(2,1)S(1)}, u32[]{:S(2)}, u32[]{:S(2)}) collective-permute-start(bf16[256,1024]{1,0:T(8,128)(2,1)} %get-tuple-element.177), channel_id=1, source_target_pairs={{0,4},{4,0},{1,5},{5,1},{2,6},{6,2},{3,7},{7,3},{8,12},{12,8},{9,1... | collective-permute-start | bytes 1572872 | tf_op jit(solution)/shard_map/ppermute | solution.py:765
  473.2 48.1 %collective-permute-start.53 = (bf16[128,2048]{1,0:T(8,128)(2,1)}, bf16[128,2048]{1,0:T(8,128)(2,1)}, u32[]{:S(2)}, u32[]{:S(2)}) collective-permute-start(bf16[128,2048]{1,0:T(8,128)(2,1)} %get-tuple-element.173), channel_id=1, source_target_pairs={{0,4},{4,0},{1,5},{5,1},{2,6},{6,2},{3,7},{7,3},{8,12},{12,8},{9,1... | collective-permute-start | bytes 1572872 | tf_op jit(solution)/shard_map/ppermute | solution.py:765
  475.5 23.5 %collective-permute-start.48 = (bf16[512,1536]{1,0:T(8,128)(2,1)}, bf16[512,1536]{1,0:T(8,128)(2,1)}, u32[]{:S(2)}, u32[]{:S(2)}) collective-permute-start(bf16[512,1536]{1,0:T(8,128)(2,1)} %gradient.18), channel_id=1, source_target_pairs={{0,2},{2,0},{1,3},{3,1},{4,6},{6,4},{5,7},{7,5},{8,10},{10,8},{9,1... | collective-permute-start | bytes 4718600 | tf_op jit(solution)/shard_map/ppermute | solution.py:765
  489.4 52.1 %collective-permute-start.51 = (bf16[128,2048]{1,0:T(8,128)(2,1)}, bf16[128,2048]{1,0:T(8,128)(2,1)}, u32[]{:S(2)}, u32[]{:S(2)}) collective-permute-start(bf16[128,2048]{1,0:T(8,128)(2,1)} %get-tuple-element.175), channel_id=1, source_target_pairs={{0,1},{1,0},{2,3},{3,2},{4,5},{5,4},{6,7},{7,6},{8,9},{9,8},{10,11... | collective-permute-start | bytes 1572872 | tf_op jit(solution)/shard_map/ppermute | solution.py:765
  498.2 22.1 %collective-permute-start.80 = (bf16[128,1024]{1,0:T(8,128)(2,1)}, bf16[128,1024]{1,0:T(8,128)(2,1)}, u32[]{:S(2)}, u32[]{:S(2)}) collective-permute-start(bf16[128,1024]{1,0:T(8,128)(2,1)} %dynamic-slice_bitcast_fusion.17), channel_id=1, source_target_pairs={{0,1},{1,0},{2,3},{3,2},{4,5},{5,4},{6,7},{7,6},{8,9},{9,8},{10,11... | collective-permute-start | bytes 786440 | tf_op jit(solution)/shard_map/ppermute | solution.py:765
  499.0 39.6 %collective-permute-start.52 = (bf16[256,1536]{1,0:T(8,128)(2,1)}, bf16[256,1536]{1,0:T(8,128)(2,1)}, u32[]{:S(2)}, u32[]{:S(2)}) collective-permute-start(bf16[256,1536]{1,0:T(8,128)(2,1)} %get-tuple-element.171), channel_id=1, source_target_pairs={{0,4},{4,0},{1,5},{5,1},{2,6},{6,2},{3,7},{7,3},{8,12},{12,8},{9,1... | collective-permute-start | bytes 2359304 | tf_op jit(solution)/shard_map/ppermute | solution.py:765
  502.6 16.3 %collective-permute-start.66 = (f32[8,384]{1,0:T(8,128)S(1)}, f32[8,384]{1,0:T(8,128)S(1)}, u32[]{:S(2)}, u32[]{:S(2)}) collective-permute-start(f32[8,384]{1,0:T(8,128)S(1)} %fusion.34), channel_id=1, source_target_pairs={{0,4},{4,0},{1,5},{5,1},{2,6},{6,2},{3,7},{7,3},{8,12},{12,8},{9,1... | collective-permute-start | bytes 36872 | tf_op jit(solution)/shard_map/ppermute | solution.py:765
  530.9 25.9 %collective-permute-start.50 = (bf16[128,1024]{1,0:T(8,128)(2,1)S(1)}, bf16[128,1024]{1,0:T(8,128)(2,1)S(1)}, u32[]{:S(2)}, u32[]{:S(2)}) collective-permute-start(bf16[128,1024]{1,0:T(8,128)(2,1)S(1)} %copy-done.75), channel_id=1, source_target_pairs={{0,1},{1,0},{2,3},{3,2},{4,5},{5,4},{6,7},{7,6},{8,9},{9,8},{10,11... | collective-permute-start | bytes 786440 | tf_op jit(solution)/shard_map/ppermute | solution.py:765
  534.6 86.7 %collective-permute-start.47 = (bf16[592,1024]{1,0:T(8,128)(2,1)}, bf16[592,1024]{1,0:T(8,128)(2,1)}, u32[]{:S(2)}, u32[]{:S(2)}) collective-permute-start(bf16[592,1024]{1,0:T(8,128)(2,1)} %fusion.10), channel_id=1, source_target_pairs={{0,1},{1,0},{2,3},{3,2},{4,5},{5,4},{6,7},{7,6},{8,9},{9,8},{10,11... | collective-permute-start | bytes 3637256 | tf_op jit(solution)/shard_map/ppermute | solution.py:765
  552.2 29.1 %collective-permute-start.49 = (bf16[256,1536]{1,0:T(8,128)(2,1)S(1)}, bf16[256,1536]{1,0:T(8,128)(2,1)S(1)}, u32[]{:S(2)}, u32[]{:S(2)}) collective-permute-start(bf16[256,1536]{1,0:T(8,128)(2,1)S(1)} %bitcast.227), channel_id=1, source_target_pairs={{0,1},{1,0},{2,3},{3,2},{4,5},{5,4},{6,7},{7,6},{8,9},{9,8},{10,11... | collective-permute-start | bytes 2359304 | tf_op jit(solution)/shard_map/ppermute | solution.py:765
  563.1 25.4 %collective-permute-start.58 = (bf16[128,1536]{1,0:T(8,128)(2,1)S(1)}, bf16[128,1536]{1,0:T(8,128)(2,1)S(1)}, u32[]{:S(2)}, u32[]{:S(2)}) collective-permute-start(bf16[128,1536]{1,0:T(8,128)(2,1)S(1)} %get-tuple-element.181), channel_id=1, source_target_pairs={{0,1},{1,0},{2,3},{3,2},{4,5},{5,4},{6,7},{7,6},{8,9},{9,8},{10,11... | collective-permute-start | bytes 1179656 | tf_op jit(solution)/shard_map/ppermute | solution.py:765
  (154 other events, 1464.2 us)

commit v6 on v5

--- a/solution.py
+++ b/solution.py
@@ -361,7 +361,8 @@
     return lax.broadcasted_iota(jnp.int32, (rows, PAIR), 1) < HD
 
 
-def forward_kernel(query_ref, key_ref, value_ref, bias_ref, attended_ref, log_ref):
+def forward_kernel(query_ref, key_ref, value_ref, bias_ref, *refs):
+    attended_ref, log_ref = refs[-2:]
     rows = query_ref.shape[1]
     first = half_mask(rows)
     zero = jnp.zeros((rows, PAIR), jnp.bfloat16)
@@ -428,26 +429,29 @@
     return pl.BlockSpec((1, rows, PAIR), lambda i: (part, 0, i))
 
 
-def attention_forward(joined, bias):
+def attention_forward(joined, bias, total, first_pair, base=None):
     rows, width = joined.shape[1:]
     pairs = width // PAIR
+    extra = [] if base is None else [base]
     return pl.pallas_call(
         forward_kernel,
         grid=(pairs,),
         in_specs=[pair_spec(rows, part) for part in range(3)]
-        + [pl.BlockSpec((rows, rows), lambda i: (0, 0))],
+        + [pl.BlockSpec((rows, rows), lambda i: (0, 0))]
+        + [pl.BlockSpec(memory_space=pl.ANY) for _ in extra],
         out_specs=[
-            pl.BlockSpec((rows, PAIR), lambda i: (0, i)),
+            pl.BlockSpec((rows, PAIR), lambda i: (0, first_pair + i)),
             pl.BlockSpec((1, 2, rows), lambda i: (i, 0, 0)),
         ],
         out_shape=[
-            jax.ShapeDtypeStruct((rows, width), jnp.bfloat16),
+            jax.ShapeDtypeStruct((rows, total), jnp.bfloat16),
             jax.ShapeDtypeStruct((pairs, 2, rows), jnp.float32),
         ],
+        input_output_aliases={4: 0} if extra else {},
         compiler_params=limit(32),
         cost_estimate=HINT,
         name="attention_forward",
-    )(joined, joined, joined, bias)
+    )(joined, joined, joined, bias, *extra)
 
 
 def attention_backward(joined, d_attended, first_pair, log_total, bias):
@@ -560,7 +564,7 @@
         out_specs=whole_spec((rows, width)),
         out_shape=jax.ShapeDtypeStruct((rows, width), jnp.bfloat16),
         scratch_shapes=[pltpu.VMEM((rows, width), jnp.float32)],
-        compiler_params=limit(24),
+        compiler_params=limit(52),
         cost_estimate=HINT,
         name="last_layer",
     )(active, weight, middle, bias[None, :])
@@ -788,6 +792,10 @@
     return blocks | {key | {axis}: trade(block, axis) for key, block in blocks.items()}
 
 
+def tie_received(blocks, other):
+    return {key: after(block, other) if key else block for key, block in blocks.items()}
+
+
 def places(blocks, axes):
     indices = []
     for key in blocks:
@@ -806,7 +814,6 @@
 
 
 OWN = frozenset()
-X, Y, XY = frozenset({"x"}), frozenset({"ctx"}), frozenset({"x", "ctx"})
 
 
 def send_half(matrix, axis, outer=1):
@@ -874,13 +881,16 @@
 
         inputs_far = swap(inputs)
         segment_far = swap(segment)
-        small = jnp.concatenate(
-            [b_query, b_value, b_out, norm1_gain, norm1_shift, norm2_gain, norm2_shift, b_down, b_up]
+        shard_rows = w_qkv.shape[0] // 8
+        small = [b_query, b_value, b_out, norm1_gain, norm1_shift, norm2_gain, norm2_shift, b_down]
+        small = jnp.concatenate([jnp.stack(small), b_up.reshape(-1, near_width)], axis=0)
+        small_rows = small.shape[0]
+        pad_small = lambda table: jnp.pad(
+            table,
+            [(0, 0)] * (table.ndim - 2)
+            + [(0, shard_rows - small_rows), (0, 128 - near_width)],
         )
-        shard_rows = w_qkv.shape[0] // 8
-        small_count = small.shape[0]
-        small_rows = round_up(small_count, 128) // 128
-        small = jnp.pad(small, (0, shard_rows * 128 - small_count)).reshape(shard_rows, 128)
+        small = pad_small(small)
         shard_qkv = unfold(w_qkv).reshape(shard_rows, 3, 2, half_width)
         halves = [shard_qkv[:, :, side].reshape(shard_rows, 3 * half_width) for side in range(2)]
         half_qkv = 3 * half_width
@@ -896,7 +906,8 @@
         far_one, far_two = after(far_one, inputs_far), after(far_two, inputs_far)
         one = spread(spread({OWN: far_one}, "x"), "ctx")
         two = spread(spread({OWN: far_two}, "ctx"), "x")
-        shard_down = after(to_local(unfold(w_down), 1, far), far_up[0])
+        all_one = list(one.values()) + list(two.values())
+        shard_down = after(to_local(unfold(w_down), 1, far), far_up[0], *all_one)
         near_down = order_blocks(spread({OWN: shard_down}, "ctx"), ["ctx"])
         one_core, two_core = spread(one, "core"), spread(two, "core")
         axes = ["core", "x", "ctx"]
@@ -908,22 +919,21 @@
             routes,
         )
         qkv_two = order_blocks(two_core, axes)
-        up_one = spread(spread({OWN: after(far_up[0], one[XY])}, "x"), "ctx")
-        up_two = spread(spread({OWN: after(far_up[1], two[XY])}, "ctx"), "x")
+        up_one = spread({OWN: after(far_up[0], *all_one)}, "x")
+        up_two = spread({OWN: after(far_up[1], *all_one)}, "ctx")
+        up_one = spread(tie_received(up_one, qkv_one), "ctx")
+        up_two = spread(tie_received(up_two, qkv_one), "x")
         far_down = gather_far(near_down, far)[0]
 
         devices = 8 * far
-        small_core = small_local.reshape(devices, shard_rows, 128)[:, :small_rows]
-        small_core = small_core.astype(jnp.float32).reshape(devices, -1)
+        small_core = small_local.reshape(devices, shard_rows, 128)[:, :small_rows, :near_width]
+        small_core = small_core.astype(jnp.float32)
         small_all = to_natural(small_core, 0, far)
-        piece = lambda table, index: table[:, index * near_width : (index + 1) * near_width].reshape(-1)
-        query_bias = piece(small_all, 0)
-        value_bias = piece(small_all, 1)
+        query_bias, value_bias = (small_all[:, index].reshape(-1) for index in range(2))
         out_bias, first_gain, first_shift, second_gain, second_shift, down_bias = (
-            piece(small_core, index) for index in range(2, 8)
+            small_core[:, index].reshape(-1) for index in range(2, 8)
         )
-        up_bias = small_all[:, 8 * near_width : small_count].reshape(-1)
-        up_bias = hidden_to_local(up_bias, 0, far)
+        up_bias = hidden_to_local(small_all[:, 8:].reshape(-1), 0, far)
 
         slot = jnp.arange(slots)
         earlier = slot[:, None] < slot[None, :]
@@ -960,7 +970,8 @@
 
         def give(both, *follow):
             near, other = both
-            return matmul(give_near, near) + matmul(give_far, after(other, *follow))
+            other = after(other, *follow) if follow else other
+            return matmul(give_near, near) + matmul(give_far, other)
 
         kind = (row >= SEQ).astype(jnp.int32) + (row >= SEQ + pads).astype(jnp.int32)
         bias = jnp.where(kind[:, None] == kind[None, :], 0.0, -1e30).astype(jnp.float32)
@@ -975,8 +986,9 @@
             for cut in (slice(0, half_width), slice(half_width, width))
         ]
         joined_one = project(normed1, qkv_one, joined_bias[0])
-        attended_one, log_one = attention_forward(after(joined_one, near_down), bias)
-        joined_two = project(after(normed1, attended_one), qkv_two, joined_bias[1])
+        attended, log_one = attention_forward(after(joined_one, near_down), bias, width, 0)
+        joined_two = project(after(normed1, log_one), qkv_two, joined_bias[1])
+        up_one, up_two = tie_received(up_one, log_one), tie_received(up_two, log_one)
         up_near = assemble(
             list(up_one.values()) + list(up_two.values()),
             places(up_one, ["x", "ctx"]) + places(up_two, ["x", "ctx"]),
@@ -984,8 +996,9 @@
             [[(0, up_cut, 0, 0)]] * 4 + [[(0, up_cut, 0, up_cut)]] * 4,
         )[0]
         up_blocks = spread({OWN: up_near}, "core")
-        attended_two, log_two = attention_forward(joined_two, bias)
-        attended = jnp.concatenate([attended_one, attended_two], axis=1)
+        attended, log_two = attention_forward(
+            joined_two, bias, width, half_width // PAIR, attended
+        )
         cotangent_far = swap(after(cotangent, up_near))
         down_blocks = spread({OWN: after(far_down, up_near)}, "x")
         out_rows, up_weight = assemble(
@@ -1035,68 +1048,63 @@
         d_one = attention_backward(joined_one, d_attended, 0, log_one, bias)
         one_core = trade(gradient(normed1, d_one, 1 - core), "core")
         partial = d_normed(d_one, qkv_one)
-        d_two = attention_backward(
-            joined_two, after(d_attended, partial), half_width // PAIR, log_two, bias
-        )
+        up_one = send_half(add_half(up_one, partial), "x")
+        up_two = send_half(add_half(up_two, partial), "ctx")
+        out_y = send_half(add_half(out_x, partial), "ctx")
+        d_attended = after(d_attended, partial, up_one[0], up_two[0], out_y[0])
+        d_two = attention_backward(joined_two, d_attended, half_width // PAIR, log_two, bias)
         two_core = trade(gradient(normed1, d_two, 1 - core), "core")
         qkv_one_x = send_half(gradient(normed1, d_one, core, got=after(one_core, d_two)), "x")
-        up_one = send_half(add_half(up_one, d_two), "x")
-        up_two = send_half(add_half(up_two, d_two), "ctx")
-        out_y = send_half(add_half(out_x, d_two), "ctx")
-        d_two_tied = after(d_two, qkv_one_x[0], up_one[0], up_two[0], out_y[0])
+        down_y = send_half(add_far(down_far, d_two).astype(jnp.bfloat16), "ctx")
+        d_two_tied = after(d_two, qkv_one_x[0], down_y[0])
         d_normed1 = d_normed(d_two_tied, qkv_two, partial)
         d_last = d_middle + norm_backward(d_normed1, normal1, scale1, first_gain)
         d_last_given = to_give(d_last)
-        qkv_two_y = send_half(
-            gradient(normed1, d_two, core, got=after(two_core, d_last_given[0])), "ctx", 2
-        )
-        down_y = send_half(add_far(down_far, d_last_given[0]).astype(jnp.bfloat16), "ctx")
-        up_one_far = send_far(add_half(up_one, qkv_two_y[0], down_y[0]), far)
-        qkv_one_y = send_half(add_half(qkv_one_x, up_one_far[0]), "ctx")
-        up_two_far = send_far(add_half(up_two, qkv_one_y[0]), far)
-        out_far = send_far(add_half(out_y, up_two_far[0]), far)
-        qkv_two_x = send_half(add_half(qkv_two_y, out_far[0]), "x")
-        qkv_one_far = send_far(add_half(qkv_one_y, qkv_two_x[0]), far)
-        qkv_two_far = send_far(add_half(qkv_two_x, qkv_one_far[0]), far)
-
-        part = lambda vector: vector.reshape(devices, -1)
-        core_sums = jnp.concatenate(
-            [
-                part(column_sums(array))
-                for array in (
-                    d_branch,
-                    d_normed1 * normal1,
-                    d_normed1,
-                    d_normed2 * normal2,
-                    d_normed2,
-                    d_out_low,
-                )
-            ],
+        qkv_two = gradient(normed1, d_two, core, got=after(two_core, d_last_given[0]))
+
+        vectors = [
+            column_sums(array)
+            for array in (
+                d_branch,
+                d_normed1 * normal1,
+                d_normed1,
+                d_normed2 * normal2,
+                d_normed2,
+                d_out_low,
+            )
+        ]
+        joined_vectors = [
+            jnp.concatenate([column_sums(d_one[index]), column_sums(d_two[index])])
+            for index in (0, 2)
+        ]
+        vectors = [to_local(vector, 0, far) for vector in joined_vectors] + vectors
+        table = jnp.stack([vector.reshape(devices, near_width) for vector in vectors], axis=1)
+        up_sums = to_local(hidden_to_natural(up_sums[0], 0, far), 0, far)
+        table = jnp.concatenate([table, up_sums.reshape(devices, -1, near_width)], axis=1)
+        table = pad_small(table).reshape(width, 128).astype(jnp.bfloat16)
+        qkv_two_y = send_half(qkv_two, "ctx", 2)
+        qkv_one_y = send_half(add_half(qkv_one_x, d_last_given[0]), "ctx")
+        table = send_half(add_half(send_half(table, "core")), "ctx", 2)
+        up_far = jnp.concatenate(
+            [add_half(halves, qkv_two_y[0], qkv_one_y[0]) for halves in (up_one, up_two, out_y)],
             axis=1,
         )
-        joined_sums = [
-            part(jnp.concatenate([column_sums(d_one[index]), column_sums(d_two[index])]))
-            for index in (0, 2)
-        ]
-        joined_sums = jnp.concatenate(joined_sums, axis=1)
-        up_sums = part(hidden_to_natural(up_sums[0], 0, far))
-        small_sums = jnp.concatenate(
-            [to_local(joined_sums, 0, far), core_sums, to_local(up_sums, 0, far)], axis=1
-        )
-        for axis in axes:
-            small_sums = add_half(send_half(small_sums, axis))
-        small_sums = add_far(send_far(small_sums, far))[0]
+        up_far = send_far(up_far, far)
+        qkv_two = jnp.concatenate([add_half(qkv_two_y), add_half(table)], axis=1)
+        qkv_two_x = send_half(qkv_two, "x")
+        qkv_one_far = send_far(add_half(qkv_one_y), far)
+        qkv_two_far = send_far(add_half(qkv_two_x), far)
 
         sum_down = add_half(down_y).astype(jnp.float32)
-        sum_up = jnp.concatenate([add_far(up_one_far), add_far(up_two_far)], axis=1)
-        sum_out = add_far(out_far)
-        sum_qkv = [
-            add_far(arrays).reshape(shard_rows, 3, 1, half_width)
-            for arrays in (qkv_one_far, qkv_two_far)
-        ]
-        sum_qkv = jnp.concatenate(sum_qkv, axis=2).reshape(shard_rows, 3 * width)
-        input_grad = give(d_last_given, qkv_two_far[0])
-        own = lambda index: small_sums[index * near_width : (index + 1) * near_width]
+        sum_up = add_far(up_far)
+        sum_up, sum_out = sum_up[:, :up_width], sum_up[:, up_width:]
+        sum_one, sum_two = add_far(qkv_one_far), add_far(qkv_two_far)
+        small_sums = sum_two[:small_rows, half_qkv : half_qkv + near_width]
+        cut_qkv = lambda matrix: matrix[:, :half_qkv].reshape(shard_rows, 3, 1, half_width)
+        sum_qkv = jnp.concatenate([cut_qkv(sum_one), cut_qkv(sum_two)], axis=2)
+        sum_qkv = sum_qkv.reshape(shard_rows, 3 * width)
+        input_grad = give(d_last_given)
+        own = lambda index: small_sums[index]
         back = lambda matrix: refold(to_natural(matrix, 1, far))
         return (
             outputs,
@@ -1111,7 +1119,7 @@
             own(5),
             own(6),
             refold(hidden_to_natural(sum_up, 1, far)),
-            small_sums[8 * near_width :],
+            small_sums[8:].reshape(-1),
             back(sum_down),
             own(7),
         )

time: 630 us -> 629 us (level)
  starting transfers between devices: 101 us -> 82.3 us
  waiting for transfers between devices: 169 us -> 177 us
    ppermute x51 -> x50, waiting for transfers between devices: 119 us -> 161 us  [trade(): return lax.ppermute(array, axis, [(0, 1), (1, 0)])]
    ppermute x21 -> x12, starting transfers between devices: 42.3 us -> 22.6 us  [send_far(): lax.ppermute(sent, 'z', [(i, (i + step) % far) for i in range(far)])]
    ppermute x9, waiting for transfers between devices: 32.8 us -> 14.5 us  [gather_far(): lax.ppermute(shard, 'z', [(i, (i + step) % far) for i in range(far)])]
    ppermute x21 -> x12, waiting for transfers between devices: 17.1 us -> 1.55 us  [send_far(): lax.ppermute(sent, 'z', [(i, (i + step) % far) for i in range(far)])]
    concatenate x9 -> x3, local copies, waits for them, and re-layouts: 11 us -> 1.36 us  [the longest x1 0.82 us: on_device(): jnp.concatenate([jnp.stack(small), b_up.reshape(-1, near_width)], axis=0)]
    dot_general x11, matrix products: 43.3 us -> 35.4 us  [matmul(): return jnp.dot(left, right, preferred_element_type=jnp.float32)]
    convert_element_type x12 -> x14, other arithmetic: 11.9 us -> 16.3 us  [add_half(): (kept.astype(jnp.float32) + got.astype(jnp.float32)).astype(kept.dtype)]
    ppermute x51 -> x50, starting transfers between devices: 35.3 us -> 38.1 us  [trade(): return lax.ppermute(array, axis, [(0, 1), (1, 0)])]
  transfers between devices with their start and end apart: 81 -> 71, of which waited for: 27 -> 23; matrix products, arithmetic and copies ran while one was open for 21% -> 21% of each run, Pallas kernels for 25% -> 25%
where the time goes in v6:
time: 629 us; the launch traced here: 623 us
  Pallas kernels  183 us (29%)
  waiting for transfers between devices  177 us (28%)
  local copies, waits for them, and re-layouts  94.9 us (15%)
  starting transfers between devices  82.3 us (13%)
  matrix products  43 us (7%)
  other arithmetic  40 us (6%)
    ppermute x50, waiting for transfers between devices, trade(): return lax.ppermute(array, axis, [(0, 1), (1, 0)])  161 us
    pallas_call x10, Pallas kernels, gradient(): pl.pallas_call(gradient_kernel, grid_spec=pltpu.PrefetchScalarGridSpec(nu...  39.7 us
    ppermute x50, starting transfers between devices, trade(): return lax.ppermute(array, axis, [(0, 1), (1, 0)])  38.1 us
    dot_general x11, matrix products, matmul(): return jnp.dot(left, right, preferred_element_type=jnp.float32)  35.4 us
    unnamed x244, local copies, waits for them, and re-layouts  34.4 us
    pallas_call x9, Pallas kernels, assemble(): pl.pallas_call(functools.partial(assemble_kernel, routes), in_specs=[pl.B...  30.3 us
    pallas_call x2, Pallas kernels, attention_backward(): pl.pallas_call(backward_kernel, grid=(width // PAIR,), in_specs=[pair_spe...  27 us
    pallas_call x2, Pallas kernels, attention_forward(): pl.pallas_call(forward_kernel, grid=(pairs,), in_specs=[pair_spec(rows, p...  26.9 us
  transfers between devices with their start and end apart: 71, of which 23 were waited for; matrix products, arithmetic and copies ran while one was open for 21% of the time, Pallas kernels for 25%

profile of v6, /device:TPU:0, one launch (start us, length us, event | category | flops | bytes accessed | tf_op | source)
XLA Modules:
  0.0 622.8 jit_solution(3106109753871812146)
XLA Ops:
  16.9 3.5 copy.122
  21.2 17.7 %collective-permute-done = s32[584]{0:T(1024)S(1)} collective-permute-done((s32[584]{0:T(1024)}, s32[584]{0:T(1024)S(1)}, u32[]{:S(2)}, u32[]{:S(2)}) %collective-permute-start) | collective-permute-done | bytes 2368 | tf_op jit(solution)/shard_map/ppermute | solution.py:769
  50.0 3.8 fusion.12
  57.1 11.2 %collective-permute-done.13.refs_2_ = bf16[32,5120]{1,0:T(8,128)(2,1)S(1)} collective-permute-done((bf16[32,5120]{1,0:T(8,128)(2,1)S(1)}, bf16[32,5120]{1,0:T(8,128)(2,1)S(1)}, u32[]{:S(2)}, u32[]{:S(2)}) %collective-permute-start.13) | collective-permute-done | bytes 327712 | tf_op jit(solution)/shard_map/ppermute | solution.py:780
  75.5 5.8 fusion.45
  81.4 10.6 %collective-permute-done.15.refs_1_ = bf16[128,1536]{1,0:T(8,128)(2,1)} collective-permute-done((bf16[128,1536]{1,0:T(8,128)(2,1)}, bf16[128,1536]{1,0:T(8,128)(2,1)}, u32[]{:S(2)}, u32[]{:S(2)}) %collective-permute-start.15) | collective-permute-done | bytes 393248 | tf_op jit(solution)/shard_map/ppermute | solution.py:769
  94.1 4.8 collective-permute-done.7.refs_3_
  112.9 6.0 collective-permute-done.26.refs_5_
  125.6 12.9 %collective-permute-done.18.refs_1_ = bf16[128,1024]{1,0:T(8,128)(2,1)} collective-permute-done((bf16[128,1024]{1,0:T(8,128)(2,1)S(1)}, bf16[128,1024]{1,0:T(8,128)(2,1)}, u32[]{:S(2)}, u32[]{:S(2)}) %collective-permute-start.18) | collective-permute-done | bytes 262176 | tf_op jit(solution)/shard_map/ppermute | solution.py:769
  142.8 13.5 %attention_forward.2 = (bf16[592,1024]{1,0:T(8,128)(2,1)S(1)}, f32[4,2,592]{2,1,0:T(2,128)S(1)}) custom-call(bf16[3,592,512]{2,1,0:T(8,128)(2,1)S(1)} %project.2.query_ref.key_ref.value_ref, bf16[3,592,512]{2,1,0:T(8,128)(2,1)S(1)} %project.2.query_ref.key_ref.value_ref, bf16[3,592,512]{2,1,0:T(8,128)(2,1)S(1)} %project.2.query_ref.key_ref.value_ref, ...), custom_call_target="tpu_custom_call" | custom-call | flops 1 | bytes 1 | tf_op jit(solution)/shard_map/attention_forward/pallas_call | solution.py:436
  156.4 5.2 assemble.14.refs_0_
  164.3 4.6 collective-permute-done.19.refs_4_
  172.2 7.6 %collective-permute-start.30 = (bf16[256,1024]{1,0:T(8,128)(2,1)S(1)}, bf16[256,1024]{1,0:T(8,128)(2,1)}, u32[]{:S(2)}, u32[]{:S(2)}) collective-permute-start(bf16[256,1024]{1,0:T(8,128)(2,1)S(1)} %assemble.12.refs_0_), channel_id=1, source_target_pairs={{0,8},{8,16},{16,24},{24,0},{1,9},{9,17},{17,25},{25,1},{2,10},{10... | collective-permute-start | bytes 1572872 | tf_op jit(solution)/shard_map/ppermute | solution.py:780
  184.0 3.8 fusion.11
  193.9 13.4 %attention_forward.3 = (bf16[592,1024]{1,0:T(8,128)(2,1)S(1)}, f32[4,2,592]{2,1,0:T(2,128)S(1)}) custom-call(bf16[3,592,512]{2,1,0:T(8,128)(2,1)S(1)} %project.3.query_ref.key_ref.value_ref, bf16[3,592,512]{2,1,0:T(8,128)(2,1)S(1)} %project.3.query_ref.key_ref.value_ref, ...), custom_call_target="tpu_custom_call", output_to_operand_aliasing={{0}: (4, {})} | custom-call | flops 1 | bytes 1 | tf_op jit(solution)/shard_map/attention_forward/pallas_call | solution.py:436
  224.2 6.3 %fusion.41 = (bf16[1024]{0:T(1024)(128)(2,1)S(1)}, bf16[592,1024]{1,0:T(8,128)(2,1)}, f32[592,1024]{1,0:T(8,128)}) fusion(f32[592]{0:T(1024)} %fusion.40, s32[1024]{0:T(1024)} %copy-done.106, f32[592,1024]{1,0:T(8,128)} %fusion.11, bf16[584,1024]{1,0:T(8,128)(2,1)} %collective-permute-done.37, s32[584]{0:T(1024)} %copy-done.109), kind=kOutput, calls=%fused_computation.183 | convolution fusion | flops 1953989248 | bytes 7268960 | tf_op jit(solution)/shard_map/dot_general | solution.py:28
  230.4 5.6 assemble.15
  243.8 18.1 %hidden_layer.1 = (bf16[592,4096]{1,0:T(8,128)(2,1)S(1)}, bf16[592,4096]{1,0:T(8,128)(2,1)S(1)}) custom-call(bf16[592,1024]{1,0:T(8,128)(2,1)S(1)} %add_convert_fusion.3.x_ref, bf16[1024,4096]{1,0:T(8,128)(2,1)S(1)} %get-tuple-element.100.weight_ref, f32[1,4096]{1,0:T(1,128)S(1)} %bitcast.212), custom_call_target="tpu_custom_call" | custom-call | flops 1 | bytes 1 | tf_op jit(solution)/shard_map/hidden_layer/pallas_call | solution.py:522
  262.0 7.7 %gradient.10 = bf16[2048,1024]{1,0:T(8,128)(2,1)} custom-call(s32[1]{0:T(128)} %bitcast.31.index_ref, bf16[592,4096]{1,0:T(8,128)(2,1)S(1)} %get-tuple-element.101.active_ref.x_ref, bf16[592,1024]{1,0:T(8,128)(2,1)S(1)} %copy-done.30), custom_call_target="tpu_custom_call" | custom-call | flops 1 | bytes 1 | tf_op jit(solution)/shard_map/gradient/pallas_call | solution.py:662
  270.8 9.3 %collective-permute-done.35.refs_3_ = bf16[1024,1024]{1,0:T(8,128)(2,1)} collective-permute-done((bf16[1024,1024]{1,0:T(8,128)(2,1)}, bf16[1024,1024]{1,0:T(8,128)(2,1)}, u32[]{:S(2)}, u32[]{:S(2)}) %collective-permute-start.35) | collective-permute-done | bytes 2097184 | tf_op jit(solution)/shard_map/ppermute | solution.py:769
  283.1 4.2 assemble.17.weight_ref
  287.4 3.3 copy-done.5
  290.7 11.5 %last_layer.1 = bf16[592,1024]{1,0:T(8,128)(2,1)S(1)} custom-call(bf16[592,4096]{1,0:T(8,128)(2,1)} %copy-done.10, bf16[4096,1024]{1,0:T(8,128)(2,1)} %copy-done.5, f32[592,1024]{1,0:T(8,128)} %copy-done.60, f32[1,1024]{1,0:T(1,128)S(1)} %broadcast_in_dim_reshape_squeeze.2.bias_ref), custom_call_target="tpu_custom_call" | custom-call | flops 1 | bytes 1 | tf_op jit(solution)/shard_map/last_layer/pallas_call | solution.py:555
  307.3 7.6 %gradient.11 = bf16[2048,1024]{1,0:T(8,128)(2,1)S(1)} custom-call(s32[1]{0:T(128)} %bitcast.30.index_ref, bf16[592,4096]{1,0:T(8,128)(2,1)S(1)} %copy-done.11, bf16[592,1024]{1,0:T(8,128)(2,1)S(1)} %copy-done.31, bf16[2048,1024]{1,0:T(8,128)(2,1)} %collective-permute-done.38.refs_0_), custom_call_target="tpu_custom_call" | custom-call | flops 1 | bytes 1 | tf_op jit(solution)/shard_map/gradient/pallas_call | solution.py:662
  318.8 7.8 %d_hidden_layer.1 = (bf16[592,4096]{1,0:T(8,128)(2,1)S(1)}, f32[1,4096]{1,0:T(1,128)S(1)}) custom-call(bf16[592,1024]{1,0:T(8,128)(2,1)S(1)} %copy-done.31, bf16[4096,1024]{1,0:T(8,128)(2,1)S(1)} %bitcast.205, bf16[592,4096]{1,0:T(8,128)(2,1)S(1)} %copy-done.36), custom_call_target="tpu_custom_call" | custom-call | flops 1 | bytes 1 | tf_op jit(solution)/shard_map/d_hidden_layer/pallas_call | solution.py:584
  326.6 3.3 gradient.14
  334.4 3.3 gradient.12
  340.6 3.4 copy-done.23
  344.0 9.4 %d_normed.3 = f32[592,1024]{1,0:T(8,128)S(1)} custom-call(bf16[592,4096]{1,0:T(8,128)(2,1)S(1)} %copy-done.2, bf16[1024,4096]{1,0:T(8,128)(2,1)S(1)} %copy-done.23), custom_call_target="tpu_custom_call" | custom-call | flops 1 | bytes 1 | tf_op jit(solution)/shard_map/d_normed/pallas_call | solution.py:625
  357.2 4.8 fusion.42
  362.9 3.5 gradient.15
  372.7 3.3 gradient.13
  378.6 23.6 %collective-permute-done.42 = bf16[1024,1024]{1,0:T(8,128)(2,1)} collective-permute-done((bf16[1024,1024]{1,0:T(8,128)(2,1)}, bf16[1024,1024]{1,0:T(8,128)(2,1)}, u32[]{:S(2)}, u32[]{:S(2)}) %collective-permute-start.42) | collective-permute-done | bytes 2097184 | tf_op jit(solution)/shard_map/ppermute | solution.py:769
  409.8 6.3 %collective-permute-start.47 = (bf16[256,1024]{1,0:T(8,128)(2,1)}, bf16[256,1024]{1,0:T(8,128)(2,1)}, u32[]{:S(2)}, u32[]{:S(2)}) collective-permute-start(bf16[256,1024]{1,0:T(8,128)(2,1)} %get-tuple-element.161), channel_id=1, source_target_pairs={{0,8},{8,16},{16,24},{24,0},{1,9},{9,17},{17,25},{25,1},{2,10},{10... | collective-permute-start | bytes 1572872 | tf_op jit(solution)/shard_map/ppermute | solution.py:840
  416.1 3.5 collective-permute-start.48
  419.6 3.4 add_convert_fusion.6
  428.2 13.6 %attention_backward.2.d_ref = bf16[3,592,512]{2,1,0:T(8,128)(2,1)S(1)} custom-call(bf16[3,592,512]{2,1,0:T(8,128)(2,1)S(1)} %copy-done.4, bf16[3,592,512]{2,1,0:T(8,128)(2,1)S(1)} %copy-done.4, bf16[3,592,512]{2,1,0:T(8,128)(2,1)S(1)} %copy-done.4, bf16[592,1024]{1,0:T(8,128)(2,1)S(1)} %copy-done.37, f32[4,2,592]{2,1,0:T(2,128)S(1)} %copy-done.52, ...), custom_call_target="tpu_custom_call" | custom-call | flops 1 | bytes 1 | tf_op jit(solution)/shard_map/attention_backward/pallas_call | solution.py:459
  447.8 3.3 d_normed.4.refs_0_
  471.4 13.4 %attention_backward.3.d_ref = bf16[3,592,512]{2,1,0:T(8,128)(2,1)S(1)} custom-call(bf16[3,592,512]{2,1,0:T(8,128)(2,1)S(1)} %project.3.query_ref.key_ref.value_ref, bf16[3,592,512]{2,1,0:T(8,128)(2,1)S(1)} %project.3.query_ref.key_ref.value_ref, bf16[3,592,512]{2,1,0:T(8,128)(2,1)S(1)} %project.3.query_ref.key_ref.value_ref, ...), custom_call_target="tpu_custom_call" | custom-call | flops 1 | bytes 1 | tf_op jit(solution)/shard_map/attention_backward/pallas_call | solution.py:459
  493.1 11.6 %collective-permute-done.70 = bf16[128,1024]{1,0:T(8,128)(2,1)S(1)} collective-permute-done((bf16[128,1024]{1,0:T(8,128)(2,1)S(1)}, bf16[128,1024]{1,0:T(8,128)(2,1)S(1)}, u32[]{:S(2)}, u32[]{:S(2)}) %collective-permute-start.70) | collective-permute-done | bytes 262176 | tf_op jit(solution)/shard_map/ppermute | solution.py:769
  507.3 4.0 reshape.568
  516.4 3.4 d_normed.5
  522.6 5.1 fusion.10
  529.6 11.0 %collective-permute-done.51 = bf16[256,1536]{1,0:T(8,128)(2,1)} collective-permute-done((bf16[256,1536]{1,0:T(8,128)(2,1)}, bf16[256,1536]{1,0:T(8,128)(2,1)}, u32[]{:S(2)}, u32[]{:S(2)}) %collective-permute-start.51) | collective-permute-done | bytes 786464 | tf_op jit(solution)/shard_map/ppermute | solution.py:769
  550.1 6.9 %collective-permute-done.52 = bf16[128,1536]{1,0:T(8,128)(2,1)S(1)} collective-permute-done((bf16[128,1536]{1,0:T(8,128)(2,1)S(1)}, bf16[128,1536]{1,0:T(8,128)(2,1)S(1)}, u32[]{:S(2)}, u32[]{:S(2)}) %collective-permute-start.52) | collective-permute-done | bytes 393248 | tf_op jit(solution)/shard_map/ppermute | solution.py:769
  565.7 17.3 %collective-permute-done.50 = bf16[592,1024]{1,0:T(8,128)(2,1)S(1)} collective-permute-done((bf16[592,1024]{1,0:T(8,128)(2,1)S(1)}, bf16[592,1024]{1,0:T(8,128)(2,1)S(1)}, u32[]{:S(2)}, u32[]{:S(2)}) %collective-permute-start.50) | collective-permute-done | bytes 1212448 | tf_op jit(solution)/shard_map/ppermute | solution.py:769
  586.9 9.2 %collective-permute-done.57 = bf16[256,1536]{1,0:T(8,128)(2,1)S(1)} collective-permute-done((bf16[256,1536]{1,0:T(8,128)(2,1)S(1)}, bf16[256,1536]{1,0:T(8,128)(2,1)S(1)}, u32[]{:S(2)}, u32[]{:S(2)}) %collective-permute-start.57) | collective-permute-done | bytes 786464 | tf_op jit(solution)/shard_map/ppermute | solution.py:769
  601.8 6.1 collective-permute-done.60
  (537 shorter events, 241.0 us)
Async XLA Ops:
  4.4 35.9 %collective-permute-start.2 = (bf16[32,3200]{1,0:T(8,128)(2,1)S(1)}, bf16[32,3200]{1,0:T(8,128)(2,1)S(1)}, u32[]{:S(2)}, u32[]{:S(2)}) collective-permute-start(bf16[32,3200]{1,0:T(8,128)(2,1)S(1)} %fusion.36.refs_0_), channel_id=1, source_target_pairs={{0,8},{8,16},{16,24},{24,0},{1,9},{9,17},{17,25},{25,1},{2,10},{10... | collective-permute-start | bytes 614408 | tf_op jit(solution)/shard_map/ppermute | solution.py:780
  7.4 32.8 %collective-permute-start.3 = (bf16[32,3200]{1,0:T(8,128)(2,1)S(1)}, bf16[32,3200]{1,0:T(8,128)(2,1)S(1)}, u32[]{:S(2)}, u32[]{:S(2)}) collective-permute-start(bf16[32,3200]{1,0:T(8,128)(2,1)S(1)} %fusion.36.refs_0_), channel_id=1, source_target_pairs={{0,16},{8,24},{16,0},{24,8},{1,17},{9,25},{17,1},{25,9},{2,18},{10... | collective-permute-start | bytes 614408 | tf_op jit(solution)/shard_map/ppermute | solution.py:780
  10.0 30.2 %collective-permute-start.4 = (bf16[32,3200]{1,0:T(8,128)(2,1)S(1)}, bf16[32,3200]{1,0:T(8,128)(2,1)S(1)}, u32[]{:S(2)}, u32[]{:S(2)}) collective-permute-start(bf16[32,3200]{1,0:T(8,128)(2,1)S(1)} %fusion.36.refs_0_), channel_id=1, source_target_pairs={{0,24},{8,0},{16,8},{24,16},{1,25},{9,1},{17,9},{25,17},{2,26},{10... | collective-permute-start | bytes 614408 | tf_op jit(solution)/shard_map/ppermute | solution.py:780
  11.4 37.1 %collective-permute-start.1 = (bf16[584,1024]{1,0:T(8,128)(2,1)}, bf16[584,1024]{1,0:T(8,128)(2,1)}, u32[]{:S(2)}, u32[]{:S(2)}) collective-permute-start(bf16[584,1024]{1,0:T(8,128)(2,1)} %param.16), channel_id=1, source_target_pairs={{0,1},{1,0},{2,3},{3,2},{4,5},{5,4},{6,7},{7,6},{8,9},{9,8},{10,11... | collective-permute-start | bytes 3588104 | tf_op jit(solution)/shard_map/ppermute | solution.py:769
  12.9 26.1 %collective-permute-start = (s32[584]{0:T(1024)}, s32[584]{0:T(1024)S(1)}, u32[]{:S(2)}, u32[]{:S(2)}) collective-permute-start(s32[584]{0:T(1024)} %param.18), channel_id=1, source_target_pairs={{0,1},{1,0},{2,3},{3,2},{4,5},{5,4},{6,7},{7,6},{8,9},{9,8},{10,11... | collective-permute-start | bytes 7016 | tf_op jit(solution)/shard_map/ppermute | solution.py:769
  45.2 23.1 %collective-permute-start.13 = (bf16[32,5120]{1,0:T(8,128)(2,1)S(1)}, bf16[32,5120]{1,0:T(8,128)(2,1)S(1)}, u32[]{:S(2)}, u32[]{:S(2)}) collective-permute-start(bf16[32,5120]{1,0:T(8,128)(2,1)S(1)} %pad_maximum_fusion.3.refs_0_), channel_id=1, source_target_pairs={{0,16},{8,24},{16,0},{24,8},{1,17},{9,25},{17,1},{25,9},{2,18},{10... | collective-permute-start | bytes 983048 | tf_op jit(solution)/shard_map/ppermute | solution.py:780
  45.5 22.8 %collective-permute-start.14 = (bf16[32,5120]{1,0:T(8,128)(2,1)S(1)}, bf16[32,5120]{1,0:T(8,128)(2,1)S(1)}, u32[]{:S(2)}, u32[]{:S(2)}) collective-permute-start(bf16[32,5120]{1,0:T(8,128)(2,1)S(1)} %pad_maximum_fusion.3.refs_0_), channel_id=1, source_target_pairs={{0,24},{8,0},{16,8},{24,16},{1,25},{9,1},{17,9},{25,17},{2,26},{10... | collective-permute-start | bytes 983048 | tf_op jit(solution)/shard_map/ppermute | solution.py:780
  48.5 25.5 %collective-permute-start.5 = (bf16[128,1664]{1,0:T(8,128)(2,1)}, bf16[128,1664]{1,0:T(8,128)(2,1)S(1)}, u32[]{:S(2)}, u32[]{:S(2)}) collective-permute-start(bf16[128,1664]{1,0:T(8,128)(2,1)} %get-tuple-element.75.refs_0_), channel_id=1, source_target_pairs={{0,4},{4,0},{1,5},{5,1},{2,6},{6,2},{3,7},{7,3},{8,12},{12,8},{9,1... | collective-permute-start | bytes 1277960 | tf_op jit(solution)/shard_map/ppermute | solution.py:769
  70.4 23.1 %collective-permute-start.6 = (bf16[128,1664]{1,0:T(8,128)(2,1)}, bf16[128,1664]{1,0:T(8,128)(2,1)S(1)}, u32[]{:S(2)}, u32[]{:S(2)}) collective-permute-start(bf16[128,1664]{1,0:T(8,128)(2,1)} %get-tuple-element.75.refs_0_), channel_id=1, source_target_pairs={{0,1},{1,0},{2,3},{3,2},{4,5},{5,4},{6,7},{7,6},{8,9},{9,8},{10,11... | collective-permute-start | bytes 1277960 | tf_op jit(solution)/shard_map/ppermute | solution.py:769
  72.0 20.0 %collective-permute-start.15 = (bf16[128,1536]{1,0:T(8,128)(2,1)}, bf16[128,1536]{1,0:T(8,128)(2,1)}, u32[]{:S(2)}, u32[]{:S(2)}) collective-permute-start(bf16[128,1536]{1,0:T(8,128)(2,1)} %get-tuple-element.81.refs_0_), channel_id=1, source_target_pairs={{0,1},{1,0},{2,3},{3,2},{4,5},{5,4},{6,7},{7,6},{8,9},{9,8},{10,11... | collective-permute-start | bytes 1179656 | tf_op jit(solution)/shard_map/ppermute | solution.py:769
  72.5 21.0 %collective-permute-start.16 = (bf16[128,1536]{1,0:T(8,128)(2,1)}, bf16[128,1536]{1,0:T(8,128)(2,1)}, u32[]{:S(2)}, u32[]{:S(2)}) collective-permute-start(bf16[128,1536]{1,0:T(8,128)(2,1)} %get-tuple-element.81.refs_0_), channel_id=1, source_target_pairs={{0,4},{4,0},{1,5},{5,1},{2,6},{6,2},{3,7},{7,3},{8,12},{12,8},{9,1... | collective-permute-start | bytes 1179656 | tf_op jit(solution)/shard_map/ppermute | solution.py:769
  74.0 28.5 %collective-permute-start.8 = (bf16[128,1664]{1,0:T(8,128)(2,1)}, bf16[128,1664]{1,0:T(8,128)(2,1)S(1)}, u32[]{:S(2)}, u32[]{:S(2)}) collective-permute-start(bf16[128,1664]{1,0:T(8,128)(2,1)} %get-tuple-element.75.refs_0_), channel_id=1, source_target_pairs={{0,2},{2,0},{1,3},{3,1},{4,6},{6,4},{5,7},{7,5},{8,10},{10,8},{9,1... | collective-permute-start | bytes 1277960 | tf_op jit(solution)/shard_map/ppermute | solution.py:769
  74.0 24.9 %collective-permute-start.7 = (bf16[128,1664]{1,0:T(8,128)(2,1)S(1)}, bf16[128,1664]{1,0:T(8,128)(2,1)}, u32[]{:S(2)}, u32[]{:S(2)}) collective-permute-start(bf16[128,1664]{1,0:T(8,128)(2,1)S(1)} %collective-permute-done.5.refs_1_), channel_id=1, source_target_pairs={{0,1},{1,0},{2,3},{3,2},{4,5},{5,4},{6,7},{7,6},{8,9},{9,8},{10,11... | collective-permute-start | bytes 1277960 | tf_op jit(solution)/shard_map/ppermute | solution.py:769
  100.9 17.9 %collective-permute-start.26 = (bf16[128,2560]{1,0:T(8,128)(2,1)}, bf16[128,2560]{1,0:T(8,128)(2,1)}, u32[]{:S(2)}, u32[]{:S(2)}) collective-permute-start(bf16[128,2560]{1,0:T(8,128)(2,1)} %get-tuple-element.94.refs_4_), channel_id=1, source_target_pairs={{0,1},{1,0},{2,3},{3,2},{4,5},{5,4},{6,7},{7,6},{8,9},{9,8},{10,11... | collective-permute-start | bytes 1966088 | tf_op jit(solution)/shard_map/ppermute | solution.py:769
  102.5 17.9 %collective-permute-start.23 = (bf16[128,2560]{1,0:T(8,128)(2,1)}, bf16[128,2560]{1,0:T(8,128)(2,1)}, u32[]{:S(2)}, u32[]{:S(2)}) collective-permute-start(bf16[128,2560]{1,0:T(8,128)(2,1)} %get-tuple-element.88.refs_0_), channel_id=1, source_target_pairs={{0,4},{4,0},{1,5},{5,1},{2,6},{6,2},{3,7},{7,3},{8,12},{12,8},{9,1... | collective-permute-start | bytes 1966088 | tf_op jit(solution)/shard_map/ppermute | solution.py:769
  104.2 52.1 %collective-permute-start.27 = (bf16[128,2560]{1,0:T(8,128)(2,1)}, bf16[128,2560]{1,0:T(8,128)(2,1)}, u32[]{:S(2)}, u32[]{:S(2)}) collective-permute-start(bf16[128,2560]{1,0:T(8,128)(2,1)} %get-tuple-element.94.refs_4_), channel_id=1, source_target_pairs={{0,4},{4,0},{1,5},{5,1},{2,6},{6,2},{3,7},{7,3},{8,12},{12,8},{9,1... | collective-permute-start | bytes 1966088 | tf_op jit(solution)/shard_map/ppermute | solution.py:769
  104.8 51.5 %collective-permute-start.24 = (bf16[128,2560]{1,0:T(8,128)(2,1)}, bf16[128,2560]{1,0:T(8,128)(2,1)}, u32[]{:S(2)}, u32[]{:S(2)}) collective-permute-start(bf16[128,2560]{1,0:T(8,128)(2,1)} %get-tuple-element.88.refs_0_), channel_id=1, source_target_pairs={{0,1},{1,0},{2,3},{3,2},{4,5},{5,4},{6,7},{7,6},{8,9},{9,8},{10,11... | collective-permute-start | bytes 1966088 | tf_op jit(solution)/shard_map/ppermute | solution.py:769
  105.3 33.2 %collective-permute-start.18 = (bf16[128,1024]{1,0:T(8,128)(2,1)S(1)}, bf16[128,1024]{1,0:T(8,128)(2,1)}, u32[]{:S(2)}, u32[]{:S(2)}) collective-permute-start(bf16[128,1024]{1,0:T(8,128)(2,1)S(1)} %copy.126.refs_0_), channel_id=1, source_target_pairs={{0,1},{1,0},{2,3},{3,2},{4,5},{5,4},{6,7},{7,6},{8,9},{9,8},{10,11... | collective-permute-start | bytes 786440 | tf_op jit(solution)/shard_map/ppermute | solution.py:769
  118.9 37.5 %collective-permute-start.28 = (bf16[128,2560]{1,0:T(8,128)(2,1)}, bf16[128,2560]{1,0:T(8,128)(2,1)}, u32[]{:S(2)}, u32[]{:S(2)}) collective-permute-start(bf16[128,2560]{1,0:T(8,128)(2,1)} %collective-permute-done.26.refs_5_), channel_id=1, source_target_pairs={{0,4},{4,0},{1,5},{5,1},{2,6},{6,2},{3,7},{7,3},{8,12},{12,8},{9,1... | collective-permute-start | bytes 1966088 | tf_op jit(solution)/shard_map/ppermute | solution.py:769
  120.4 35.9 %collective-permute-start.25 = (bf16[128,2560]{1,0:T(8,128)(2,1)}, bf16[128,2560]{1,0:T(8,128)(2,1)}, u32[]{:S(2)}, u32[]{:S(2)}) collective-permute-start(bf16[128,2560]{1,0:T(8,128)(2,1)} %collective-permute-done.23.refs_1_), channel_id=1, source_target_pairs={{0,1},{1,0},{2,3},{3,2},{4,5},{5,4},{6,7},{7,6},{8,9},{9,8},{10,11... | collective-permute-start | bytes 1966088 | tf_op jit(solution)/shard_map/ppermute | solution.py:769
  161.6 68.8 %collective-permute-start.29 = (bf16[512,5120]{1,0:T(8,128)(2,1)}, bf16[512,5120]{1,0:T(8,128)(2,1)}, u32[]{:S(2)}, u32[]{:S(2)}) collective-permute-start(bf16[512,5120]{1,0:T(8,128)(2,1)} %assemble.14.refs_0_), channel_id=1, source_target_pairs={{0,2},{2,0},{1,3},{3,1},{4,6},{6,4},{5,7},{7,5},{8,10},{10,8},{9,1... | collective-permute-start | bytes 15728648 | tf_op jit(solution)/shard_map/ppermute | solution.py:769
  162.2 62.0 %collective-permute-start.37 = (bf16[584,1024]{1,0:T(8,128)(2,1)}, bf16[584,1024]{1,0:T(8,128)(2,1)}, u32[]{:S(2)}, u32[]{:S(2)}) collective-permute-start(bf16[584,1024]{1,0:T(8,128)(2,1)} %param.17), channel_id=1, source_target_pairs={{0,1},{1,0},{2,3},{3,2},{4,5},{5,4},{6,7},{7,6},{8,9},{9,8},{10,11... | collective-permute-start | bytes 3588104 | tf_op jit(solution)/shard_map/ppermute | solution.py:769
  172.2 46.7 %collective-permute-start.30 = (bf16[256,1024]{1,0:T(8,128)(2,1)S(1)}, bf16[256,1024]{1,0:T(8,128)(2,1)}, u32[]{:S(2)}, u32[]{:S(2)}) collective-permute-start(bf16[256,1024]{1,0:T(8,128)(2,1)S(1)} %assemble.12.refs_0_), channel_id=1, source_target_pairs={{0,8},{8,16},{16,24},{24,0},{1,9},{9,17},{17,25},{25,1},{2,10},{10... | collective-permute-start | bytes 1572872 | tf_op jit(solution)/shard_map/ppermute | solution.py:780
  179.8 39.1 %collective-permute-start.31 = (bf16[256,1024]{1,0:T(8,128)(2,1)S(1)}, bf16[256,1024]{1,0:T(8,128)(2,1)}, u32[]{:S(2)}, u32[]{:S(2)}) collective-permute-start(bf16[256,1024]{1,0:T(8,128)(2,1)S(1)} %assemble.12.refs_0_), channel_id=1, source_target_pairs={{0,16},{8,24},{16,0},{24,8},{1,17},{9,25},{17,1},{25,9},{2,18},{10... | collective-permute-start | bytes 1572872 | tf_op jit(solution)/shard_map/ppermute | solution.py:780
  179.9 39.1 %collective-permute-start.32 = (bf16[256,1024]{1,0:T(8,128)(2,1)S(1)}, bf16[256,1024]{1,0:T(8,128)(2,1)}, u32[]{:S(2)}, u32[]{:S(2)}) collective-permute-start(bf16[256,1024]{1,0:T(8,128)(2,1)S(1)} %assemble.12.refs_0_), channel_id=1, source_target_pairs={{0,24},{8,0},{16,8},{24,16},{1,25},{9,1},{17,9},{25,17},{2,26},{10... | collective-permute-start | bytes 1572872 | tf_op jit(solution)/shard_map/ppermute | solution.py:780
  222.6 47.5 %collective-permute-start.33 = (bf16[1024,1024]{1,0:T(8,128)(2,1)}, bf16[1024,1024]{1,0:T(8,128)(2,1)}, u32[]{:S(2)}, u32[]{:S(2)}) collective-permute-start(bf16[1024,1024]{1,0:T(8,128)(2,1)} %assemble.16.refs_0_), channel_id=1, source_target_pairs={{0,4},{4,0},{1,5},{5,1},{2,6},{6,2},{3,7},{7,3},{8,12},{12,8},{9,1... | collective-permute-start | bytes 6291464 | tf_op jit(solution)/shard_map/ppermute | solution.py:769
  269.6 35.2 %collective-permute-start.38 = (bf16[2048,1024]{1,0:T(8,128)(2,1)}, bf16[2048,1024]{1,0:T(8,128)(2,1)}, u32[]{:S(2)}, u32[]{:S(2)}) collective-permute-start(bf16[2048,1024]{1,0:T(8,128)(2,1)} %gradient.10), channel_id=1, source_target_pairs={{0,2},{2,0},{1,3},{3,1},{4,6},{6,4},{5,7},{7,5},{8,10},{10,8},{9,1... | collective-permute-start | bytes 12582920 | tf_op jit(solution)/shard_map/ppermute | solution.py:769
  329.9 32.1 %collective-permute-start.40 = (bf16[512,2048]{1,0:T(8,128)(2,1)}, bf16[512,2048]{1,0:T(8,128)(2,1)}, u32[]{:S(2)}, u32[]{:S(2)}) collective-permute-start(bf16[512,2048]{1,0:T(8,128)(2,1)} %gradient.14), channel_id=1, source_target_pairs={{0,2},{2,0},{1,3},{3,1},{4,6},{6,4},{5,7},{7,5},{8,10},{10,8},{9,1... | collective-permute-start | bytes 6291464 | tf_op jit(solution)/shard_map/ppermute | solution.py:769
  330.7 85.4 %collective-permute-start.36 = (bf16[592,1024]{1,0:T(8,128)(2,1)}, bf16[592,1024]{1,0:T(8,128)(2,1)}, u32[]{:S(2)}, u32[]{:S(2)}) collective-permute-start(bf16[592,1024]{1,0:T(8,128)(2,1)} %fusion.9), channel_id=1, source_target_pairs={{0,1},{1,0},{2,3},{3,2},{4,5},{5,4},{6,7},{7,6},{8,9},{9,8},{10,11... | collective-permute-start | bytes 3637256 | tf_op jit(solution)/shard_map/ppermute | solution.py:769
  337.7 35.1 %collective-permute-start.39 = (bf16[512,2048]{1,0:T(8,128)(2,1)}, bf16[512,2048]{1,0:T(8,128)(2,1)}, u32[]{:S(2)}, u32[]{:S(2)}) collective-permute-start(bf16[512,2048]{1,0:T(8,128)(2,1)} %gradient.12), channel_id=1, source_target_pairs={{0,2},{2,0},{1,3},{3,1},{4,6},{6,4},{5,7},{7,5},{8,10},{10,8},{9,1... | collective-permute-start | bytes 6291464 | tf_op jit(solution)/shard_map/ppermute | solution.py:769
  353.4 48.9 %collective-permute-start.42 = (bf16[1024,1024]{1,0:T(8,128)(2,1)}, bf16[1024,1024]{1,0:T(8,128)(2,1)}, u32[]{:S(2)}, u32[]{:S(2)}) collective-permute-start(bf16[1024,1024]{1,0:T(8,128)(2,1)} %get-tuple-element.159), channel_id=1, source_target_pairs={{0,4},{4,0},{1,5},{5,1},{2,6},{6,2},{3,7},{7,3},{8,12},{12,8},{9,1... | collective-permute-start | bytes 6291464 | tf_op jit(solution)/shard_map/ppermute | solution.py:769
  371.3 53.8 %collective-permute-start.41 = (bf16[512,1024]{1,0:T(8,128)(2,1)}, bf16[512,1024]{1,0:T(8,128)(2,1)}, u32[]{:S(2)}, u32[]{:S(2)}) collective-permute-start(bf16[512,1024]{1,0:T(8,128)(2,1)} %dynamic-slice_bitcast_fusion.3), channel_id=1, source_target_pairs={{0,2},{2,0},{1,3},{3,1},{4,6},{6,4},{5,7},{7,5},{8,10},{10,8},{9,1... | collective-permute-start | bytes 3145736 | tf_op jit(solution)/shard_map/ppermute | solution.py:769
  371.3 83.9 %collective-permute-start.44 = (bf16[256,2048]{1,0:T(8,128)(2,1)}, bf16[256,2048]{1,0:T(8,128)(2,1)}, u32[]{:S(2)}, u32[]{:S(2)}) collective-permute-start(bf16[256,2048]{1,0:T(8,128)(2,1)} %get-tuple-element.165), channel_id=1, source_target_pairs={{0,4},{4,0},{1,5},{5,1},{2,6},{6,2},{3,7},{7,3},{8,12},{12,8},{9,1... | collective-permute-start | bytes 3145736 | tf_op jit(solution)/shard_map/ppermute | solution.py:769
  406.4 51.9 %collective-permute-start.43 = (bf16[256,2048]{1,0:T(8,128)(2,1)}, bf16[256,2048]{1,0:T(8,128)(2,1)}, u32[]{:S(2)}, u32[]{:S(2)}) collective-permute-start(bf16[256,2048]{1,0:T(8,128)(2,1)} %bitcast.61), channel_id=1, source_target_pairs={{0,1},{1,0},{2,3},{3,2},{4,5},{5,4},{6,7},{7,6},{8,9},{9,8},{10,11... | collective-permute-start | bytes 3145736 | tf_op jit(solution)/shard_map/ppermute | solution.py:769
  409.8 75.0 %collective-permute-start.47 = (bf16[256,1024]{1,0:T(8,128)(2,1)}, bf16[256,1024]{1,0:T(8,128)(2,1)}, u32[]{:S(2)}, u32[]{:S(2)}) collective-permute-start(bf16[256,1024]{1,0:T(8,128)(2,1)} %get-tuple-element.161), channel_id=1, source_target_pairs={{0,8},{8,16},{16,24},{24,0},{1,9},{9,17},{17,25},{25,1},{2,10},{10... | collective-permute-start | bytes 1572872 | tf_op jit(solution)/shard_map/ppermute | solution.py:840
  416.1 69.3 %collective-permute-start.48 = (bf16[256,1024]{1,0:T(8,128)(2,1)}, bf16[256,1024]{1,0:T(8,128)(2,1)}, u32[]{:S(2)}, u32[]{:S(2)}) collective-permute-start(bf16[256,1024]{1,0:T(8,128)(2,1)} %get-tuple-element.163), channel_id=1, source_target_pairs={{0,16},{8,24},{16,0},{24,8},{1,17},{9,25},{17,1},{25,9},{2,18},{10... | collective-permute-start | bytes 1572872 | tf_op jit(solution)/shard_map/ppermute | solution.py:840
  425.1 60.3 %collective-permute-start.49 = (bf16[256,1024]{1,0:T(8,128)(2,1)}, bf16[256,1024]{1,0:T(8,128)(2,1)}, u32[]{:S(2)}, u32[]{:S(2)}) collective-permute-start(bf16[256,1024]{1,0:T(8,128)(2,1)} %get-tuple-element.162), channel_id=1, source_target_pairs={{0,24},{8,0},{16,8},{24,16},{1,25},{9,1},{17,9},{25,17},{2,26},{10... | collective-permute-start | bytes 1572872 | tf_op jit(solution)/shard_map/ppermute | solution.py:840
  458.3 53.0 %collective-permute-start.46 = (bf16[512,1536]{1,0:T(8,128)(2,1)}, bf16[512,1536]{1,0:T(8,128)(2,1)}, u32[]{:S(2)}, u32[]{:S(2)}) collective-permute-start(bf16[512,1536]{1,0:T(8,128)(2,1)} %gradient.16), channel_id=1, source_target_pairs={{0,2},{2,0},{1,3},{3,1},{4,6},{6,4},{5,7},{7,5},{8,10},{10,8},{9,1... | collective-permute-start | bytes 4718600 | tf_op jit(solution)/shard_map/ppermute | solution.py:769
  467.9 89.8 %collective-permute-start.64 = (bf16[128,2048]{1,0:T(8,128)(2,1)}, bf16[128,2048]{1,0:T(8,128)(2,1)}, u32[]{:S(2)}, u32[]{:S(2)}) collective-permute-start(bf16[128,2048]{1,0:T(8,128)(2,1)} %get-tuple-element.176), channel_id=1, source_target_pairs={{0,4},{4,0},{1,5},{5,1},{2,6},{6,2},{3,7},{7,3},{8,12},{12,8},{9,1... | collective-permute-start | bytes 1572872 | tf_op jit(solution)/shard_map/ppermute | solution.py:769
  484.8 74.0 %collective-permute-start.65 = (bf16[128,2048]{1,0:T(8,128)(2,1)}, bf16[128,2048]{1,0:T(8,128)(2,1)}, u32[]{:S(2)}, u32[]{:S(2)}) collective-permute-start(bf16[128,2048]{1,0:T(8,128)(2,1)} %get-tuple-element.178), channel_id=1, source_target_pairs={{0,1},{1,0},{2,3},{3,2},{4,5},{5,4},{6,7},{7,6},{8,9},{9,8},{10,11... | collective-permute-start | bytes 1572872 | tf_op jit(solution)/shard_map/ppermute | solution.py:769
  491.6 53.9 %collective-permute-start.56 = (bf16[512,1536]{1,0:T(8,128)(2,1)}, bf16[512,1536]{1,0:T(8,128)(2,1)}, u32[]{:S(2)}, u32[]{:S(2)}) collective-permute-start(bf16[512,1536]{1,0:T(8,128)(2,1)} %gradient.18), channel_id=1, source_target_pairs={{0,2},{2,0},{1,3},{3,1},{4,6},{6,4},{5,7},{7,5},{8,10},{10,8},{9,1... | collective-permute-start | bytes 4718600 | tf_op jit(solution)/shard_map/ppermute | solution.py:769
  521.4 19.2 %collective-permute-start.51 = (bf16[256,1536]{1,0:T(8,128)(2,1)}, bf16[256,1536]{1,0:T(8,128)(2,1)}, u32[]{:S(2)}, u32[]{:S(2)}) collective-permute-start(bf16[256,1536]{1,0:T(8,128)(2,1)} %get-tuple-element.169), channel_id=1, source_target_pairs={{0,4},{4,0},{1,5},{5,1},{2,6},{6,2},{3,7},{7,3},{8,12},{12,8},{9,1... | collective-permute-start | bytes 2359304 | tf_op jit(solution)/shard_map/ppermute | solution.py:769
  528.9 31.2 %collective-permute-start.66 = (bf16[128,1024]{1,0:T(8,128)(2,1)S(1)}, bf16[128,1024]{1,0:T(8,128)(2,1)S(1)}, u32[]{:S(2)}, u32[]{:S(2)}) collective-permute-start(bf16[128,1024]{1,0:T(8,128)(2,1)S(1)} %copy-done.80), channel_id=1, source_target_pairs={{0,1},{1,0},{2,3},{3,2},{4,5},{5,4},{6,7},{7,6},{8,9},{9,8},{10,11... | collective-permute-start | bytes 786440 | tf_op jit(solution)/shard_map/ppermute | solution.py:769
  545.5 37.4 %collective-permute-start.50 = (bf16[592,1024]{1,0:T(8,128)(2,1)S(1)}, bf16[592,1024]{1,0:T(8,128)(2,1)S(1)}, u32[]{:S(2)}, u32[]{:S(2)}) collective-permute-start(bf16[592,1024]{1,0:T(8,128)(2,1)S(1)} %fusion.10), channel_id=1, source_target_pairs={{0,1},{1,0},{2,3},{3,2},{4,5},{5,4},{6,7},{7,6},{8,9},{9,8},{10,11... | collective-permute-start | bytes 3637256 | tf_op jit(solution)/shard_map/ppermute | solution.py:769
  557.0 39.1 %collective-permute-start.57 = (bf16[256,1536]{1,0:T(8,128)(2,1)S(1)}, bf16[256,1536]{1,0:T(8,128)(2,1)S(1)}, u32[]{:S(2)}, u32[]{:S(2)}) collective-permute-start(bf16[256,1536]{1,0:T(8,128)(2,1)S(1)} %bitcast.239), channel_id=1, source_target_pairs={{0,1},{1,0},{2,3},{3,2},{4,5},{5,4},{6,7},{7,6},{8,9},{9,8},{10,11... | collective-permute-start | bytes 2359304 | tf_op jit(solution)/shard_map/ppermute | solution.py:769
  561.2 51.0 %collective-permute-start.67 = (bf16[32,5120]{1,0:T(8,128)(2,1)}, bf16[32,5120]{1,0:T(8,128)(2,1)S(1)}, u32[]{:S(2)}, u32[]{:S(2)}) collective-permute-start(bf16[32,5120]{1,0:T(8,128)(2,1)} %get-tuple-element.173), channel_id=1, source_target_pairs={{0,8},{8,16},{16,24},{24,0},{1,9},{9,17},{17,25},{25,1},{2,10},{10... | collective-permute-start | bytes 983048 | tf_op jit(solution)/shard_map/ppermute | solution.py:840
  562.9 50.6 %collective-permute-start.68 = (bf16[32,5120]{1,0:T(8,128)(2,1)}, bf16[32,5120]{1,0:T(8,128)(2,1)}, u32[]{:S(2)}, u32[]{:S(2)}) collective-permute-start(bf16[32,5120]{1,0:T(8,128)(2,1)} %get-tuple-element.175), channel_id=1, source_target_pairs={{0,16},{8,24},{16,0},{24,8},{1,17},{9,25},{17,1},{25,9},{2,18},{10... | collective-permute-start | bytes 983048 | tf_op jit(solution)/shard_map/ppermute | solution.py:840
  563.0 34.8 %collective-permute-start.53 = (bf16[32,1536]{1,0:T(8,128)(2,1)S(1)}, bf16[32,1536]{1,0:T(8,128)(2,1)S(1)}, u32[]{:S(2)}, u32[]{:S(2)}) collective-permute-start(bf16[32,1536]{1,0:T(8,128)(2,1)S(1)} %get-tuple-element.187), channel_id=1, source_target_pairs={{0,8},{8,16},{16,24},{24,0},{1,9},{9,17},{17,25},{25,1},{2,10},{10... | collective-permute-start | bytes 294920 | tf_op jit(solution)/shard_map/ppermute | solution.py:840
  (144 other events, 1304.4 us)

commit v7 on v6

--- a/solution.py
+++ b/solution.py
@@ -635,6 +635,69 @@
     )(d_rows, weight, *extra)
 
 
+def norm_back_kernel(count, d_ref, weight_ref, *refs):
+    base, (normal_ref, scale_ref, gain_ref, residual_ref) = refs[:count], refs[count : count + 4]
+    *wide_refs, low_ref, sum_ref, total = refs[count + 4 :]
+    d_rows = d_ref[0] if len(d_ref.shape) == 3 else d_ref[...]
+    product = nt_dot(d_rows, weight_ref[...])
+    step = pl.program_id(0)
+
+    @pl.when(step == 0)
+    def _():
+        total[...] = product + base[0][...] if base else product
+
+    @pl.when(step > 0)
+    def _():
+        total[...] += product
+
+    @pl.when(step == pl.num_programs(0) - 1)
+    def _():
+        rows = total.shape[0]
+        sums = [jnp.zeros((1, total.shape[1]), jnp.float32)] * 3
+        for start, size in chunks_of(rows):
+            part = slice(start, start + size)
+            d_part, normal = total[part, :], normal_ref[part, :]
+            along = d_part * normal
+            scaled = d_part * gain_ref[...]
+            mean = jnp.mean(scaled, axis=-1, keepdims=True)
+            slope = jnp.mean(scaled * normal, axis=-1, keepdims=True)
+            wide = (scaled - mean - normal * slope) * scale_ref[part, :]
+            wide = wide + residual_ref[part, :].astype(jnp.float32)
+            low = wide.astype(jnp.bfloat16)
+            for wide_ref in wide_refs:
+                wide_ref[part, :] = wide
+            low_ref[part, :] = low
+            for number, array in enumerate((along, d_part, low.astype(jnp.float32))):
+                sums[number] = sums[number] + jnp.sum(array, axis=0, keepdims=True)
+        for number, one in enumerate(sums):
+            sum_ref[number : number + 1, :] = one
+
+
+def norm_back(d_rows, weight, normal, scale, gain, residual, base=None, keep=False):
+    rows, depth = d_rows.shape[-2], weight.shape[0]
+    if d_rows.ndim == 3:
+        d_spec = pl.BlockSpec((1, rows, BLOCK), lambda i: (i, 0, 0))
+    else:
+        d_spec = pl.BlockSpec((rows, BLOCK), lambda i: (0, i))
+    extra = [] if base is None else [base]
+    full = whole_spec((rows, depth))
+    kinds = [jnp.float32] * keep + [jnp.bfloat16]
+    return pl.pallas_call(
+        functools.partial(norm_back_kernel, len(extra)),
+        grid=(weight.shape[1] // BLOCK,),
+        in_specs=[d_spec, pl.BlockSpec((depth, BLOCK), lambda i: (0, i))]
+        + [full for _ in extra]
+        + [full, whole_spec((rows, 1)), whole_spec((1, depth)), full],
+        out_specs=[full for _ in kinds] + [whole_spec((8, depth))],
+        out_shape=[jax.ShapeDtypeStruct((rows, depth), kind) for kind in kinds]
+        + [jax.ShapeDtypeStruct((8, depth), jnp.float32)],
+        scratch_shapes=[pltpu.VMEM((rows, depth), jnp.float32)],
+        compiler_params=limit(40),
+        cost_estimate=HINT,
+        name="norm_back",
+    )(d_rows, weight, *extra, normal, scale, gain[None, :], residual)
+
+
 def gradient_kernel(index_ref, x_ref, d_ref, *refs):
     out_ref = refs[-1]
     x = x_ref[...]
@@ -685,13 +748,6 @@
     return center * scale, scale
 
 
-def norm_backward(d_normed_rows, normal, scale, gain):
-    scaled = d_normed_rows * gain
-    mean = jnp.mean(scaled, axis=-1, keepdims=True)
-    along = jnp.mean(scaled * normal, axis=-1, keepdims=True)
-    return (scaled - mean - normal * along) * scale
-
-
 def reorder(array, axis, sizes, spots):
     shape = array.shape
     count = math.prod(sizes)
@@ -902,10 +958,11 @@
         )
         up_width = w_up.shape[1] * 8
         up_cut = (width + up_width) // 2
-        far_up = gather_far(after(shard_up, far_one), far, [up_cut, up_cut])
-        far_one, far_two = after(far_one, inputs_far), after(far_two, inputs_far)
-        one = spread(spread({OWN: far_one}, "x"), "ctx")
-        two = spread(spread({OWN: far_two}, "ctx"), "x")
+        one = spread({OWN: far_one}, "x")
+        two = spread({OWN: after(far_two, inputs_far)}, "ctx")
+        first = list(one.values()) + list(two.values())
+        far_up = gather_far(after(shard_up, *first), far, [up_cut, up_cut])
+        one, two = spread(one, "ctx"), spread(two, "x")
         all_one = list(one.values()) + list(two.values())
         shard_down = after(to_local(unfold(w_down), 1, far), far_up[0], *all_one)
         near_down = order_blocks(spread({OWN: shard_down}, "ctx"), ["ctx"])
@@ -918,11 +975,11 @@
             [(width, half_qkv), (width, 128)],
             routes,
         )
-        qkv_two = order_blocks(two_core, axes)
+        qkv_two_weight = order_blocks(two_core, axes)
         up_one = spread({OWN: after(far_up[0], *all_one)}, "x")
         up_two = spread({OWN: after(far_up[1], *all_one)}, "ctx")
-        up_one = spread(tie_received(up_one, qkv_one), "ctx")
-        up_two = spread(tie_received(up_two, qkv_one), "x")
+        up_one = spread(tie_received(up_one, qkv_two_weight), "ctx")
+        up_two = spread(tie_received(up_two, qkv_two_weight), "x")
         far_down = gather_far(near_down, far)[0]
 
         devices = 8 * far
@@ -986,8 +1043,8 @@
             for cut in (slice(0, half_width), slice(half_width, width))
         ]
         joined_one = project(normed1, qkv_one, joined_bias[0])
-        attended, log_one = attention_forward(after(joined_one, near_down), bias, width, 0)
-        joined_two = project(after(normed1, log_one), qkv_two, joined_bias[1])
+        attended, log_one = attention_forward(after(joined_one, qkv_two_weight), bias, width, 0)
+        joined_two = project(after(normed1, log_one), qkv_two_weight, joined_bias[1])
         up_one, up_two = tie_received(up_one, log_one), tie_received(up_two, log_one)
         up_near = assemble(
             list(up_one.values()) + list(up_two.values()),
@@ -997,7 +1054,7 @@
         )[0]
         up_blocks = spread({OWN: up_near}, "core")
         attended, log_two = attention_forward(
-            joined_two, bias, width, half_width // PAIR, attended
+            after(joined_two, near_down), bias, width, half_width // PAIR, attended
         )
         cotangent_far = swap(after(cotangent, up_near))
         down_blocks = spread({OWN: after(far_down, up_near)}, "x")
@@ -1014,8 +1071,7 @@
         active, slope = hidden_layer(normed2, up_weight, up_bias)
 
         live = (row < SEQ).astype(jnp.float32)[:, None]
-        d_out = take(cotangent, cotangent_far) * live
-        d_out_low = d_out.astype(jnp.bfloat16)
+        d_out_low = (take(cotangent, cotangent_far) * live).astype(jnp.bfloat16)
         down_core = trade(gradient(active, d_out_low, 1 - core), "core")
         down_blocks = {key: after(block, active) for key, block in down_blocks.items()}
         down_weight = order_blocks(spread(down_blocks, "core"), ["core", "x"])
@@ -1028,9 +1084,9 @@
         up_core = [
             trade(gradient(normed2, d_hidden, 1 - core, side, 2), "core") for side in range(2)
         ]
-        d_normed2 = d_normed(d_hidden, up_weight)
-        d_middle = d_out + norm_backward(d_normed2, normal2, scale2, second_gain)
-        d_branch = d_middle.astype(jnp.bfloat16)
+        d_middle, d_branch, sums_two = norm_back(
+            d_hidden, up_weight, normal2, scale2, second_gain, d_out_low, keep=True
+        )
         up_kept = [
             gradient(normed2, d_hidden, core, side, 2, after(up_core[side], d_branch))
             for side in range(2)
@@ -1056,22 +1112,23 @@
         two_core = trade(gradient(normed1, d_two, 1 - core), "core")
         qkv_one_x = send_half(gradient(normed1, d_one, core, got=after(one_core, d_two)), "x")
         down_y = send_half(add_far(down_far, d_two).astype(jnp.bfloat16), "ctx")
-        d_two_tied = after(d_two, qkv_one_x[0], down_y[0])
-        d_normed1 = d_normed(d_two_tied, qkv_two, partial)
-        d_last = d_middle + norm_backward(d_normed1, normal1, scale1, first_gain)
+        up_far = jnp.concatenate(
+            [add_half(halves, d_two) for halves in (up_one, up_two, out_y)], axis=1
+        )
+        d_two_tied = after(d_two, qkv_one_x[0], down_y[0], up_far)
+        d_last, sums_one = norm_back(
+            d_two_tied, qkv_two_weight, normal1, scale1, first_gain, d_middle, base=partial
+        )
         d_last_given = to_give(d_last)
         qkv_two = gradient(normed1, d_two, core, got=after(two_core, d_last_given[0]))
 
         vectors = [
-            column_sums(array)
-            for array in (
-                d_branch,
-                d_normed1 * normal1,
-                d_normed1,
-                d_normed2 * normal2,
-                d_normed2,
-                d_out_low,
-            )
+            sums_two[2],
+            sums_one[0],
+            sums_one[1],
+            sums_two[0],
+            sums_two[1],
+            column_sums(d_out_low),
         ]
         joined_vectors = [
             jnp.concatenate([column_sums(d_one[index]), column_sums(d_two[index])])
@@ -1082,20 +1139,16 @@
         up_sums = to_local(hidden_to_natural(up_sums[0], 0, far), 0, far)
         table = jnp.concatenate([table, up_sums.reshape(devices, -1, near_width)], axis=1)
         table = pad_small(table).reshape(width, 128).astype(jnp.bfloat16)
-        qkv_two_y = send_half(qkv_two, "ctx", 2)
+        qkv_two_x = send_half(qkv_two, "x")
         qkv_one_y = send_half(add_half(qkv_one_x, d_last_given[0]), "ctx")
-        table = send_half(add_half(send_half(table, "core")), "ctx", 2)
-        up_far = jnp.concatenate(
-            [add_half(halves, qkv_two_y[0], qkv_one_y[0]) for halves in (up_one, up_two, out_y)],
-            axis=1,
-        )
-        up_far = send_far(up_far, far)
-        qkv_two = jnp.concatenate([add_half(qkv_two_y), add_half(table)], axis=1)
-        qkv_two_x = send_half(qkv_two, "x")
+        table = send_half(add_half(send_half(table, "core")), "x")
+        up_far = send_far(after(up_far, qkv_two_x[0], qkv_one_y[0]), far)
+        qkv_two = jnp.concatenate([add_half(qkv_two_x), add_half(table)], axis=1)
+        qkv_two_y = send_half(qkv_two, "ctx")
         qkv_one_far = send_far(add_half(qkv_one_y), far)
-        qkv_two_far = send_far(add_half(qkv_two_x), far)
-
-        sum_down = add_half(down_y).astype(jnp.float32)
+        qkv_two_far = send_far(add_half(qkv_two_y), far)
+
+        sum_down = add_half(down_y, d_last_given[0]).astype(jnp.float32)
         sum_up = add_far(up_far)
         sum_up, sum_out = sum_up[:, :up_width], sum_up[:, up_width:]
         sum_one, sum_two = add_far(qkv_one_far), add_far(qkv_two_far)

time: 629 us -> 590 us (0.938)
  waiting for transfers between devices: 177 us -> 156 us
  local copies, waits for them, and re-layouts: 94.9 us -> 81.7 us
  other arithmetic: 40 us -> 29.1 us
    ppermute x50, waiting for transfers between devices: 161 us -> 100 us  [trade(): return lax.ppermute(array, axis, [(0, 1), (1, 0)])]
    ppermute x9, waiting for transfers between devices: 14.5 us -> 47.2 us  [gather_far(): lax.ppermute(shard, 'z', [(i, (i + step) % far) for i in range(far)])]
    pallas_call x0 -> x2, Pallas kernels: none -> 17 us  [norm_back(): pl.pallas_call(functools.partial(norm_back_kernel, len(extra)), grid=(wei...]
    pallas_call x3 -> x1, Pallas kernels: 16.1 us -> 3.27 us  [d_normed(): pl.pallas_call(d_normed_kernel, grid=(weight.shape[1] // BLOCK,), in_spec...]
    ppermute x12, starting transfers between devices: 22.6 us -> 33.2 us  [send_far(): lax.ppermute(sent, 'z', [(i, (i + step) % far) for i in range(far)])]
    ppermute x9, starting transfers between devices: 21.6 us -> 14 us  [gather_far(): lax.ppermute(shard, 'z', [(i, (i + step) % far) for i in range(far)])]
    ppermute x12, waiting for transfers between devices: 1.55 us -> 8.83 us  [send_far(): lax.ppermute(sent, 'z', [(i, (i + step) % far) for i in range(far)])]
    unnamed x244 -> x234, local copies, waits for them, and re-layouts: 34.4 us -> 40.7 us
  transfers between devices with their start and end apart: 71 -> 71, of which waited for: 23 -> 21; matrix products, arithmetic and copies ran while one was open for 21% -> 18% of each run, Pallas kernels for 25% -> 27%
where the time goes in v7:
time: 590 us; the launch traced here: 583 us
  Pallas kernels  183 us (31%)
  waiting for transfers between devices  156 us (26%)
  starting transfers between devices  85.5 us (14%)
  local copies, waits for them, and re-layouts  81.7 us (14%)
  matrix products  45.2 us (8%)
  other arithmetic  29.1 us (5%)
    ppermute x50, waiting for transfers between devices, trade(): return lax.ppermute(array, axis, [(0, 1), (1, 0)])  100 us
    ppermute x9, waiting for transfers between devices, gather_far(): lax.ppermute(shard, 'z', [(i, (i + step) % far) for i in range(far)])  47.2 us
    unnamed x234, local copies, waits for them, and re-layouts  40.7 us
    dot_general x11, matrix products, matmul(): return jnp.dot(left, right, preferred_element_type=jnp.float32)  40.1 us
    ppermute x50, starting transfers between devices, trade(): return lax.ppermute(array, axis, [(0, 1), (1, 0)])  38.3 us
    pallas_call x10, Pallas kernels, gradient(): pl.pallas_call(gradient_kernel, grid_spec=pltpu.PrefetchScalarGridSpec(nu...  38 us
    ppermute x12, starting transfers between devices, send_far(): lax.ppermute(sent, 'z', [(i, (i + step) % far) for i in range(far)])  33.2 us
    pallas_call x9, Pallas kernels, assemble(): pl.pallas_call(functools.partial(assemble_kernel, routes), in_specs=[pl.B...  28.4 us
  transfers between devices with their start and end apart: 71, of which 21 were waited for; matrix products, arithmetic and copies ran while one was open for 18% of the time, Pallas kernels for 27%

profile of v7, /device:TPU:0, one launch (start us, length us, event | category | flops | bytes accessed | tf_op | source)
XLA Modules:
  0.0 583.4 jit_solution(1701160436046312624)
XLA Ops:
  4.4 5.1 collective-permute-start.4
  15.0 11.9 %collective-permute-done.3.refs_2_ = bf16[32,3200]{1,0:T(8,128)(2,1)S(1)} collective-permute-done((bf16[32,3200]{1,0:T(8,128)(2,1)S(1)}, bf16[32,3200]{1,0:T(8,128)(2,1)S(1)}, u32[]{:S(2)}, u32[]{:S(2)}) %collective-permute-start.3) | collective-permute-done | bytes 204832 | tf_op jit(solution)/shard_map/ppermute | solution.py:836
  35.4 6.7 %collective-permute-done.5.refs_1_ = bf16[128,1664]{1,0:T(8,128)(2,1)} collective-permute-done((bf16[128,1664]{1,0:T(8,128)(2,1)}, bf16[128,1664]{1,0:T(8,128)(2,1)}, u32[]{:S(2)}, u32[]{:S(2)}) %collective-permute-start.5) | collective-permute-done | bytes 426016 | tf_op jit(solution)/shard_map/ppermute | solution.py:825
  44.2 3.8 fusion.12
  49.5 16.5 %collective-permute-done.12.refs_1_ = bf16[128,1536]{1,0:T(8,128)(2,1)} collective-permute-done((bf16[128,1536]{1,0:T(8,128)(2,1)}, bf16[128,1536]{1,0:T(8,128)(2,1)}, u32[]{:S(2)}, u32[]{:S(2)}) %collective-permute-start.12) | collective-permute-done | bytes 393248 | tf_op jit(solution)/shard_map/ppermute | solution.py:825
  71.9 5.9 %fusion.38 = (f32[592]{0:T(1024)S(1)}, f32[592,1024]{1,0:T(8,128)}) fusion(s32[1024]{0:T(1024)S(1)} %reshape.573, f32[592,1024]{1,0:T(8,128)} %fusion.12, bf16[584,1024]{1,0:T(8,128)(2,1)} %collective-permute-done.1, s32[584]{0:T(1024)S(1)} %select_select_fusion), kind=kOutput, calls=%fused_computation.172 | convolution fusion | flops 1952777216 | bytes 6054496 | tf_op jit(solution)/shard_map/dot_general | solution.py:28
  78.3 18.1 %collective-permute-done.20.refs_2_ = bf16[32,5120]{1,0:T(8,128)(2,1)S(1)} collective-permute-done((bf16[32,5120]{1,0:T(8,128)(2,1)S(1)}, bf16[32,5120]{1,0:T(8,128)(2,1)S(1)}, u32[]{:S(2)}, u32[]{:S(2)}) %collective-permute-start.20) | collective-permute-done | bytes 327712 | tf_op jit(solution)/shard_map/ppermute | solution.py:836
  128.2 3.7 add_convert_fusion.3
  134.6 13.5 %attention_forward.2 = (bf16[592,1024]{1,0:T(8,128)(2,1)S(1)}, f32[4,2,592]{2,1,0:T(2,128)S(1)}) custom-call(bf16[3,592,512]{2,1,0:T(8,128)(2,1)S(1)} %project.2.query_ref.key_ref.value_ref, bf16[3,592,512]{2,1,0:T(8,128)(2,1)S(1)} %project.2.query_ref.key_ref.value_ref, bf16[3,592,512]{2,1,0:T(8,128)(2,1)S(1)} %project.2.query_ref.key_ref.value_ref, ...), custom_call_target="tpu_custom_call" | custom-call | flops 1 | bytes 1 | tf_op jit(solution)/shard_map/attention_forward/pallas_call | solution.py:436
  148.7 4.6 assemble.14.refs_0_
  157.7 30.3 %collective-permute-done.22.refs_1_ = bf16[128,1024]{1,0:T(8,128)(2,1)S(1)} collective-permute-done((bf16[128,1024]{1,0:T(8,128)(2,1)S(1)}, bf16[128,1024]{1,0:T(8,128)(2,1)S(1)}, u32[]{:S(2)}, u32[]{:S(2)}) %collective-permute-start.22) | collective-permute-done | bytes 262176 | tf_op jit(solution)/shard_map/ppermute | solution.py:825
  193.3 3.8 fusion.11
  205.7 13.5 %attention_forward.3 = (bf16[592,1024]{1,0:T(8,128)(2,1)S(1)}, f32[4,2,592]{2,1,0:T(2,128)S(1)}) custom-call(bf16[3,592,512]{2,1,0:T(8,128)(2,1)S(1)} %project.3.query_ref.key_ref.value_ref, bf16[3,592,512]{2,1,0:T(8,128)(2,1)S(1)} %project.3.query_ref.key_ref.value_ref, ...), custom_call_target="tpu_custom_call", output_to_operand_aliasing={{0}: (4, {})} | custom-call | flops 1 | bytes 1 | tf_op jit(solution)/shard_map/attention_forward/pallas_call | solution.py:436
  219.3 16.4 %collective-permute-done.31.refs_2_ = bf16[256,1024]{1,0:T(8,128)(2,1)} collective-permute-done((bf16[256,1024]{1,0:T(8,128)(2,1)S(1)}, bf16[256,1024]{1,0:T(8,128)(2,1)}, u32[]{:S(2)}, u32[]{:S(2)}) %collective-permute-start.31) | collective-permute-done | bytes 524320 | tf_op jit(solution)/shard_map/ppermute | solution.py:836
  239.4 5.6 fusion.40
  244.9 5.6 assemble.15
  259.5 18.1 %hidden_layer.1 = (bf16[592,4096]{1,0:T(8,128)(2,1)S(1)}, bf16[592,4096]{1,0:T(8,128)(2,1)S(1)}) custom-call(bf16[592,1024]{1,0:T(8,128)(2,1)S(1)} %get-tuple-element.166.x_ref, bf16[1024,4096]{1,0:T(8,128)(2,1)S(1)} %get-tuple-element.107.weight_ref, f32[1,4096]{1,0:T(1,128)S(1)} %bitcast.218), custom_call_target="tpu_custom_call" | custom-call | flops 1 | bytes 1 | tf_op jit(solution)/shard_map/hidden_layer/pallas_call | solution.py:522
  277.7 7.7 %gradient.10 = bf16[2048,1024]{1,0:T(8,128)(2,1)} custom-call(s32[1]{0:T(128)} %bitcast.31.index_ref, bf16[592,4096]{1,0:T(8,128)(2,1)S(1)} %get-tuple-element.108.active_ref.x_ref, bf16[592,1024]{1,0:T(8,128)(2,1)S(1)} %copy-done.23), custom_call_target="tpu_custom_call" | custom-call | flops 1 | bytes 1 | tf_op jit(solution)/shard_map/gradient/pallas_call | solution.py:725
  286.4 9.5 %collective-permute-done.34.refs_2_ = bf16[1024,1024]{1,0:T(8,128)(2,1)} collective-permute-done((bf16[1024,1024]{1,0:T(8,128)(2,1)}, bf16[1024,1024]{1,0:T(8,128)(2,1)}, u32[]{:S(2)}, u32[]{:S(2)}) %collective-permute-start.34) | collective-permute-done | bytes 2097184 | tf_op jit(solution)/shard_map/ppermute | solution.py:825
  298.9 4.2 assemble.17.weight_ref
  303.1 3.3 copy-done.5
  306.4 11.3 %last_layer.1 = bf16[592,1024]{1,0:T(8,128)(2,1)S(1)} custom-call(bf16[592,4096]{1,0:T(8,128)(2,1)} %copy-done.9, bf16[4096,1024]{1,0:T(8,128)(2,1)} %copy-done.5, f32[592,1024]{1,0:T(8,128)} %copy-done.69, f32[1,1024]{1,0:T(1,128)S(1)} %broadcast_in_dim_reshape_squeeze.6.bias_ref), custom_call_target="tpu_custom_call" | custom-call | flops 1 | bytes 1 | tf_op jit(solution)/shard_map/last_layer/pallas_call | solution.py:555
  322.8 7.6 %gradient.11 = bf16[2048,1024]{1,0:T(8,128)(2,1)S(1)} custom-call(s32[1]{0:T(128)} %bitcast.30.index_ref, bf16[592,4096]{1,0:T(8,128)(2,1)S(1)} %copy-done.10, bf16[592,1024]{1,0:T(8,128)(2,1)S(1)} %copy-done.24, bf16[2048,1024]{1,0:T(8,128)(2,1)} %collective-permute-done.38.refs_0_), custom_call_target="tpu_custom_call" | custom-call | flops 1 | bytes 1 | tf_op jit(solution)/shard_map/gradient/pallas_call | solution.py:725
  334.3 7.8 %d_hidden_layer.1 = (bf16[592,4096]{1,0:T(8,128)(2,1)S(1)}, f32[1,4096]{1,0:T(1,128)S(1)}) custom-call(bf16[592,1024]{1,0:T(8,128)(2,1)S(1)} %copy-done.24, bf16[4096,1024]{1,0:T(8,128)(2,1)S(1)} %bitcast.210, bf16[592,4096]{1,0:T(8,128)(2,1)S(1)} %copy-done.35), custom_call_target="tpu_custom_call" | custom-call | flops 1 | bytes 1 | tf_op jit(solution)/shard_map/d_hidden_layer/pallas_call | solution.py:584
  342.1 3.3 gradient.14
  352.7 4.3 fusion.14
  358.6 12.0 %norm_back.2 = (f32[592,1024]{1,0:T(8,128)S(1)}, bf16[592,1024]{1,0:T(8,128)(2,1)S(1)}, f32[8,1024]{1,0:T(8,128)S(1)}) custom-call(bf16[592,4096]{1,0:T(8,128)(2,1)S(1)} %copy-done.1, bf16[1024,4096]{1,0:T(8,128)(2,1)} %copy-done.19, f32[592,1024]{1,0:T(8,128)S(1)} %copy-done.29, f32[592,1]{1,0:T(8,128)S(1)} %rsqrt.14.refs_1_, ...), custom_call_target="tpu_custom_call" | custom-call | flops 1 | bytes 1 | tf_op jit(solution)/shard_map/norm_back/pallas_call | solution.py:685
  377.3 3.3 gradient.15
  384.6 3.7 gradient.13
  391.8 6.3 %collective-permute-done.42 = bf16[1024,1024]{1,0:T(8,128)(2,1)} collective-permute-done((bf16[1024,1024]{1,0:T(8,128)(2,1)}, bf16[1024,1024]{1,0:T(8,128)(2,1)}, u32[]{:S(2)}, u32[]{:S(2)}) %collective-permute-start.42) | collective-permute-done | bytes 2097184 | tf_op jit(solution)/shard_map/ppermute | solution.py:825
  402.0 3.8 collective-permute-start.49
  408.2 13.3 %attention_backward.2.d_ref = bf16[3,592,512]{2,1,0:T(8,128)(2,1)S(1)} custom-call(bf16[3,592,512]{2,1,0:T(8,128)(2,1)S(1)} %copy-done.4, bf16[3,592,512]{2,1,0:T(8,128)(2,1)S(1)} %copy-done.4, bf16[3,592,512]{2,1,0:T(8,128)(2,1)S(1)} %copy-done.4, bf16[592,1024]{1,0:T(8,128)(2,1)S(1)} %convolution_convert_fusion.1.d_ref, f32[4,2,592]{2,1,0:T(2,128)S(1)} %copy-done.61, ...), custom_call_target="tpu_custom_call" | custom-call | flops 1 | bytes 1 | tf_op jit(solution)/shard_map/attention_backward/pallas_call | solution.py:459
  421.6 4.2 add_convert_fusion.5
  425.7 3.3 d_normed.1.refs_0_
  439.4 8.1 %collective-permute-done.45 = bf16[256,1024]{1,0:T(8,128)(2,1)} collective-permute-done((bf16[256,1024]{1,0:T(8,128)(2,1)}, bf16[256,1024]{1,0:T(8,128)(2,1)}, u32[]{:S(2)}, u32[]{:S(2)}) %collective-permute-start.45) | collective-permute-done | bytes 524320 | tf_op jit(solution)/shard_map/ppermute | solution.py:825
  450.8 13.4 %attention_backward.3.d_ref = bf16[3,592,512]{2,1,0:T(8,128)(2,1)S(1)} custom-call(bf16[3,592,512]{2,1,0:T(8,128)(2,1)S(1)} %project.3.query_ref.key_ref.value_ref, bf16[3,592,512]{2,1,0:T(8,128)(2,1)S(1)} %project.3.query_ref.key_ref.value_ref, bf16[3,592,512]{2,1,0:T(8,128)(2,1)S(1)} %project.3.query_ref.key_ref.value_ref, ...), custom_call_target="tpu_custom_call" | custom-call | flops 1 | bytes 1 | tf_op jit(solution)/shard_map/attention_backward/pallas_call | solution.py:459
  482.3 5.0 norm_back.3
  494.7 3.8 fusion.13
  502.9 3.8 reshape.578
  508.4 5.5 collective-permute-done.54
  521.3 4.9 collective-permute-done.55
  526.4 4.0 collective-permute-start.58
  530.8 3.9 convolution_add_fusion
  540.8 3.8 collective-permute-start.69
  545.0 5.3 collective-permute-done.63
  550.5 3.8 collective-permute-start.66
  554.3 16.7 %collective-permute-start.65 = (bf16[32,1664]{1,0:T(8,128)(2,1)S(1)}, bf16[32,1664]{1,0:T(8,128)(2,1)S(1)}, u32[]{:S(2)}, u32[]{:S(2)}) collective-permute-start(bf16[32,1664]{1,0:T(8,128)(2,1)S(1)} %get-tuple-element.197), channel_id=1, source_target_pairs={{0,16},{8,24},{16,0},{24,8},{1,17},{9,25},{17,1},{25,9},{2,18},{10... | collective-permute-start | bytes 319496 | tf_op jit(solution)/shard_map/ppermute | solution.py:896
  571.1 5.0 collective-permute-done.68
  (526 shorter events, 201.6 us)
Async XLA Ops:
  9.5 17.4 %collective-permute-start.3 = (bf16[32,3200]{1,0:T(8,128)(2,1)S(1)}, bf16[32,3200]{1,0:T(8,128)(2,1)S(1)}, u32[]{:S(2)}, u32[]{:S(2)}) collective-permute-start(bf16[32,3200]{1,0:T(8,128)(2,1)S(1)} %fusion.31.refs_0_), channel_id=1, source_target_pairs={{0,16},{8,24},{16,0},{24,8},{1,17},{9,25},{17,1},{25,9},{2,18},{10... | collective-permute-start | bytes 614408 | tf_op jit(solution)/shard_map/ppermute | solution.py:836
  9.5 17.4 %collective-permute-start.2 = (bf16[32,3200]{1,0:T(8,128)(2,1)S(1)}, bf16[32,3200]{1,0:T(8,128)(2,1)S(1)}, u32[]{:S(2)}, u32[]{:S(2)}) collective-permute-start(bf16[32,3200]{1,0:T(8,128)(2,1)S(1)} %fusion.31.refs_0_), channel_id=1, source_target_pairs={{0,8},{8,16},{16,24},{24,0},{1,9},{9,17},{17,25},{25,1},{2,10},{10... | collective-permute-start | bytes 614408 | tf_op jit(solution)/shard_map/ppermute | solution.py:836
  10.5 22.1 %collective-permute-start = (s32[584]{0:T(1024)}, s32[584]{0:T(1024)S(1)}, u32[]{:S(2)}, u32[]{:S(2)}) collective-permute-start(s32[584]{0:T(1024)} %param.18), channel_id=1, source_target_pairs={{0,1},{1,0},{2,3},{3,2},{4,5},{5,4},{6,7},{7,6},{8,9},{9,8},{10,11... | collective-permute-start | bytes 7016 | tf_op jit(solution)/shard_map/ppermute | solution.py:825
  12.0 31.7 %collective-permute-start.1 = (bf16[584,1024]{1,0:T(8,128)(2,1)}, bf16[584,1024]{1,0:T(8,128)(2,1)}, u32[]{:S(2)}, u32[]{:S(2)}) collective-permute-start(bf16[584,1024]{1,0:T(8,128)(2,1)} %param.16), channel_id=1, source_target_pairs={{0,1},{1,0},{2,3},{3,2},{4,5},{5,4},{6,7},{7,6},{8,9},{9,8},{10,11... | collective-permute-start | bytes 3588104 | tf_op jit(solution)/shard_map/ppermute | solution.py:825
  33.9 36.0 %collective-permute-start.6 = (bf16[128,1664]{1,0:T(8,128)(2,1)}, bf16[128,1664]{1,0:T(8,128)(2,1)}, u32[]{:S(2)}, u32[]{:S(2)}) collective-permute-start(bf16[128,1664]{1,0:T(8,128)(2,1)} %get-tuple-element.81.refs_0_), channel_id=1, source_target_pairs={{0,1},{1,0},{2,3},{3,2},{4,5},{5,4},{6,7},{7,6},{8,9},{9,8},{10,11... | collective-permute-start | bytes 1277960 | tf_op jit(solution)/shard_map/ppermute | solution.py:825
  42.1 28.3 %collective-permute-start.7 = (bf16[128,1664]{1,0:T(8,128)(2,1)}, bf16[128,1664]{1,0:T(8,128)(2,1)}, u32[]{:S(2)}, u32[]{:S(2)}) collective-permute-start(bf16[128,1664]{1,0:T(8,128)(2,1)} %collective-permute-done.5.refs_1_), channel_id=1, source_target_pairs={{0,1},{1,0},{2,3},{3,2},{4,5},{5,4},{6,7},{7,6},{8,9},{9,8},{10,11... | collective-permute-start | bytes 1277960 | tf_op jit(solution)/shard_map/ppermute | solution.py:825
  43.7 22.3 %collective-permute-start.12 = (bf16[128,1536]{1,0:T(8,128)(2,1)}, bf16[128,1536]{1,0:T(8,128)(2,1)}, u32[]{:S(2)}, u32[]{:S(2)}) collective-permute-start(bf16[128,1536]{1,0:T(8,128)(2,1)} %get-tuple-element.85.refs_0_), channel_id=1, source_target_pairs={{0,1},{1,0},{2,3},{3,2},{4,5},{5,4},{6,7},{7,6},{8,9},{9,8},{10,11... | collective-permute-start | bytes 1179656 | tf_op jit(solution)/shard_map/ppermute | solution.py:825
  48.0 29.7 %collective-permute-start.13 = (bf16[128,1536]{1,0:T(8,128)(2,1)}, bf16[128,1536]{1,0:T(8,128)(2,1)}, u32[]{:S(2)}, u32[]{:S(2)}) collective-permute-start(bf16[128,1536]{1,0:T(8,128)(2,1)} %get-tuple-element.85.refs_0_), channel_id=1, source_target_pairs={{0,4},{4,0},{1,5},{5,1},{2,6},{6,2},{3,7},{7,3},{8,12},{12,8},{9,1... | collective-permute-start | bytes 1179656 | tf_op jit(solution)/shard_map/ppermute | solution.py:825
  69.1 27.3 %collective-permute-start.20 = (bf16[32,5120]{1,0:T(8,128)(2,1)S(1)}, bf16[32,5120]{1,0:T(8,128)(2,1)S(1)}, u32[]{:S(2)}, u32[]{:S(2)}) collective-permute-start(bf16[32,5120]{1,0:T(8,128)(2,1)S(1)} %pad_maximum_fusion.3.refs_0_), channel_id=1, source_target_pairs={{0,16},{8,24},{16,0},{24,8},{1,17},{9,25},{17,1},{25,9},{2,18},{10... | collective-permute-start | bytes 983048 | tf_op jit(solution)/shard_map/ppermute | solution.py:836
  69.9 26.5 %collective-permute-start.19 = (bf16[32,5120]{1,0:T(8,128)(2,1)S(1)}, bf16[32,5120]{1,0:T(8,128)(2,1)S(1)}, u32[]{:S(2)}, u32[]{:S(2)}) collective-permute-start(bf16[32,5120]{1,0:T(8,128)(2,1)S(1)} %pad_maximum_fusion.3.refs_0_), channel_id=1, source_target_pairs={{0,8},{8,16},{16,24},{24,0},{1,9},{9,17},{17,25},{25,1},{2,10},{10... | collective-permute-start | bytes 983048 | tf_op jit(solution)/shard_map/ppermute | solution.py:836
  70.4 27.3 %collective-permute-start.14 = (bf16[128,1536]{1,0:T(8,128)(2,1)}, bf16[128,1536]{1,0:T(8,128)(2,1)}, u32[]{:S(2)}, u32[]{:S(2)}) collective-permute-start(bf16[128,1536]{1,0:T(8,128)(2,1)} %collective-permute-done.12.refs_1_), channel_id=1, source_target_pairs={{0,4},{4,0},{1,5},{5,1},{2,6},{6,2},{3,7},{7,3},{8,12},{12,8},{9,1... | collective-permute-start | bytes 1179656 | tf_op jit(solution)/shard_map/ppermute | solution.py:825
  77.8 24.2 %collective-permute-start.8 = (bf16[128,1664]{1,0:T(8,128)(2,1)}, bf16[128,1664]{1,0:T(8,128)(2,1)S(1)}, u32[]{:S(2)}, u32[]{:S(2)}) collective-permute-start(bf16[128,1664]{1,0:T(8,128)(2,1)} %get-tuple-element.81.refs_0_), channel_id=1, source_target_pairs={{0,2},{2,0},{1,3},{3,1},{4,6},{6,4},{5,7},{7,5},{8,10},{10,8},{9,1... | collective-permute-start | bytes 1277960 | tf_op jit(solution)/shard_map/ppermute | solution.py:825
  77.8 25.8 %collective-permute-start.10 = (bf16[128,1664]{1,0:T(8,128)(2,1)}, bf16[128,1664]{1,0:T(8,128)(2,1)S(1)}, u32[]{:S(2)}, u32[]{:S(2)}) collective-permute-start(bf16[128,1664]{1,0:T(8,128)(2,1)} %collective-permute-done.6.refs_2_), channel_id=1, source_target_pairs={{0,2},{2,0},{1,3},{3,1},{4,6},{6,4},{5,7},{7,5},{8,10},{10,8},{9,1... | collective-permute-start | bytes 1277960 | tf_op jit(solution)/shard_map/ppermute | solution.py:825
  102.0 23.3 %collective-permute-start.23 = (bf16[128,2560]{1,0:T(8,128)(2,1)}, bf16[128,2560]{1,0:T(8,128)(2,1)S(1)}, u32[]{:S(2)}, u32[]{:S(2)}) collective-permute-start(bf16[128,2560]{1,0:T(8,128)(2,1)} %get-tuple-element.95.refs_0_), channel_id=1, source_target_pairs={{0,4},{4,0},{1,5},{5,1},{2,6},{6,2},{3,7},{7,3},{8,12},{12,8},{9,1... | collective-permute-start | bytes 1966088 | tf_op jit(solution)/shard_map/ppermute | solution.py:825
  103.5 22.2 %collective-permute-start.26 = (bf16[128,2560]{1,0:T(8,128)(2,1)}, bf16[128,2560]{1,0:T(8,128)(2,1)}, u32[]{:S(2)}, u32[]{:S(2)}) collective-permute-start(bf16[128,2560]{1,0:T(8,128)(2,1)} %get-tuple-element.101.refs_4_), channel_id=1, source_target_pairs={{0,1},{1,0},{2,3},{3,2},{4,5},{5,4},{6,7},{7,6},{8,9},{9,8},{10,11... | collective-permute-start | bytes 1966088 | tf_op jit(solution)/shard_map/ppermute | solution.py:825
  112.8 35.3 %collective-permute-start.24 = (bf16[128,2560]{1,0:T(8,128)(2,1)}, bf16[128,2560]{1,0:T(8,128)(2,1)}, u32[]{:S(2)}, u32[]{:S(2)}) collective-permute-start(bf16[128,2560]{1,0:T(8,128)(2,1)} %get-tuple-element.95.refs_0_), channel_id=1, source_target_pairs={{0,1},{1,0},{2,3},{3,2},{4,5},{5,4},{6,7},{7,6},{8,9},{9,8},{10,11... | collective-permute-start | bytes 1966088 | tf_op jit(solution)/shard_map/ppermute | solution.py:825
  115.1 33.0 %collective-permute-start.27 = (bf16[128,2560]{1,0:T(8,128)(2,1)}, bf16[128,2560]{1,0:T(8,128)(2,1)}, u32[]{:S(2)}, u32[]{:S(2)}) collective-permute-start(bf16[128,2560]{1,0:T(8,128)(2,1)} %get-tuple-element.101.refs_4_), channel_id=1, source_target_pairs={{0,4},{4,0},{1,5},{5,1},{2,6},{6,2},{3,7},{7,3},{8,12},{12,8},{9,1... | collective-permute-start | bytes 1966088 | tf_op jit(solution)/shard_map/ppermute | solution.py:825
  125.3 23.5 %collective-permute-start.25 = (bf16[128,2560]{1,0:T(8,128)(2,1)S(1)}, bf16[128,2560]{1,0:T(8,128)(2,1)}, u32[]{:S(2)}, u32[]{:S(2)}) collective-permute-start(bf16[128,2560]{1,0:T(8,128)(2,1)S(1)} %collective-permute-done.23.refs_1_), channel_id=1, source_target_pairs={{0,1},{1,0},{2,3},{3,2},{4,5},{5,4},{6,7},{7,6},{8,9},{9,8},{10,11... | collective-permute-start | bytes 1966088 | tf_op jit(solution)/shard_map/ppermute | solution.py:825
  125.8 22.4 %collective-permute-start.28 = (bf16[128,2560]{1,0:T(8,128)(2,1)}, bf16[128,2560]{1,0:T(8,128)(2,1)}, u32[]{:S(2)}, u32[]{:S(2)}) collective-permute-start(bf16[128,2560]{1,0:T(8,128)(2,1)} %collective-permute-done.26.refs_5_), channel_id=1, source_target_pairs={{0,4},{4,0},{1,5},{5,1},{2,6},{6,2},{3,7},{7,3},{8,12},{12,8},{9,1... | collective-permute-start | bytes 1966088 | tf_op jit(solution)/shard_map/ppermute | solution.py:825
  153.4 91.5 %collective-permute-start.29 = (bf16[512,5120]{1,0:T(8,128)(2,1)}, bf16[512,5120]{1,0:T(8,128)(2,1)}, u32[]{:S(2)}, u32[]{:S(2)}) collective-permute-start(bf16[512,5120]{1,0:T(8,128)(2,1)} %assemble.14.refs_0_), channel_id=1, source_target_pairs={{0,2},{2,0},{1,3},{3,1},{4,6},{6,4},{5,7},{7,5},{8,10},{10,8},{9,1... | collective-permute-start | bytes 15728648 | tf_op jit(solution)/shard_map/ppermute | solution.py:825
  153.5 85.9 %collective-permute-start.37 = (bf16[584,1024]{1,0:T(8,128)(2,1)}, bf16[584,1024]{1,0:T(8,128)(2,1)}, u32[]{:S(2)}, u32[]{:S(2)}) collective-permute-start(bf16[584,1024]{1,0:T(8,128)(2,1)} %param.17), channel_id=1, source_target_pairs={{0,1},{1,0},{2,3},{3,2},{4,5},{5,4},{6,7},{7,6},{8,9},{9,8},{10,11... | collective-permute-start | bytes 3588104 | tf_op jit(solution)/shard_map/ppermute | solution.py:825
  156.5 31.6 %collective-permute-start.22 = (bf16[128,1024]{1,0:T(8,128)(2,1)S(1)}, bf16[128,1024]{1,0:T(8,128)(2,1)S(1)}, u32[]{:S(2)}, u32[]{:S(2)}) collective-permute-start(bf16[128,1024]{1,0:T(8,128)(2,1)S(1)} %copy.139.refs_0_), channel_id=1, source_target_pairs={{0,1},{1,0},{2,3},{3,2},{4,5},{5,4},{6,7},{7,6},{8,9},{9,8},{10,11... | collective-permute-start | bytes 786440 | tf_op jit(solution)/shard_map/ppermute | solution.py:825
  188.7 30.5 %collective-permute-start.32 = (bf16[256,1024]{1,0:T(8,128)(2,1)S(1)}, bf16[256,1024]{1,0:T(8,128)(2,1)}, u32[]{:S(2)}, u32[]{:S(2)}) collective-permute-start(bf16[256,1024]{1,0:T(8,128)(2,1)S(1)} %assemble.13.refs_0_), channel_id=1, source_target_pairs={{0,24},{8,0},{16,8},{24,16},{1,25},{9,1},{17,9},{25,17},{2,26},{10... | collective-permute-start | bytes 1572872 | tf_op jit(solution)/shard_map/ppermute | solution.py:836
  188.8 46.9 %collective-permute-start.31 = (bf16[256,1024]{1,0:T(8,128)(2,1)S(1)}, bf16[256,1024]{1,0:T(8,128)(2,1)}, u32[]{:S(2)}, u32[]{:S(2)}) collective-permute-start(bf16[256,1024]{1,0:T(8,128)(2,1)S(1)} %assemble.13.refs_0_), channel_id=1, source_target_pairs={{0,16},{8,24},{16,0},{24,8},{1,17},{9,25},{17,1},{25,9},{2,18},{10... | collective-permute-start | bytes 1572872 | tf_op jit(solution)/shard_map/ppermute | solution.py:836
  190.2 45.5 %collective-permute-start.30 = (bf16[256,1024]{1,0:T(8,128)(2,1)S(1)}, bf16[256,1024]{1,0:T(8,128)(2,1)}, u32[]{:S(2)}, u32[]{:S(2)}) collective-permute-start(bf16[256,1024]{1,0:T(8,128)(2,1)S(1)} %assemble.13.refs_0_), channel_id=1, source_target_pairs={{0,8},{8,16},{16,24},{24,0},{1,9},{9,17},{17,25},{25,1},{2,10},{10... | collective-permute-start | bytes 1572872 | tf_op jit(solution)/shard_map/ppermute | solution.py:836
  238.7 47.0 %collective-permute-start.33 = (bf16[1024,1024]{1,0:T(8,128)(2,1)}, bf16[1024,1024]{1,0:T(8,128)(2,1)}, u32[]{:S(2)}, u32[]{:S(2)}) collective-permute-start(bf16[1024,1024]{1,0:T(8,128)(2,1)} %assemble.16.refs_0_), channel_id=1, source_target_pairs={{0,4},{4,0},{1,5},{5,1},{2,6},{6,2},{3,7},{7,3},{8,12},{12,8},{9,1... | collective-permute-start | bytes 6291464 | tf_op jit(solution)/shard_map/ppermute | solution.py:825
  285.4 34.9 %collective-permute-start.38 = (bf16[2048,1024]{1,0:T(8,128)(2,1)}, bf16[2048,1024]{1,0:T(8,128)(2,1)}, u32[]{:S(2)}, u32[]{:S(2)}) collective-permute-start(bf16[2048,1024]{1,0:T(8,128)(2,1)} %gradient.10), channel_id=1, source_target_pairs={{0,2},{2,0},{1,3},{3,1},{4,6},{6,4},{5,7},{7,5},{8,10},{10,8},{9,1... | collective-permute-start | bytes 12582920 | tf_op jit(solution)/shard_map/ppermute | solution.py:825
  345.4 28.2 %collective-permute-start.40 = (bf16[512,2048]{1,0:T(8,128)(2,1)}, bf16[512,2048]{1,0:T(8,128)(2,1)}, u32[]{:S(2)}, u32[]{:S(2)}) collective-permute-start(bf16[512,2048]{1,0:T(8,128)(2,1)} %gradient.14), channel_id=1, source_target_pairs={{0,2},{2,0},{1,3},{3,1},{4,6},{6,4},{5,7},{7,5},{8,10},{10,8},{9,1... | collective-permute-start | bytes 6291464 | tf_op jit(solution)/shard_map/ppermute | solution.py:825
  348.9 35.6 %collective-permute-start.39 = (bf16[512,2048]{1,0:T(8,128)(2,1)}, bf16[512,2048]{1,0:T(8,128)(2,1)}, u32[]{:S(2)}, u32[]{:S(2)}) collective-permute-start(bf16[512,2048]{1,0:T(8,128)(2,1)} %gradient.12), channel_id=1, source_target_pairs={{0,2},{2,0},{1,3},{3,1},{4,6},{6,4},{5,7},{7,5},{8,10},{10,8},{9,1... | collective-permute-start | bytes 6291464 | tf_op jit(solution)/shard_map/ppermute | solution.py:825
  349.3 48.8 %collective-permute-start.42 = (bf16[1024,1024]{1,0:T(8,128)(2,1)}, bf16[1024,1024]{1,0:T(8,128)(2,1)}, u32[]{:S(2)}, u32[]{:S(2)}) collective-permute-start(bf16[1024,1024]{1,0:T(8,128)(2,1)} %get-tuple-element.170), channel_id=1, source_target_pairs={{0,4},{4,0},{1,5},{5,1},{2,6},{6,2},{3,7},{7,3},{8,12},{12,8},{9,1... | collective-permute-start | bytes 6291464 | tf_op jit(solution)/shard_map/ppermute | solution.py:825
  351.3 49.3 %collective-permute-start.36 = (bf16[592,1024]{1,0:T(8,128)(2,1)}, bf16[592,1024]{1,0:T(8,128)(2,1)}, u32[]{:S(2)}, u32[]{:S(2)}) collective-permute-start(bf16[592,1024]{1,0:T(8,128)(2,1)} %fusion.9), channel_id=1, source_target_pairs={{0,1},{1,0},{2,3},{3,2},{4,5},{5,4},{6,7},{7,6},{8,9},{9,8},{10,11... | collective-permute-start | bytes 3637256 | tf_op jit(solution)/shard_map/ppermute | solution.py:825
  388.9 45.1 %collective-permute-start.43 = (bf16[256,2048]{1,0:T(8,128)(2,1)S(1)}, bf16[256,2048]{1,0:T(8,128)(2,1)S(1)}, u32[]{:S(2)}, u32[]{:S(2)}) collective-permute-start(bf16[256,2048]{1,0:T(8,128)(2,1)S(1)} %bitcast.239), channel_id=1, source_target_pairs={{0,1},{1,0},{2,3},{3,2},{4,5},{5,4},{6,7},{7,6},{8,9},{9,8},{10,11... | collective-permute-start | bytes 3145736 | tf_op jit(solution)/shard_map/ppermute | solution.py:825
  389.6 42.5 %collective-permute-start.44 = (bf16[256,2048]{1,0:T(8,128)(2,1)S(1)}, bf16[256,2048]{1,0:T(8,128)(2,1)S(1)}, u32[]{:S(2)}, u32[]{:S(2)}) collective-permute-start(bf16[256,2048]{1,0:T(8,128)(2,1)S(1)} %get-tuple-element.176), channel_id=1, source_target_pairs={{0,4},{4,0},{1,5},{5,1},{2,6},{6,2},{3,7},{7,3},{8,12},{12,8},{9,1... | collective-permute-start | bytes 3145736 | tf_op jit(solution)/shard_map/ppermute | solution.py:825
  402.0 65.5 %collective-permute-start.47 = (bf16[256,1024]{1,0:T(8,128)(2,1)}, bf16[256,1024]{1,0:T(8,128)(2,1)}, u32[]{:S(2)}, u32[]{:S(2)}) collective-permute-start(bf16[256,1024]{1,0:T(8,128)(2,1)} %get-tuple-element.172), channel_id=1, source_target_pairs={{0,8},{8,16},{16,24},{24,0},{1,9},{9,17},{17,25},{25,1},{2,10},{10... | collective-permute-start | bytes 1572872 | tf_op jit(solution)/shard_map/ppermute | solution.py:896
  402.0 65.6 %collective-permute-start.49 = (bf16[256,1024]{1,0:T(8,128)(2,1)}, bf16[256,1024]{1,0:T(8,128)(2,1)}, u32[]{:S(2)}, u32[]{:S(2)}) collective-permute-start(bf16[256,1024]{1,0:T(8,128)(2,1)} %get-tuple-element.173), channel_id=1, source_target_pairs={{0,24},{8,0},{16,8},{24,16},{1,25},{9,1},{17,9},{25,17},{2,26},{10... | collective-permute-start | bytes 1572872 | tf_op jit(solution)/shard_map/ppermute | solution.py:896
  405.9 62.6 %collective-permute-start.48 = (bf16[256,1024]{1,0:T(8,128)(2,1)}, bf16[256,1024]{1,0:T(8,128)(2,1)}, u32[]{:S(2)}, u32[]{:S(2)}) collective-permute-start(bf16[256,1024]{1,0:T(8,128)(2,1)} %get-tuple-element.174), channel_id=1, source_target_pairs={{0,16},{8,24},{16,0},{24,8},{1,17},{9,25},{17,1},{25,9},{2,18},{10... | collective-permute-start | bytes 1572872 | tf_op jit(solution)/shard_map/ppermute | solution.py:896
  435.6 34.7 %collective-permute-start.50 = (bf16[128,2048]{1,0:T(8,128)(2,1)}, bf16[128,2048]{1,0:T(8,128)(2,1)}, u32[]{:S(2)}, u32[]{:S(2)}) collective-permute-start(bf16[128,2048]{1,0:T(8,128)(2,1)} %get-tuple-element.185), channel_id=1, source_target_pairs={{0,4},{4,0},{1,5},{5,1},{2,6},{6,2},{3,7},{7,3},{8,12},{12,8},{9,1... | collective-permute-start | bytes 1572872 | tf_op jit(solution)/shard_map/ppermute | solution.py:825
  447.5 22.9 %collective-permute-start.51 = (bf16[128,2048]{1,0:T(8,128)(2,1)}, bf16[128,2048]{1,0:T(8,128)(2,1)}, u32[]{:S(2)}, u32[]{:S(2)}) collective-permute-start(bf16[128,2048]{1,0:T(8,128)(2,1)} %get-tuple-element.187), channel_id=1, source_target_pairs={{0,1},{1,0},{2,3},{3,2},{4,5},{5,4},{6,7},{7,6},{8,9},{9,8},{10,11... | collective-permute-start | bytes 1572872 | tf_op jit(solution)/shard_map/ppermute | solution.py:825
  471.1 19.5 %collective-permute-start.70 = (bf16[128,1024]{1,0:T(8,128)(2,1)S(1)}, bf16[128,1024]{1,0:T(8,128)(2,1)S(1)}, u32[]{:S(2)}, u32[]{:S(2)}) collective-permute-start(bf16[128,1024]{1,0:T(8,128)(2,1)S(1)} %get-tuple-element.191), channel_id=1, source_target_pairs={{0,1},{1,0},{2,3},{3,2},{4,5},{5,4},{6,7},{7,6},{8,9},{9,8},{10,11... | collective-permute-start | bytes 786440 | tf_op jit(solution)/shard_map/ppermute | solution.py:825
  472.4 44.4 %collective-permute-start.59 = (bf16[512,1536]{1,0:T(8,128)(2,1)}, bf16[512,1536]{1,0:T(8,128)(2,1)}, u32[]{:S(2)}, u32[]{:S(2)}) collective-permute-start(bf16[512,1536]{1,0:T(8,128)(2,1)} %gradient.18), channel_id=1, source_target_pairs={{0,2},{2,0},{1,3},{3,1},{4,6},{6,4},{5,7},{7,5},{8,10},{10,8},{9,1... | collective-permute-start | bytes 4718600 | tf_op jit(solution)/shard_map/ppermute | solution.py:825
  489.8 41.0 %collective-permute-start.53 = (bf16[592,1024]{1,0:T(8,128)(2,1)}, bf16[592,1024]{1,0:T(8,128)(2,1)}, u32[]{:S(2)}, u32[]{:S(2)}) collective-permute-start(bf16[592,1024]{1,0:T(8,128)(2,1)} %fusion.10), channel_id=1, source_target_pairs={{0,1},{1,0},{2,3},{3,2},{4,5},{5,4},{6,7},{7,6},{8,9},{9,8},{10,11... | collective-permute-start | bytes 3637256 | tf_op jit(solution)/shard_map/ppermute | solution.py:825
  493.2 20.7 %collective-permute-start.54 = (bf16[256,1536]{1,0:T(8,128)(2,1)}, bf16[256,1536]{1,0:T(8,128)(2,1)}, u32[]{:S(2)}, u32[]{:S(2)}) collective-permute-start(bf16[256,1536]{1,0:T(8,128)(2,1)} %get-tuple-element.180), channel_id=1, source_target_pairs={{0,4},{4,0},{1,5},{5,1},{2,6},{6,2},{3,7},{7,3},{8,12},{12,8},{9,1... | collective-permute-start | bytes 2359304 | tf_op jit(solution)/shard_map/ppermute | solution.py:825
  519.7 18.6 %collective-permute-start.60 = (bf16[256,1536]{1,0:T(8,128)(2,1)S(1)}, bf16[256,1536]{1,0:T(8,128)(2,1)S(1)}, u32[]{:S(2)}, u32[]{:S(2)}) collective-permute-start(bf16[256,1536]{1,0:T(8,128)(2,1)S(1)} %dynamic-slice_bitcast_fusion.5), channel_id=1, source_target_pairs={{0,4},{4,0},{1,5},{5,1},{2,6},{6,2},{3,7},{7,3},{8,12},{12,8},{9,1... | collective-permute-start | bytes 2359304 | tf_op jit(solution)/shard_map/ppermute | solution.py:825
  540.8 30.3 %collective-permute-start.69 = (bf16[32,5120]{1,0:T(8,128)(2,1)S(1)}, bf16[32,5120]{1,0:T(8,128)(2,1)S(1)}, u32[]{:S(2)}, u32[]{:S(2)}) collective-permute-start(bf16[32,5120]{1,0:T(8,128)(2,1)S(1)} %get-tuple-element.183), channel_id=1, source_target_pairs={{0,24},{8,0},{16,8},{24,16},{1,25},{9,1},{17,9},{25,17},{2,26},{10... | collective-permute-start | bytes 983048 | tf_op jit(solution)/shard_map/ppermute | solution.py:896
  544.6 31.5 %collective-permute-start.68 = (bf16[32,5120]{1,0:T(8,128)(2,1)S(1)}, bf16[32,5120]{1,0:T(8,128)(2,1)S(1)}, u32[]{:S(2)}, u32[]{:S(2)}) collective-permute-start(bf16[32,5120]{1,0:T(8,128)(2,1)S(1)} %get-tuple-element.184), channel_id=1, source_target_pairs={{0,16},{8,24},{16,0},{24,8},{1,17},{9,25},{17,1},{25,9},{2,18},{10... | collective-permute-start | bytes 983048 | tf_op jit(solution)/shard_map/ppermute | solution.py:896
  550.4 29.4 %collective-permute-start.64 = (bf16[32,1664]{1,0:T(8,128)(2,1)S(1)}, bf16[32,1664]{1,0:T(8,128)(2,1)S(1)}, u32[]{:S(2)}, u32[]{:S(2)}) collective-permute-start(bf16[32,1664]{1,0:T(8,128)(2,1)S(1)} %get-tuple-element.195), channel_id=1, source_target_pairs={{0,8},{8,16},{16,24},{24,0},{1,9},{9,17},{17,25},{25,1},{2,10},{10... | collective-permute-start | bytes 319496 | tf_op jit(solution)/shard_map/ppermute | solution.py:896
  550.5 29.3 %collective-permute-start.66 = (bf16[32,1664]{1,0:T(8,128)(2,1)S(1)}, bf16[32,1664]{1,0:T(8,128)(2,1)S(1)}, u32[]{:S(2)}, u32[]{:S(2)}) collective-permute-start(bf16[32,1664]{1,0:T(8,128)(2,1)S(1)} %get-tuple-element.196), channel_id=1, source_target_pairs={{0,24},{8,0},{16,8},{24,16},{1,25},{9,1},{17,9},{25,17},{2,26},{10... | collective-permute-start | bytes 319496 | tf_op jit(solution)/shard_map/ppermute | solution.py:896
  554.3 26.0 %collective-permute-start.65 = (bf16[32,1664]{1,0:T(8,128)(2,1)S(1)}, bf16[32,1664]{1,0:T(8,128)(2,1)S(1)}, u32[]{:S(2)}, u32[]{:S(2)}) collective-permute-start(bf16[32,1664]{1,0:T(8,128)(2,1)S(1)} %get-tuple-element.197), channel_id=1, source_target_pairs={{0,16},{8,24},{16,0},{24,8},{1,17},{9,25},{17,1},{25,9},{2,18},{10... | collective-permute-start | bytes 319496 | tf_op jit(solution)/shard_map/ppermute | solution.py:896
  (139 other events, 1275.3 us)

commit v8 on v7

--- a/solution.py
+++ b/solution.py
@@ -829,11 +829,12 @@
     return lax.optimization_barrier((array, *others))[0]
 
 
-def gather_far(shard, far, widths=None):
+def gather_far(shard, far, widths=None, follow=()):
     place = lax.axis_index("z")
     pieces, indices = [shard], [place]
     for step in range(1, far):
-        pieces.append(lax.ppermute(shard, "z", [(i, (i + step) % far) for i in range(far)]))
+        got = lax.ppermute(shard, "z", [(i, (i + step) % far) for i in range(far)])
+        pieces.append(after(got, *follow) if follow else got)
         indices.append((place - step) % far)
     rows, width = shard.shape
     widths = widths or [width]
@@ -961,11 +962,13 @@
         one = spread({OWN: far_one}, "x")
         two = spread({OWN: after(far_two, inputs_far)}, "ctx")
         first = list(one.values()) + list(two.values())
-        far_up = gather_far(after(shard_up, *first), far, [up_cut, up_cut])
         one, two = spread(one, "ctx"), spread(two, "x")
         all_one = list(one.values()) + list(two.values())
-        shard_down = after(to_local(unfold(w_down), 1, far), far_up[0], *all_one)
+        shard_down = after(to_local(unfold(w_down), 1, far), *first)
         near_down = order_blocks(spread({OWN: shard_down}, "ctx"), ["ctx"])
+        far_up = gather_far(
+            after(shard_up, *all_one), far, [up_cut, up_cut], [near_down]
+        )
         one_core, two_core = spread(one, "core"), spread(two, "core")
         axes = ["core", "x", "ctx"]
         routes = [[(0, half_qkv, 0, 0), (half_qkv, 128, 1, 0)]] * 8
@@ -980,7 +983,7 @@
         up_two = spread({OWN: after(far_up[1], *all_one)}, "ctx")
         up_one = spread(tie_received(up_one, qkv_two_weight), "ctx")
         up_two = spread(tie_received(up_two, qkv_two_weight), "x")
-        far_down = gather_far(near_down, far)[0]
+        far_down = gather_far(after(near_down, far_up[0]), far)[0]
 
         devices = 8 * far
         small_core = small_local.reshape(devices, shard_rows, 128)[:, :small_rows, :near_width]
@@ -1043,7 +1046,9 @@
             for cut in (slice(0, half_width), slice(half_width, width))
         ]
         joined_one = project(normed1, qkv_one, joined_bias[0])
-        attended, log_one = attention_forward(after(joined_one, qkv_two_weight), bias, width, 0)
+        attended, log_one = attention_forward(
+            after(joined_one, qkv_two_weight), bias, width, 0
+        )
         joined_two = project(after(normed1, log_one), qkv_two_weight, joined_bias[1])
         up_one, up_two = tie_received(up_one, log_one), tie_received(up_two, log_one)
         up_near = assemble(
@@ -1054,7 +1059,7 @@
         )[0]
         up_blocks = spread({OWN: up_near}, "core")
         attended, log_two = attention_forward(
-            after(joined_two, near_down), bias, width, half_width // PAIR, attended
+            joined_two, bias, width, half_width // PAIR, attended
         )
         cotangent_far = swap(after(cotangent, up_near))
         down_blocks = spread({OWN: after(far_down, up_near)}, "x")
@@ -1106,21 +1111,19 @@
         partial = d_normed(d_one, qkv_one)
         up_one = send_half(add_half(up_one, partial), "x")
         up_two = send_half(add_half(up_two, partial), "ctx")
-        out_y = send_half(add_half(out_x, partial), "ctx")
-        d_attended = after(d_attended, partial, up_one[0], up_two[0], out_y[0])
+        d_attended = after(d_attended, partial, up_one[0], up_two[0])
         d_two = attention_backward(joined_two, d_attended, half_width // PAIR, log_two, bias)
         two_core = trade(gradient(normed1, d_two, 1 - core), "core")
         qkv_one_x = send_half(gradient(normed1, d_one, core, got=after(one_core, d_two)), "x")
         down_y = send_half(add_far(down_far, d_two).astype(jnp.bfloat16), "ctx")
-        up_far = jnp.concatenate(
-            [add_half(halves, d_two) for halves in (up_one, up_two, out_y)], axis=1
-        )
-        d_two_tied = after(d_two, qkv_one_x[0], down_y[0], up_far)
+        out_y = send_half(add_half(out_x, d_two), "ctx")
+        up_halves = [add_half(halves, d_two) for halves in (up_one, up_two)]
+        d_two_tied = after(d_two, qkv_one_x[0], down_y[0], out_y[0], *up_halves)
         d_last, sums_one = norm_back(
             d_two_tied, qkv_two_weight, normal1, scale1, first_gain, d_middle, base=partial
         )
         d_last_given = to_give(d_last)
-        qkv_two = gradient(normed1, d_two, core, got=after(two_core, d_last_given[0]))
+        qkv_two = gradient(normed1, d_two, core, got=after(two_core, d_last))
 
         vectors = [
             sums_two[2],
@@ -1140,16 +1143,19 @@
         table = jnp.concatenate([table, up_sums.reshape(devices, -1, near_width)], axis=1)
         table = pad_small(table).reshape(width, 128).astype(jnp.bfloat16)
         qkv_two_x = send_half(qkv_two, "x")
-        qkv_one_y = send_half(add_half(qkv_one_x, d_last_given[0]), "ctx")
+        up_far = jnp.concatenate([*up_halves, add_half(out_y, d_last)], axis=1)
+        up_far = send_far(up_far, far)
+        qkv_one_y = send_half(
+            add_half(qkv_one_x, d_last_given[0], qkv_two_x[0], up_far[0]), "ctx"
+        )
         table = send_half(add_half(send_half(table, "core")), "x")
-        up_far = send_far(after(up_far, qkv_two_x[0], qkv_one_y[0]), far)
         qkv_two = jnp.concatenate([add_half(qkv_two_x), add_half(table)], axis=1)
         qkv_two_y = send_half(qkv_two, "ctx")
         qkv_one_far = send_far(add_half(qkv_one_y), far)
         qkv_two_far = send_far(add_half(qkv_two_y), far)
 
         sum_down = add_half(down_y, d_last_given[0]).astype(jnp.float32)
-        sum_up = add_far(up_far)
+        sum_up = add_far(up_far, qkv_one_y[0])
         sum_up, sum_out = sum_up[:, :up_width], sum_up[:, up_width:]
         sum_one, sum_two = add_far(qkv_one_far), add_far(qkv_two_far)
         small_sums = sum_two[:small_rows, half_qkv : half_qkv + near_width]

time: 590 us -> 564 us (0.956)
  waiting for transfers between devices: 156 us -> 125 us
  starting transfers between devices: 85.5 us -> 67.1 us
  local copies, waits for them, and re-layouts: 81.7 us -> 98.6 us
    ppermute x50, waiting for transfers between devices: 100 us -> 75.8 us  [trade(): return lax.ppermute(array, axis, [(0, 1), (1, 0)])]
    ppermute x12, starting transfers between devices: 33.2 us -> 16.9 us  [send_far(): lax.ppermute(sent, 'z', [(i, (i + step) % far) for i in range(far)])]
    ppermute x9, waiting for transfers between devices: 47.2 us -> 37.8 us  [gather_far(): got = lax.ppermute(shard, 'z', [(i, (i + step) % far) for i in range(far)])]
    another operation x8, local copies, waits for them, and re-layouts: 0.5 us -> 6.64 us  [on_device(): jnp.stack([vector.reshape(devices, near_width) for vector in vectors], ax...]
    unnamed x234 -> x222, local copies, waits for them, and re-layouts: 40.7 us -> 36.8 us
  transfers between devices with their start and end apart: 71 -> 71, of which waited for: 21 -> 20; matrix products, arithmetic and copies ran while one was open for 18% -> 23% of each run, Pallas kernels for 27% -> 29%
where the time goes in v8:
time: 564 us; the launch traced here: 557 us
  Pallas kernels  188 us (33%)
  waiting for transfers between devices  125 us (22%)
  local copies, waits for them, and re-layouts  98.6 us (17%)
  starting transfers between devices  67.1 us (12%)
  matrix products  44.9 us (8%)
  other arithmetic  31.3 us (6%)
    ppermute x50, waiting for transfers between devices, trade(): return lax.ppermute(array, axis, [(0, 1), (1, 0)])  75.8 us
    pallas_call x10, Pallas kernels, gradient(): pl.pallas_call(gradient_kernel, grid_spec=pltpu.PrefetchScalarGridSpec(nu...  40.1 us
    dot_general x11, matrix products, matmul(): return jnp.dot(left, right, preferred_element_type=jnp.float32)  39.9 us
    ppermute x9, waiting for transfers between devices, gather_far(): got = lax.ppermute(shard, 'z', [(i, (i + step) % far) for i in range(far)])  37.8 us
    unnamed x222, local copies, waits for them, and re-layouts  36.8 us
    ppermute x50, starting transfers between devices, trade(): return lax.ppermute(array, axis, [(0, 1), (1, 0)])  35.2 us
    pallas_call x9, Pallas kernels, assemble(): pl.pallas_call(functools.partial(assemble_kernel, routes), in_specs=[pl.B...  30.7 us
    pallas_call x2, Pallas kernels, attention_forward(): pl.pallas_call(forward_kernel, grid=(pairs,), in_specs=[pair_spec(rows, p...  26.9 us
  transfers between devices with their start and end apart: 71, of which 20 were waited for; matrix products, arithmetic and copies ran while one was open for 23% of the time, Pallas kernels for 29%

profile of v8, /device:TPU:0, one launch (start us, length us, event | category | flops | bytes accessed | tf_op | source)
XLA Modules:
  0.0 556.9 jit_solution(6119791876555232613)
XLA Ops:
  4.4 5.1 collective-permute-start.4
  17.4 3.5 copy.137
  21.5 5.4 collective-permute-done.3.refs_2_
  30.9 8.4 %collective-permute-done.1 = bf16[584,1024]{1,0:T(8,128)(2,1)} collective-permute-done((bf16[584,1024]{1,0:T(8,128)(2,1)}, bf16[584,1024]{1,0:T(8,128)(2,1)}, u32[]{:S(2)}, u32[]{:S(2)}) %collective-permute-start.1) | collective-permute-done | bytes 1196064 | tf_op jit(solution)/shard_map/ppermute | solution.py:825
  44.6 6.9 %collective-permute-done.12.refs_1_ = bf16[128,1536]{1,0:T(8,128)(2,1)S(1)} collective-permute-done((bf16[128,1536]{1,0:T(8,128)(2,1)}, bf16[128,1536]{1,0:T(8,128)(2,1)S(1)}, u32[]{:S(2)}, u32[]{:S(2)}) %collective-permute-start.12) | collective-permute-done | bytes 393248 | tf_op jit(solution)/shard_map/ppermute | solution.py:825
  53.1 3.8 fusion.12
  61.3 8.2 %collective-permute-done.7.refs_3_ = bf16[128,1664]{1,0:T(8,128)(2,1)} collective-permute-done((bf16[128,1664]{1,0:T(8,128)(2,1)S(1)}, bf16[128,1664]{1,0:T(8,128)(2,1)}, u32[]{:S(2)}, u32[]{:S(2)}) %collective-permute-start.7) | collective-permute-done | bytes 426016 | tf_op jit(solution)/shard_map/ppermute | solution.py:825
  69.5 3.4 collective-permute-start.22
  74.2 5.9 %fusion.38 = (f32[592]{0:T(1024)S(1)}, f32[592,1024]{1,0:T(8,128)}) fusion(s32[1024]{0:T(1024)S(1)} %reshape.573, f32[592,1024]{1,0:T(8,128)} %fusion.12, bf16[584,1024]{1,0:T(8,128)(2,1)} %collective-permute-done.1, s32[584]{0:T(1024)S(1)} %select_select_fusion), kind=kOutput, calls=%fused_computation.173 | convolution fusion | flops 1952777216 | bytes 6054496 | tf_op jit(solution)/shard_map/dot_general | solution.py:28
  82.1 14.2 %collective-permute-done.21.refs_2_ = bf16[32,5120]{1,0:T(8,128)(2,1)} collective-permute-done((bf16[32,5120]{1,0:T(8,128)(2,1)S(1)}, bf16[32,5120]{1,0:T(8,128)(2,1)}, u32[]{:S(2)}, u32[]{:S(2)}) %collective-permute-start.21) | collective-permute-done | bytes 327712 | tf_op jit(solution)/shard_map/ppermute | solution.py:836
  124.2 3.7 add_convert_fusion.3
  130.6 13.5 %attention_forward.2 = (bf16[592,1024]{1,0:T(8,128)(2,1)S(1)}, f32[4,2,592]{2,1,0:T(2,128)S(1)}) custom-call(bf16[3,592,512]{2,1,0:T(8,128)(2,1)S(1)} %project.2.query_ref.key_ref.value_ref, bf16[3,592,512]{2,1,0:T(8,128)(2,1)S(1)} %project.2.query_ref.key_ref.value_ref, bf16[3,592,512]{2,1,0:T(8,128)(2,1)S(1)} %project.2.query_ref.key_ref.value_ref, ...), custom_call_target="tpu_custom_call" | custom-call | flops 1 | bytes 1 | tf_op jit(solution)/shard_map/attention_forward/pallas_call | solution.py:436
  144.2 4.3 collective-permute-done.28.refs_7_
  149.7 5.2 assemble.14.refs_0_
  160.9 3.8 fusion.11
  173.3 13.5 %attention_forward.3 = (bf16[592,1024]{1,0:T(8,128)(2,1)S(1)}, f32[4,2,592]{2,1,0:T(2,128)S(1)}) custom-call(bf16[3,592,512]{2,1,0:T(8,128)(2,1)S(1)} %project.3.query_ref.key_ref.value_ref, bf16[3,592,512]{2,1,0:T(8,128)(2,1)S(1)} %project.3.query_ref.key_ref.value_ref, ...), custom_call_target="tpu_custom_call", output_to_operand_aliasing={{0}: (4, {})} | custom-call | flops 1 | bytes 1 | tf_op jit(solution)/shard_map/attention_forward/pallas_call | solution.py:436
  186.8 16.9 %collective-permute-done.31.refs_2_ = bf16[256,1024]{1,0:T(8,128)(2,1)} collective-permute-done((bf16[256,1024]{1,0:T(8,128)(2,1)S(1)}, bf16[256,1024]{1,0:T(8,128)(2,1)}, u32[]{:S(2)}, u32[]{:S(2)}) %collective-permute-start.31) | collective-permute-done | bytes 524320 | tf_op jit(solution)/shard_map/ppermute | solution.py:836
  207.4 5.6 %fusion.40 = (bf16[1024]{0:T(1024)(128)(2,1)S(1)}, bf16[592,1024]{1,0:T(8,128)(2,1)}) fusion(f32[592]{0:T(1024)} %fusion.35, s32[1024]{0:T(1024)} %copy-done.98, f32[592,1024]{1,0:T(8,128)} %fusion.11, bf16[584,1024]{1,0:T(8,128)(2,1)} %collective-permute-done.37, s32[584]{0:T(1024)} %copy-done.101), kind=kOutput, calls=%fused_computation.175 | convolution fusion | flops 1953989248 | bytes 4844128 | tf_op jit(solution)/shard_map/dot_general | solution.py:28
  213.0 5.6 assemble.15
  227.6 18.1 %hidden_layer.1 = (bf16[592,4096]{1,0:T(8,128)(2,1)S(1)}, bf16[592,4096]{1,0:T(8,128)(2,1)S(1)}) custom-call(bf16[592,1024]{1,0:T(8,128)(2,1)S(1)} %get-tuple-element.176.x_ref, bf16[1024,4096]{1,0:T(8,128)(2,1)S(1)} %get-tuple-element.114.weight_ref, f32[1,4096]{1,0:T(1,128)S(1)} %bitcast.218), custom_call_target="tpu_custom_call" | custom-call | flops 1 | bytes 1 | tf_op jit(solution)/shard_map/hidden_layer/pallas_call | solution.py:522
  245.8 7.6 %gradient.10 = bf16[2048,1024]{1,0:T(8,128)(2,1)} custom-call(s32[1]{0:T(128)} %bitcast.25.index_ref, bf16[592,4096]{1,0:T(8,128)(2,1)S(1)} %get-tuple-element.115.active_ref.x_ref, bf16[592,1024]{1,0:T(8,128)(2,1)S(1)} %copy-done.22), custom_call_target="tpu_custom_call" | custom-call | flops 1 | bytes 1 | tf_op jit(solution)/shard_map/gradient/pallas_call | solution.py:725
  255.1 8.8 %collective-permute-done.34.refs_2_ = bf16[1024,1024]{1,0:T(8,128)(2,1)} collective-permute-done((bf16[1024,1024]{1,0:T(8,128)(2,1)}, bf16[1024,1024]{1,0:T(8,128)(2,1)}, u32[]{:S(2)}, u32[]{:S(2)}) %collective-permute-start.34) | collective-permute-done | bytes 2097184 | tf_op jit(solution)/shard_map/ppermute | solution.py:825
  266.9 4.2 assemble.17.weight_ref
  271.2 3.3 copy-done.5
  274.4 11.3 %last_layer.1 = bf16[592,1024]{1,0:T(8,128)(2,1)S(1)} custom-call(bf16[592,4096]{1,0:T(8,128)(2,1)} %copy-done.9, bf16[4096,1024]{1,0:T(8,128)(2,1)} %copy-done.5, f32[592,1024]{1,0:T(8,128)} %copy-done.66, f32[1,1024]{1,0:T(1,128)S(1)} %broadcast_in_dim_reshape_squeeze.6.bias_ref), custom_call_target="tpu_custom_call" | custom-call | flops 1 | bytes 1 | tf_op jit(solution)/shard_map/last_layer/pallas_call | solution.py:555
  290.8 7.6 %gradient.11 = bf16[2048,1024]{1,0:T(8,128)(2,1)S(1)} custom-call(s32[1]{0:T(128)} %bitcast.24.index_ref, bf16[592,4096]{1,0:T(8,128)(2,1)S(1)} %copy-done.10, bf16[592,1024]{1,0:T(8,128)(2,1)S(1)} %copy-done.23, bf16[2048,1024]{1,0:T(8,128)(2,1)} %collective-permute-done.38.refs_0_), custom_call_target="tpu_custom_call" | custom-call | flops 1 | bytes 1 | tf_op jit(solution)/shard_map/gradient/pallas_call | solution.py:725
  302.3 7.8 %d_hidden_layer.1 = (bf16[592,4096]{1,0:T(8,128)(2,1)S(1)}, f32[1,4096]{1,0:T(1,128)S(1)}) custom-call(bf16[592,1024]{1,0:T(8,128)(2,1)S(1)} %copy-done.23, bf16[4096,1024]{1,0:T(8,128)(2,1)S(1)} %bitcast.210, bf16[592,4096]{1,0:T(8,128)(2,1)S(1)} %copy-done.35), custom_call_target="tpu_custom_call" | custom-call | flops 1 | bytes 1 | tf_op jit(solution)/shard_map/d_hidden_layer/pallas_call | solution.py:584
  310.1 3.3 gradient.14
  321.6 4.1 fusion.14
  327.3 12.0 %norm_back.2 = (f32[592,1024]{1,0:T(8,128)S(1)}, bf16[592,1024]{1,0:T(8,128)(2,1)S(1)}, f32[8,1024]{1,0:T(8,128)S(1)}) custom-call(bf16[592,4096]{1,0:T(8,128)(2,1)S(1)} %copy-done.1, bf16[1024,4096]{1,0:T(8,128)(2,1)} %copy-done.18, f32[592,1024]{1,0:T(8,128)S(1)} %copy-done.28, f32[592,1]{1,0:T(8,128)S(1)} %rsqrt.14.refs_1_, ...), custom_call_target="tpu_custom_call" | custom-call | flops 1 | bytes 1 | tf_op jit(solution)/shard_map/norm_back/pallas_call | solution.py:685
  348.4 3.3 gradient.15
  355.2 3.7 gradient.13
  362.4 3.7 collective-permute-done.42
  370.1 3.8 collective-permute-start.48
  376.3 13.5 %attention_backward.2.d_ref = bf16[3,592,512]{2,1,0:T(8,128)(2,1)S(1)} custom-call(bf16[3,592,512]{2,1,0:T(8,128)(2,1)S(1)} %copy-done.4, bf16[3,592,512]{2,1,0:T(8,128)(2,1)S(1)} %copy-done.4, bf16[3,592,512]{2,1,0:T(8,128)(2,1)S(1)} %copy-done.4, bf16[592,1024]{1,0:T(8,128)(2,1)S(1)} %convolution_convert_fusion.1.d_ref, f32[4,2,592]{2,1,0:T(2,128)S(1)} %copy-done.51, ...), custom_call_target="tpu_custom_call" | custom-call | flops 1 | bytes 1 | tf_op jit(solution)/shard_map/attention_backward/pallas_call | solution.py:459
  389.8 4.2 add_convert_fusion.5
  405.9 13.4 %attention_backward.3.d_ref = bf16[3,592,512]{2,1,0:T(8,128)(2,1)S(1)} custom-call(bf16[3,592,512]{2,1,0:T(8,128)(2,1)S(1)} %project.3.query_ref.key_ref.value_ref, bf16[3,592,512]{2,1,0:T(8,128)(2,1)S(1)} %project.3.query_ref.key_ref.value_ref, bf16[3,592,512]{2,1,0:T(8,128)(2,1)S(1)} %project.3.query_ref.key_ref.value_ref, ...), custom_call_target="tpu_custom_call" | custom-call | flops 1 | bytes 1 | tf_op jit(solution)/shard_map/attention_backward/pallas_call | solution.py:459
  432.0 3.8 collective-permute-done.50
  444.2 5.0 norm_back.3
  465.7 3.9 fusion.13
  480.2 3.9 reshape.578
  484.1 15.0 %collective-permute-done.62 = bf16[256,128]{1,0:T(8,128)(2,1)S(1)} collective-permute-done((bf16[256,128]{1,0:T(8,128)(2,1)S(1)}, bf16[256,128]{1,0:T(8,128)(2,1)S(1)}, u32[]{:S(2)}, u32[]{:S(2)}) %collective-permute-start.62) | collective-permute-done | bytes 65568 | tf_op jit(solution)/shard_map/ppermute | solution.py:825
  499.1 3.7 collective-permute-start.69
  507.9 8.1 %collective-permute-done.56 = bf16[128,1536]{1,0:T(8,128)(2,1)S(1)} collective-permute-done((bf16[128,1536]{1,0:T(8,128)(2,1)S(1)}, bf16[128,1536]{1,0:T(8,128)(2,1)S(1)}, u32[]{:S(2)}, u32[]{:S(2)}) %collective-permute-start.56) | collective-permute-done | bytes 393248 | tf_op jit(solution)/shard_map/ppermute | solution.py:825
  517.0 7.3 %collective-permute-done.68 = bf16[32,5120]{1,0:T(8,128)(2,1)S(1)} collective-permute-done((bf16[32,5120]{1,0:T(8,128)(2,1)}, bf16[32,5120]{1,0:T(8,128)(2,1)S(1)}, u32[]{:S(2)}, u32[]{:S(2)}) %collective-permute-start.68) | collective-permute-done | bytes 327712 | tf_op jit(solution)/shard_map/ppermute | solution.py:897
  528.2 3.6 collective-permute-start.59
  543.0 3.8 convolution_add_fusion
  549.2 3.7 collective-permute-done.65
  (514 shorter events, 221.8 us)
Async XLA Ops:
  10.5 29.3 %collective-permute-start = (s32[584]{0:T(1024)}, s32[584]{0:T(1024)S(1)}, u32[]{:S(2)}, u32[]{:S(2)}) collective-permute-start(s32[584]{0:T(1024)} %param.18), channel_id=1, source_target_pairs={{0,1},{1,0},{2,3},{3,2},{4,5},{5,4},{6,7},{7,6},{8,9},{9,8},{10,11... | collective-permute-start | bytes 7016 | tf_op jit(solution)/shard_map/ppermute | solution.py:825
  12.0 27.3 %collective-permute-start.1 = (bf16[584,1024]{1,0:T(8,128)(2,1)}, bf16[584,1024]{1,0:T(8,128)(2,1)}, u32[]{:S(2)}, u32[]{:S(2)}) collective-permute-start(bf16[584,1024]{1,0:T(8,128)(2,1)} %param.16), channel_id=1, source_target_pairs={{0,1},{1,0},{2,3},{3,2},{4,5},{5,4},{6,7},{7,6},{8,9},{9,8},{10,11... | collective-permute-start | bytes 3588104 | tf_op jit(solution)/shard_map/ppermute | solution.py:825
  41.1 19.7 %collective-permute-start.6 = (bf16[128,1664]{1,0:T(8,128)(2,1)S(1)}, bf16[128,1664]{1,0:T(8,128)(2,1)}, u32[]{:S(2)}, u32[]{:S(2)}) collective-permute-start(bf16[128,1664]{1,0:T(8,128)(2,1)S(1)} %get-tuple-element.86.refs_0_), channel_id=1, source_target_pairs={{0,1},{1,0},{2,3},{3,2},{4,5},{5,4},{6,7},{7,6},{8,9},{9,8},{10,11... | collective-permute-start | bytes 1277960 | tf_op jit(solution)/shard_map/ppermute | solution.py:825
  42.6 26.9 %collective-permute-start.7 = (bf16[128,1664]{1,0:T(8,128)(2,1)S(1)}, bf16[128,1664]{1,0:T(8,128)(2,1)}, u32[]{:S(2)}, u32[]{:S(2)}) collective-permute-start(bf16[128,1664]{1,0:T(8,128)(2,1)S(1)} %collective-permute-done.5.refs_1_), channel_id=1, source_target_pairs={{0,1},{1,0},{2,3},{3,2},{4,5},{5,4},{6,7},{7,6},{8,9},{9,8},{10,11... | collective-permute-start | bytes 1277960 | tf_op jit(solution)/shard_map/ppermute | solution.py:825
  43.1 26.4 %collective-permute-start.13 = (bf16[128,1536]{1,0:T(8,128)(2,1)}, bf16[128,1536]{1,0:T(8,128)(2,1)}, u32[]{:S(2)}, u32[]{:S(2)}) collective-permute-start(bf16[128,1536]{1,0:T(8,128)(2,1)} %get-tuple-element.90.refs_0_), channel_id=1, source_target_pairs={{0,4},{4,0},{1,5},{5,1},{2,6},{6,2},{3,7},{7,3},{8,12},{12,8},{9,1... | collective-permute-start | bytes 1179656 | tf_op jit(solution)/shard_map/ppermute | solution.py:825
  51.6 18.0 %collective-permute-start.14 = (bf16[128,1536]{1,0:T(8,128)(2,1)S(1)}, bf16[128,1536]{1,0:T(8,128)(2,1)}, u32[]{:S(2)}, u32[]{:S(2)}) collective-permute-start(bf16[128,1536]{1,0:T(8,128)(2,1)S(1)} %collective-permute-done.12.refs_1_), channel_id=1, source_target_pairs={{0,4},{4,0},{1,5},{5,1},{2,6},{6,2},{3,7},{7,3},{8,12},{12,8},{9,1... | collective-permute-start | bytes 1179656 | tf_op jit(solution)/shard_map/ppermute | solution.py:825
  56.9 46.4 %collective-permute-start.8 = (bf16[128,1664]{1,0:T(8,128)(2,1)S(1)}, bf16[128,1664]{1,0:T(8,128)(2,1)}, u32[]{:S(2)}, u32[]{:S(2)}) collective-permute-start(bf16[128,1664]{1,0:T(8,128)(2,1)S(1)} %get-tuple-element.86.refs_0_), channel_id=1, source_target_pairs={{0,2},{2,0},{1,3},{3,1},{4,6},{6,4},{5,7},{7,5},{8,10},{10,8},{9,1... | collective-permute-start | bytes 1277960 | tf_op jit(solution)/shard_map/ppermute | solution.py:825
  60.8 19.3 %collective-permute-start.20 = (bf16[128,1024]{1,0:T(8,128)(2,1)S(1)}, bf16[128,1024]{1,0:T(8,128)(2,1)}, u32[]{:S(2)}, u32[]{:S(2)}) collective-permute-start(bf16[128,1024]{1,0:T(8,128)(2,1)S(1)} %copy.139.refs_0_), channel_id=1, source_target_pairs={{0,1},{1,0},{2,3},{3,2},{4,5},{5,4},{6,7},{7,6},{8,9},{9,8},{10,11... | collective-permute-start | bytes 786440 | tf_op jit(solution)/shard_map/ppermute | solution.py:825
  72.9 23.4 %collective-permute-start.21 = (bf16[32,5120]{1,0:T(8,128)(2,1)S(1)}, bf16[32,5120]{1,0:T(8,128)(2,1)}, u32[]{:S(2)}, u32[]{:S(2)}) collective-permute-start(bf16[32,5120]{1,0:T(8,128)(2,1)S(1)} %pad_maximum_fusion.3.refs_0_), channel_id=1, source_target_pairs={{0,16},{8,24},{16,0},{24,8},{1,17},{9,25},{17,1},{25,9},{2,18},{10... | collective-permute-start | bytes 983048 | tf_op jit(solution)/shard_map/ppermute | solution.py:836
  73.5 22.9 %collective-permute-start.19 = (bf16[32,5120]{1,0:T(8,128)(2,1)S(1)}, bf16[32,5120]{1,0:T(8,128)(2,1)}, u32[]{:S(2)}, u32[]{:S(2)}) collective-permute-start(bf16[32,5120]{1,0:T(8,128)(2,1)S(1)} %pad_maximum_fusion.3.refs_0_), channel_id=1, source_target_pairs={{0,8},{8,16},{16,24},{24,0},{1,9},{9,17},{17,25},{25,1},{2,10},{10... | collective-permute-start | bytes 983048 | tf_op jit(solution)/shard_map/ppermute | solution.py:836
  80.1 24.8 %collective-permute-start.10 = (bf16[128,1664]{1,0:T(8,128)(2,1)}, bf16[128,1664]{1,0:T(8,128)(2,1)S(1)}, u32[]{:S(2)}, u32[]{:S(2)}) collective-permute-start(bf16[128,1664]{1,0:T(8,128)(2,1)} %collective-permute-done.6.refs_2_), channel_id=1, source_target_pairs={{0,2},{2,0},{1,3},{3,1},{4,6},{6,4},{5,7},{7,5},{8,10},{10,8},{9,1... | collective-permute-start | bytes 1277960 | tf_op jit(solution)/shard_map/ppermute | solution.py:825
  82.1 23.9 %collective-permute-start.9 = (bf16[128,1664]{1,0:T(8,128)(2,1)S(1)}, bf16[128,1664]{1,0:T(8,128)(2,1)S(1)}, u32[]{:S(2)}, u32[]{:S(2)}) collective-permute-start(bf16[128,1664]{1,0:T(8,128)(2,1)S(1)} %collective-permute-done.5.refs_1_), channel_id=1, source_target_pairs={{0,2},{2,0},{1,3},{3,1},{4,6},{6,4},{5,7},{7,5},{8,10},{10,8},{9,1... | collective-permute-start | bytes 1277960 | tf_op jit(solution)/shard_map/ppermute | solution.py:825
  103.3 18.6 %collective-permute-start.23 = (bf16[128,2560]{1,0:T(8,128)(2,1)}, bf16[128,2560]{1,0:T(8,128)(2,1)}, u32[]{:S(2)}, u32[]{:S(2)}) collective-permute-start(bf16[128,2560]{1,0:T(8,128)(2,1)} %get-tuple-element.102.refs_0_), channel_id=1, source_target_pairs={{0,4},{4,0},{1,5},{5,1},{2,6},{6,2},{3,7},{7,3},{8,12},{12,8},{9,1... | collective-permute-start | bytes 1966088 | tf_op jit(solution)/shard_map/ppermute | solution.py:825
  104.9 18.0 %collective-permute-start.26 = (bf16[128,2560]{1,0:T(8,128)(2,1)}, bf16[128,2560]{1,0:T(8,128)(2,1)}, u32[]{:S(2)}, u32[]{:S(2)}) collective-permute-start(bf16[128,2560]{1,0:T(8,128)(2,1)} %get-tuple-element.108.refs_4_), channel_id=1, source_target_pairs={{0,1},{1,0},{2,3},{3,2},{4,5},{5,4},{6,7},{7,6},{8,9},{9,8},{10,11... | collective-permute-start | bytes 1966088 | tf_op jit(solution)/shard_map/ppermute | solution.py:825
  113.9 30.3 %collective-permute-start.24 = (bf16[128,2560]{1,0:T(8,128)(2,1)}, bf16[128,2560]{1,0:T(8,128)(2,1)}, u32[]{:S(2)}, u32[]{:S(2)}) collective-permute-start(bf16[128,2560]{1,0:T(8,128)(2,1)} %get-tuple-element.102.refs_0_), channel_id=1, source_target_pairs={{0,1},{1,0},{2,3},{3,2},{4,5},{5,4},{6,7},{7,6},{8,9},{9,8},{10,11... | collective-permute-start | bytes 1966088 | tf_op jit(solution)/shard_map/ppermute | solution.py:825
  115.5 28.7 %collective-permute-start.27 = (bf16[128,2560]{1,0:T(8,128)(2,1)}, bf16[128,2560]{1,0:T(8,128)(2,1)}, u32[]{:S(2)}, u32[]{:S(2)}) collective-permute-start(bf16[128,2560]{1,0:T(8,128)(2,1)} %get-tuple-element.108.refs_4_), channel_id=1, source_target_pairs={{0,4},{4,0},{1,5},{5,1},{2,6},{6,2},{3,7},{7,3},{8,12},{12,8},{9,1... | collective-permute-start | bytes 1966088 | tf_op jit(solution)/shard_map/ppermute | solution.py:825
  121.9 27.8 %collective-permute-start.25 = (bf16[128,2560]{1,0:T(8,128)(2,1)}, bf16[128,2560]{1,0:T(8,128)(2,1)}, u32[]{:S(2)}, u32[]{:S(2)}) collective-permute-start(bf16[128,2560]{1,0:T(8,128)(2,1)} %collective-permute-done.23.refs_1_), channel_id=1, source_target_pairs={{0,1},{1,0},{2,3},{3,2},{4,5},{5,4},{6,7},{7,6},{8,9},{9,8},{10,11... | collective-permute-start | bytes 1966088 | tf_op jit(solution)/shard_map/ppermute | solution.py:825
  122.9 25.6 %collective-permute-start.28 = (bf16[128,2560]{1,0:T(8,128)(2,1)}, bf16[128,2560]{1,0:T(8,128)(2,1)}, u32[]{:S(2)}, u32[]{:S(2)}) collective-permute-start(bf16[128,2560]{1,0:T(8,128)(2,1)} %collective-permute-done.26.refs_5_), channel_id=1, source_target_pairs={{0,4},{4,0},{1,5},{5,1},{2,6},{6,2},{3,7},{7,3},{8,12},{12,8},{9,1... | collective-permute-start | bytes 1966088 | tf_op jit(solution)/shard_map/ppermute | solution.py:825
  154.9 58.1 %collective-permute-start.29 = (bf16[512,5120]{1,0:T(8,128)(2,1)}, bf16[512,5120]{1,0:T(8,128)(2,1)}, u32[]{:S(2)}, u32[]{:S(2)}) collective-permute-start(bf16[512,5120]{1,0:T(8,128)(2,1)} %assemble.14.refs_0_), channel_id=1, source_target_pairs={{0,2},{2,0},{1,3},{3,1},{4,6},{6,4},{5,7},{7,5},{8,10},{10,8},{9,1... | collective-permute-start | bytes 15728648 | tf_op jit(solution)/shard_map/ppermute | solution.py:825
  155.0 52.4 %collective-permute-start.37 = (bf16[584,1024]{1,0:T(8,128)(2,1)}, bf16[584,1024]{1,0:T(8,128)(2,1)}, u32[]{:S(2)}, u32[]{:S(2)}) collective-permute-start(bf16[584,1024]{1,0:T(8,128)(2,1)} %param.17), channel_id=1, source_target_pairs={{0,1},{1,0},{2,3},{3,2},{4,5},{5,4},{6,7},{7,6},{8,9},{9,8},{10,11... | collective-permute-start | bytes 3588104 | tf_op jit(solution)/shard_map/ppermute | solution.py:825
  155.6 31.3 %collective-permute-start.32 = (bf16[256,1024]{1,0:T(8,128)(2,1)S(1)}, bf16[256,1024]{1,0:T(8,128)(2,1)}, u32[]{:S(2)}, u32[]{:S(2)}) collective-permute-start(bf16[256,1024]{1,0:T(8,128)(2,1)S(1)} %assemble.12.refs_0_), channel_id=1, source_target_pairs={{0,24},{8,0},{16,8},{24,16},{1,25},{9,1},{17,9},{25,17},{2,26},{10... | collective-permute-start | bytes 1572872 | tf_op jit(solution)/shard_map/ppermute | solution.py:836
  155.6 48.2 %collective-permute-start.31 = (bf16[256,1024]{1,0:T(8,128)(2,1)S(1)}, bf16[256,1024]{1,0:T(8,128)(2,1)}, u32[]{:S(2)}, u32[]{:S(2)}) collective-permute-start(bf16[256,1024]{1,0:T(8,128)(2,1)S(1)} %assemble.12.refs_0_), channel_id=1, source_target_pairs={{0,16},{8,24},{16,0},{24,8},{1,17},{9,25},{17,1},{25,9},{2,18},{10... | collective-permute-start | bytes 1572872 | tf_op jit(solution)/shard_map/ppermute | solution.py:836
  157.7 46.1 %collective-permute-start.30 = (bf16[256,1024]{1,0:T(8,128)(2,1)S(1)}, bf16[256,1024]{1,0:T(8,128)(2,1)}, u32[]{:S(2)}, u32[]{:S(2)}) collective-permute-start(bf16[256,1024]{1,0:T(8,128)(2,1)S(1)} %assemble.12.refs_0_), channel_id=1, source_target_pairs={{0,8},{8,16},{16,24},{24,0},{1,9},{9,17},{17,25},{25,1},{2,10},{10... | collective-permute-start | bytes 1572872 | tf_op jit(solution)/shard_map/ppermute | solution.py:836
  206.8 47.6 %collective-permute-start.33 = (bf16[1024,1024]{1,0:T(8,128)(2,1)}, bf16[1024,1024]{1,0:T(8,128)(2,1)}, u32[]{:S(2)}, u32[]{:S(2)}) collective-permute-start(bf16[1024,1024]{1,0:T(8,128)(2,1)} %assemble.16.refs_0_), channel_id=1, source_target_pairs={{0,4},{4,0},{1,5},{5,1},{2,6},{6,2},{3,7},{7,3},{8,12},{12,8},{9,1... | collective-permute-start | bytes 6291464 | tf_op jit(solution)/shard_map/ppermute | solution.py:825
  253.4 34.9 %collective-permute-start.38 = (bf16[2048,1024]{1,0:T(8,128)(2,1)}, bf16[2048,1024]{1,0:T(8,128)(2,1)}, u32[]{:S(2)}, u32[]{:S(2)}) collective-permute-start(bf16[2048,1024]{1,0:T(8,128)(2,1)} %gradient.10), channel_id=1, source_target_pairs={{0,2},{2,0},{1,3},{3,1},{4,6},{6,4},{5,7},{7,5},{8,10},{10,8},{9,1... | collective-permute-start | bytes 12582920 | tf_op jit(solution)/shard_map/ppermute | solution.py:825
  313.5 31.3 %collective-permute-start.40 = (bf16[512,2048]{1,0:T(8,128)(2,1)}, bf16[512,2048]{1,0:T(8,128)(2,1)}, u32[]{:S(2)}, u32[]{:S(2)}) collective-permute-start(bf16[512,2048]{1,0:T(8,128)(2,1)} %gradient.14), channel_id=1, source_target_pairs={{0,2},{2,0},{1,3},{3,1},{4,6},{6,4},{5,7},{7,5},{8,10},{10,8},{9,1... | collective-permute-start | bytes 6291464 | tf_op jit(solution)/shard_map/ppermute | solution.py:825
  316.9 38.3 %collective-permute-start.39 = (bf16[512,2048]{1,0:T(8,128)(2,1)}, bf16[512,2048]{1,0:T(8,128)(2,1)}, u32[]{:S(2)}, u32[]{:S(2)}) collective-permute-start(bf16[512,2048]{1,0:T(8,128)(2,1)} %gradient.12), channel_id=1, source_target_pairs={{0,2},{2,0},{1,3},{3,1},{4,6},{6,4},{5,7},{7,5},{8,10},{10,8},{9,1... | collective-permute-start | bytes 6291464 | tf_op jit(solution)/shard_map/ppermute | solution.py:825
  317.3 48.8 %collective-permute-start.42 = (bf16[1024,1024]{1,0:T(8,128)(2,1)}, bf16[1024,1024]{1,0:T(8,128)(2,1)}, u32[]{:S(2)}, u32[]{:S(2)}) collective-permute-start(bf16[1024,1024]{1,0:T(8,128)(2,1)} %get-tuple-element.180), channel_id=1, source_target_pairs={{0,4},{4,0},{1,5},{5,1},{2,6},{6,2},{3,7},{7,3},{8,12},{12,8},{9,1... | collective-permute-start | bytes 6291464 | tf_op jit(solution)/shard_map/ppermute | solution.py:825
  320.0 48.7 %collective-permute-start.36 = (bf16[592,1024]{1,0:T(8,128)(2,1)}, bf16[592,1024]{1,0:T(8,128)(2,1)}, u32[]{:S(2)}, u32[]{:S(2)}) collective-permute-start(bf16[592,1024]{1,0:T(8,128)(2,1)} %fusion.9), channel_id=1, source_target_pairs={{0,1},{1,0},{2,3},{3,2},{4,5},{5,4},{6,7},{7,6},{8,9},{9,8},{10,11... | collective-permute-start | bytes 3637256 | tf_op jit(solution)/shard_map/ppermute | solution.py:825
  359.6 44.7 %collective-permute-start.43 = (bf16[256,2048]{1,0:T(8,128)(2,1)S(1)}, bf16[256,2048]{1,0:T(8,128)(2,1)S(1)}, u32[]{:S(2)}, u32[]{:S(2)}) collective-permute-start(bf16[256,2048]{1,0:T(8,128)(2,1)S(1)} %bitcast.239), channel_id=1, source_target_pairs={{0,1},{1,0},{2,3},{3,2},{4,5},{5,4},{6,7},{7,6},{8,9},{9,8},{10,11... | collective-permute-start | bytes 3145736 | tf_op jit(solution)/shard_map/ppermute | solution.py:825
  360.3 41.0 %collective-permute-start.44 = (bf16[256,2048]{1,0:T(8,128)(2,1)S(1)}, bf16[256,2048]{1,0:T(8,128)(2,1)S(1)}, u32[]{:S(2)}, u32[]{:S(2)}) collective-permute-start(bf16[256,2048]{1,0:T(8,128)(2,1)S(1)} %get-tuple-element.186), channel_id=1, source_target_pairs={{0,4},{4,0},{1,5},{5,1},{2,6},{6,2},{3,7},{7,3},{8,12},{12,8},{9,1... | collective-permute-start | bytes 3145736 | tf_op jit(solution)/shard_map/ppermute | solution.py:825
  370.1 51.2 %collective-permute-start.46 = (bf16[256,1024]{1,0:T(8,128)(2,1)}, bf16[256,1024]{1,0:T(8,128)(2,1)}, u32[]{:S(2)}, u32[]{:S(2)}) collective-permute-start(bf16[256,1024]{1,0:T(8,128)(2,1)} %get-tuple-element.182), channel_id=1, source_target_pairs={{0,8},{8,16},{16,24},{24,0},{1,9},{9,17},{17,25},{25,1},{2,10},{10... | collective-permute-start | bytes 1572872 | tf_op jit(solution)/shard_map/ppermute | solution.py:897
  370.1 51.7 %collective-permute-start.48 = (bf16[256,1024]{1,0:T(8,128)(2,1)}, bf16[256,1024]{1,0:T(8,128)(2,1)}, u32[]{:S(2)}, u32[]{:S(2)}) collective-permute-start(bf16[256,1024]{1,0:T(8,128)(2,1)} %get-tuple-element.183), channel_id=1, source_target_pairs={{0,24},{8,0},{16,8},{24,16},{1,25},{9,1},{17,9},{25,17},{2,26},{10... | collective-permute-start | bytes 1572872 | tf_op jit(solution)/shard_map/ppermute | solution.py:897
  373.9 49.4 %collective-permute-start.47 = (bf16[256,1024]{1,0:T(8,128)(2,1)}, bf16[256,1024]{1,0:T(8,128)(2,1)}, u32[]{:S(2)}, u32[]{:S(2)}) collective-permute-start(bf16[256,1024]{1,0:T(8,128)(2,1)} %get-tuple-element.184), channel_id=1, source_target_pairs={{0,16},{8,24},{16,0},{24,8},{1,17},{9,25},{17,1},{25,9},{2,18},{10... | collective-permute-start | bytes 1572872 | tf_op jit(solution)/shard_map/ppermute | solution.py:897
  401.3 29.4 %collective-permute-start.49 = (bf16[256,1024]{1,0:T(8,128)(2,1)}, bf16[256,1024]{1,0:T(8,128)(2,1)}, u32[]{:S(2)}, u32[]{:S(2)}) collective-permute-start(bf16[256,1024]{1,0:T(8,128)(2,1)} %get-tuple-element.200), channel_id=1, source_target_pairs={{0,4},{4,0},{1,5},{5,1},{2,6},{6,2},{3,7},{7,3},{8,12},{12,8},{9,1... | collective-permute-start | bytes 1572872 | tf_op jit(solution)/shard_map/ppermute | solution.py:825
  405.9 32.9 %collective-permute-start.45 = (bf16[512,1536]{1,0:T(8,128)(2,1)}, bf16[512,1536]{1,0:T(8,128)(2,1)}, u32[]{:S(2)}, u32[]{:S(2)}) collective-permute-start(bf16[512,1536]{1,0:T(8,128)(2,1)} %gradient.16), channel_id=1, source_target_pairs={{0,2},{2,0},{1,3},{3,1},{4,6},{6,4},{5,7},{7,5},{8,10},{10,8},{9,1... | collective-permute-start | bytes 4718600 | tf_op jit(solution)/shard_map/ppermute | solution.py:825
  430.2 34.0 %collective-permute-start.70 = (bf16[128,1024]{1,0:T(8,128)(2,1)}, bf16[128,1024]{1,0:T(8,128)(2,1)}, u32[]{:S(2)}, u32[]{:S(2)}) collective-permute-start(bf16[128,1024]{1,0:T(8,128)(2,1)} %get-tuple-element.202), channel_id=1, source_target_pairs={{0,1},{1,0},{2,3},{3,2},{4,5},{5,4},{6,7},{7,6},{8,9},{9,8},{10,11... | collective-permute-start | bytes 786440 | tf_op jit(solution)/shard_map/ppermute | solution.py:825
  430.7 38.9 %collective-permute-start.54 = (bf16[512,1536]{1,0:T(8,128)(2,1)}, bf16[512,1536]{1,0:T(8,128)(2,1)}, u32[]{:S(2)}, u32[]{:S(2)}) collective-permute-start(bf16[512,1536]{1,0:T(8,128)(2,1)} %gradient.18), channel_id=1, source_target_pairs={{0,2},{2,0},{1,3},{3,1},{4,6},{6,4},{5,7},{7,5},{8,10},{10,8},{9,1... | collective-permute-start | bytes 4718600 | tf_op jit(solution)/shard_map/ppermute | solution.py:825
  460.8 63.5 %collective-permute-start.67 = (bf16[32,5120]{1,0:T(8,128)(2,1)}, bf16[32,5120]{1,0:T(8,128)(2,1)}, u32[]{:S(2)}, u32[]{:S(2)}) collective-permute-start(bf16[32,5120]{1,0:T(8,128)(2,1)} %get-tuple-element.192), channel_id=1, source_target_pairs={{0,8},{8,16},{16,24},{24,0},{1,9},{9,17},{17,25},{25,1},{2,10},{10... | collective-permute-start | bytes 983048 | tf_op jit(solution)/shard_map/ppermute | solution.py:897
  460.8 43.9 %collective-permute-start.53 = (bf16[256,1536]{1,0:T(8,128)(2,1)}, bf16[256,1536]{1,0:T(8,128)(2,1)}, u32[]{:S(2)}, u32[]{:S(2)}) collective-permute-start(bf16[256,1536]{1,0:T(8,128)(2,1)} %get-tuple-element.190), channel_id=1, source_target_pairs={{0,4},{4,0},{1,5},{5,1},{2,6},{6,2},{3,7},{7,3},{8,12},{12,8},{9,1... | collective-permute-start | bytes 2359304 | tf_op jit(solution)/shard_map/ppermute | solution.py:825
  464.2 76.6 %collective-permute-start.52 = (bf16[592,1024]{1,0:T(8,128)(2,1)}, bf16[592,1024]{1,0:T(8,128)(2,1)}, u32[]{:S(2)}, u32[]{:S(2)}) collective-permute-start(bf16[592,1024]{1,0:T(8,128)(2,1)} %fusion.10), channel_id=1, source_target_pairs={{0,1},{1,0},{2,3},{3,2},{4,5},{5,4},{6,7},{7,6},{8,9},{9,8},{10,11... | collective-permute-start | bytes 3637256 | tf_op jit(solution)/shard_map/ppermute | solution.py:825
  474.5 28.4 %collective-permute-start.60 = (bf16[256,1536]{1,0:T(8,128)(2,1)}, bf16[256,1536]{1,0:T(8,128)(2,1)}, u32[]{:S(2)}, u32[]{:S(2)}) collective-permute-start(bf16[256,1536]{1,0:T(8,128)(2,1)} %dynamic-slice_bitcast_fusion.5), channel_id=1, source_target_pairs={{0,4},{4,0},{1,5},{5,1},{2,6},{6,2},{3,7},{7,3},{8,12},{12,8},{9,1... | collective-permute-start | bytes 2359304 | tf_op jit(solution)/shard_map/ppermute | solution.py:825
  475.1 24.0 %collective-permute-start.62 = (bf16[256,128]{1,0:T(8,128)(2,1)S(1)}, bf16[256,128]{1,0:T(8,128)(2,1)S(1)}, u32[]{:S(2)}, u32[]{:S(2)}) collective-permute-start(bf16[256,128]{1,0:T(8,128)(2,1)S(1)} %dynamic-slice_bitcast_fusion.23), channel_id=1, source_target_pairs={{0,4},{4,0},{1,5},{5,1},{2,6},{6,2},{3,7},{7,3},{8,12},{12,8},{9,1... | collective-permute-start | bytes 196616 | tf_op jit(solution)/shard_map/ppermute | solution.py:825
  499.1 25.2 %collective-permute-start.69 = (bf16[32,5120]{1,0:T(8,128)(2,1)S(1)}, bf16[32,5120]{1,0:T(8,128)(2,1)S(1)}, u32[]{:S(2)}, u32[]{:S(2)}) collective-permute-start(bf16[32,5120]{1,0:T(8,128)(2,1)S(1)} %copy-done.81), channel_id=1, source_target_pairs={{0,24},{8,0},{16,8},{24,16},{1,25},{9,1},{17,9},{25,17},{2,26},{10... | collective-permute-start | bytes 983048 | tf_op jit(solution)/shard_map/ppermute | solution.py:897
  502.9 21.4 %collective-permute-start.68 = (bf16[32,5120]{1,0:T(8,128)(2,1)}, bf16[32,5120]{1,0:T(8,128)(2,1)S(1)}, u32[]{:S(2)}, u32[]{:S(2)}) collective-permute-start(bf16[32,5120]{1,0:T(8,128)(2,1)} %get-tuple-element.194), channel_id=1, source_target_pairs={{0,16},{8,24},{16,0},{24,8},{1,17},{9,25},{17,1},{25,9},{2,18},{10... | collective-permute-start | bytes 983048 | tf_op jit(solution)/shard_map/ppermute | solution.py:897
  516.0 21.2 %collective-permute-start.63 = (bf16[128,1664]{1,0:T(8,128)(2,1)}, bf16[128,1664]{1,0:T(8,128)(2,1)}, u32[]{:S(2)}, u32[]{:S(2)}) collective-permute-start(bf16[128,1664]{1,0:T(8,128)(2,1)} %dynamic-slice_bitcast_fusion.15), channel_id=1, source_target_pairs={{0,1},{1,0},{2,3},{3,2},{4,5},{5,4},{6,7},{7,6},{8,9},{9,8},{10,11... | collective-permute-start | bytes 1277960 | tf_op jit(solution)/shard_map/ppermute | solution.py:825
  528.1 18.8 %collective-permute-start.57 = (bf16[32,1536]{1,0:T(8,128)(2,1)}, bf16[32,1536]{1,0:T(8,128)(2,1)S(1)}, u32[]{:S(2)}, u32[]{:S(2)}) collective-permute-start(bf16[32,1536]{1,0:T(8,128)(2,1)} %get-tuple-element.209), channel_id=1, source_target_pairs={{0,8},{8,16},{16,24},{24,0},{1,9},{9,17},{17,25},{25,1},{2,10},{10... | collective-permute-start | bytes 294920 | tf_op jit(solution)/shard_map/ppermute | solution.py:897
  528.2 19.7 %collective-permute-start.59 = (bf16[32,1536]{1,0:T(8,128)(2,1)}, bf16[32,1536]{1,0:T(8,128)(2,1)}, u32[]{:S(2)}, u32[]{:S(2)}) collective-permute-start(bf16[32,1536]{1,0:T(8,128)(2,1)} %get-tuple-element.210), channel_id=1, source_target_pairs={{0,24},{8,0},{16,8},{24,16},{1,25},{9,1},{17,9},{25,17},{2,26},{10... | collective-permute-start | bytes 294920 | tf_op jit(solution)/shard_map/ppermute | solution.py:897
  (133 other events, 1311.0 us)

commit v9 on v8

--- a/solution.py
+++ b/solution.py
@@ -710,10 +710,11 @@
         out_ref[:, columns] = product.astype(out_ref.dtype)
 
 
-def gradient(x, d_rows, half, column=0, columns=1, got=None):
+def gradient(x, d_rows, half, column=0, columns=1, got=None, runs=1):
     rows, depth = x.shape
     size = depth // 2
     blocks = size // CHUNK
+    run = blocks // runs
     if d_rows.ndim == 3:
         d_spec = pl.BlockSpec(d_rows.shape, lambda i, index: (0, 0, 0))
         width = d_rows.shape[0] * d_rows.shape[2]
@@ -728,7 +729,10 @@
             num_scalar_prefetch=1,
             grid=(blocks,),
             in_specs=[
-                pl.BlockSpec((rows, CHUNK), lambda i, index: (0, index[0] * blocks + i)),
+                pl.BlockSpec(
+                    (rows, CHUNK),
+                    lambda i, index: (0, (2 * (i // run) + index[0]) * run + i % run),
+                ),
                 d_spec,
             ]
             + [block for _ in extra],
@@ -762,14 +766,6 @@
 
 def to_natural(array, axis, far):
     return reorder(array, axis, (2, 2, 2, far), (3, 1, 0, 2))
-
-
-def hidden_to_local(array, axis, far):
-    return reorder(array, axis, (far, 2, 2, 2), (2, 1, 0, 3))
-
-
-def hidden_to_natural(array, axis, far):
-    return reorder(array, axis, (2, 2, far, 2), (2, 1, 0, 3))
 
 
 def assemble_kernel(routes, index_ref, *refs):
@@ -955,7 +951,7 @@
             jnp.concatenate([halves[0], small, halves[1]], axis=1), far, [half_qkv + 128, half_qkv]
         )
         shard_up = jnp.concatenate(
-            [to_local(unfold(w_out), 1, far), hidden_to_local(unfold(w_up), 1, far)], axis=1
+            [to_local(unfold(w_out), 1, far), unfold(w_up)], axis=1
         )
         up_width = w_up.shape[1] * 8
         up_cut = (width + up_width) // 2
@@ -964,12 +960,15 @@
         first = list(one.values()) + list(two.values())
         one, two = spread(one, "ctx"), spread(two, "x")
         all_one = list(one.values()) + list(two.values())
-        shard_down = after(to_local(unfold(w_down), 1, far), *first)
-        near_down = order_blocks(spread({OWN: shard_down}, "ctx"), ["ctx"])
-        far_up = gather_far(
-            after(shard_up, *all_one), far, [up_cut, up_cut], [near_down]
-        )
         one_core, two_core = spread(one, "core"), spread(two, "core")
+        all_core = list(one_core.values()) + list(two_core.values())
+        far_up = gather_far(after(shard_up, *all_core), far, [up_cut, up_cut])
+        down_weight = lax.all_gather(
+            after(to_local(unfold(w_down), 1, far), *all_one),
+            ("z", "x", "core", "ctx"),
+            axis=0,
+            tiled=True,
+        )
         axes = ["core", "x", "ctx"]
         routes = [[(0, half_qkv, 0, 0), (half_qkv, 128, 1, 0)]] * 8
         qkv_one, small_local = assemble(
@@ -983,7 +982,6 @@
         up_two = spread({OWN: after(far_up[1], *all_one)}, "ctx")
         up_one = spread(tie_received(up_one, qkv_two_weight), "ctx")
         up_two = spread(tie_received(up_two, qkv_two_weight), "x")
-        far_down = gather_far(after(near_down, far_up[0]), far)[0]
 
         devices = 8 * far
         small_core = small_local.reshape(devices, shard_rows, 128)[:, :small_rows, :near_width]
@@ -993,7 +991,7 @@
         out_bias, first_gain, first_shift, second_gain, second_shift, down_bias = (
             small_core[:, index].reshape(-1) for index in range(2, 8)
         )
-        up_bias = hidden_to_local(small_all[:, 8:].reshape(-1), 0, far)
+        up_bias = small_all[:, 8:].reshape(-1)
 
         slot = jnp.arange(slots)
         earlier = slot[:, None] < slot[None, :]
@@ -1050,7 +1048,10 @@
             after(joined_one, qkv_two_weight), bias, width, 0
         )
         joined_two = project(after(normed1, log_one), qkv_two_weight, joined_bias[1])
-        up_one, up_two = tie_received(up_one, log_one), tie_received(up_two, log_one)
+        attended, log_two = attention_forward(
+            joined_two, bias, width, half_width // PAIR, attended
+        )
+        up_one, up_two = tie_received(up_one, log_two), tie_received(up_two, log_two)
         up_near = assemble(
             list(up_one.values()) + list(up_two.values()),
             places(up_one, ["x", "ctx"]) + places(up_two, ["x", "ctx"]),
@@ -1058,11 +1059,7 @@
             [[(0, up_cut, 0, 0)]] * 4 + [[(0, up_cut, 0, up_cut)]] * 4,
         )[0]
         up_blocks = spread({OWN: up_near}, "core")
-        attended, log_two = attention_forward(
-            joined_two, bias, width, half_width // PAIR, attended
-        )
         cotangent_far = swap(after(cotangent, up_near))
-        down_blocks = spread({OWN: after(far_down, up_near)}, "x")
         out_rows, up_weight = assemble(
             list(up_blocks.values()),
             places(up_blocks, ["core"]),
@@ -1077,13 +1074,15 @@
 
         live = (row < SEQ).astype(jnp.float32)[:, None]
         d_out_low = (take(cotangent, cotangent_far) * live).astype(jnp.bfloat16)
-        down_core = trade(gradient(active, d_out_low, 1 - core), "core")
-        down_blocks = {key: after(block, active) for key, block in down_blocks.items()}
-        down_weight = order_blocks(spread(down_blocks, "core"), ["core", "x"])
+        down_core = trade(gradient(active, d_out_low, 1 - core, runs=2 * far), "core")
         last = last_layer(active, down_weight, middle, down_bias)
         last_given = to_give(last)
         down_x = send_half(
-            gradient(active, d_out_low, core, got=after(down_core, last_given[0])), "x"
+            gradient(
+                active, d_out_low, core, got=after(down_core, last_given[0]), runs=2 * far
+            ),
+            "x",
+            far,
         )
         d_hidden, up_sums = d_hidden_layer(after(d_out_low, down_x[0]), down_weight, slope)
         up_core = [
@@ -1139,18 +1138,17 @@
         ]
         vectors = [to_local(vector, 0, far) for vector in joined_vectors] + vectors
         table = jnp.stack([vector.reshape(devices, near_width) for vector in vectors], axis=1)
-        up_sums = to_local(hidden_to_natural(up_sums[0], 0, far), 0, far)
+        up_sums = to_local(up_sums[0], 0, far)
         table = jnp.concatenate([table, up_sums.reshape(devices, -1, near_width)], axis=1)
         table = pad_small(table).reshape(width, 128).astype(jnp.bfloat16)
-        qkv_two_x = send_half(qkv_two, "x")
+        table = add_half(send_half(table, "core"))
+        qkv_two_x = send_half(jnp.concatenate([qkv_two, table], axis=1), "x")
         up_far = jnp.concatenate([*up_halves, add_half(out_y, d_last)], axis=1)
         up_far = send_far(up_far, far)
         qkv_one_y = send_half(
             add_half(qkv_one_x, d_last_given[0], qkv_two_x[0], up_far[0]), "ctx"
         )
-        table = send_half(add_half(send_half(table, "core")), "x")
-        qkv_two = jnp.concatenate([add_half(qkv_two_x), add_half(table)], axis=1)
-        qkv_two_y = send_half(qkv_two, "ctx")
+        qkv_two_y = send_half(add_half(qkv_two_x), "ctx")
         qkv_one_far = send_far(add_half(qkv_one_y), far)
         qkv_two_far = send_far(add_half(qkv_two_y), far)
 
@@ -1177,7 +1175,7 @@
             own(4),
             own(5),
             own(6),
-            refold(hidden_to_natural(sum_up, 1, far)),
+            refold(sum_up),
             small_sums[8:].reshape(-1),
             back(sum_down),
             own(7),

time: 564 us -> 567 us (level)
  waiting for transfers between devices: 125 us -> 146 us
  local copies, waits for them, and re-layouts: 98.6 us -> 80.4 us
  between operations: 2.65 us -> 15.9 us
  Pallas kernels: 188 us -> 180 us
    ppermute x50 -> x45, waiting for transfers between devices: 75.8 us -> 89.6 us  [trade(): return lax.ppermute(array, axis, [(0, 1), (1, 0)])]
    ppermute x9 -> x6, waiting for transfers between devices: 37.8 us -> 46.8 us  [gather_far(): got = lax.ppermute(shard, 'z', [(i, (i + step) % far) for i in range(far)])]
    pallas_call x9 -> x6, Pallas kernels: 30.7 us -> 22 us  [assemble(): pl.pallas_call(functools.partial(assemble_kernel, routes), in_specs=[pl.B...]
    another operation x8, local copies, waits for them, and re-layouts: 6.64 us -> 0.5 us  [on_device(): jnp.stack([vector.reshape(devices, near_width) for vector in vectors], ax...]
    ppermute x9 -> x6, starting transfers between devices: 15 us -> 10.3 us  [gather_far(): got = lax.ppermute(shard, 'z', [(i, (i + step) % far) for i in range(far)])]
    unnamed x222 -> x184, local copies, waits for them, and re-layouts: 36.8 us -> 40.2 us
    ppermute x50 -> x45, starting transfers between devices: 35.2 us -> 34.6 us  [trade(): return lax.ppermute(array, axis, [(0, 1), (1, 0)])]
    convert_element_type x13 -> x12, other arithmetic: 11.1 us -> 11.4 us  [add_half(): (kept.astype(jnp.float32) + got.astype(jnp.float32)).astype(kept.dtype)]
  transfers between devices with their start and end apart: 71 -> 64, of which waited for: 20 -> 19; matrix products, arithmetic and copies ran while one was open for 23% -> 20% of each run, Pallas kernels for 29% -> 32%
where the time goes in v9:
time: 567 us; the launch traced here: 560 us
  Pallas kernels  180 us (32%)
  waiting for transfers between devices  146 us (26%)
  local copies, waits for them, and re-layouts  80.4 us (14%)
  starting transfers between devices  62.7 us (11%)
  matrix products  42.7 us (8%)
  other arithmetic  32.9 us (6%)
  between operations  15.9 us (3%)
    ppermute x45, waiting for transfers between devices, trade(): return lax.ppermute(array, axis, [(0, 1), (1, 0)])  89.6 us
    ppermute x6, waiting for transfers between devices, gather_far(): got = lax.ppermute(shard, 'z', [(i, (i + step) % far) for i in range(far)])  46.8 us
    unnamed x184, local copies, waits for them, and re-layouts  40.2 us
    pallas_call x10, Pallas kernels, gradient(): pl.pallas_call(gradient_kernel, grid_spec=pltpu.PrefetchScalarGridSpec(nu...  40 us
    dot_general x11, matrix products, matmul(): return jnp.dot(left, right, preferred_element_type=jnp.float32)  37.6 us
    ppermute x45, starting transfers between devices, trade(): return lax.ppermute(array, axis, [(0, 1), (1, 0)])  34.6 us
    pallas_call x2, Pallas kernels, attention_forward(): pl.pallas_call(forward_kernel, grid=(pairs,), in_specs=[pair_spec(rows, p...  27.6 us
    pallas_call x2, Pallas kernels, attention_backward(): pl.pallas_call(backward_kernel, grid=(width // PAIR,), in_specs=[pair_spe...  27.2 us
  transfers between devices with their start and end apart: 64, of which 19 were waited for; matrix products, arithmetic and copies ran while one was open for 20% of the time, Pallas kernels for 32%

profile of v9, /device:TPU:0, one launch (start us, length us, event | category | flops | bytes accessed | tf_op | source)
XLA Modules:
  0.0 560.1 jit_solution(12365774338484002020)
XLA Ops:
  7.2 3.0 collective-permute-start.1
  13.9 3.7 collective-permute-start.4
  18.7 4.5 collective-permute-done.4.refs_3_
  23.1 11.6 %collective-permute-done.3.refs_2_ = bf16[32,3200]{1,0:T(8,128)(2,1)S(1)} collective-permute-done((bf16[32,3200]{1,0:T(8,128)(2,1)S(1)}, bf16[32,3200]{1,0:T(8,128)(2,1)S(1)}, u32[]{:S(2)}, u32[]{:S(2)}) %collective-permute-start.3) | collective-permute-done | bytes 204832 | tf_op jit(solution)/shard_map/ppermute | solution.py:832
  40.3 7.2 %collective-permute-done.5.refs_1_ = bf16[128,1664]{1,0:T(8,128)(2,1)S(1)} collective-permute-done((bf16[128,1664]{1,0:T(8,128)(2,1)S(1)}, bf16[128,1664]{1,0:T(8,128)(2,1)S(1)}, u32[]{:S(2)}, u32[]{:S(2)}) %collective-permute-start.5) | collective-permute-done | bytes 426016 | tf_op jit(solution)/shard_map/ppermute | solution.py:821
  54.7 4.8 collective-permute-done.6.refs_2_
  59.4 6.8 %collective-permute-done.7.refs_3_ = bf16[128,1664]{1,0:T(8,128)(2,1)S(1)} collective-permute-done((bf16[128,1664]{1,0:T(8,128)(2,1)S(1)}, bf16[128,1664]{1,0:T(8,128)(2,1)S(1)}, u32[]{:S(2)}, u32[]{:S(2)}) %collective-permute-start.7) | collective-permute-done | bytes 426016 | tf_op jit(solution)/shard_map/ppermute | solution.py:821
  84.0 3.8 fusion.12
  91.6 3.6 collective-permute-start.21
  97.2 6.5 %fusion.36 = (f32[592]{0:T(1024)}, f32[592,1024]{1,0:T(8,128)}) fusion(s32[1024]{0:T(1024)} %reshape.560, f32[592,1024]{1,0:T(8,128)} %fusion.12, bf16[584,1024]{1,0:T(8,128)(2,1)} %collective-permute-done.1, s32[584]{0:T(1024)} %select_select_fusion), kind=kOutput, calls=%fused_computation.170 | convolution fusion | flops 1952777216 | bytes 6054496 | tf_op jit(solution)/shard_map/dot_general | solution.py:28
  104.5 5.8 %collective-permute-done.21.refs_3_ = bf16[32,5120]{1,0:T(8,128)(2,1)} collective-permute-done((bf16[32,5120]{1,0:T(8,128)(2,1)S(1)}, bf16[32,5120]{1,0:T(8,128)(2,1)}, u32[]{:S(2)}, u32[]{:S(2)}) %collective-permute-start.21) | collective-permute-done | bytes 327712 | tf_op jit(solution)/shard_map/ppermute | solution.py:832
  110.3 25.0 %collective-permute-done.20.refs_2_ = bf16[32,5120]{1,0:T(8,128)(2,1)} collective-permute-done((bf16[32,5120]{1,0:T(8,128)(2,1)S(1)}, bf16[32,5120]{1,0:T(8,128)(2,1)}, u32[]{:S(2)}, u32[]{:S(2)}) %collective-permute-start.20) | collective-permute-done | bytes 327712 | tf_op jit(solution)/shard_map/ppermute | solution.py:832
  147.1 3.5 assemble.8.weight_ref
  154.3 10.6 %collective-permute-done.25.refs_5_ = bf16[128,2560]{1,0:T(8,128)(2,1)} collective-permute-done((bf16[128,2560]{1,0:T(8,128)(2,1)}, bf16[128,2560]{1,0:T(8,128)(2,1)}, u32[]{:S(2)}, u32[]{:S(2)}) %collective-permute-start.25) | collective-permute-done | bytes 655392 | tf_op jit(solution)/shard_map/ppermute | solution.py:821
  167.7 3.7 add_convert_fusion.3
  174.2 13.6 %attention_forward.2 = (bf16[592,1024]{1,0:T(8,128)(2,1)S(1)}, f32[4,2,592]{2,1,0:T(2,128)S(1)}) custom-call(bf16[3,592,512]{2,1,0:T(8,128)(2,1)S(1)} %project.2.query_ref.key_ref.value_ref, bf16[3,592,512]{2,1,0:T(8,128)(2,1)S(1)} %project.2.query_ref.key_ref.value_ref, bf16[3,592,512]{2,1,0:T(8,128)(2,1)S(1)} %project.2.query_ref.key_ref.value_ref, ...), custom_call_target="tpu_custom_call" | custom-call | flops 1 | bytes 1 | tf_op jit(solution)/shard_map/attention_forward/pallas_call | solution.py:436
  190.5 14.0 %attention_forward.3 = (bf16[592,1024]{1,0:T(8,128)(2,1)S(1)}, f32[4,2,592]{2,1,0:T(2,128)S(1)}) custom-call(bf16[3,592,512]{2,1,0:T(8,128)(2,1)S(1)} %project.3.query_ref.key_ref.value_ref, bf16[3,592,512]{2,1,0:T(8,128)(2,1)S(1)} %project.3.query_ref.key_ref.value_ref, ...), custom_call_target="tpu_custom_call", output_to_operand_aliasing={{0}: (4, {})} | custom-call | flops 1 | bytes 1 | tf_op jit(solution)/shard_map/attention_forward/pallas_call | solution.py:436
  204.6 5.2 assemble.10.refs_0_
  211.4 3.9 fusion.11
  216.6 22.4 %collective-permute-done.30 = bf16[584,1024]{1,0:T(8,128)(2,1)} collective-permute-done((bf16[584,1024]{1,0:T(8,128)(2,1)}, bf16[584,1024]{1,0:T(8,128)(2,1)}, u32[]{:S(2)}, u32[]{:S(2)}) %collective-permute-start.30) | collective-permute-done | bytes 1196064 | tf_op jit(solution)/shard_map/ppermute | solution.py:821
  239.0 5.5 fusion.38
  244.5 5.6 assemble.11
  258.7 18.1 %hidden_layer.1 = (bf16[592,4096]{1,0:T(8,128)(2,1)S(1)}, bf16[592,4096]{1,0:T(8,128)(2,1)S(1)}) custom-call(bf16[592,1024]{1,0:T(8,128)(2,1)S(1)} %get-tuple-element.166.x_ref, bf16[1024,4096]{1,0:T(8,128)(2,1)S(1)} %get-tuple-element.104.weight_ref, f32[1,4096]{1,0:T(1,128)S(1)} %broadcast_in_dim_reshape.4.bias_ref), custom_call_target="tpu_custom_call" | custom-call | flops 1 | bytes 1 | tf_op jit(solution)/shard_map/hidden_layer/pallas_call | solution.py:522
  276.9 7.7 %gradient.10 = bf16[2048,1024]{1,0:T(8,128)(2,1)} custom-call(s32[1]{0:T(128)} %bitcast.25.index_ref, bf16[592,4096]{1,0:T(8,128)(2,1)S(1)} %get-tuple-element.105.active_ref.x_ref, bf16[592,1024]{1,0:T(8,128)(2,1)S(1)} %copy-done.22), custom_call_target="tpu_custom_call" | custom-call | flops 1 | bytes 1 | tf_op jit(solution)/shard_map/gradient/pallas_call | solution.py:726
  284.7 3.4 copy-done.17
  291.8 7.8 %d_hidden_layer.1 = (bf16[592,4096]{1,0:T(8,128)(2,1)S(1)}, f32[1,4096]{1,0:T(1,128)S(1)}) custom-call(bf16[592,1024]{1,0:T(8,128)(2,1)S(1)} %copy-done.23, bf16[4096,1024]{1,0:T(8,128)(2,1)S(1)} %copy-done.17, bf16[592,4096]{1,0:T(8,128)(2,1)S(1)} %copy-done.34), custom_call_target="tpu_custom_call" | custom-call | flops 1 | bytes 1 | tf_op jit(solution)/shard_map/d_hidden_layer/pallas_call | solution.py:584
  299.5 3.4 gradient.14
  303.4 3.3 gradient.12
  306.8 11.3 %last_layer.1 = bf16[592,1024]{1,0:T(8,128)(2,1)S(1)} custom-call(bf16[592,4096]{1,0:T(8,128)(2,1)} %copy-done.8, bf16[4096,1024]{1,0:T(8,128)(2,1)} %all-gather.2.cloned.1.call-done.weight_ref, f32[592,1024]{1,0:T(8,128)} %copy-done.68, f32[1,1024]{1,0:T(1,128)S(1)} %broadcast_in_dim_reshape_squeeze.6.bias_ref), custom_call_target="tpu_custom_call" | custom-call | flops 1 | bytes 1 | tf_op jit(solution)/shard_map/last_layer/pallas_call | solution.py:555
  323.1 7.5 %gradient.11 = bf16[2048,1024]{1,0:T(8,128)(2,1)S(1)} custom-call(s32[1]{0:T(128)} %bitcast.24.index_ref, bf16[592,4096]{1,0:T(8,128)(2,1)S(1)} %copy-done.9, bf16[592,1024]{1,0:T(8,128)(2,1)S(1)} %copy-done.24, bf16[2048,1024]{1,0:T(8,128)(2,1)} %collective-permute-done.31.refs_0_), custom_call_target="tpu_custom_call" | custom-call | flops 1 | bytes 1 | tf_op jit(solution)/shard_map/gradient/pallas_call | solution.py:726
  341.1 12.2 %norm_back.2 = (f32[592,1024]{1,0:T(8,128)S(1)}, bf16[592,1024]{1,0:T(8,128)(2,1)S(1)}, f32[8,1024]{1,0:T(8,128)S(1)}) custom-call(bf16[592,4096]{1,0:T(8,128)(2,1)S(1)} %copy-done.1, bf16[1024,4096]{1,0:T(8,128)(2,1)} %copy-done.18, f32[592,1024]{1,0:T(8,128)S(1)} %copy-done.29, f32[592,1]{1,0:T(8,128)S(1)} %rsqrt.14.refs_1_, ...), custom_call_target="tpu_custom_call" | custom-call | flops 1 | bytes 1 | tf_op jit(solution)/shard_map/norm_back/pallas_call | solution.py:685
  361.2 3.3 gradient.15
  368.1 3.4 gradient.13
  375.4 6.3 %collective-permute-done.35 = bf16[1024,1024]{1,0:T(8,128)(2,1)} collective-permute-done((bf16[1024,1024]{1,0:T(8,128)(2,1)}, bf16[1024,1024]{1,0:T(8,128)(2,1)}, u32[]{:S(2)}, u32[]{:S(2)}) %collective-permute-start.35) | collective-permute-done | bytes 2097184 | tf_op jit(solution)/shard_map/ppermute | solution.py:821
  391.8 13.8 %attention_backward.2.d_ref = bf16[3,592,512]{2,1,0:T(8,128)(2,1)S(1)} custom-call(bf16[3,592,512]{2,1,0:T(8,128)(2,1)S(1)} %copy-done.4, bf16[3,592,512]{2,1,0:T(8,128)(2,1)S(1)} %copy-done.4, bf16[3,592,512]{2,1,0:T(8,128)(2,1)S(1)} %copy-done.4, bf16[592,1024]{1,0:T(8,128)(2,1)S(1)} %convolution_convert_fusion.1.d_ref, ...), custom_call_target="tpu_custom_call" | custom-call | flops 1 | bytes 1 | tf_op jit(solution)/shard_map/attention_backward/pallas_call | solution.py:459
  405.6 4.2 add_convert_fusion.5
  409.8 3.3 d_normed.1.refs_0_
  421.6 13.4 %attention_backward.3.d_ref = bf16[3,592,512]{2,1,0:T(8,128)(2,1)S(1)} custom-call(bf16[3,592,512]{2,1,0:T(8,128)(2,1)S(1)} %project.3.query_ref.key_ref.value_ref, bf16[3,592,512]{2,1,0:T(8,128)(2,1)S(1)} %project.3.query_ref.key_ref.value_ref, bf16[3,592,512]{2,1,0:T(8,128)(2,1)S(1)} %project.3.query_ref.key_ref.value_ref, ...), custom_call_target="tpu_custom_call" | custom-call | flops 1 | bytes 1 | tf_op jit(solution)/shard_map/attention_backward/pallas_call | solution.py:459
  447.3 4.2 collective-permute-done.43
  459.4 5.0 norm_back.3
  469.6 3.7 collective-permute-start.61
  491.4 19.8 %collective-permute-done.54 = bf16[256,1664]{1,0:T(8,128)(2,1)} collective-permute-done((bf16[256,1664]{1,0:T(8,128)(2,1)}, bf16[256,1664]{1,0:T(8,128)(2,1)}, u32[]{:S(2)}, u32[]{:S(2)}) %collective-permute-start.54) | collective-permute-done | bytes 852000 | tf_op jit(solution)/shard_map/ppermute | solution.py:821
  516.6 3.9 convolution_add_fusion
  520.4 6.1 %collective-permute-done.50 = bf16[128,1536]{1,0:T(8,128)(2,1)S(1)} collective-permute-done((bf16[128,1536]{1,0:T(8,128)(2,1)S(1)}, bf16[128,1536]{1,0:T(8,128)(2,1)S(1)}, u32[]{:S(2)}, u32[]{:S(2)}) %collective-permute-start.50) | collective-permute-done | bytes 393248 | tf_op jit(solution)/shard_map/ppermute | solution.py:821
  529.4 3.5 collective-permute-start.53
  536.4 3.8 collective-permute-start.58
  540.8 4.3 collective-permute-done.52
  545.4 4.8 collective-permute-done.57
  (449 shorter events, 188.7 us)
Async XLA Ops:
  7.2 277.5 %all-gather.2.cloned.1.call-start = ((), (), s32[]{:S(2)}) async-start(), calls=%async_computation | async-start | bytes 8650752 | tf_op jit(solution)/shard_map/all_gather | solution.py:966
  7.2 31.0 %collective-permute-start.1 = (bf16[584,1024]{1,0:T(8,128)(2,1)}, bf16[584,1024]{1,0:T(8,128)(2,1)}, u32[]{:S(2)}, u32[]{:S(2)}) collective-permute-start(bf16[584,1024]{1,0:T(8,128)(2,1)} %param.16), channel_id=1, source_target_pairs={{0,1},{1,0},{2,3},{3,2},{4,5},{5,4},{6,7},{7,6},{8,9},{9,8},{10,11... | collective-permute-start | bytes 3588104 | tf_op jit(solution)/shard_map/ppermute | solution.py:821
  17.6 17.1 %collective-permute-start.3 = (bf16[32,3200]{1,0:T(8,128)(2,1)S(1)}, bf16[32,3200]{1,0:T(8,128)(2,1)S(1)}, u32[]{:S(2)}, u32[]{:S(2)}) collective-permute-start(bf16[32,3200]{1,0:T(8,128)(2,1)S(1)} %fusion.31.refs_0_), channel_id=1, source_target_pairs={{0,16},{8,24},{16,0},{24,8},{1,17},{9,25},{17,1},{25,9},{2,18},{10... | collective-permute-start | bytes 614408 | tf_op jit(solution)/shard_map/ppermute | solution.py:832
  17.6 17.1 %collective-permute-start.2 = (bf16[32,3200]{1,0:T(8,128)(2,1)S(1)}, bf16[32,3200]{1,0:T(8,128)(2,1)S(1)}, u32[]{:S(2)}, u32[]{:S(2)}) collective-permute-start(bf16[32,3200]{1,0:T(8,128)(2,1)S(1)} %fusion.31.refs_0_), channel_id=1, source_target_pairs={{0,8},{8,16},{16,24},{24,0},{1,9},{9,17},{17,25},{25,1},{2,10},{10... | collective-permute-start | bytes 614408 | tf_op jit(solution)/shard_map/ppermute | solution.py:832
  38.3 12.1 %collective-permute-start.12 = (bf16[128,1536]{1,0:T(8,128)(2,1)S(1)}, bf16[128,1536]{1,0:T(8,128)(2,1)S(1)}, u32[]{:S(2)}, u32[]{:S(2)}) collective-permute-start(bf16[128,1536]{1,0:T(8,128)(2,1)S(1)} %get-tuple-element.83.refs_0_), channel_id=1, source_target_pairs={{0,1},{1,0},{2,3},{3,2},{4,5},{5,4},{6,7},{7,6},{8,9},{9,8},{10,11... | collective-permute-start | bytes 1179656 | tf_op jit(solution)/shard_map/ppermute | solution.py:821
  38.8 20.7 %collective-permute-start.6 = (bf16[128,1664]{1,0:T(8,128)(2,1)S(1)}, bf16[128,1664]{1,0:T(8,128)(2,1)S(1)}, u32[]{:S(2)}, u32[]{:S(2)}) collective-permute-start(bf16[128,1664]{1,0:T(8,128)(2,1)S(1)} %get-tuple-element.79.refs_0_), channel_id=1, source_target_pairs={{0,1},{1,0},{2,3},{3,2},{4,5},{5,4},{6,7},{7,6},{8,9},{9,8},{10,11... | collective-permute-start | bytes 1277960 | tf_op jit(solution)/shard_map/ppermute | solution.py:821
  47.5 18.8 %collective-permute-start.7 = (bf16[128,1664]{1,0:T(8,128)(2,1)S(1)}, bf16[128,1664]{1,0:T(8,128)(2,1)S(1)}, u32[]{:S(2)}, u32[]{:S(2)}) collective-permute-start(bf16[128,1664]{1,0:T(8,128)(2,1)S(1)} %collective-permute-done.5.refs_1_), channel_id=1, source_target_pairs={{0,1},{1,0},{2,3},{3,2},{4,5},{5,4},{6,7},{7,6},{8,9},{9,8},{10,11... | collective-permute-start | bytes 1277960 | tf_op jit(solution)/shard_map/ppermute | solution.py:821
  48.0 18.3 %collective-permute-start.13 = (bf16[128,1536]{1,0:T(8,128)(2,1)S(1)}, bf16[128,1536]{1,0:T(8,128)(2,1)S(1)}, u32[]{:S(2)}, u32[]{:S(2)}) collective-permute-start(bf16[128,1536]{1,0:T(8,128)(2,1)S(1)} %get-tuple-element.83.refs_0_), channel_id=1, source_target_pairs={{0,4},{4,0},{1,5},{5,1},{2,6},{6,2},{3,7},{7,3},{8,12},{12,8},{9,1... | collective-permute-start | bytes 1179656 | tf_op jit(solution)/shard_map/ppermute | solution.py:821
  50.3 15.9 %collective-permute-start.14 = (bf16[128,1536]{1,0:T(8,128)(2,1)S(1)}, bf16[128,1536]{1,0:T(8,128)(2,1)}, u32[]{:S(2)}, u32[]{:S(2)}) collective-permute-start(bf16[128,1536]{1,0:T(8,128)(2,1)S(1)} %collective-permute-done.12.refs_1_), channel_id=1, source_target_pairs={{0,4},{4,0},{1,5},{5,1},{2,6},{6,2},{3,7},{7,3},{8,12},{12,8},{9,1... | collective-permute-start | bytes 1179656 | tf_op jit(solution)/shard_map/ppermute | solution.py:821
  91.6 18.7 %collective-permute-start.21 = (bf16[32,5120]{1,0:T(8,128)(2,1)S(1)}, bf16[32,5120]{1,0:T(8,128)(2,1)}, u32[]{:S(2)}, u32[]{:S(2)}) collective-permute-start(bf16[32,5120]{1,0:T(8,128)(2,1)S(1)} %pad_maximum_fusion.3.refs_0_), channel_id=1, source_target_pairs={{0,24},{8,0},{16,8},{24,16},{1,25},{9,1},{17,9},{25,17},{2,26},{10... | collective-permute-start | bytes 983048 | tf_op jit(solution)/shard_map/ppermute | solution.py:832
  95.2 40.1 %collective-permute-start.20 = (bf16[32,5120]{1,0:T(8,128)(2,1)S(1)}, bf16[32,5120]{1,0:T(8,128)(2,1)}, u32[]{:S(2)}, u32[]{:S(2)}) collective-permute-start(bf16[32,5120]{1,0:T(8,128)(2,1)S(1)} %pad_maximum_fusion.3.refs_0_), channel_id=1, source_target_pairs={{0,16},{8,24},{16,0},{24,8},{1,17},{9,25},{17,1},{25,9},{2,18},{10... | collective-permute-start | bytes 983048 | tf_op jit(solution)/shard_map/ppermute | solution.py:832
  95.2 40.1 %collective-permute-start.19 = (bf16[32,5120]{1,0:T(8,128)(2,1)S(1)}, bf16[32,5120]{1,0:T(8,128)(2,1)}, u32[]{:S(2)}, u32[]{:S(2)}) collective-permute-start(bf16[32,5120]{1,0:T(8,128)(2,1)S(1)} %pad_maximum_fusion.3.refs_0_), channel_id=1, source_target_pairs={{0,8},{8,16},{16,24},{24,0},{1,9},{9,17},{17,25},{25,1},{2,10},{10... | collective-permute-start | bytes 983048 | tf_op jit(solution)/shard_map/ppermute | solution.py:832
  138.1 26.9 %collective-permute-start.25 = (bf16[128,2560]{1,0:T(8,128)(2,1)}, bf16[128,2560]{1,0:T(8,128)(2,1)}, u32[]{:S(2)}, u32[]{:S(2)}) collective-permute-start(bf16[128,2560]{1,0:T(8,128)(2,1)} %get-tuple-element.98.refs_4_), channel_id=1, source_target_pairs={{0,1},{1,0},{2,3},{3,2},{4,5},{5,4},{6,7},{7,6},{8,9},{9,8},{10,11... | collective-permute-start | bytes 1966088 | tf_op jit(solution)/shard_map/ppermute | solution.py:821
  139.2 25.7 %collective-permute-start.22 = (bf16[128,2560]{1,0:T(8,128)(2,1)}, bf16[128,2560]{1,0:T(8,128)(2,1)}, u32[]{:S(2)}, u32[]{:S(2)}) collective-permute-start(bf16[128,2560]{1,0:T(8,128)(2,1)} %get-tuple-element.91.refs_0_), channel_id=1, source_target_pairs={{0,4},{4,0},{1,5},{5,1},{2,6},{6,2},{3,7},{7,3},{8,12},{12,8},{9,1... | collective-permute-start | bytes 1966088 | tf_op jit(solution)/shard_map/ppermute | solution.py:821
  152.3 52.3 %collective-permute-start.26 = (bf16[128,2560]{1,0:T(8,128)(2,1)}, bf16[128,2560]{1,0:T(8,128)(2,1)}, u32[]{:S(2)}, u32[]{:S(2)}) collective-permute-start(bf16[128,2560]{1,0:T(8,128)(2,1)} %get-tuple-element.98.refs_4_), channel_id=1, source_target_pairs={{0,4},{4,0},{1,5},{5,1},{2,6},{6,2},{3,7},{7,3},{8,12},{12,8},{9,1... | collective-permute-start | bytes 1966088 | tf_op jit(solution)/shard_map/ppermute | solution.py:821
  153.4 51.2 %collective-permute-start.23 = (bf16[128,2560]{1,0:T(8,128)(2,1)}, bf16[128,2560]{1,0:T(8,128)(2,1)}, u32[]{:S(2)}, u32[]{:S(2)}) collective-permute-start(bf16[128,2560]{1,0:T(8,128)(2,1)} %get-tuple-element.91.refs_0_), channel_id=1, source_target_pairs={{0,1},{1,0},{2,3},{3,2},{4,5},{5,4},{6,7},{7,6},{8,9},{9,8},{10,11... | collective-permute-start | bytes 1966088 | tf_op jit(solution)/shard_map/ppermute | solution.py:821
  165.0 39.6 %collective-permute-start.24 = (bf16[128,2560]{1,0:T(8,128)(2,1)}, bf16[128,2560]{1,0:T(8,128)(2,1)}, u32[]{:S(2)}, u32[]{:S(2)}) collective-permute-start(bf16[128,2560]{1,0:T(8,128)(2,1)} %collective-permute-done.22.refs_1_), channel_id=1, source_target_pairs={{0,1},{1,0},{2,3},{3,2},{4,5},{5,4},{6,7},{7,6},{8,9},{9,8},{10,11... | collective-permute-start | bytes 1966088 | tf_op jit(solution)/shard_map/ppermute | solution.py:821
  166.4 38.1 %collective-permute-start.27 = (bf16[128,2560]{1,0:T(8,128)(2,1)}, bf16[128,2560]{1,0:T(8,128)(2,1)}, u32[]{:S(2)}, u32[]{:S(2)}) collective-permute-start(bf16[128,2560]{1,0:T(8,128)(2,1)} %collective-permute-done.25.refs_5_), channel_id=1, source_target_pairs={{0,4},{4,0},{1,5},{5,1},{2,6},{6,2},{3,7},{7,3},{8,12},{12,8},{9,1... | collective-permute-start | bytes 1966088 | tf_op jit(solution)/shard_map/ppermute | solution.py:821
  209.8 34.7 %collective-permute-start.28 = (bf16[512,5120]{1,0:T(8,128)(2,1)}, bf16[512,5120]{1,0:T(8,128)(2,1)}, u32[]{:S(2)}, u32[]{:S(2)}) collective-permute-start(bf16[512,5120]{1,0:T(8,128)(2,1)} %assemble.10.refs_0_), channel_id=1, source_target_pairs={{0,2},{2,0},{1,3},{3,1},{4,6},{6,4},{5,7},{7,5},{8,10},{10,8},{9,1... | collective-permute-start | bytes 15728648 | tf_op jit(solution)/shard_map/ppermute | solution.py:821
  209.9 29.1 %collective-permute-start.30 = (bf16[584,1024]{1,0:T(8,128)(2,1)}, bf16[584,1024]{1,0:T(8,128)(2,1)}, u32[]{:S(2)}, u32[]{:S(2)}) collective-permute-start(bf16[584,1024]{1,0:T(8,128)(2,1)} %param.17), channel_id=1, source_target_pairs={{0,1},{1,0},{2,3},{3,2},{4,5},{5,4},{6,7},{7,6},{8,9},{9,8},{10,11... | collective-permute-start | bytes 3588104 | tf_op jit(solution)/shard_map/ppermute | solution.py:821
  284.7 36.0 %collective-permute-start.31 = (bf16[2048,1024]{1,0:T(8,128)(2,1)}, bf16[2048,1024]{1,0:T(8,128)(2,1)}, u32[]{:S(2)}, u32[]{:S(2)}) collective-permute-start(bf16[2048,1024]{1,0:T(8,128)(2,1)} %gradient.10), channel_id=1, source_target_pairs={{0,2},{2,0},{1,3},{3,1},{4,6},{6,4},{5,7},{7,5},{8,10},{10,8},{9,1... | collective-permute-start | bytes 12582920 | tf_op jit(solution)/shard_map/ppermute | solution.py:821
  302.9 55.9 %collective-permute-start.33 = (bf16[512,2048]{1,0:T(8,128)(2,1)}, bf16[512,2048]{1,0:T(8,128)(2,1)}, u32[]{:S(2)}, u32[]{:S(2)}) collective-permute-start(bf16[512,2048]{1,0:T(8,128)(2,1)} %gradient.14), channel_id=1, source_target_pairs={{0,2},{2,0},{1,3},{3,1},{4,6},{6,4},{5,7},{7,5},{8,10},{10,8},{9,1... | collective-permute-start | bytes 6291464 | tf_op jit(solution)/shard_map/ppermute | solution.py:821
  306.7 61.4 %collective-permute-start.32 = (bf16[512,2048]{1,0:T(8,128)(2,1)}, bf16[512,2048]{1,0:T(8,128)(2,1)}, u32[]{:S(2)}, u32[]{:S(2)}) collective-permute-start(bf16[512,2048]{1,0:T(8,128)(2,1)} %gradient.12), channel_id=1, source_target_pairs={{0,2},{2,0},{1,3},{3,1},{4,6},{6,4},{5,7},{7,5},{8,10},{10,8},{9,1... | collective-permute-start | bytes 6291464 | tf_op jit(solution)/shard_map/ppermute | solution.py:821
  333.0 48.7 %collective-permute-start.35 = (bf16[1024,1024]{1,0:T(8,128)(2,1)}, bf16[1024,1024]{1,0:T(8,128)(2,1)}, u32[]{:S(2)}, u32[]{:S(2)}) collective-permute-start(bf16[1024,1024]{1,0:T(8,128)(2,1)} %bitcast.51), channel_id=1, source_target_pairs={{0,4},{4,0},{1,5},{5,1},{2,6},{6,2},{3,7},{7,3},{8,12},{12,8},{9,1... | collective-permute-start | bytes 6291464 | tf_op jit(solution)/shard_map/ppermute | solution.py:821
  335.0 49.3 %collective-permute-start.29 = (bf16[592,1024]{1,0:T(8,128)(2,1)}, bf16[592,1024]{1,0:T(8,128)(2,1)}, u32[]{:S(2)}, u32[]{:S(2)}) collective-permute-start(bf16[592,1024]{1,0:T(8,128)(2,1)} %fusion.9), channel_id=1, source_target_pairs={{0,1},{1,0},{2,3},{3,2},{4,5},{5,4},{6,7},{7,6},{8,9},{9,8},{10,11... | collective-permute-start | bytes 3637256 | tf_op jit(solution)/shard_map/ppermute | solution.py:821
  371.8 17.8 %collective-permute-start.34 = (bf16[512,1024]{1,0:T(8,128)(2,1)S(1)}, bf16[512,1024]{1,0:T(8,128)(2,1)S(1)}, u32[]{:S(2)}, u32[]{:S(2)}) collective-permute-start(bf16[512,1024]{1,0:T(8,128)(2,1)S(1)} %dynamic-slice_bitcast_fusion.1), channel_id=1, source_target_pairs={{0,2},{2,0},{1,3},{3,1},{4,6},{6,4},{5,7},{7,5},{8,10},{10,8},{9,1... | collective-permute-start | bytes 3145736 | tf_op jit(solution)/shard_map/ppermute | solution.py:821
  372.0 48.0 %collective-permute-start.36 = (bf16[256,2048]{1,0:T(8,128)(2,1)S(1)}, bf16[256,2048]{1,0:T(8,128)(2,1)S(1)}, u32[]{:S(2)}, u32[]{:S(2)}) collective-permute-start(bf16[256,2048]{1,0:T(8,128)(2,1)S(1)} %bitcast.209), channel_id=1, source_target_pairs={{0,1},{1,0},{2,3},{3,2},{4,5},{5,4},{6,7},{7,6},{8,9},{9,8},{10,11... | collective-permute-start | bytes 3145736 | tf_op jit(solution)/shard_map/ppermute | solution.py:821
  373.4 43.8 %collective-permute-start.37 = (bf16[256,2048]{1,0:T(8,128)(2,1)S(1)}, bf16[256,2048]{1,0:T(8,128)(2,1)S(1)}, u32[]{:S(2)}, u32[]{:S(2)}) collective-permute-start(bf16[256,2048]{1,0:T(8,128)(2,1)S(1)} %get-tuple-element.176), channel_id=1, source_target_pairs={{0,4},{4,0},{1,5},{5,1},{2,6},{6,2},{3,7},{7,3},{8,12},{12,8},{9,1... | collective-permute-start | bytes 3145736 | tf_op jit(solution)/shard_map/ppermute | solution.py:821
  385.7 51.3 %collective-permute-start.39 = (bf16[256,1024]{1,0:T(8,128)(2,1)}, bf16[256,1024]{1,0:T(8,128)(2,1)}, u32[]{:S(2)}, u32[]{:S(2)}) collective-permute-start(bf16[256,1024]{1,0:T(8,128)(2,1)} %get-tuple-element.172), channel_id=1, source_target_pairs={{0,8},{8,16},{16,24},{24,0},{1,9},{9,17},{17,25},{25,1},{2,10},{10... | collective-permute-start | bytes 1572872 | tf_op jit(solution)/shard_map/ppermute | solution.py:893
  387.1 50.5 %collective-permute-start.41 = (bf16[256,1024]{1,0:T(8,128)(2,1)}, bf16[256,1024]{1,0:T(8,128)(2,1)}, u32[]{:S(2)}, u32[]{:S(2)}) collective-permute-start(bf16[256,1024]{1,0:T(8,128)(2,1)} %get-tuple-element.173), channel_id=1, source_target_pairs={{0,24},{8,0},{16,8},{24,16},{1,25},{9,1},{17,9},{25,17},{2,26},{10... | collective-permute-start | bytes 1572872 | tf_op jit(solution)/shard_map/ppermute | solution.py:893
  389.5 49.4 %collective-permute-start.40 = (bf16[256,1024]{1,0:T(8,128)(2,1)}, bf16[256,1024]{1,0:T(8,128)(2,1)}, u32[]{:S(2)}, u32[]{:S(2)}) collective-permute-start(bf16[256,1024]{1,0:T(8,128)(2,1)} %get-tuple-element.174), channel_id=1, source_target_pairs={{0,16},{8,24},{16,0},{24,8},{1,17},{9,25},{17,1},{25,9},{2,18},{10... | collective-permute-start | bytes 1572872 | tf_op jit(solution)/shard_map/ppermute | solution.py:893
  417.2 28.2 %collective-permute-start.42 = (bf16[256,1024]{1,0:T(8,128)(2,1)}, bf16[256,1024]{1,0:T(8,128)(2,1)}, u32[]{:S(2)}, u32[]{:S(2)}) collective-permute-start(bf16[256,1024]{1,0:T(8,128)(2,1)} %get-tuple-element.190), channel_id=1, source_target_pairs={{0,4},{4,0},{1,5},{5,1},{2,6},{6,2},{3,7},{7,3},{8,12},{12,8},{9,1... | collective-permute-start | bytes 1572872 | tf_op jit(solution)/shard_map/ppermute | solution.py:821
  434.9 19.0 %collective-permute-start.38 = (bf16[512,1536]{1,0:T(8,128)(2,1)}, bf16[512,1536]{1,0:T(8,128)(2,1)}, u32[]{:S(2)}, u32[]{:S(2)}) collective-permute-start(bf16[512,1536]{1,0:T(8,128)(2,1)} %gradient.16), channel_id=1, source_target_pairs={{0,2},{2,0},{1,3},{3,1},{4,6},{6,4},{5,7},{7,5},{8,10},{10,8},{9,1... | collective-permute-start | bytes 4718600 | tf_op jit(solution)/shard_map/ppermute | solution.py:821
  437.0 14.5 %collective-permute-start.43 = (bf16[128,2048]{1,0:T(8,128)(2,1)}, bf16[128,2048]{1,0:T(8,128)(2,1)S(1)}, u32[]{:S(2)}, u32[]{:S(2)}) collective-permute-start(bf16[128,2048]{1,0:T(8,128)(2,1)} %get-tuple-element.188), channel_id=1, source_target_pairs={{0,4},{4,0},{1,5},{5,1},{2,6},{6,2},{3,7},{7,3},{8,12},{12,8},{9,1... | collective-permute-start | bytes 1572872 | tf_op jit(solution)/shard_map/ppermute | solution.py:821
  437.6 15.0 %collective-permute-start.44 = (bf16[128,2048]{1,0:T(8,128)(2,1)}, bf16[128,2048]{1,0:T(8,128)(2,1)S(1)}, u32[]{:S(2)}, u32[]{:S(2)}) collective-permute-start(bf16[128,2048]{1,0:T(8,128)(2,1)} %get-tuple-element.186), channel_id=1, source_target_pairs={{0,1},{1,0},{2,3},{3,2},{4,5},{5,4},{6,7},{7,6},{8,9},{9,8},{10,11... | collective-permute-start | bytes 1572872 | tf_op jit(solution)/shard_map/ppermute | solution.py:821
  444.7 37.3 %collective-permute-start.62 = (bf16[128,1024]{1,0:T(8,128)(2,1)}, bf16[128,1024]{1,0:T(8,128)(2,1)}, u32[]{:S(2)}, u32[]{:S(2)}) collective-permute-start(bf16[128,1024]{1,0:T(8,128)(2,1)} %get-tuple-element.192), channel_id=1, source_target_pairs={{0,1},{1,0},{2,3},{3,2},{4,5},{5,4},{6,7},{7,6},{8,9},{9,8},{10,11... | collective-permute-start | bytes 786440 | tf_op jit(solution)/shard_map/ppermute | solution.py:821
  445.3 27.9 %collective-permute-start.47 = (bf16[512,1536]{1,0:T(8,128)(2,1)}, bf16[512,1536]{1,0:T(8,128)(2,1)}, u32[]{:S(2)}, u32[]{:S(2)}) collective-permute-start(bf16[512,1536]{1,0:T(8,128)(2,1)} %gradient.18), channel_id=1, source_target_pairs={{0,2},{2,0},{1,3},{3,1},{4,6},{6,4},{5,7},{7,5},{8,10},{10,8},{9,1... | collective-permute-start | bytes 4718600 | tf_op jit(solution)/shard_map/ppermute | solution.py:821
  451.5 13.9 %collective-permute-start.49 = (bf16[128,1024]{1,0:T(8,128)(2,1)S(1)}, bf16[128,1024]{1,0:T(8,128)(2,1)}, u32[]{:S(2)}, u32[]{:S(2)}) collective-permute-start(bf16[128,1024]{1,0:T(8,128)(2,1)S(1)} %get-tuple-element.194), channel_id=1, source_target_pairs={{0,1},{1,0},{2,3},{3,2},{4,5},{5,4},{6,7},{7,6},{8,9},{9,8},{10,11... | collective-permute-start | bytes 786440 | tf_op jit(solution)/shard_map/ppermute | solution.py:821
  466.0 11.6 %collective-permute-start.48 = (bf16[512,128]{1,0:T(8,128)(2,1)S(1)}, bf16[512,128]{1,0:T(8,128)(2,1)S(1)}, u32[]{:S(2)}, u32[]{:S(2)}) collective-permute-start(bf16[512,128]{1,0:T(8,128)(2,1)S(1)} %dynamic-slice_bitcast_fusion.20), channel_id=1, source_target_pairs={{0,2},{2,0},{1,3},{3,1},{4,6},{6,4},{5,7},{7,5},{8,10},{10,8},{9,1... | collective-permute-start | bytes 393224 | tf_op jit(solution)/shard_map/ppermute | solution.py:821
  469.4 57.3 %collective-permute-start.59 = (bf16[32,5120]{1,0:T(8,128)(2,1)}, bf16[32,5120]{1,0:T(8,128)(2,1)}, u32[]{:S(2)}, u32[]{:S(2)}) collective-permute-start(bf16[32,5120]{1,0:T(8,128)(2,1)} %get-tuple-element.182), channel_id=1, source_target_pairs={{0,8},{8,16},{16,24},{24,0},{1,9},{9,17},{17,25},{25,1},{2,10},{10... | collective-permute-start | bytes 983048 | tf_op jit(solution)/shard_map/ppermute | solution.py:893
  469.6 57.2 %collective-permute-start.61 = (bf16[32,5120]{1,0:T(8,128)(2,1)}, bf16[32,5120]{1,0:T(8,128)(2,1)}, u32[]{:S(2)}, u32[]{:S(2)}) collective-permute-start(bf16[32,5120]{1,0:T(8,128)(2,1)} %get-tuple-element.183), channel_id=1, source_target_pairs={{0,24},{8,0},{16,8},{24,16},{1,25},{9,1},{17,9},{25,17},{2,26},{10... | collective-permute-start | bytes 983048 | tf_op jit(solution)/shard_map/ppermute | solution.py:893
  473.3 39.7 %collective-permute-start.46 = (bf16[256,1536]{1,0:T(8,128)(2,1)}, bf16[256,1536]{1,0:T(8,128)(2,1)}, u32[]{:S(2)}, u32[]{:S(2)}) collective-permute-start(bf16[256,1536]{1,0:T(8,128)(2,1)} %get-tuple-element.180), channel_id=1, source_target_pairs={{0,4},{4,0},{1,5},{5,1},{2,6},{6,2},{3,7},{7,3},{8,12},{12,8},{9,1... | collective-permute-start | bytes 2359304 | tf_op jit(solution)/shard_map/ppermute | solution.py:821
  478.8 32.4 %collective-permute-start.54 = (bf16[256,1664]{1,0:T(8,128)(2,1)}, bf16[256,1664]{1,0:T(8,128)(2,1)}, u32[]{:S(2)}, u32[]{:S(2)}) collective-permute-start(bf16[256,1664]{1,0:T(8,128)(2,1)} %dynamic-slice_bitcast_fusion.3), channel_id=1, source_target_pairs={{0,4},{4,0},{1,5},{5,1},{2,6},{6,2},{3,7},{7,3},{8,12},{12,8},{9,1... | collective-permute-start | bytes 2555912 | tf_op jit(solution)/shard_map/ppermute | solution.py:821
  481.9 33.9 %collective-permute-start.45 = (bf16[592,1024]{1,0:T(8,128)(2,1)}, bf16[592,1024]{1,0:T(8,128)(2,1)}, u32[]{:S(2)}, u32[]{:S(2)}) collective-permute-start(bf16[592,1024]{1,0:T(8,128)(2,1)} %fusion.10), channel_id=1, source_target_pairs={{0,1},{1,0},{2,3},{3,2},{4,5},{5,4},{6,7},{7,6},{8,9},{9,8},{10,11... | collective-permute-start | bytes 3637256 | tf_op jit(solution)/shard_map/ppermute | solution.py:821
  511.2 15.5 %collective-permute-start.60 = (bf16[32,5120]{1,0:T(8,128)(2,1)S(1)}, bf16[32,5120]{1,0:T(8,128)(2,1)S(1)}, u32[]{:S(2)}, u32[]{:S(2)}) collective-permute-start(bf16[32,5120]{1,0:T(8,128)(2,1)S(1)} %copy-done.81), channel_id=1, source_target_pairs={{0,16},{8,24},{16,0},{24,8},{1,17},{9,25},{17,1},{25,9},{2,18},{10... | collective-permute-start | bytes 983048 | tf_op jit(solution)/shard_map/ppermute | solution.py:893
  514.4 12.1 %collective-permute-start.50 = (bf16[128,1536]{1,0:T(8,128)(2,1)S(1)}, bf16[128,1536]{1,0:T(8,128)(2,1)S(1)}, u32[]{:S(2)}, u32[]{:S(2)}) collective-permute-start(bf16[128,1536]{1,0:T(8,128)(2,1)S(1)} %dynamic-slice_bitcast_fusion.14), channel_id=1, source_target_pairs={{0,1},{1,0},{2,3},{3,2},{4,5},{5,4},{6,7},{7,6},{8,9},{9,8},{10,11... | collective-permute-start | bytes 1179656 | tf_op jit(solution)/shard_map/ppermute | solution.py:821
  515.9 19.3 %collective-permute-start.55 = (bf16[128,1664]{1,0:T(8,128)(2,1)S(1)}, bf16[128,1664]{1,0:T(8,128)(2,1)}, u32[]{:S(2)}, u32[]{:S(2)}) collective-permute-start(bf16[128,1664]{1,0:T(8,128)(2,1)S(1)} %dynamic-slice_bitcast_fusion.13), channel_id=1, source_target_pairs={{0,1},{1,0},{2,3},{3,2},{4,5},{5,4},{6,7},{7,6},{8,9},{9,8},{10,11... | collective-permute-start | bytes 1277960 | tf_op jit(solution)/shard_map/ppermute | solution.py:821
  532.9 12.3 %collective-permute-start.52 = (bf16[32,1536]{1,0:T(8,128)(2,1)S(1)}, bf16[32,1536]{1,0:T(8,128)(2,1)S(1)}, u32[]{:S(2)}, u32[]{:S(2)}) collective-permute-start(bf16[32,1536]{1,0:T(8,128)(2,1)S(1)} %get-tuple-element.201), channel_id=1, source_target_pairs={{0,16},{8,24},{16,0},{24,8},{1,17},{9,25},{17,1},{25,9},{2,18},{10... | collective-permute-start | bytes 294920 | tf_op jit(solution)/shard_map/ppermute | solution.py:893
  (107 other events, 1124.4 us)
Sparse Core Ops, SparseCore 0:
  67.3 105.8 all-gather.1
